TPU v7x, 256 devices: a whole 4x4x8 slice. The times are simulated.
256 devices in a mesh: row: 8 (over z_lo, core), col: 32 (over z_hi, y, x).
Axes of the slice: x: 4, y: 4, z: 8 (z_hi: 2, z_lo: 4; z = z_hi * 4 + z_lo), core: 2. Of those that a mesh axis runs over, the one named last changes fastest.
Arguments:
- tokens: bfloat16 [1024, 16384], P('row', 'col'), may hold values from -6 to 6
- w_query: bfloat16 [16384, 8192], P('col', 'row'), may hold values from -0.078125 to 0.078125
- w_keyval: bfloat16 [16384, 1024], P('col', 'row'), may hold values from -0.078125 to 0.078125
- w_output: bfloat16 [8192, 16384], P('row', 'col'), may hold values from -0.0625 to 0.0625
Outputs:
- result: bfloat16 [1024, 16384], P('row', 'col')
All inputs are finite; a program needn't handle non-finite values.
Results may differ from a plain program's by a relative error of at most 0.02.
Values may be sent and summed in bfloat16 or wider, within the bound.
No kernel may reach another device: no remote copies, remote signals or barrier semaphores. Data moves between devices by JAX's collectives and lax.ppermute only.
A program may use at most 64 MiB of HBM per device.

v0:
```python
import math

import jax
import jax.numpy as jnp
from jax import lax
from jax.sharding import PartitionSpec as P

HQ = 64
KVH = 4
HD = 128


def angles(positions, width):
    half_width = width // 2
    frequency = 500000.0 ** (-(jnp.arange(half_width).astype(jnp.float32) * 2.0 / width))
    angle_v = positions[:, None] * frequency[None, :]
    return (jnp.cos(angle_v), jnp.sin(angle_v))


def rotate(values_in, cosine, sine_v):
    half_width = values_in.shape[-1] // 2
    lower_half = values_in[..., :half_width]
    upper_half = values_in[..., half_width:]
    return jnp.concatenate(
        [lower_half * cosine - upper_half * sine_v, upper_half * cosine + lower_half * sine_v], -1
    )


def shards(tokens, w_query, w_keyval, w_output):
    n_row = lax.axis_size("row")
    n_col = lax.axis_size("col")
    row_index = lax.axis_index("row")
    col_index = lax.axis_index("col")
    gathered = lax.all_gather(tokens, "row", axis=0, tiled=True)
    all_rows = gathered.shape[0]
    per_col = all_rows // n_col
    query_width = w_query.shape[1]
    keyval_width = w_keyval.shape[1]
    heads_local = query_width // HD
    heads_per_block = keyval_width // HD
    query_part = jnp.dot(gathered, w_query, preferred_element_type=jnp.float32)
    keyval_part = jnp.dot(gathered, w_keyval, preferred_element_type=jnp.float32)
    query_cols = lax.psum_scatter(query_part, "col", scatter_dimension=1, tiled=True)
    keyval_block = lax.psum_scatter(keyval_part, "col", scatter_dimension=0, tiled=True)
    query_local = lax.all_to_all(query_cols, "col", split_axis=0, concat_axis=1, tiled=True)
    keyval_all = lax.all_gather(
        keyval_block.astype(jnp.bfloat16), ("row", "col"), axis=0, tiled=True
    )
    keyval_heads = keyval_all.reshape(n_row, all_rows, heads_per_block, HD)
    pattern = "hrm,rtmd->htd"
    query_index = col_index * per_col + jnp.arange(per_col, dtype=jnp.int32)
    key_index = jnp.arange(all_rows, dtype=jnp.int32)
    query_cos, query_sin = angles(query_index.astype(jnp.float32), HD)
    key_cos, key_sin = angles(key_index.astype(jnp.float32), HD)
    query = rotate(
        query_local.reshape(per_col, heads_local, HD), query_cos[:, None, :], query_sin[:, None, :]
    ).astype(jnp.bfloat16)
    global_head = row_index * heads_local + jnp.arange(heads_local, dtype=jnp.int32)
    key_head = global_head // (HQ // KVH)
    block_head = (
        jnp.arange(n_row, dtype=jnp.int32)[:, None] * heads_per_block
        + jnp.arange(heads_per_block, dtype=jnp.int32)[None, :]
    )
    pick_keys = (block_head[None, :, :] == key_head[:, None, None]).astype(jnp.bfloat16)
    pick_values = (block_head[None, :, :] == (key_head + KVH)[:, None, None]).astype(jnp.bfloat16)
    keys_sel = jnp.einsum(pattern, pick_keys, keyval_heads, preferred_element_type=jnp.float32)
    keys = rotate(keys_sel, key_cos[None, :, :], key_sin[None, :, :]).astype(jnp.bfloat16)
    values = jnp.einsum(
        pattern, pick_values, keyval_heads, preferred_element_type=jnp.float32
    ).astype(jnp.bfloat16)
    score_scale = 1.0 / math.sqrt(HD)
    scores = (
        jnp.einsum("thd,hsd->hts", query, keys, preferred_element_type=jnp.float32) * score_scale
    )
    causal = (key_index[None, :] <= query_index[:, None])[None, :, :]
    weights_raw = jnp.where(causal, jnp.exp(jnp.where(causal, scores, 0.0)), 0.0)
    totals = jnp.sum(weights_raw, -1)
    weights_b = weights_raw.astype(jnp.bfloat16)
    heads_mixed = jnp.einsum("hts,hsd->thd", weights_b, values, preferred_element_type=jnp.float32)
    heads_mixed = heads_mixed / jnp.transpose(totals)[:, :, None]
    attended = heads_mixed.astype(jnp.bfloat16).reshape(per_col, query_width)
    partial_out = jnp.dot(
        lax.all_gather(attended, "col", axis=0, tiled=True),
        w_output,
        preferred_element_type=jnp.float32,
    )
    return lax.psum_scatter(
        partial_out.astype(jnp.bfloat16), "row", scatter_dimension=0, tiled=True
    )


def solution(mesh):
    return jax.shard_map(
        shards,
        mesh=mesh,
        in_specs=(P("row", "col"), P("col", "row"), P("col", "row"), P("row", "col")),
        out_specs=P("row", "col"),
        check_vma=False,
    )
```

profile of v0, /device:TPU:1, one launch (start us, length us, event | category | flops | bytes accessed | tf_op | source)
XLA Modules:
  0.0 1359.7 jit_solution(6192898784604710600)
XLA Ops:
  7.3 40.1 %all-gather.4.cloned.1.call-done = bf16[1024,512]{1,0:T(8,128)(2,1)} async-done(((bf16[128,512]{1,0:T(8,128)(2,1)}), bf16[1024,512]{1,0:T(8,128)(2,1)}) %all-gather.4.cloned.1.call-update) | async-done | bytes 1048592 | tf_op jit(solution)/shard_map/all_gather | solution.py:34
  47.4 2.6 fusion.45
  50.1 201.4 %reduce-scatter.4.cloned.1.call-done = f32[32,128]{1,0:T(8,128)} async-done(((f32[1024,128]{1,0:T(8,128)}), f32[32,128]{1,0:T(8,128)}) %reduce-scatter.4.cloned.1.call-update) | async-done | bytes 16400 | tf_op jit(solution)/shard_map/reduce_scatter | solution.py:44
  251.4 1.3 convert_element_type.55
  252.9 3.3 fusion.46
  256.4 1.9 multiply_cosine_fusion
  258.3 708.1 %all-gather.6.cloned.1.call-done = bf16[8192,128]{1,0:T(8,128)(2,1)} async-done(((bf16[32,128]{1,0:T(8,128)(2,1)}), bf16[8192,128]{1,0:T(8,128)(2,1)}) %all-gather.6.cloned.1.call-update) | async-done | bytes 2097168 | tf_op jit(solution)/shard_map/all_gather | solution.py:46
  966.5 2.9 fusion.4
  969.4 1.8 subtract_convert_fusion
  971.2 2.5 pad_maximum_fusion
  973.7 205.7 %reduce-scatter.6.cloned.1.call-done = f32[1024,32]{0,1:T(8,128)} async-done(((f32[1024,1024]{0,1:T(8,128)}), f32[1024,32]{0,1:T(8,128)}) %reduce-scatter.6.cloned.1.call-update) | async-done | bytes 131088 | tf_op jit(solution)/shard_map/reduce_scatter | solution.py:43
  1179.4 1.9 copy.22
  1181.3 1.9 reshape.298
  1183.3 9.3 all-to-all-start
  1192.8 2.7 convolution_convert_fusion
  1195.5 8.5 all-to-all-done
  1204.4 0.9 reduce
  1205.4 1.0 reshape.299
  1206.4 2.1 copy.15
  1208.5 1.2 reshape.294
  1209.9 1.0 fusion.44
  1212.8 106.2 %all-gather.8.cloned.1.call-done = bf16[1024,1024]{1,0:T(8,128)(2,1)} async-done(((bf16[32,1024]{1,0:T(8,128)(2,1)}), bf16[1024,1024]{1,0:T(8,128)(2,1)}) %all-gather.8.cloned.1.call-update) | async-done | bytes 2097168 | tf_op jit(solution)/shard_map/all_gather | solution.py:83
  1319.0 3.8 convolution_convert_fusion.1
  1322.8 30.0 %reduce-scatter.8.cloned.1.call-done = bf16[128,512]{1,0:T(8,128)(2,1)} async-done(((bf16[1024,512]{1,0:T(8,128)(2,1)}), bf16[128,512]{1,0:T(8,128)(2,1)}) %reduce-scatter.8.cloned.1.call-update) | async-done | bytes 131088 | tf_op jit(solution)/shard_map/reduce_scatter | solution.py:87
  (35 shorter events, 3.9 us)
Async XLA Ops:
  6.5 246.3 %copy-start = (bf16[512,1024]{1,0:T(8,128)(2,1)S(1)}, bf16[512,1024]{1,0:T(8,128)(2,1)}, u32[]{:S(2)}) copy-start(bf16[512,1024]{1,0:T(8,128)(2,1)} %param.5) | copy-start | bytes 3145732
  6.5 40.9 %all-gather.4.cloned.1.call-start = ((), (), s32[]{:S(2)}) async-start(), calls=%async_computation.4 | async-start | bytes 1179648 | tf_op jit(solution)/shard_map/all_gather | solution.py:34
  7.3 244.2 %reduce-scatter.4.cloned.1.call-start = ((), (), s32[]{:S(2)}) async-start(), calls=%async_computation.5 | async-start | bytes 540672 | tf_op jit(solution)/shard_map/reduce_scatter | solution.py:44
  47.4 205.4 %copy-start.4 = (bf16[1024,512]{1,0:T(8,128)(2,1)S(1)}, bf16[1024,512]{1,0:T(8,128)(2,1)}, u32[]{:S(2)}) copy-start(bf16[1024,512]{1,0:T(8,128)(2,1)} %all-gather.4.cloned.1.call-done) | copy-start | bytes 3145732
  50.0 916.4 %all-gather.6.cloned.1.call-start = ((), (), s32[]{:S(2)}) async-start(), calls=%async_computation.6 | async-start | bytes 2105344 | tf_op jit(solution)/shard_map/all_gather | solution.py:46
  252.8 926.6 %reduce-scatter.6.cloned.1.call-start = ((), (), s32[]{:S(2)}) async-start(), calls=%async_computation.7 | async-start | bytes 4325376 | tf_op jit(solution)/shard_map/reduce_scatter | solution.py:43
  971.2 221.6 %copy-start.1 = (bf16[8192,128]{1,0:T(8,128)(2,1)S(1)}, bf16[8192,128]{1,0:T(8,128)(2,1)}, u32[]{:S(2)}) copy-start(bf16[8192,128]{1,0:T(8,128)(2,1)} %all-gather.6.cloned.1.call-done) | copy-start | bytes 6291460
  1183.3 20.7 %all-to-all-start = ((f32[32,1,1024]{2,1,0:T(1,128)}), f32[32,1,1024]{2,1,0:T(1,128)S(1)}, u32[]{:S(2)}, u32[]{:S(2)}) async-start(f32[32,1,1024]{2,1,0:T(1,128)} %reshape.298), calls=%async_computation.2 | async-start | bytes 262144 | tf_op jit(solution)/shard_map/all_to_all | solution.py:45
  1192.5 126.5 %all-gather.8.cloned.1.call-start = ((), (), s32[]{:S(2)}) async-start(), calls=%async_computation.8 | async-start | bytes 2162688 | tf_op jit(solution)/shard_map/all_gather | solution.py:83
  1195.5 14.4 %copy-start.2 = (bf16[8,1024,128]{2,0,1:T(8,128)(2,1)S(1)}, bf16[8,1024,128]{2,0,1:T(8,128)(2,1)}, u32[]{:S(2)}) copy-start(bf16[8,1024,128]{2,0,1:T(8,128)(2,1)} %pad_maximum_fusion) | copy-start | bytes 6291460
  1209.9 1.6 copy-start.3
  1211.0 108.1 %copy-start.5 = (bf16[1024,512]{1,0:T(8,128)(2,1)S(1)}, bf16[1024,512]{1,0:T(8,128)(2,1)}, u32[]{:S(2)}) copy-start(bf16[1024,512]{1,0:T(8,128)(2,1)} %param.7) | copy-start | bytes 3145732
  1212.8 140.1 %reduce-scatter.8.cloned.1.call-start = ((), (), s32[]{:S(2)}) async-start(), calls=%async_computation.9 | async-start | bytes 1179648 | tf_op jit(solution)/shard_map/reduce_scatter | solution.py:87
Sparse Core Ops, SparseCore 0:
  9.1 38.2 all-gather.3
  50.1 201.2 reduce-scatter.3
  253.5 712.9 all-gather.5
  969.0 210.3 reduce-scatter.5
  1212.9 106.0 all-gather.7
  1323.0 29.8 reduce-scatter.7
where the time goes:
time: 1360 us
  waiting for transfers between devices  1300 us (96%)
  matrix products  16.9 us (1%)
  between operations  13.6 us (1%)
    all_gather x1, waiting for transfers between devices, shards(): lax.all_gather(keyval_block.astype(jnp.bfloat16), ('row', 'col'), axis=0,...  708 us
    reduce_scatter x1, waiting for transfers between devices, shards(): lax.psum_scatter(query_part, 'col', scatter_dimension=1, tiled=True)  206 us
    reduce_scatter x1, waiting for transfers between devices, shards(): lax.psum_scatter(keyval_part, 'col', scatter_dimension=0, tiled=True)  201 us
    all_gather x1, waiting for transfers between devices, shards(): lax.all_gather(attended, 'col', axis=0, tiled=True)  106 us
    all_gather x1, waiting for transfers between devices, shards(): gathered = lax.all_gather(tokens, 'row', axis=0, tiled=True)  40.1 us
    reduce_scatter x1, waiting for transfers between devices, shards(): lax.psum_scatter(partial_out.astype(jnp.bfloat16), 'row', scatter_dimensi...  30 us
  transfers between devices with their start and end apart: 7, of which 7 were waited for; matrix products, arithmetic and copies ran while one was open for 1% of the time, Pallas kernels for 0%

commit v1 on v0

v1 whole, which is shorter than its diff:
```python
import math

import jax
import jax.numpy as jnp
from jax import lax
from jax.sharding import Mesh
from jax.sharding import PartitionSpec as P

HD = 128
Z_LO, CORE, Z_HI, Y, X = 4, 2, 2, 4, 4
ROW = ("zl", "core")
COL = ("zh", "y", "x")
PLANE = ("y", "x")
BF16 = jnp.bfloat16
F32 = jnp.float32


def angles(positions, width):
    half_width = width // 2
    frequency = 500000.0 ** (-(jnp.arange(half_width).astype(F32) * 2.0 / width))
    angle_v = positions[:, None] * frequency[None, :]
    return (jnp.cos(angle_v), jnp.sin(angle_v))


def rotate(values_in, cosine, sine_v):
    half_width = values_in.shape[-1] // 2
    lower_half = values_in[..., :half_width]
    upper_half = values_in[..., half_width:]
    return jnp.concatenate(
        [lower_half * cosine - upper_half * sine_v, upper_half * cosine + lower_half * sine_v], -1
    )


def gather(block, axes, count):
    spread = jnp.broadcast_to(block[None], (count, *block.shape))
    return lax.all_to_all(spread, axes, 0, 0, tiled=True)


def swap(block, axis):
    return lax.ppermute(block, axis, ((0, 1), (1, 0)))


def shards(tokens, w_query, w_keyval, w_output):
    core = lax.axis_index("core")
    chunk = lax.axis_index("y") * X + lax.axis_index("x")
    per_row, features = tokens.shape
    half = per_row * Z_LO
    total = half * 2
    per_chunk = total // (Y * X)
    width = w_query.shape[1]
    heads = width // HD

    kv_moves = [(e, 2 * e if e < 4 else 2 * (e - 4) + 1) for e in range(8)]
    w_kv = lax.ppermute(w_keyval, ROW, kv_moves)

    mine = gather(tokens, "zl", Z_LO).reshape(half, features)
    other = swap(mine, "core")
    everyone = jnp.concatenate([mine, other], 0)
    query_part = jnp.dot(everyone, w_query, preferred_element_type=F32).astype(BF16)
    kv_part = jnp.dot(everyone, w_kv, preferred_element_type=F32).astype(BF16)
    part = jnp.concatenate([query_part, kv_part], 1)

    part = part.reshape(Y * X, per_chunk, width + HD)
    part = lax.all_to_all(part, PLANE, 0, 0, tiled=True)
    part = jnp.sum(part.astype(F32), 0).astype(BF16)
    sums = part.astype(F32) + swap(part, "zh").astype(F32)

    def positions(index):
        side = index // half
        inner = index % half
        which = jnp.where(side == 0, core, 1 - core)
        return (inner // per_row) * (2 * per_row) + which * per_row + inner % per_row

    query_pos = positions(chunk * per_chunk + jnp.arange(per_chunk, dtype=jnp.int32))
    key_pos = positions(jnp.arange(total, dtype=jnp.int32))
    cosine, sine_v = angles(query_pos.astype(F32), HD)

    kv_own = sums[:, width:].astype(BF16)
    kv_rot = rotate(kv_own.astype(F32), cosine, sine_v).astype(BF16)
    kv_own = jnp.where(core == 0, kv_rot, kv_own)
    kv_all = gather(kv_own, PLANE, Y * X).reshape(total, HD)
    kv_got = swap(kv_all, "core")
    kv_got = jnp.concatenate([kv_got[half:], kv_got[:half]], 0)
    keys = jnp.where(core == 0, kv_all, kv_got)
    values = jnp.where(core == 0, kv_got, kv_all)

    query = rotate(
        sums[:, :width].reshape(per_chunk, heads, HD), cosine[:, None, :], sine_v[:, None, :]
    ).astype(BF16)
    query = jnp.transpose(query, (1, 0, 2))
    scores = jnp.einsum("htd,sd->hts", query, keys, preferred_element_type=F32) * (
        1.0 / math.sqrt(HD)
    )
    causal = (key_pos[None, :] <= query_pos[:, None])[None]
    weights_raw = jnp.where(causal, jnp.exp(jnp.where(causal, scores, 0.0)), 0.0)
    totals = jnp.sum(weights_raw, -1)
    mixed = jnp.einsum(
        "hts,sd->htd", weights_raw.astype(BF16), values, preferred_element_type=F32
    )
    attended = (mixed / totals[:, :, None]).astype(BF16)
    attended = jnp.transpose(attended, (1, 0, 2)).reshape(per_chunk, width)

    attended_all = gather(attended, PLANE, Y * X).reshape(total, width)
    partial_out = jnp.dot(attended_all, w_output, preferred_element_type=F32).astype(BF16)
    kept, sent = partial_out[:half], partial_out[half:]
    chip = (kept.astype(F32) + swap(sent, "core").astype(F32)).astype(BF16)
    chip = chip.reshape(Z_LO, per_row, features)
    chip = lax.all_to_all(chip, "zl", 0, 0, tiled=True)
    return jnp.sum(chip.astype(F32), 0).astype(BF16)


def solution(mesh):
    fine = Mesh(
        mesh.devices.reshape(Z_LO, CORE, Z_HI, Y, X), ("zl", "core", "zh", "y", "x")
    )
    return jax.shard_map(
        shards,
        mesh=fine,
        in_specs=(P(ROW, COL), P(COL, ROW), P(COL, ROW), P(ROW, COL)),
        out_specs=P(ROW, COL),
        check_vma=False,
    )
```

time: 1360 us -> 154 us (0.11)
  waiting for transfers between devices: 1300 us -> 46.8 us
  blocking collectives: 0 us -> 70.6 us
  starting transfers between devices: 9.67 us -> 23.3 us
    all_gather x3 -> x0, waiting for transfers between devices: 854 us -> none  [the longest x1 708 us: shards(): lax.all_gather(keyval_block.astype(jnp.bfloat16), ('row', 'col'), axis=0,...]
    reduce_scatter x3 -> x0, waiting for transfers between devices: 437 us -> none  [the longest x1 206 us: shards(): lax.psum_scatter(query_part, 'col', scatter_dimension=1, tiled=True)]
    all_to_all x0 -> x3, blocking collectives: none -> 70.6 us  [the longest x2 50.2 us: gather(): return lax.all_to_all(spread, axes, 0, 0, tiled=True)]
    all_to_all x1 -> x2, waiting for transfers between devices: 8.46 us -> 36.4 us  [the longest x1 29.7 us: shards(): part = lax.all_to_all(part, PLANE, 0, 0, tiled=True)]
  transfers between devices with their start and end apart: 7 -> 7, of which waited for: 7 -> 6; matrix products, arithmetic and copies ran while one was open for 1% -> 2% of each run, Pallas kernels for 0% -> 0%
where the time goes in v1:
time: 154 us
  blocking collectives  70.6 us (46%)
  waiting for transfers between devices  46.8 us (30%)
  starting transfers between devices  23.3 us (15%)
  local copies, waits for them, and re-layouts  4.87 us (3%)
  matrix products  4.35 us (3%)
  other arithmetic  3.92 us (3%)
    all_to_all x2, blocking collectives, gather(): return lax.all_to_all(spread, axes, 0, 0, tiled=True)  50.2 us
    all_to_all x1, waiting for transfers between devices, shards(): part = lax.all_to_all(part, PLANE, 0, 0, tiled=True)  29.7 us
    all_to_all x1, blocking collectives, shards(): chip = lax.all_to_all(chip, 'zl', 0, 0, tiled=True)  20.4 us
    ppermute x4, starting transfers between devices, swap(): return lax.ppermute(block, axis, ((0, 1), (1, 0)))  10.7 us
    all_to_all x1, starting transfers between devices, shards(): part = lax.all_to_all(part, PLANE, 0, 0, tiled=True)  6.76 us
    all_to_all x1, waiting for transfers between devices, gather(): return lax.all_to_all(spread, axes, 0, 0, tiled=True)  6.7 us
    ppermute x4, waiting for transfers between devices, swap(): return lax.ppermute(block, axis, ((0, 1), (1, 0)))  6.22 us
    ppermute x1, waiting for transfers between devices, shards(): w_kv = lax.ppermute(w_keyval, ROW, kv_moves)  4.12 us
  transfers between devices with their start and end apart: 7, of which 6 were waited for; matrix products, arithmetic and copies ran while one was open for 2% of the time, Pallas kernels for 0%

profile of v1, /device:TPU:1, one launch (start us, length us, event | category | flops | bytes accessed | tf_op | source)
XLA Modules:
  0.0 154.0 jit_solution(11729280465021472872)
XLA Ops:
  0.0 1.0 broadcast_in_dim.64
  1.0 19.9 %all_to_all.25 = bf16[4,128,512]{2,1,0:T(8,128)(2,1)S(1)} all-to-all(bf16[4,128,512]{2,1,0:T(8,128)(2,1)S(1)} %broadcast_in_dim.64), channel_id=1, replica_groups=mesh['zl'=4,'core'=2,'zh'=2,'y'=4,'x'=4] {'zl'}, dimensions={0} | all-to-all | bytes 1048576 | tf_op jit(solution)/shard_map/all_to_all | solution.py:36
  20.9 1.8 %collective-permute-start = (bf16[512,512]{1,0:T(8,128)(2,1)S(1)}, bf16[512,512]{1,0:T(8,128)(2,1)S(1)}, u32[]{:S(2)}, u32[]{:S(2)}) collective-permute-start(bf16[512,512]{1,0:T(8,128)(2,1)S(1)} %bitcast.45), channel_id=1, source_target_pairs={{0,32},{32,0},{1,33},{33,1},{2,34},{34,2},{3,35},{35,3},{4,36},{36... | collective-permute-start | bytes 1572872 | tf_op jit(solution)/shard_map/ppermute | solution.py:40
  22.7 1.9 %collective-permute-start.1 = (bf16[512,128]{1,0:T(8,128)(2,1)}, bf16[512,128]{1,0:T(8,128)(2,1)S(1)}, u32[]{:S(2)}, u32[]{:S(2)}) collective-permute-start(bf16[512,128]{1,0:T(8,128)(2,1)} %param.6), channel_id=1, source_target_pairs={{0,0},{32,64},{64,128},{96,192},{128,32},{160,96},{192,160},{224,2... | collective-permute-start | bytes 393224 | tf_op jit(solution)/shard_map/ppermute | solution.py:54
  24.7 1.3 convolution_convert_fusion
  26.0 4.1 %collective-permute-done.1 = bf16[512,128]{1,0:T(8,128)(2,1)S(1)} collective-permute-done((bf16[512,128]{1,0:T(8,128)(2,1)}, bf16[512,128]{1,0:T(8,128)(2,1)S(1)}, u32[]{:S(2)}, u32[]{:S(2)}) %collective-permute-start.1) | collective-permute-done | bytes 131104 | tf_op jit(solution)/shard_map/ppermute | solution.py:54
  30.8 2.6 %copy.5 = bf16[1024,1152]{1,0:T(8,128)(2,1)} copy(bf16[1024,1152]{0,1:T(8,128)(2,1)S(1)} %pad_maximum_fusion) | data formatting | bytes 4718592 | tf_op jit(solution)/shard_map/concatenate | solution.py:61
  33.4 6.8 %all-to-all-start.1 = ((bf16[16,64,1152]{2,1,0:T(8,128)(2,1)}), bf16[16,64,1152]{2,1,0:T(8,128)(2,1)S(1)}, u32[]{:S(2)}, u32[]{:S(2)}) async-start(bf16[16,64,1152]{2,1,0:T(8,128)(2,1)} %bitcast.40), calls=%async_computation.1 | async-start | bytes 4718592 | tf_op jit(solution)/shard_map/all_to_all | solution.py:64
  40.8 29.7 %all-to-all-done.1 = bf16[16,64,1152]{2,1,0:T(8,128)(2,1)S(1)} async-done(((bf16[16,64,1152]{2,1,0:T(8,128)(2,1)}), bf16[16,64,1152]{2,1,0:T(8,128)(2,1)S(1)}, u32[]{:S(2)}, u32[]{:S(2)}) %all-to-all-start.1) | async-done | bytes 2359328 | tf_op jit(solution)/shard_map/all_to_all | solution.py:64
  70.8 4.3 %collective-permute-start.2 = (bf16[64,1152]{1,0:T(8,128)(2,1)S(1)}, bf16[64,1152]{1,0:T(8,128)(2,1)S(1)}, u32[]{:S(2)}, u32[]{:S(2)}) collective-permute-start(bf16[64,1152]{1,0:T(8,128)(2,1)S(1)} %reduce_sum.33), channel_id=1, source_target_pairs={{0,16},{16,0},{1,17},{17,1},{2,18},{18,2},{3,19},{19,3},{4,20},{20... | collective-permute-start | bytes 442376 | tf_op jit(solution)/shard_map/ppermute | solution.py:40
  75.1 3.8 %collective-permute-done.2 = bf16[64,1152]{1,0:T(8,128)(2,1)S(1)} collective-permute-done((bf16[64,1152]{1,0:T(8,128)(2,1)S(1)}, bf16[64,1152]{1,0:T(8,128)(2,1)S(1)}, u32[]{:S(2)}, u32[]{:S(2)}) %collective-permute-start.2) | collective-permute-done | bytes 147488 | tf_op jit(solution)/shard_map/ppermute | solution.py:40
  78.9 0.8 multiply_cosine_fusion
  79.9 0.7 broadcast_in_dim.65
  80.6 3.9 %all-to-all-start.2 = ((bf16[16,64,128]{2,1,0:T(8,128)(2,1)}), bf16[16,64,128]{2,1,0:T(8,128)(2,1)S(1)}, u32[]{:S(2)}, u32[]{:S(2)}) async-start(bf16[16,64,128]{2,1,0:T(8,128)(2,1)} %broadcast_in_dim.65), calls=%async_computation.2 | async-start | bytes 524288 | tf_op jit(solution)/shard_map/all_to_all | solution.py:36
  84.5 0.8 broadcast_compare_fusion
  85.4 6.7 %all-to-all-done.2 = bf16[16,64,128]{2,1,0:T(8,128)(2,1)S(1)} async-done(((bf16[16,64,128]{2,1,0:T(8,128)(2,1)}), bf16[16,64,128]{2,1,0:T(8,128)(2,1)S(1)}, u32[]{:S(2)}, u32[]{:S(2)}) %all-to-all-start.2) | async-done | bytes 262176 | tf_op jit(solution)/shard_map/all_to_all | solution.py:36
  92.1 2.7 %collective-permute-start.3 = (bf16[1024,128]{1,0:T(8,128)(2,1)S(1)}, bf16[1024,128]{1,0:T(8,128)(2,1)S(1)}, u32[]{:S(2)}, u32[]{:S(2)}) collective-permute-start(bf16[1024,128]{1,0:T(8,128)(2,1)S(1)} %bitcast.48), channel_id=1, source_target_pairs={{0,32},{32,0},{1,33},{33,1},{2,34},{34,2},{3,35},{35,3},{4,36},{36... | collective-permute-start | bytes 786440 | tf_op jit(solution)/shard_map/ppermute | solution.py:40
  95.1 0.9 collective-permute-done.3
  96.0 0.8 fusion.38
  97.6 30.4 %all_to_all.26 = bf16[16,64,1024]{2,1,0:T(8,128)(2,1)S(1)} all-to-all(bf16[16,64,1024]{2,1,0:T(8,128)(2,1)S(1)} %broadcast_in_dim.68), channel_id=1, replica_groups=mesh['zl'=4,'core'=2,'zh'=2,'y'=4,'x'=4] {'y','x'}, dimensions={0} | all-to-all | bytes 4194304 | tf_op jit(solution)/shard_map/all_to_all | solution.py:36
  128.0 1.2 convolution_convert_fusion.1
  129.3 1.9 %collective-permute-start.4 = (bf16[512,512]{1,0:T(8,128)(2,1)S(1)}, bf16[512,512]{1,0:T(8,128)(2,1)S(1)}, u32[]{:S(2)}, u32[]{:S(2)}) collective-permute-start(bf16[512,512]{1,0:T(8,128)(2,1)S(1)} %slice.50), channel_id=1, source_target_pairs={{0,32},{32,0},{1,33},{33,1},{2,34},{34,2},{3,35},{35,3},{4,36},{36... | collective-permute-start | bytes 1572872 | tf_op jit(solution)/shard_map/ppermute | solution.py:40
  131.2 1.5 collective-permute-done.4
  132.8 20.4 %all_to_all.27 = bf16[4,128,512]{2,1,0:T(8,128)(2,1)S(1)} all-to-all(bf16[4,128,512]{2,1,0:T(8,128)(2,1)S(1)} %bitcast.42), channel_id=1, replica_groups=mesh['zl'=4,'core'=2,'zh'=2,'y'=4,'x'=4] {'zl'}, dimensions={0} | all-to-all | bytes 1048576 | tf_op jit(solution)/shard_map/all_to_all | solution.py:108
  (25 shorter events, 3.8 us)
Async XLA Ops:
  0.0 24.7 %copy-start = (bf16[512,1024]{1,0:T(8,128)(2,1)S(1)}, bf16[512,1024]{1,0:T(8,128)(2,1)}, u32[]{:S(2)}) copy-start(bf16[512,1024]{1,0:T(8,128)(2,1)} %param.5) | copy-start | bytes 3145732
  20.9 3.7 %collective-permute-start = (bf16[512,512]{1,0:T(8,128)(2,1)S(1)}, bf16[512,512]{1,0:T(8,128)(2,1)S(1)}, u32[]{:S(2)}, u32[]{:S(2)}) collective-permute-start(bf16[512,512]{1,0:T(8,128)(2,1)S(1)} %bitcast.45), channel_id=1, source_target_pairs={{0,32},{32,0},{1,33},{33,1},{2,34},{34,2},{3,35},{35,3},{4,36},{36... | collective-permute-start | bytes 1572872 | tf_op jit(solution)/shard_map/ppermute | solution.py:40
  22.7 7.4 %collective-permute-start.1 = (bf16[512,128]{1,0:T(8,128)(2,1)}, bf16[512,128]{1,0:T(8,128)(2,1)S(1)}, u32[]{:S(2)}, u32[]{:S(2)}) collective-permute-start(bf16[512,128]{1,0:T(8,128)(2,1)} %param.6), channel_id=1, source_target_pairs={{0,0},{32,64},{64,128},{96,192},{128,32},{160,96},{192,160},{224,2... | collective-permute-start | bytes 393224 | tf_op jit(solution)/shard_map/ppermute | solution.py:54
  33.4 37.1 %all-to-all-start.1 = ((bf16[16,64,1152]{2,1,0:T(8,128)(2,1)}), bf16[16,64,1152]{2,1,0:T(8,128)(2,1)S(1)}, u32[]{:S(2)}, u32[]{:S(2)}) async-start(bf16[16,64,1152]{2,1,0:T(8,128)(2,1)} %bitcast.40), calls=%async_computation.1 | async-start | bytes 4718592 | tf_op jit(solution)/shard_map/all_to_all | solution.py:64
  70.8 8.1 %collective-permute-start.2 = (bf16[64,1152]{1,0:T(8,128)(2,1)S(1)}, bf16[64,1152]{1,0:T(8,128)(2,1)S(1)}, u32[]{:S(2)}, u32[]{:S(2)}) collective-permute-start(bf16[64,1152]{1,0:T(8,128)(2,1)S(1)} %reduce_sum.33), channel_id=1, source_target_pairs={{0,16},{16,0},{1,17},{17,1},{2,18},{18,2},{3,19},{19,3},{4,20},{20... | collective-permute-start | bytes 442376 | tf_op jit(solution)/shard_map/ppermute | solution.py:40
  80.6 11.5 %all-to-all-start.2 = ((bf16[16,64,128]{2,1,0:T(8,128)(2,1)}), bf16[16,64,128]{2,1,0:T(8,128)(2,1)S(1)}, u32[]{:S(2)}, u32[]{:S(2)}) async-start(bf16[16,64,128]{2,1,0:T(8,128)(2,1)} %broadcast_in_dim.65), calls=%async_computation.2 | async-start | bytes 524288 | tf_op jit(solution)/shard_map/all_to_all | solution.py:36
  92.1 3.9 %collective-permute-start.3 = (bf16[1024,128]{1,0:T(8,128)(2,1)S(1)}, bf16[1024,128]{1,0:T(8,128)(2,1)S(1)}, u32[]{:S(2)}, u32[]{:S(2)}) collective-permute-start(bf16[1024,128]{1,0:T(8,128)(2,1)S(1)} %bitcast.48), channel_id=1, source_target_pairs={{0,32},{32,0},{1,33},{33,1},{2,34},{34,2},{3,35},{35,3},{4,36},{36... | collective-permute-start | bytes 786440 | tf_op jit(solution)/shard_map/ppermute | solution.py:40
  97.6 30.4 %copy-start.1 = (bf16[1024,512]{1,0:T(8,128)(2,1)S(1)}, bf16[1024,512]{1,0:T(8,128)(2,1)}, u32[]{:S(2)}) copy-start(bf16[1024,512]{1,0:T(8,128)(2,1)} %param.7) | copy-start | bytes 3145732
  129.3 3.4 %collective-permute-start.4 = (bf16[512,512]{1,0:T(8,128)(2,1)S(1)}, bf16[512,512]{1,0:T(8,128)(2,1)S(1)}, u32[]{:S(2)}, u32[]{:S(2)}) collective-permute-start(bf16[512,512]{1,0:T(8,128)(2,1)S(1)} %slice.50), channel_id=1, source_target_pairs={{0,32},{32,0},{1,33},{33,1},{2,34},{34,2},{3,35},{35,3},{4,36},{36... | collective-permute-start | bytes 1572872 | tf_op jit(solution)/shard_map/ppermute | solution.py:40

commit v2 on v1

v2 whole, which is shorter than its diff:
```python
import functools
import math

import jax
import jax.numpy as jnp
from jax import lax
from jax.experimental import pallas as pl
from jax.experimental.pallas import tpu as pltpu
from jax.sharding import Mesh
from jax.sharding import PartitionSpec as P

HD = 128
Z_LO, CORE, Z_HI, Y, X = 4, 2, 2, 4, 4
ROW = ("zl", "core")
COL = ("zh", "y", "x")
PLANE = ("y", "x")
BF16 = jnp.bfloat16
F32 = jnp.float32
VMEM = pl.BlockSpec(memory_space=pltpu.VMEM)
SMEM = pl.BlockSpec(memory_space=pltpu.SMEM)
PARAMS = pltpu.CompilerParams(vmem_limit_bytes=32 * 1024 * 1024)


def tables(positions, width):
    half_width = width // 2
    frequency = 500000.0 ** (-(jnp.arange(half_width).astype(F32) * 2.0 / width))
    angle_v = positions[:, None] * frequency[None, :]
    cosine, sine_v = jnp.cos(angle_v), jnp.sin(angle_v)
    return jnp.concatenate([cosine, cosine], 1), jnp.concatenate([-sine_v, sine_v], 1)


def rotate(values_in, cosine, sine_v):
    return values_in * cosine + pltpu.roll(values_in, HD // 2, 1) * sine_v


def partner(block, axis, step):
    size = {"zl": Z_LO, "core": CORE, "zh": Z_HI, "y": Y, "x": X}[axis]
    return lax.ppermute(block, axis, [(i, i ^ step) for i in range(size)])


def kv_kernel(pick, *refs):
    blocks, weight, outs, parts = refs[:8], refs[8], refs[9:13], refs[13]
    rows = blocks[0].shape[0]
    for i, block in enumerate(blocks):
        product = jnp.dot(block[...], weight[...], preferred_element_type=F32)
        parts[i // 2, pl.ds((i % 2) * rows, rows), :] = product.astype(BF16)
    for s, out in enumerate(outs):
        out[...] = parts[pick[s]]


def query_kernel(*refs):
    blocks, weight, out = refs[:8], refs[8], refs[9]
    per_chunk = out.shape[1]
    for i, block in enumerate(blocks):
        product = jnp.dot(block[...], weight[...], preferred_element_type=F32).astype(BF16)
        out[2 * i] = product[:per_chunk]
        out[2 * i + 1] = product[per_chunk:]


def keys_kernel(a, b, cosine, sine_v, out):
    total = (a[...].astype(F32) + b[...].astype(F32)).astype(BF16).astype(F32)
    out[...] = rotate(total, cosine[...], sine_v[...]).astype(BF16)


def attention_kernel(heads, base, own, got, cosine, sine_v, *refs):
    keys, values, out, queries = refs[:4], refs[4:8], refs[8], refs[9]
    per_chunk = own.shape[0]
    for h in range(heads):
        cols = slice(h * HD, (h + 1) * HD)
        total = own[:, cols].astype(F32) + got[:, cols].astype(F32)
        queries[h * per_chunk : (h + 1) * per_chunk, :] = rotate(
            total, cosine[...], sine_v[...]
        ).astype(BF16)
    query = queries[...]
    rows = heads * per_chunk
    row_pos = base[8] + lax.broadcasted_iota(jnp.int32, (rows, HD), 0) % per_chunk
    lane = lax.broadcasted_iota(jnp.int32, (rows, HD), 1)
    score_scale = 1.0 / math.sqrt(HD)
    totals = jnp.zeros((rows, 1), F32)
    mixed = jnp.zeros((rows, HD), F32)
    for s in range(4):
        scores = (
            lax.dot_general(
                query, keys[s][...], (((1,), (1,)), ((), ())), preferred_element_type=F32
            )
            * score_scale
        )
        causal = jnp.concatenate(
            [base[2 * s] + lane <= row_pos, base[2 * s + 1] + lane <= row_pos], 1
        )
        weights = jnp.where(causal, jnp.exp(jnp.where(causal, scores, 0.0)), 0.0)
        totals += jnp.sum(weights, 1, keepdims=True)
        mixed += jnp.dot(weights.astype(BF16), values[s][...], preferred_element_type=F32)
    attended = (mixed / totals).astype(BF16)
    for h in range(heads):
        block = attended[h * per_chunk : (h + 1) * per_chunk]
        for c in range(out.shape[0]):
            out[c, :, h * HD : (h + 1) * HD] = block


def chip_kernel(kept, got, *outs):
    rows = outs[0].shape[0]
    for s, out in enumerate(outs):
        part = slice(s * rows, (s + 1) * rows)
        out[...] = (kept[part, :].astype(F32) + got[part, :].astype(F32)).astype(BF16)


def call(kernel, outs, args, scratch=(), scalars=0):
    return pl.pallas_call(
        kernel,
        out_shape=[jax.ShapeDtypeStruct(s, BF16) for s in outs],
        in_specs=[SMEM] * scalars + [VMEM] * (len(args) - scalars),
        out_specs=[VMEM] * len(outs),
        scratch_shapes=list(scratch),
        compiler_params=PARAMS,
    )(*args)


def shards(tokens, w_query, w_keyval, w_output):
    zl = lax.axis_index("zl")
    core = lax.axis_index("core")
    y = lax.axis_index("y")
    x = lax.axis_index("x")
    per_row, features = tokens.shape
    half = per_row * Z_LO
    total = half * 2
    per_chunk = total // (Y * X)
    quarter = total // X
    width = w_query.shape[1]
    heads = width // HD

    mine = [tokens] + [partner(tokens, "zl", s) for s in (1, 2, 3)]
    others = [partner(block, "core", 1) for block in mine]
    everyone = mine + others
    kv_moves = [(e, 2 * e if e < 4 else 2 * (e - 4) + 1) for e in range(8)]
    w_kv = lax.ppermute(w_keyval, ROW, kv_moves)

    def block_start(chip_step, side):
        return (2 * (zl ^ chip_step) + side) * per_row

    starts = []
    for s in range(X):
        j = x ^ s
        for b in range(2):
            starts.append(block_start(2 * (j % 2) + b, j // 2))
    chunk = y * X + x
    row_block = chunk // 2
    row_start = block_start(row_block % 4, (row_block // 4) ^ core) + (chunk % 2) * per_chunk
    base = jnp.stack([*starts, row_start]).astype(jnp.int32)
    pick = jnp.stack([(x ^ s) ^ (2 * core) for s in range(X)]).astype(jnp.int32)
    query_cos, query_sin = tables((row_start + jnp.arange(per_chunk)).astype(F32), HD)
    key_pos = jnp.concatenate([starts[0] + jnp.arange(per_row), starts[1] + jnp.arange(per_row)])
    key_cos, key_sin = tables(key_pos.astype(F32), HD)
    key_cos = jnp.where(core == 0, key_cos, 1.0)
    key_sin = jnp.where(core == 0, key_sin, 0.0)

    kv_parts = call(
        kv_kernel,
        [(quarter, HD)] * 4,
        [pick, *everyone, w_kv],
        [pltpu.VMEM((4, quarter, HD), BF16)],
        scalars=1,
    )
    (query_parts,) = call(query_kernel, [(Y * X, per_chunk, width)], [*everyone, w_query])
    query_parts = lax.all_to_all(query_parts, PLANE, 0, 0, tiled=True)

    def add(blocks):
        return functools.reduce(jnp.add, [b.astype(F32) for b in blocks]).astype(BF16)

    kv_x = add([kv_parts[0]] + [partner(kv_parts[s], "x", s) for s in (1, 2, 3)])
    kv_y = add([kv_x] + [partner(kv_x, "y", s) for s in (1, 2, 3)])
    (kv_done,) = call(
        keys_kernel, [(quarter, HD)], [kv_y, partner(kv_y, "zh", 1), key_cos, key_sin]
    )
    kv_other = partner(kv_done, "core", 1)
    keys = jnp.where(core == 0, kv_done, kv_other)
    values = jnp.where(core == 0, kv_other, kv_done)
    both = jnp.stack([keys, values])
    both = [both] + [partner(both, "x", s) for s in (1, 2, 3)]

    own = jnp.sum(query_parts.astype(F32), 0).astype(BF16)
    got = partner(own, "zh", 1)
    (attended,) = call(
        functools.partial(attention_kernel, heads),
        [(Y * X, per_chunk, width)],
        [base, own, got, query_cos, query_sin, *[b[0] for b in both], *[b[1] for b in both]],
        [pltpu.VMEM((heads * per_chunk, HD), BF16)],
        scalars=1,
    )
    attended = lax.all_to_all(attended, PLANE, 0, 0, tiled=True).reshape(total, width)

    sent = jnp.dot(attended[half:], w_output, preferred_element_type=F32).astype(BF16)
    kept = jnp.dot(attended[:half], w_output, preferred_element_type=F32).astype(BF16)
    chip = call(chip_kernel, [(per_row, features)] * 4, [kept, partner(sent, "core", 1)])
    return add([chip[0]] + [partner(chip[s], "zl", s) for s in (3, 2, 1)])


def solution(mesh):
    fine = Mesh(
        mesh.devices.reshape(Z_LO, CORE, Z_HI, Y, X), ("zl", "core", "zh", "y", "x")
    )
    return jax.shard_map(
        shards,
        mesh=fine,
        in_specs=(P(ROW, COL), P(COL, ROW), P(COL, ROW), P(ROW, COL)),
        out_specs=P(ROW, COL),
        check_vma=False,
    )
```

time: 154 us -> 150 us (0.974)
  blocking collectives: 70.6 us -> 34.9 us
  starting transfers between devices: 23.3 us -> 50.8 us
  Pallas kernels: 0 us -> 5.74 us
  waiting for transfers between devices: 46.8 us -> 50.5 us
  matrix products: 4.35 us -> 1.41 us
  local copies, waits for them, and re-layouts: 4.87 us -> 2.42 us
    ppermute x4 -> x23, waiting for transfers between devices: 6.22 us -> 48.8 us  [partner(): return lax.ppermute(block, axis, [(i, i ^ step) for i in range(size)])]
    all_to_all x2 -> x1, waiting for transfers between devices: 36.4 us -> 0.01 us  [shards(): query_parts = lax.all_to_all(query_parts, PLANE, 0, 0, tiled=True)]
    all_to_all x3 -> x1, blocking collectives: 70.6 us -> 34.9 us  [shards(): lax.all_to_all(attended, PLANE, 0, 0, tiled=True).reshape(total, width)]
    ppermute x4 -> x23, starting transfers between devices: 10.7 us -> 41.3 us  [partner(): return lax.ppermute(block, axis, [(i, i ^ step) for i in range(size)])]
    pallas_call x0 -> x5, Pallas kernels: none -> 5.74 us  [call(): pl.pallas_call(kernel, out_shape=[jax.ShapeDtypeStruct(s, BF16) for s in...]
    all_to_all x2 -> x1, starting transfers between devices: 10.7 us -> 6.55 us  [shards(): query_parts = lax.all_to_all(query_parts, PLANE, 0, 0, tiled=True)]
    dot_general x5 -> x2, matrix products: 4.35 us -> 1.41 us  [the longest x1 0.71 us: shards(): jnp.dot(attended[half:], w_output, preferred_element_type=F32).astype(BF16)]
    concatenate x1 -> x0, local copies, waits for them, and re-layouts: 2.56 us -> none  [shards(): part = jnp.concatenate([query_part, kv_part], 1)]
  transfers between devices with their start and end apart: 7 -> 25, of which waited for: 6 -> 14; matrix products, arithmetic and copies ran while one was open for 2% -> 3% of each run, Pallas kernels for 0% -> 2%
where the time goes in v2:
time: 150 us
  starting transfers between devices  50.8 us (34%)
  waiting for transfers between devices  50.5 us (34%)
  blocking collectives  34.9 us (23%)
  Pallas kernels  5.74 us (4%)
  other arithmetic  3.94 us (3%)
  local copies, waits for them, and re-layouts  2.42 us (2%)
    ppermute x23, waiting for transfers between devices, partner(): return lax.ppermute(block, axis, [(i, i ^ step) for i in range(size)])  48.8 us
    ppermute x23, starting transfers between devices, partner(): return lax.ppermute(block, axis, [(i, i ^ step) for i in range(size)])  41.3 us
    all_to_all x1, blocking collectives, shards(): lax.all_to_all(attended, PLANE, 0, 0, tiled=True).reshape(total, width)  34.9 us
    all_to_all x1, starting transfers between devices, shards(): query_parts = lax.all_to_all(query_parts, PLANE, 0, 0, tiled=True)  6.55 us
    pallas_call x5, Pallas kernels, call(): pl.pallas_call(kernel, out_shape=[jax.ShapeDtypeStruct(s, BF16) for s in...  5.74 us
  transfers between devices with their start and end apart: 25, of which 14 were waited for; matrix products, arithmetic and copies ran while one was open for 3% of the time, Pallas kernels for 2%

profile of v2, /device:TPU:1, one launch (start us, length us, event | category | flops | bytes accessed | tf_op | source)
XLA Modules:
  0.0 150.2 jit_solution(3342728024821876619)
XLA Ops:
  0.0 3.2 %collective-permute-start.3 = (bf16[128,512]{1,0:T(8,128)(2,1)}, bf16[128,512]{1,0:T(8,128)(2,1)S(1)}, u32[]{:S(2)}, u32[]{:S(2)}) collective-permute-start(bf16[128,512]{1,0:T(8,128)(2,1)} %refs_0_.3), channel_id=1, source_target_pairs={{0,32},{32,0},{1,33},{33,1},{2,34},{34,2},{3,35},{35,3},{4,36},{36... | collective-permute-start | bytes 393224 | tf_op jit(solution)/shard_map/ppermute | solution.py:38
  3.2 2.6 %collective-permute-start.2 = (bf16[128,512]{1,0:T(8,128)(2,1)}, bf16[128,512]{1,0:T(8,128)(2,1)S(1)}, u32[]{:S(2)}, u32[]{:S(2)}) collective-permute-start(bf16[128,512]{1,0:T(8,128)(2,1)} %refs_0_.3), channel_id=1, source_target_pairs={{0,192},{64,128},{128,64},{192,0},{1,193},{65,129},{129,65},{193,1... | collective-permute-start | bytes 393224 | tf_op jit(solution)/shard_map/ppermute | solution.py:38
  6.8 3.0 %collective-permute-start.8 = (bf16[512,128]{1,0:T(8,128)(2,1)}, bf16[512,128]{1,0:T(8,128)(2,1)S(1)}, u32[]{:S(2)}, u32[]{:S(2)}) collective-permute-start(bf16[512,128]{1,0:T(8,128)(2,1)} %param.6), channel_id=1, source_target_pairs={{0,0},{32,64},{64,128},{96,192},{128,32},{160,96},{192,160},{224,2... | collective-permute-start | bytes 393224 | tf_op jit(solution)/shard_map/ppermute | solution.py:136
  11.7 5.2 %collective-permute-done.1.refs_2_ = bf16[128,512]{1,0:T(8,128)(2,1)S(1)} collective-permute-done((bf16[128,512]{1,0:T(8,128)(2,1)}, bf16[128,512]{1,0:T(8,128)(2,1)S(1)}, u32[]{:S(2)}, u32[]{:S(2)}) %collective-permute-start.1) | collective-permute-done | bytes 131104 | tf_op jit(solution)/shard_map/ppermute | solution.py:38
  22.9 2.4 %collective-permute-start.10 = (bf16[256,128]{1,0:T(8,128)(2,1)S(1)}, bf16[256,128]{1,0:T(8,128)(2,1)S(1)}, u32[]{:S(2)}, u32[]{:S(2)}) collective-permute-start(bf16[256,128]{1,0:T(8,128)(2,1)S(1)} %get-tuple-element.15), channel_id=1, source_target_pairs={{0,2},{1,3},{2,0},{3,1},{4,6},{5,7},{6,4},{7,5},{8,10},{9,11},{10,... | collective-permute-start | bytes 196616 | tf_op jit(solution)/shard_map/ppermute | solution.py:38
  26.8 2.6 %shard_map.46 = bf16[16,64,1024]{2,1,0:T(8,128)(2,1)} custom-call(bf16[128,512]{1,0:T(8,128)(2,1)S(1)} %copy-done.2, bf16[128,512]{1,0:T(8,128)(2,1)S(1)} %collective-permute-done.refs_1_, bf16[128,512]{1,0:T(8,128)(2,1)S(1)} %collective-permute-done.1.refs_2_, bf16[128,512]{1,0:T(8,128)(2,1)S(1)} %collective-permute-done.2.refs_3_, ...), custom_call_target="tpu_custom_call" | custom-call | tf_op jit(solution)/shard_map/pallas_call | solution.py:109
  29.4 6.5 %all-to-all-start = ((bf16[16,64,1024]{2,1,0:T(8,128)(2,1)}), bf16[16,64,1024]{2,1,0:T(8,128)(2,1)}, u32[]{:S(2)}, u32[]{:S(2)}) async-start(bf16[16,64,1024]{2,1,0:T(8,128)(2,1)} %shard_map.46), calls=%async_computation | async-start | bytes 4194304 | tf_op jit(solution)/shard_map/all_to_all | solution.py:165
  36.6 2.6 %collective-permute-start.14 = (bf16[256,128]{1,0:T(8,128)(2,1)S(1)}, bf16[256,128]{1,0:T(8,128)(2,1)S(1)}, u32[]{:S(2)}, u32[]{:S(2)}) collective-permute-start(bf16[256,128]{1,0:T(8,128)(2,1)S(1)} %add_convert_fusion.2), channel_id=1, source_target_pairs={{0,12},{4,8},{8,4},{12,0},{1,13},{5,9},{9,5},{13,1},{2,14},{6,10},... | collective-permute-start | bytes 196616 | tf_op jit(solution)/shard_map/ppermute | solution.py:38
  40.1 8.1 %collective-permute-done.14 = bf16[256,128]{1,0:T(8,128)(2,1)S(1)} collective-permute-done((bf16[256,128]{1,0:T(8,128)(2,1)S(1)}, bf16[256,128]{1,0:T(8,128)(2,1)S(1)}, u32[]{:S(2)}, u32[]{:S(2)}) %collective-permute-start.14) | collective-permute-done | bytes 65568 | tf_op jit(solution)/shard_map/ppermute | solution.py:38
  48.2 1.9 %collective-permute-done.13 = bf16[256,128]{1,0:T(8,128)(2,1)S(1)} collective-permute-done((bf16[256,128]{1,0:T(8,128)(2,1)S(1)}, bf16[256,128]{1,0:T(8,128)(2,1)S(1)}, u32[]{:S(2)}, u32[]{:S(2)}) %collective-permute-start.13) | collective-permute-done | bytes 65568 | tf_op jit(solution)/shard_map/ppermute | solution.py:38
  50.1 12.8 %collective-permute-done.12 = bf16[256,128]{1,0:T(8,128)(2,1)S(1)} collective-permute-done((bf16[256,128]{1,0:T(8,128)(2,1)S(1)}, bf16[256,128]{1,0:T(8,128)(2,1)S(1)}, u32[]{:S(2)}, u32[]{:S(2)}) %collective-permute-start.12) | collective-permute-done | bytes 65568 | tf_op jit(solution)/shard_map/ppermute | solution.py:38
  63.0 5.7 %collective-permute-start.15 = (bf16[256,128]{1,0:T(8,128)(2,1)S(1)}, bf16[256,128]{1,0:T(8,128)(2,1)S(1)}, u32[]{:S(2)}, u32[]{:S(2)}) collective-permute-start(bf16[256,128]{1,0:T(8,128)(2,1)S(1)} %add_convert_fusion.1.a), channel_id=1, source_target_pairs={{0,16},{16,0},{1,17},{17,1},{2,18},{18,2},{3,19},{19,3},{4,20},{20... | collective-permute-start | bytes 196616 | tf_op jit(solution)/shard_map/ppermute | solution.py:38
  70.4 2.7 %collective-permute-start.16 = (bf16[256,128]{1,0:T(8,128)(2,1)S(1)}, bf16[256,128]{1,0:T(8,128)(2,1)S(1)}, u32[]{:S(2)}, u32[]{:S(2)}) collective-permute-start(bf16[256,128]{1,0:T(8,128)(2,1)S(1)} %shard_map.48), channel_id=1, source_target_pairs={{0,32},{32,0},{1,33},{33,1},{2,34},{34,2},{3,35},{35,3},{4,36},{36... | collective-permute-start | bytes 196616 | tf_op jit(solution)/shard_map/ppermute | solution.py:38
  74.1 3.8 %collective-permute-start.19 = (bf16[2,256,128]{2,1,0:T(8,128)(2,1)S(1)}, bf16[2,256,128]{2,1,0:T(8,128)(2,1)S(1)}, u32[]{:S(2)}, u32[]{:S(2)}) collective-permute-start(bf16[2,256,128]{2,1,0:T(8,128)(2,1)S(1)} %pad_maximum_fusion), channel_id=1, source_target_pairs={{0,3},{1,2},{2,1},{3,0},{4,7},{5,6},{6,5},{7,4},{8,11},{9,10},{10,... | collective-permute-start | bytes 393224 | tf_op jit(solution)/shard_map/ppermute | solution.py:38
  79.5 3.4 %collective-permute-done.19 = bf16[2,256,128]{2,1,0:T(8,128)(2,1)S(1)} collective-permute-done((bf16[2,256,128]{2,1,0:T(8,128)(2,1)S(1)}, bf16[2,256,128]{2,1,0:T(8,128)(2,1)S(1)}, u32[]{:S(2)}, u32[]{:S(2)}) %collective-permute-start.19) | collective-permute-done | bytes 131104 | tf_op jit(solution)/shard_map/ppermute | solution.py:38
  84.6 2.0 %reduce_sum.12.own = bf16[64,1024]{1,0:T(8,128)(2,1)S(1)} reduce(bf16[16,64,1024]{2,1,0:T(8,128)(2,1)} %all-to-all-done, bf16[]{:T(256)} %constant.134.clone.1), dimensions={0}, to_apply=%region_0.1 | reduce | flops 983040 | bytes 2228226 | tf_op jit(solution)/shard_map/reduce_sum | solution.py:181
  86.6 5.5 %collective-permute-start.7 = (bf16[64,1024]{1,0:T(8,128)(2,1)S(1)}, bf16[64,1024]{1,0:T(8,128)(2,1)S(1)}, u32[]{:S(2)}, u32[]{:S(2)}) collective-permute-start(bf16[64,1024]{1,0:T(8,128)(2,1)S(1)} %reduce_sum.12.own), channel_id=1, source_target_pairs={{0,16},{16,0},{1,17},{17,1},{2,18},{18,2},{3,19},{19,3},{4,20},{20... | collective-permute-start | bytes 393224 | tf_op jit(solution)/shard_map/ppermute | solution.py:38
  92.2 2.4 %collective-permute-done.7.got = bf16[64,1024]{1,0:T(8,128)(2,1)S(1)} collective-permute-done((bf16[64,1024]{1,0:T(8,128)(2,1)S(1)}, bf16[64,1024]{1,0:T(8,128)(2,1)S(1)}, u32[]{:S(2)}, u32[]{:S(2)}) %collective-permute-start.7) | collective-permute-done | bytes 131104 | tf_op jit(solution)/shard_map/ppermute | solution.py:38
  94.6 1.9 %shard_map.49 = bf16[16,64,1024]{2,1,0:T(8,128)(2,1)S(1)} custom-call(s32[9]{0:T(128)S(1)} %stack.63.base, bf16[64,1024]{1,0:T(8,128)(2,1)S(1)} %reduce_sum.12.own, bf16[64,1024]{1,0:T(8,128)(2,1)S(1)} %collective-permute-done.7.got, f32[64,128]{1,0:T(8,128)S(1)} %get-tuple-element.37.cosine, f32[64,128]{1,0:T(8,128)S(1)} %get-tuple-element.38.sine_v, ...), custom_call_target="tpu_custom_call" | custom-call | tf_op jit(solution)/shard_map/pallas_call | solution.py:109
  96.5 34.9 %all_to_all.10 = bf16[16,64,1024]{2,1,0:T(8,128)(2,1)S(1)} all-to-all(bf16[16,64,1024]{2,1,0:T(8,128)(2,1)S(1)} %shard_map.49), channel_id=1, replica_groups=mesh['zl'=4,'core'=2,'zh'=2,'y'=4,'x'=4] {'y','x'}, dimensions={0} | all-to-all | bytes 4194304 | tf_op jit(solution)/shard_map/all_to_all | solution.py:190
  132.3 2.5 %collective-permute-start.20 = (bf16[512,512]{1,0:T(8,128)(2,1)S(1)}, bf16[512,512]{1,0:T(8,128)(2,1)S(1)}, u32[]{:S(2)}, u32[]{:S(2)}) collective-permute-start(bf16[512,512]{1,0:T(8,128)(2,1)S(1)} %convolution_convert_fusion), channel_id=1, source_target_pairs={{0,32},{32,0},{1,33},{33,1},{2,34},{34,2},{3,35},{35,3},{4,36},{36... | collective-permute-start | bytes 1572872 | tf_op jit(solution)/shard_map/ppermute | solution.py:38
  137.7 2.4 %collective-permute-start.23 = (bf16[128,512]{1,0:T(8,128)(2,1)S(1)}, bf16[128,512]{1,0:T(8,128)(2,1)S(1)}, u32[]{:S(2)}, u32[]{:S(2)}) collective-permute-start(bf16[128,512]{1,0:T(8,128)(2,1)S(1)} %get-tuple-element.20), channel_id=1, source_target_pairs={{0,64},{64,0},{128,192},{192,128},{1,65},{65,1},{129,193},{193,129... | collective-permute-start | bytes 393224 | tf_op jit(solution)/shard_map/ppermute | solution.py:38
  140.1 3.0 %collective-permute-done.21 = bf16[128,512]{1,0:T(8,128)(2,1)S(1)} collective-permute-done((bf16[128,512]{1,0:T(8,128)(2,1)S(1)}, bf16[128,512]{1,0:T(8,128)(2,1)S(1)}, u32[]{:S(2)}, u32[]{:S(2)}) %collective-permute-start.21) | collective-permute-done | bytes 131104 | tf_op jit(solution)/shard_map/ppermute | solution.py:38
  143.1 6.3 %collective-permute-done.22 = bf16[128,512]{1,0:T(8,128)(2,1)S(1)} collective-permute-done((bf16[128,512]{1,0:T(8,128)(2,1)S(1)}, bf16[128,512]{1,0:T(8,128)(2,1)S(1)}, u32[]{:S(2)}, u32[]{:S(2)}) %collective-permute-start.22) | collective-permute-done | bytes 131104 | tf_op jit(solution)/shard_map/ppermute | solution.py:38
  (61 shorter events, 22.0 us)
Async XLA Ops:
  0.0 19.7 %collective-permute-start.3 = (bf16[128,512]{1,0:T(8,128)(2,1)}, bf16[128,512]{1,0:T(8,128)(2,1)S(1)}, u32[]{:S(2)}, u32[]{:S(2)}) collective-permute-start(bf16[128,512]{1,0:T(8,128)(2,1)} %refs_0_.3), channel_id=1, source_target_pairs={{0,32},{32,0},{1,33},{33,1},{2,34},{34,2},{3,35},{35,3},{4,36},{36... | collective-permute-start | bytes 393224 | tf_op jit(solution)/shard_map/ppermute | solution.py:38
  3.2 7.2 %collective-permute-start.2 = (bf16[128,512]{1,0:T(8,128)(2,1)}, bf16[128,512]{1,0:T(8,128)(2,1)S(1)}, u32[]{:S(2)}, u32[]{:S(2)}) collective-permute-start(bf16[128,512]{1,0:T(8,128)(2,1)} %refs_0_.3), channel_id=1, source_target_pairs={{0,192},{64,128},{128,64},{192,0},{1,193},{65,129},{129,65},{193,1... | collective-permute-start | bytes 393224 | tf_op jit(solution)/shard_map/ppermute | solution.py:38
  5.9 11.0 %collective-permute-start.1 = (bf16[128,512]{1,0:T(8,128)(2,1)}, bf16[128,512]{1,0:T(8,128)(2,1)S(1)}, u32[]{:S(2)}, u32[]{:S(2)}) collective-permute-start(bf16[128,512]{1,0:T(8,128)(2,1)} %refs_0_.3), channel_id=1, source_target_pairs={{0,128},{64,192},{128,0},{192,64},{1,129},{65,193},{129,1},{193,65... | collective-permute-start | bytes 393224 | tf_op jit(solution)/shard_map/ppermute | solution.py:38
  5.9 12.0 %collective-permute-start = (bf16[128,512]{1,0:T(8,128)(2,1)}, bf16[128,512]{1,0:T(8,128)(2,1)S(1)}, u32[]{:S(2)}, u32[]{:S(2)}) collective-permute-start(bf16[128,512]{1,0:T(8,128)(2,1)} %refs_0_.3), channel_id=1, source_target_pairs={{0,64},{64,0},{128,192},{192,128},{1,65},{65,1},{129,193},{193,129... | collective-permute-start | bytes 393224 | tf_op jit(solution)/shard_map/ppermute | solution.py:38
  6.8 12.9 %collective-permute-start.8 = (bf16[512,128]{1,0:T(8,128)(2,1)}, bf16[512,128]{1,0:T(8,128)(2,1)S(1)}, u32[]{:S(2)}, u32[]{:S(2)}) collective-permute-start(bf16[512,128]{1,0:T(8,128)(2,1)} %param.6), channel_id=1, source_target_pairs={{0,0},{32,64},{64,128},{96,192},{128,32},{160,96},{192,160},{224,2... | collective-permute-start | bytes 393224 | tf_op jit(solution)/shard_map/ppermute | solution.py:136
  10.4 9.3 %collective-permute-start.6 = (bf16[128,512]{1,0:T(8,128)(2,1)S(1)}, bf16[128,512]{1,0:T(8,128)(2,1)S(1)}, u32[]{:S(2)}, u32[]{:S(2)}) collective-permute-start(bf16[128,512]{1,0:T(8,128)(2,1)S(1)} %collective-permute-done.2.refs_3_), channel_id=1, source_target_pairs={{0,32},{32,0},{1,33},{33,1},{2,34},{34,2},{3,35},{35,3},{4,36},{36... | collective-permute-start | bytes 393224 | tf_op jit(solution)/shard_map/ppermute | solution.py:38
  16.9 2.8 %collective-permute-start.5 = (bf16[128,512]{1,0:T(8,128)(2,1)S(1)}, bf16[128,512]{1,0:T(8,128)(2,1)S(1)}, u32[]{:S(2)}, u32[]{:S(2)}) collective-permute-start(bf16[128,512]{1,0:T(8,128)(2,1)S(1)} %collective-permute-done.1.refs_2_), channel_id=1, source_target_pairs={{0,32},{32,0},{1,33},{33,1},{2,34},{34,2},{3,35},{35,3},{4,36},{36... | collective-permute-start | bytes 393224 | tf_op jit(solution)/shard_map/ppermute | solution.py:38
  21.6 14.9 %collective-permute-start.9 = (bf16[256,128]{1,0:T(8,128)(2,1)S(1)}, bf16[256,128]{1,0:T(8,128)(2,1)S(1)}, u32[]{:S(2)}, u32[]{:S(2)}) collective-permute-start(bf16[256,128]{1,0:T(8,128)(2,1)S(1)} %get-tuple-element.14), channel_id=1, source_target_pairs={{0,1},{1,0},{2,3},{3,2},{4,5},{5,4},{6,7},{7,6},{8,9},{9,8},{10,11... | collective-permute-start | bytes 196616 | tf_op jit(solution)/shard_map/ppermute | solution.py:38
  22.9 13.6 %collective-permute-start.10 = (bf16[256,128]{1,0:T(8,128)(2,1)S(1)}, bf16[256,128]{1,0:T(8,128)(2,1)S(1)}, u32[]{:S(2)}, u32[]{:S(2)}) collective-permute-start(bf16[256,128]{1,0:T(8,128)(2,1)S(1)} %get-tuple-element.15), channel_id=1, source_target_pairs={{0,2},{1,3},{2,0},{3,1},{4,6},{5,7},{6,4},{7,5},{8,10},{9,11},{10,... | collective-permute-start | bytes 196616 | tf_op jit(solution)/shard_map/ppermute | solution.py:38
  25.4 11.2 %collective-permute-start.11 = (bf16[256,128]{1,0:T(8,128)(2,1)S(1)}, bf16[256,128]{1,0:T(8,128)(2,1)S(1)}, u32[]{:S(2)}, u32[]{:S(2)}) collective-permute-start(bf16[256,128]{1,0:T(8,128)(2,1)S(1)} %get-tuple-element.16), channel_id=1, source_target_pairs={{0,3},{1,2},{2,1},{3,0},{4,7},{5,6},{6,5},{7,4},{8,11},{9,10},{10,... | collective-permute-start | bytes 196616 | tf_op jit(solution)/shard_map/ppermute | solution.py:38
  29.4 55.2 %all-to-all-start = ((bf16[16,64,1024]{2,1,0:T(8,128)(2,1)}), bf16[16,64,1024]{2,1,0:T(8,128)(2,1)}, u32[]{:S(2)}, u32[]{:S(2)}) async-start(bf16[16,64,1024]{2,1,0:T(8,128)(2,1)} %shard_map.46), calls=%async_computation | async-start | bytes 4194304 | tf_op jit(solution)/shard_map/all_to_all | solution.py:165
  36.6 11.6 %collective-permute-start.14 = (bf16[256,128]{1,0:T(8,128)(2,1)S(1)}, bf16[256,128]{1,0:T(8,128)(2,1)S(1)}, u32[]{:S(2)}, u32[]{:S(2)}) collective-permute-start(bf16[256,128]{1,0:T(8,128)(2,1)S(1)} %add_convert_fusion.2), channel_id=1, source_target_pairs={{0,12},{4,8},{8,4},{12,0},{1,13},{5,9},{9,5},{13,1},{2,14},{6,10},... | collective-permute-start | bytes 196616 | tf_op jit(solution)/shard_map/ppermute | solution.py:38
  39.3 10.8 %collective-permute-start.13 = (bf16[256,128]{1,0:T(8,128)(2,1)S(1)}, bf16[256,128]{1,0:T(8,128)(2,1)S(1)}, u32[]{:S(2)}, u32[]{:S(2)}) collective-permute-start(bf16[256,128]{1,0:T(8,128)(2,1)S(1)} %add_convert_fusion.2), channel_id=1, source_target_pairs={{0,8},{4,12},{8,0},{12,4},{1,9},{5,13},{9,1},{13,5},{2,10},{6,14},... | collective-permute-start | bytes 196616 | tf_op jit(solution)/shard_map/ppermute | solution.py:38
  39.8 23.1 %collective-permute-start.12 = (bf16[256,128]{1,0:T(8,128)(2,1)S(1)}, bf16[256,128]{1,0:T(8,128)(2,1)S(1)}, u32[]{:S(2)}, u32[]{:S(2)}) collective-permute-start(bf16[256,128]{1,0:T(8,128)(2,1)S(1)} %add_convert_fusion.2), channel_id=1, source_target_pairs={{0,4},{4,0},{8,12},{12,8},{1,5},{5,1},{9,13},{13,9},{2,6},{6,2},{1... | collective-permute-start | bytes 196616 | tf_op jit(solution)/shard_map/ppermute | solution.py:38
  63.0 7.3 %collective-permute-start.15 = (bf16[256,128]{1,0:T(8,128)(2,1)S(1)}, bf16[256,128]{1,0:T(8,128)(2,1)S(1)}, u32[]{:S(2)}, u32[]{:S(2)}) collective-permute-start(bf16[256,128]{1,0:T(8,128)(2,1)S(1)} %add_convert_fusion.1.a), channel_id=1, source_target_pairs={{0,16},{16,0},{1,17},{17,1},{2,18},{18,2},{3,19},{19,3},{4,20},{20... | collective-permute-start | bytes 196616 | tf_op jit(solution)/shard_map/ppermute | solution.py:38
  70.4 3.6 %collective-permute-start.16 = (bf16[256,128]{1,0:T(8,128)(2,1)S(1)}, bf16[256,128]{1,0:T(8,128)(2,1)S(1)}, u32[]{:S(2)}, u32[]{:S(2)}) collective-permute-start(bf16[256,128]{1,0:T(8,128)(2,1)S(1)} %shard_map.48), channel_id=1, source_target_pairs={{0,32},{32,0},{1,33},{33,1},{2,34},{34,2},{3,35},{35,3},{4,36},{36... | collective-permute-start | bytes 196616 | tf_op jit(solution)/shard_map/ppermute | solution.py:38
  74.1 8.8 %collective-permute-start.19 = (bf16[2,256,128]{2,1,0:T(8,128)(2,1)S(1)}, bf16[2,256,128]{2,1,0:T(8,128)(2,1)S(1)}, u32[]{:S(2)}, u32[]{:S(2)}) collective-permute-start(bf16[2,256,128]{2,1,0:T(8,128)(2,1)S(1)} %pad_maximum_fusion), channel_id=1, source_target_pairs={{0,3},{1,2},{2,1},{3,0},{4,7},{5,6},{6,5},{7,4},{8,11},{9,10},{10,... | collective-permute-start | bytes 393224 | tf_op jit(solution)/shard_map/ppermute | solution.py:38
  78.4 6.2 %collective-permute-start.18 = (bf16[2,256,128]{2,1,0:T(8,128)(2,1)S(1)}, bf16[2,256,128]{2,1,0:T(8,128)(2,1)S(1)}, u32[]{:S(2)}, u32[]{:S(2)}) collective-permute-start(bf16[2,256,128]{2,1,0:T(8,128)(2,1)S(1)} %pad_maximum_fusion), channel_id=1, source_target_pairs={{0,2},{1,3},{2,0},{3,1},{4,6},{5,7},{6,4},{7,5},{8,10},{9,11},{10,... | collective-permute-start | bytes 393224 | tf_op jit(solution)/shard_map/ppermute | solution.py:38
  79.5 12.7 %collective-permute-start.17 = (bf16[2,256,128]{2,1,0:T(8,128)(2,1)S(1)}, bf16[2,256,128]{2,1,0:T(8,128)(2,1)S(1)}, u32[]{:S(2)}, u32[]{:S(2)}) collective-permute-start(bf16[2,256,128]{2,1,0:T(8,128)(2,1)S(1)} %pad_maximum_fusion), channel_id=1, source_target_pairs={{0,1},{1,0},{2,3},{3,2},{4,5},{5,4},{6,7},{7,6},{8,9},{9,8},{10,11... | collective-permute-start | bytes 393224 | tf_op jit(solution)/shard_map/ppermute | solution.py:38
  86.6 8.0 %collective-permute-start.7 = (bf16[64,1024]{1,0:T(8,128)(2,1)S(1)}, bf16[64,1024]{1,0:T(8,128)(2,1)S(1)}, u32[]{:S(2)}, u32[]{:S(2)}) collective-permute-start(bf16[64,1024]{1,0:T(8,128)(2,1)S(1)} %reduce_sum.12.own), channel_id=1, source_target_pairs={{0,16},{16,0},{1,17},{17,1},{2,18},{18,2},{3,19},{19,3},{4,20},{20... | collective-permute-start | bytes 393224 | tf_op jit(solution)/shard_map/ppermute | solution.py:38
  132.3 4.1 %collective-permute-start.20 = (bf16[512,512]{1,0:T(8,128)(2,1)S(1)}, bf16[512,512]{1,0:T(8,128)(2,1)S(1)}, u32[]{:S(2)}, u32[]{:S(2)}) collective-permute-start(bf16[512,512]{1,0:T(8,128)(2,1)S(1)} %convolution_convert_fusion), channel_id=1, source_target_pairs={{0,32},{32,0},{1,33},{33,1},{2,34},{34,2},{3,35},{35,3},{4,36},{36... | collective-permute-start | bytes 1572872 | tf_op jit(solution)/shard_map/ppermute | solution.py:38
  136.5 6.6 %collective-permute-start.21 = (bf16[128,512]{1,0:T(8,128)(2,1)S(1)}, bf16[128,512]{1,0:T(8,128)(2,1)S(1)}, u32[]{:S(2)}, u32[]{:S(2)}) collective-permute-start(bf16[128,512]{1,0:T(8,128)(2,1)S(1)} %get-tuple-element.18), channel_id=1, source_target_pairs={{0,192},{64,128},{128,64},{192,0},{1,193},{65,129},{129,65},{193,1... | collective-permute-start | bytes 393224 | tf_op jit(solution)/shard_map/ppermute | solution.py:38
  136.6 12.8 %collective-permute-start.22 = (bf16[128,512]{1,0:T(8,128)(2,1)S(1)}, bf16[128,512]{1,0:T(8,128)(2,1)S(1)}, u32[]{:S(2)}, u32[]{:S(2)}) collective-permute-start(bf16[128,512]{1,0:T(8,128)(2,1)S(1)} %get-tuple-element.19), channel_id=1, source_target_pairs={{0,128},{64,192},{128,0},{192,64},{1,129},{65,193},{129,1},{193,65... | collective-permute-start | bytes 393224 | tf_op jit(solution)/shard_map/ppermute | solution.py:38
  137.7 11.7 %collective-permute-start.23 = (bf16[128,512]{1,0:T(8,128)(2,1)S(1)}, bf16[128,512]{1,0:T(8,128)(2,1)S(1)}, u32[]{:S(2)}, u32[]{:S(2)}) collective-permute-start(bf16[128,512]{1,0:T(8,128)(2,1)S(1)} %get-tuple-element.20), channel_id=1, source_target_pairs={{0,64},{64,0},{128,192},{192,128},{1,65},{65,1},{129,193},{193,129... | collective-permute-start | bytes 393224 | tf_op jit(solution)/shard_map/ppermute | solution.py:38
  (4 other events, 135.6 us)

commit v3 on v2

v3 whole, which is shorter than its diff:
```python
import functools
import math

import jax
import jax.numpy as jnp
from jax import lax
from jax.experimental import pallas as pl
from jax.experimental.pallas import tpu as pltpu
from jax.sharding import Mesh
from jax.sharding import PartitionSpec as P

HD = 128
Z_LO, CORE, Z_HI, Y, X = 4, 2, 2, 4, 4
ROW = ("zl", "core")
COL = ("zh", "y", "x")
PLANE = ("y", "x")
BF16 = jnp.bfloat16
F32 = jnp.float32
VMEM = pl.BlockSpec(memory_space=pltpu.VMEM)
SMEM = pl.BlockSpec(memory_space=pltpu.SMEM)
PARAMS = pltpu.CompilerParams(vmem_limit_bytes=32 * 1024 * 1024)


def tables(positions, width):
    half_width = width // 2
    frequency = 500000.0 ** (-(jnp.arange(half_width).astype(F32) * 2.0 / width))
    angle_v = positions[:, None] * frequency[None, :]
    cosine, sine_v = jnp.cos(angle_v), jnp.sin(angle_v)
    return jnp.concatenate([cosine, cosine], 1), jnp.concatenate([-sine_v, sine_v], 1)


def rotate(values_in, cosine, sine_v):
    return values_in * cosine + pltpu.roll(values_in, HD // 2, 1) * sine_v


def partner(block, axis, step):
    size = {"zl": Z_LO, "core": CORE, "zh": Z_HI, "y": Y, "x": X}[axis]
    return lax.ppermute(block, axis, [(i, i ^ step) for i in range(size)])


def projection_kernel(*refs):
    blocks, w_query, w_kv, out = refs[:8], refs[8], refs[9], refs[10]
    per_chunk = out.shape[1]
    width = w_query.shape[1]
    for i, block in enumerate(blocks):
        query = jnp.dot(block[...], w_query[...], preferred_element_type=F32).astype(BF16)
        keyval = jnp.dot(block[...], w_kv[...], preferred_element_type=F32).astype(BF16)
        for b in range(2):
            part = slice(b * per_chunk, (b + 1) * per_chunk)
            out[2 * i + b, :, :width] = query[part]
            out[2 * i + b, :, width:] = keyval[part]


def sums_kernel(parts, query, keyval):
    width = query.shape[1]
    total = parts[0].astype(F32)
    for c in range(1, parts.shape[0]):
        total += parts[c].astype(F32)
    query[...] = total[:, :width].astype(BF16)
    keyval[...] = total[:, width:].astype(BF16)


def keys_kernel(a, b, cosine, sine_v, out):
    total = (a[...].astype(F32) + b[...].astype(F32)).astype(BF16).astype(F32)
    block = rotate(total, cosine[...], sine_v[...]).astype(BF16)
    for c in range(out.shape[0]):
        out[c] = block


def attention_kernel(heads, base, own, got, cosine, sine_v, kv_own, kv_other, out, queries, pair):
    per_chunk = own.shape[0]
    half = kv_own.shape[0] // 2
    for side in range(2):
        pair[0, side * half : (side + 1) * half, :] = kv_own[side * half : (side + 1) * half, :]
        pair[1, side * half : (side + 1) * half, :] = kv_other[
            (1 - side) * half : (2 - side) * half, :
        ]
    for h in range(heads):
        cols = slice(h * HD, (h + 1) * HD)
        total = own[:, cols].astype(F32) + got[:, cols].astype(F32)
        queries[h * per_chunk : (h + 1) * per_chunk, :] = rotate(
            total, cosine[...], sine_v[...]
        ).astype(BF16)
    query = queries[...]
    core = base[9]
    rows = heads * per_chunk
    row_pos = base[8] + lax.broadcasted_iota(jnp.int32, (rows, HD), 0) % per_chunk
    lane = lax.broadcasted_iota(jnp.int32, (rows, HD), 1)
    score_scale = 1.0 / math.sqrt(HD)
    totals = jnp.zeros((rows, 1), F32)
    mixed = jnp.zeros((rows, HD), F32)
    for s in range(4):
        part = slice(s * 2 * HD, (s + 1) * 2 * HD)
        keys, values = pair[core, part, :], pair[1 - core, part, :]
        scores = (
            lax.dot_general(query, keys, (((1,), (1,)), ((), ())), preferred_element_type=F32)
            * score_scale
        )
        causal = jnp.concatenate(
            [base[2 * s] + lane <= row_pos, base[2 * s + 1] + lane <= row_pos], 1
        )
        weights = jnp.where(causal, jnp.exp(jnp.where(causal, scores, 0.0)), 0.0)
        totals += jnp.sum(weights, 1, keepdims=True)
        mixed += jnp.dot(weights.astype(BF16), values, preferred_element_type=F32)
    attended = (mixed / totals).astype(BF16)
    for h in range(heads):
        block = attended[h * per_chunk : (h + 1) * per_chunk]
        for c in range(out.shape[0]):
            out[c, :, h * HD : (h + 1) * HD] = block


def chip_kernel(kept, got, *outs):
    rows = outs[0].shape[0]
    for s, out in enumerate(outs):
        part = slice(s * rows, (s + 1) * rows)
        out[...] = (kept[part, :].astype(F32) + got[part, :].astype(F32)).astype(BF16)


def call(kernel, outs, args, scratch=(), scalars=0):
    return pl.pallas_call(
        kernel,
        out_shape=[jax.ShapeDtypeStruct(s, BF16) for s in outs],
        in_specs=[SMEM] * scalars + [VMEM] * (len(args) - scalars),
        out_specs=[VMEM] * len(outs),
        scratch_shapes=list(scratch),
        compiler_params=PARAMS,
    )(*args)


def shards(tokens, w_query, w_keyval, w_output):
    zl = lax.axis_index("zl")
    core = lax.axis_index("core")
    y = lax.axis_index("y")
    x = lax.axis_index("x")
    per_row, features = tokens.shape
    half = per_row * Z_LO
    total = half * 2
    per_chunk = total // (Y * X)
    width = w_query.shape[1]
    heads = width // HD

    mine = [tokens] + [partner(tokens, "zl", s) for s in (1, 2, 3)]
    others = [partner(block, "core", 1) for block in mine]
    everyone = mine + others
    kv_moves = [(e, 2 * e if e < 4 else 2 * (e - 4) + 1) for e in range(8)]
    w_kv = lax.ppermute(w_keyval, ROW, kv_moves)

    def block_start(index):
        return (((zl ^ (index & 3)) << 1) + ((index >> 2) ^ core)) * per_row

    chunk = y * X + x
    row_start = block_start(chunk >> 1) + (chunk & 1) * per_chunk
    base = jnp.stack([*[block_start(i) for i in range(8)], row_start, core]).astype(jnp.int32)
    cosine, sine_v = tables((row_start + jnp.arange(per_chunk)).astype(F32), HD)
    key_cos = jnp.where(core == 0, cosine, 1.0)
    key_sin = jnp.where(core == 0, sine_v, 0.0)

    (parts,) = call(
        projection_kernel, [(Y * X, per_chunk, width + HD)], [*everyone, w_query, w_kv]
    )
    parts = lax.all_to_all(parts, PLANE, 0, 0, tiled=True)
    query, kv = call(sums_kernel, [(per_chunk, width), (per_chunk, HD)], [parts])
    (kv_block,) = call(
        keys_kernel, [(Y * X, per_chunk, HD)], [kv, partner(kv, "zh", 1), key_cos, key_sin]
    )
    kv_own = lax.all_to_all(kv_block, PLANE, 0, 0, tiled=True).reshape(total, HD)
    kv_other = partner(kv_own, "core", 1)
    query_got = partner(query, "zh", 1)
    (attended,) = call(
        functools.partial(attention_kernel, heads),
        [(Y * X, per_chunk, width)],
        [base, query, query_got, cosine, sine_v, kv_own, kv_other],
        [pltpu.VMEM((heads * per_chunk, HD), BF16), pltpu.VMEM((2, total, HD), BF16)],
        scalars=1,
    )
    attended = lax.all_to_all(attended, PLANE, 0, 0, tiled=True).reshape(total, width)

    sent = jnp.dot(attended[half:], w_output, preferred_element_type=F32).astype(BF16)
    kept = jnp.dot(attended[:half], w_output, preferred_element_type=F32).astype(BF16)
    chip = call(chip_kernel, [(per_row, features)] * 4, [kept, partner(sent, "core", 1)])
    blocks = [chip[0]] + [partner(chip[s], "zl", s) for s in (3, 2, 1)]
    return functools.reduce(jnp.add, [b.astype(F32) for b in blocks]).astype(BF16)


def solution(mesh):
    fine = Mesh(
        mesh.devices.reshape(Z_LO, CORE, Z_HI, Y, X), ("zl", "core", "zh", "y", "x")
    )
    return jax.shard_map(
        shards,
        mesh=fine,
        in_specs=(P(ROW, COL), P(COL, ROW), P(COL, ROW), P(ROW, COL)),
        out_specs=P(ROW, COL),
        check_vma=False,
    )
```

time: 150 us -> 150 us (level); the launches traced: 150 us -> 149 us
  blocking collectives: 34.9 us -> 39.5 us
  starting transfers between devices: 50.8 us -> 46.6 us
  other arithmetic: 3.94 us -> 1.64 us
    ppermute x23 -> x14, waiting for transfers between devices: 48.8 us -> 14.4 us  [partner(): return lax.ppermute(block, axis, [(i, i ^ step) for i in range(size)])]
    all_to_all x1, waiting for transfers between devices: 0.01 us -> 33.2 us  [shards(): parts = lax.all_to_all(parts, PLANE, 0, 0, tiled=True)]
    all_to_all x0 -> x1, blocking collectives: none -> 11.6 us  [shards(): lax.all_to_all(kv_block, PLANE, 0, 0, tiled=True).reshape(total, HD)]
    all_to_all x1, blocking collectives: 34.9 us -> 28 us  [shards(): lax.all_to_all(attended, PLANE, 0, 0, tiled=True).reshape(total, width)]
    ppermute x23 -> x14, starting transfers between devices: 41.3 us -> 37.9 us  [partner(): return lax.ppermute(block, axis, [(i, i ^ step) for i in range(size)])]
    ppermute x1, waiting for transfers between devices: 1.74 us -> 3.81 us  [shards(): w_kv = lax.ppermute(w_keyval, ROW, kv_moves)]
    reduce_sum x1 -> x0, other arithmetic: 1.99 us -> none  [shards(): own = jnp.sum(query_parts.astype(F32), 0).astype(BF16)]
  transfers between devices with their start and end apart: 25 -> 16, of which waited for: 14 -> 8; matrix products, arithmetic and copies ran while one was open for 3% -> 1% of each run, Pallas kernels for 2% -> 0%
where the time goes in v3:
time: 150 us; the launch traced here: 149 us
  waiting for transfers between devices  51.4 us (34%)
  starting transfers between devices  46.6 us (31%)
  blocking collectives  39.5 us (26%)
  Pallas kernels  5.46 us (4%)
  local copies, waits for them, and re-layouts  2.39 us (2%)
  other arithmetic  1.64 us (1%)
    ppermute x14, starting transfers between devices, partner(): return lax.ppermute(block, axis, [(i, i ^ step) for i in range(size)])  37.9 us
    all_to_all x1, waiting for transfers between devices, shards(): parts = lax.all_to_all(parts, PLANE, 0, 0, tiled=True)  33.2 us
    all_to_all x1, blocking collectives, shards(): lax.all_to_all(attended, PLANE, 0, 0, tiled=True).reshape(total, width)  28 us
    ppermute x14, waiting for transfers between devices, partner(): return lax.ppermute(block, axis, [(i, i ^ step) for i in range(size)])  14.4 us
    all_to_all x1, blocking collectives, shards(): lax.all_to_all(kv_block, PLANE, 0, 0, tiled=True).reshape(total, HD)  11.6 us
    all_to_all x1, starting transfers between devices, shards(): parts = lax.all_to_all(parts, PLANE, 0, 0, tiled=True)  6.71 us
    pallas_call x5, Pallas kernels, call(): pl.pallas_call(kernel, out_shape=[jax.ShapeDtypeStruct(s, BF16) for s in...  5.46 us
    ppermute x1, waiting for transfers between devices, shards(): w_kv = lax.ppermute(w_keyval, ROW, kv_moves)  3.81 us
  transfers between devices with their start and end apart: 16, of which 8 were waited for; matrix products, arithmetic and copies ran while one was open for 1% of the time, Pallas kernels for 0%

profile of v3, /device:TPU:1, one launch (start us, length us, event | category | flops | bytes accessed | tf_op | source)
XLA Modules:
  0.0 148.5 jit_solution(16770175201564216303)
XLA Ops:
  0.0 2.5 %collective-permute-start = (bf16[128,512]{1,0:T(8,128)(2,1)}, bf16[128,512]{1,0:T(8,128)(2,1)S(1)}, u32[]{:S(2)}, u32[]{:S(2)}) collective-permute-start(bf16[128,512]{1,0:T(8,128)(2,1)} %refs_0_.1), channel_id=1, source_target_pairs={{0,64},{64,0},{128,192},{192,128},{1,65},{65,1},{129,193},{193,129... | collective-permute-start | bytes 393224 | tf_op jit(solution)/shard_map/ppermute | solution.py:38
  2.5 3.0 %collective-permute-start.1 = (bf16[128,512]{1,0:T(8,128)(2,1)}, bf16[128,512]{1,0:T(8,128)(2,1)S(1)}, u32[]{:S(2)}, u32[]{:S(2)}) collective-permute-start(bf16[128,512]{1,0:T(8,128)(2,1)} %refs_0_.1), channel_id=1, source_target_pairs={{0,128},{64,192},{128,0},{192,64},{1,129},{65,193},{129,1},{193,65... | collective-permute-start | bytes 393224 | tf_op jit(solution)/shard_map/ppermute | solution.py:38
  5.5 2.2 %collective-permute-start.3 = (bf16[128,512]{1,0:T(8,128)(2,1)}, bf16[128,512]{1,0:T(8,128)(2,1)S(1)}, u32[]{:S(2)}, u32[]{:S(2)}) collective-permute-start(bf16[128,512]{1,0:T(8,128)(2,1)} %refs_0_.1), channel_id=1, source_target_pairs={{0,32},{32,0},{1,33},{33,1},{2,34},{34,2},{3,35},{35,3},{4,36},{36... | collective-permute-start | bytes 393224 | tf_op jit(solution)/shard_map/ppermute | solution.py:38
  7.6 1.9 %collective-permute-start.7 = (bf16[512,128]{1,0:T(8,128)(2,1)}, bf16[512,128]{1,0:T(8,128)(2,1)S(1)}, u32[]{:S(2)}, u32[]{:S(2)}) collective-permute-start(bf16[512,128]{1,0:T(8,128)(2,1)} %param.6), channel_id=1, source_target_pairs={{0,0},{32,64},{64,128},{96,192},{128,32},{160,96},{192,160},{224,2... | collective-permute-start | bytes 393224 | tf_op jit(solution)/shard_map/ppermute | solution.py:146
  10.4 6.5 %collective-permute-start.5 = (bf16[128,512]{1,0:T(8,128)(2,1)S(1)}, bf16[128,512]{1,0:T(8,128)(2,1)S(1)}, u32[]{:S(2)}, u32[]{:S(2)}) collective-permute-start(bf16[128,512]{1,0:T(8,128)(2,1)S(1)} %collective-permute-done.1.refs_2_), channel_id=1, source_target_pairs={{0,32},{32,0},{1,33},{33,1},{2,34},{34,2},{3,35},{35,3},{4,36},{36... | collective-permute-start | bytes 393224 | tf_op jit(solution)/shard_map/ppermute | solution.py:38
  16.9 3.8 %collective-permute-done.7.refs_9_ = bf16[512,128]{1,0:T(8,128)(2,1)S(1)} collective-permute-done((bf16[512,128]{1,0:T(8,128)(2,1)}, bf16[512,128]{1,0:T(8,128)(2,1)S(1)}, u32[]{:S(2)}, u32[]{:S(2)}) %collective-permute-start.7) | collective-permute-done | bytes 131104 | tf_op jit(solution)/shard_map/ppermute | solution.py:146
  20.8 1.2 copy-done.1
  22.9 3.0 %shard_map.46 = bf16[16,64,1152]{2,1,0:T(8,128)(2,1)} custom-call(bf16[128,512]{1,0:T(8,128)(2,1)S(1)} %copy-done.2, bf16[128,512]{1,0:T(8,128)(2,1)S(1)} %collective-permute-done.refs_1_, bf16[128,512]{1,0:T(8,128)(2,1)S(1)} %collective-permute-done.1.refs_2_, bf16[128,512]{1,0:T(8,128)(2,1)S(1)} %collective-permute-done.2.refs_3_, ...), custom_call_target="tpu_custom_call" | custom-call | tf_op jit(solution)/shard_map/pallas_call | solution.py:120
  25.9 6.7 %all-to-all-start = ((bf16[16,64,1152]{2,1,0:T(8,128)(2,1)}), bf16[16,64,1152]{2,1,0:T(8,128)(2,1)S(1)}, u32[]{:S(2)}, u32[]{:S(2)}) async-start(bf16[16,64,1152]{2,1,0:T(8,128)(2,1)} %shard_map.46), calls=%async_computation | async-start | bytes 4718592 | tf_op jit(solution)/shard_map/all_to_all | solution.py:161
  33.5 33.2 %all-to-all-done.parts = bf16[16,64,1152]{2,1,0:T(8,128)(2,1)S(1)} async-done(((bf16[16,64,1152]{2,1,0:T(8,128)(2,1)}), bf16[16,64,1152]{2,1,0:T(8,128)(2,1)S(1)}, u32[]{:S(2)}, u32[]{:S(2)}) %all-to-all-start) | async-done | bytes 2359328 | tf_op jit(solution)/shard_map/all_to_all | solution.py:161
  67.0 5.6 %collective-permute-start.9 = (bf16[64,128]{1,0:T(8,128)(2,1)S(1)}, bf16[64,128]{1,0:T(8,128)(2,1)S(1)}, u32[]{:S(2)}, u32[]{:S(2)}) collective-permute-start(bf16[64,128]{1,0:T(8,128)(2,1)S(1)} %get-tuple-element.12.a), channel_id=1, source_target_pairs={{0,16},{16,0},{1,17},{17,1},{2,18},{18,2},{3,19},{19,3},{4,20},{20... | collective-permute-start | bytes 49160 | tf_op jit(solution)/shard_map/ppermute | solution.py:38
  73.8 11.6 %all_to_all.15 = bf16[16,64,128]{2,1,0:T(8,128)(2,1)S(1)} all-to-all(bf16[16,64,128]{2,1,0:T(8,128)(2,1)S(1)} %shard_map.48), channel_id=1, replica_groups=mesh['zl'=4,'core'=2,'zh'=2,'y'=4,'x'=4] {'y','x'}, dimensions={0} | all-to-all | bytes 524288 | tf_op jit(solution)/shard_map/all_to_all | solution.py:166
  85.4 1.4 collective-permute-start.10
  86.8 5.4 %collective-permute-start.8 = (bf16[64,1024]{1,0:T(8,128)(2,1)S(1)}, bf16[64,1024]{1,0:T(8,128)(2,1)S(1)}, u32[]{:S(2)}, u32[]{:S(2)}) collective-permute-start(bf16[64,1024]{1,0:T(8,128)(2,1)S(1)} %get-tuple-element.11.own), channel_id=1, source_target_pairs={{0,16},{16,0},{1,17},{17,1},{2,18},{18,2},{3,19},{19,3},{4,20},{20... | collective-permute-start | bytes 393224 | tf_op jit(solution)/shard_map/ppermute | solution.py:38
  92.2 3.6 %collective-permute-done.8.got = bf16[64,1024]{1,0:T(8,128)(2,1)S(1)} collective-permute-done((bf16[64,1024]{1,0:T(8,128)(2,1)S(1)}, bf16[64,1024]{1,0:T(8,128)(2,1)S(1)}, u32[]{:S(2)}, u32[]{:S(2)}) %collective-permute-start.8) | collective-permute-done | bytes 131104 | tf_op jit(solution)/shard_map/ppermute | solution.py:38
  95.8 1.9 %shard_map.49 = bf16[16,64,1024]{2,1,0:T(8,128)(2,1)S(1)} custom-call(s32[10]{0:T(128)S(1)} %stack.43.base, bf16[64,1024]{1,0:T(8,128)(2,1)S(1)} %get-tuple-element.11.own, bf16[64,1024]{1,0:T(8,128)(2,1)S(1)} %collective-permute-done.8.got, f32[64,128]{1,0:T(8,128)S(1)} %get-tuple-element.26.cosine, f32[64,128]{1,0:T(8,128)S(1)} %get-tuple-element.18.sine_v, ...), custom_call_target="tpu_custom_call" | custom-call | tf_op jit(solution)/shard_map/pallas_call | solution.py:120
  97.8 28.0 %all_to_all.16 = bf16[16,64,1024]{2,1,0:T(8,128)(2,1)S(1)} all-to-all(bf16[16,64,1024]{2,1,0:T(8,128)(2,1)S(1)} %shard_map.49), channel_id=1, replica_groups=mesh['zl'=4,'core'=2,'zh'=2,'y'=4,'x'=4] {'y','x'}, dimensions={0} | all-to-all | bytes 4194304 | tf_op jit(solution)/shard_map/all_to_all | solution.py:176
  126.6 4.3 %collective-permute-start.11 = (bf16[512,512]{1,0:T(8,128)(2,1)S(1)}, bf16[512,512]{1,0:T(8,128)(2,1)S(1)}, u32[]{:S(2)}, u32[]{:S(2)}) collective-permute-start(bf16[512,512]{1,0:T(8,128)(2,1)S(1)} %convolution_convert_fusion), channel_id=1, source_target_pairs={{0,32},{32,0},{1,33},{33,1},{2,34},{34,2},{3,35},{35,3},{4,36},{36... | collective-permute-start | bytes 1572872 | tf_op jit(solution)/shard_map/ppermute | solution.py:38
  132.6 4.0 %collective-permute-start.14 = (bf16[128,512]{1,0:T(8,128)(2,1)S(1)}, bf16[128,512]{1,0:T(8,128)(2,1)S(1)}, u32[]{:S(2)}, u32[]{:S(2)}) collective-permute-start(bf16[128,512]{1,0:T(8,128)(2,1)S(1)} %get-tuple-element.16), channel_id=1, source_target_pairs={{0,64},{64,0},{128,192},{192,128},{1,65},{65,1},{129,193},{193,129... | collective-permute-start | bytes 393224 | tf_op jit(solution)/shard_map/ppermute | solution.py:38
  136.5 1.3 collective-permute-start.13
  137.8 1.1 collective-permute-start.12
  138.9 1.2 collective-permute-done.14
  140.1 1.8 %collective-permute-done.13 = bf16[128,512]{1,0:T(8,128)(2,1)S(1)} collective-permute-done((bf16[128,512]{1,0:T(8,128)(2,1)S(1)}, bf16[128,512]{1,0:T(8,128)(2,1)S(1)}, u32[]{:S(2)}, u32[]{:S(2)}) %collective-permute-start.13) | collective-permute-done | bytes 131104 | tf_op jit(solution)/shard_map/ppermute | solution.py:38
  141.9 5.9 %collective-permute-done.12 = bf16[128,512]{1,0:T(8,128)(2,1)S(1)} collective-permute-done((bf16[128,512]{1,0:T(8,128)(2,1)S(1)}, bf16[128,512]{1,0:T(8,128)(2,1)S(1)}, u32[]{:S(2)}, u32[]{:S(2)}) %collective-permute-start.12) | collective-permute-done | bytes 131104 | tf_op jit(solution)/shard_map/ppermute | solution.py:38
  (36 shorter events, 7.5 us)
Async XLA Ops:
  0.0 125.9 %copy-start = (bf16[1024,512]{1,0:T(8,128)(2,1)S(1)}, bf16[1024,512]{1,0:T(8,128)(2,1)}, u32[]{:S(2)}) copy-start(bf16[1024,512]{1,0:T(8,128)(2,1)} %param.7) | copy-start | bytes 3145732
  0.0 9.5 %collective-permute-start = (bf16[128,512]{1,0:T(8,128)(2,1)}, bf16[128,512]{1,0:T(8,128)(2,1)S(1)}, u32[]{:S(2)}, u32[]{:S(2)}) collective-permute-start(bf16[128,512]{1,0:T(8,128)(2,1)} %refs_0_.1), channel_id=1, source_target_pairs={{0,64},{64,0},{128,192},{192,128},{1,65},{65,1},{129,193},{193,129... | collective-permute-start | bytes 393224 | tf_op jit(solution)/shard_map/ppermute | solution.py:38
  2.5 7.9 %collective-permute-start.1 = (bf16[128,512]{1,0:T(8,128)(2,1)}, bf16[128,512]{1,0:T(8,128)(2,1)S(1)}, u32[]{:S(2)}, u32[]{:S(2)}) collective-permute-start(bf16[128,512]{1,0:T(8,128)(2,1)} %refs_0_.1), channel_id=1, source_target_pairs={{0,128},{64,192},{128,0},{192,64},{1,129},{65,193},{129,1},{193,65... | collective-permute-start | bytes 393224 | tf_op jit(solution)/shard_map/ppermute | solution.py:38
  5.5 11.5 %collective-permute-start.2 = (bf16[128,512]{1,0:T(8,128)(2,1)}, bf16[128,512]{1,0:T(8,128)(2,1)S(1)}, u32[]{:S(2)}, u32[]{:S(2)}) collective-permute-start(bf16[128,512]{1,0:T(8,128)(2,1)} %refs_0_.1), channel_id=1, source_target_pairs={{0,192},{64,128},{128,64},{192,0},{1,193},{65,129},{129,65},{193,1... | collective-permute-start | bytes 393224 | tf_op jit(solution)/shard_map/ppermute | solution.py:38
  5.5 11.5 %collective-permute-start.3 = (bf16[128,512]{1,0:T(8,128)(2,1)}, bf16[128,512]{1,0:T(8,128)(2,1)S(1)}, u32[]{:S(2)}, u32[]{:S(2)}) collective-permute-start(bf16[128,512]{1,0:T(8,128)(2,1)} %refs_0_.1), channel_id=1, source_target_pairs={{0,32},{32,0},{1,33},{33,1},{2,34},{34,2},{3,35},{35,3},{4,36},{36... | collective-permute-start | bytes 393224 | tf_op jit(solution)/shard_map/ppermute | solution.py:38
  7.6 13.1 %collective-permute-start.7 = (bf16[512,128]{1,0:T(8,128)(2,1)}, bf16[512,128]{1,0:T(8,128)(2,1)S(1)}, u32[]{:S(2)}, u32[]{:S(2)}) collective-permute-start(bf16[512,128]{1,0:T(8,128)(2,1)} %param.6), channel_id=1, source_target_pairs={{0,0},{32,64},{64,128},{96,192},{128,32},{160,96},{192,160},{224,2... | collective-permute-start | bytes 393224 | tf_op jit(solution)/shard_map/ppermute | solution.py:146
  9.6 11.2 %collective-permute-start.4 = (bf16[128,512]{1,0:T(8,128)(2,1)S(1)}, bf16[128,512]{1,0:T(8,128)(2,1)S(1)}, u32[]{:S(2)}, u32[]{:S(2)}) collective-permute-start(bf16[128,512]{1,0:T(8,128)(2,1)S(1)} %collective-permute-done.refs_1_), channel_id=1, source_target_pairs={{0,32},{32,0},{1,33},{33,1},{2,34},{34,2},{3,35},{35,3},{4,36},{36... | collective-permute-start | bytes 393224 | tf_op jit(solution)/shard_map/ppermute | solution.py:38
  10.4 10.3 %collective-permute-start.5 = (bf16[128,512]{1,0:T(8,128)(2,1)S(1)}, bf16[128,512]{1,0:T(8,128)(2,1)S(1)}, u32[]{:S(2)}, u32[]{:S(2)}) collective-permute-start(bf16[128,512]{1,0:T(8,128)(2,1)S(1)} %collective-permute-done.1.refs_2_), channel_id=1, source_target_pairs={{0,32},{32,0},{1,33},{33,1},{2,34},{34,2},{3,35},{35,3},{4,36},{36... | collective-permute-start | bytes 393224 | tf_op jit(solution)/shard_map/ppermute | solution.py:38
  16.9 3.8 %collective-permute-start.6 = (bf16[128,512]{1,0:T(8,128)(2,1)S(1)}, bf16[128,512]{1,0:T(8,128)(2,1)S(1)}, u32[]{:S(2)}, u32[]{:S(2)}) collective-permute-start(bf16[128,512]{1,0:T(8,128)(2,1)S(1)} %collective-permute-done.2.refs_3_), channel_id=1, source_target_pairs={{0,32},{32,0},{1,33},{33,1},{2,34},{34,2},{3,35},{35,3},{4,36},{36... | collective-permute-start | bytes 393224 | tf_op jit(solution)/shard_map/ppermute | solution.py:38
  20.8 1.2 copy-start.1
  22.0 0.9 copy-start.2
  25.9 40.8 %all-to-all-start = ((bf16[16,64,1152]{2,1,0:T(8,128)(2,1)}), bf16[16,64,1152]{2,1,0:T(8,128)(2,1)S(1)}, u32[]{:S(2)}, u32[]{:S(2)}) async-start(bf16[16,64,1152]{2,1,0:T(8,128)(2,1)} %shard_map.46), calls=%async_computation | async-start | bytes 4718592 | tf_op jit(solution)/shard_map/all_to_all | solution.py:161
  66.7 5.9 %copy-start.3 = (f32[64,64]{1,0:T(8,128)S(1)}, f32[64,64]{1,0:T(8,128)}, u32[]{:S(2)}) copy-start(f32[64,64]{1,0:T(8,128)} %get-tuple-element.23) | copy-start | bytes 49156
  66.7 5.9 %copy-start.4 = (f32[64,64]{1,0:T(8,128)S(1)}, f32[64,64]{1,0:T(8,128)}, u32[]{:S(2)}) copy-start(f32[64,64]{1,0:T(8,128)} %get-tuple-element.24) | copy-start | bytes 49156
  66.7 5.9 %copy-start.5 = (f32[64,64]{1,0:T(8,128)S(1)}, f32[64,64]{1,0:T(8,128)}, u32[]{:S(2)}) copy-start(f32[64,64]{1,0:T(8,128)} %get-tuple-element.25) | copy-start | bytes 49156
  67.0 6.7 %collective-permute-start.9 = (bf16[64,128]{1,0:T(8,128)(2,1)S(1)}, bf16[64,128]{1,0:T(8,128)(2,1)S(1)}, u32[]{:S(2)}, u32[]{:S(2)}) collective-permute-start(bf16[64,128]{1,0:T(8,128)(2,1)S(1)} %get-tuple-element.12.a), channel_id=1, source_target_pairs={{0,16},{16,0},{1,17},{17,1},{2,18},{18,2},{3,19},{19,3},{4,20},{20... | collective-permute-start | bytes 49160 | tf_op jit(solution)/shard_map/ppermute | solution.py:38
  85.4 10.4 %collective-permute-start.10 = (bf16[1024,128]{1,0:T(8,128)(2,1)S(1)}, bf16[1024,128]{1,0:T(8,128)(2,1)S(1)}, u32[]{:S(2)}, u32[]{:S(2)}) collective-permute-start(bf16[1024,128]{1,0:T(8,128)(2,1)S(1)} %bitcast.17), channel_id=1, source_target_pairs={{0,32},{32,0},{1,33},{33,1},{2,34},{34,2},{3,35},{35,3},{4,36},{36... | collective-permute-start | bytes 786440 | tf_op jit(solution)/shard_map/ppermute | solution.py:38
  86.8 9.0 %collective-permute-start.8 = (bf16[64,1024]{1,0:T(8,128)(2,1)S(1)}, bf16[64,1024]{1,0:T(8,128)(2,1)S(1)}, u32[]{:S(2)}, u32[]{:S(2)}) collective-permute-start(bf16[64,1024]{1,0:T(8,128)(2,1)S(1)} %get-tuple-element.11.own), channel_id=1, source_target_pairs={{0,16},{16,0},{1,17},{17,1},{2,18},{18,2},{3,19},{19,3},{4,20},{20... | collective-permute-start | bytes 393224 | tf_op jit(solution)/shard_map/ppermute | solution.py:38
  126.6 5.8 %collective-permute-start.11 = (bf16[512,512]{1,0:T(8,128)(2,1)S(1)}, bf16[512,512]{1,0:T(8,128)(2,1)S(1)}, u32[]{:S(2)}, u32[]{:S(2)}) collective-permute-start(bf16[512,512]{1,0:T(8,128)(2,1)S(1)} %convolution_convert_fusion), channel_id=1, source_target_pairs={{0,32},{32,0},{1,33},{33,1},{2,34},{34,2},{3,35},{35,3},{4,36},{36... | collective-permute-start | bytes 1572872 | tf_op jit(solution)/shard_map/ppermute | solution.py:38
  132.6 7.6 %collective-permute-start.14 = (bf16[128,512]{1,0:T(8,128)(2,1)S(1)}, bf16[128,512]{1,0:T(8,128)(2,1)S(1)}, u32[]{:S(2)}, u32[]{:S(2)}) collective-permute-start(bf16[128,512]{1,0:T(8,128)(2,1)S(1)} %get-tuple-element.16), channel_id=1, source_target_pairs={{0,64},{64,0},{128,192},{192,128},{1,65},{65,1},{129,193},{193,129... | collective-permute-start | bytes 393224 | tf_op jit(solution)/shard_map/ppermute | solution.py:38
  136.5 5.4 %collective-permute-start.13 = (bf16[128,512]{1,0:T(8,128)(2,1)S(1)}, bf16[128,512]{1,0:T(8,128)(2,1)S(1)}, u32[]{:S(2)}, u32[]{:S(2)}) collective-permute-start(bf16[128,512]{1,0:T(8,128)(2,1)S(1)} %get-tuple-element.15), channel_id=1, source_target_pairs={{0,128},{64,192},{128,0},{192,64},{1,129},{65,193},{129,1},{193,65... | collective-permute-start | bytes 393224 | tf_op jit(solution)/shard_map/ppermute | solution.py:38
  137.8 10.0 %collective-permute-start.12 = (bf16[128,512]{1,0:T(8,128)(2,1)S(1)}, bf16[128,512]{1,0:T(8,128)(2,1)S(1)}, u32[]{:S(2)}, u32[]{:S(2)}) collective-permute-start(bf16[128,512]{1,0:T(8,128)(2,1)S(1)} %get-tuple-element.14), channel_id=1, source_target_pairs={{0,192},{64,128},{128,64},{192,0},{1,193},{65,129},{129,65},{193,1... | collective-permute-start | bytes 393224 | tf_op jit(solution)/shard_map/ppermute | solution.py:38

commit v4 on v3

--- a/solution.py
+++ b/solution.py
@@ -18,7 +18,7 @@
 F32 = jnp.float32
 VMEM = pl.BlockSpec(memory_space=pltpu.VMEM)
 SMEM = pl.BlockSpec(memory_space=pltpu.SMEM)
-PARAMS = pltpu.CompilerParams(vmem_limit_bytes=32 * 1024 * 1024)
+HBM = pl.BlockSpec(memory_space=pltpu.HBM)
 
 
 def tables(positions, width):
@@ -38,36 +38,64 @@
     return lax.ppermute(block, axis, [(i, i ^ step) for i in range(size)])
 
 
-def projection_kernel(*refs):
-    blocks, w_query, w_kv, out = refs[:8], refs[8], refs[9], refs[10]
-    per_chunk = out.shape[1]
+def projection_kernel(place, own, *refs):
+    blocks, w_hbm, w_kv = refs[:7], refs[7], refs[8]
+    outs_x, outs_y = refs[9:13], refs[13:17]
+    chunks, w_query, first, sems = refs[17:]
+    copies = [pltpu.make_async_copy(own, first, sems.at[4])]
+    rows = w_query.shape[0] // 4
+    for i in range(4):
+        part = pl.ds(i * rows, rows)
+        copies.append(pltpu.make_async_copy(w_hbm.at[part], w_query.at[part], sems.at[i]))
+    for copy in copies:
+        copy.start()
+    for copy in copies:
+        copy.wait()
+    size = chunks.shape[1]
     width = w_query.shape[1]
-    for i, block in enumerate(blocks):
+    for i, block in enumerate([first, *blocks]):
         query = jnp.dot(block[...], w_query[...], preferred_element_type=F32).astype(BF16)
         keyval = jnp.dot(block[...], w_kv[...], preferred_element_type=F32).astype(BF16)
         for b in range(2):
-            part = slice(b * per_chunk, (b + 1) * per_chunk)
-            out[2 * i + b, :, :width] = query[part]
-            out[2 * i + b, :, width:] = keyval[part]
-
-
-def sums_kernel(parts, query, keyval):
-    width = query.shape[1]
-    total = parts[0].astype(F32)
-    for c in range(1, parts.shape[0]):
-        total += parts[c].astype(F32)
-    query[...] = total[:, :width].astype(BF16)
-    keyval[...] = total[:, width:].astype(BF16)
+            part = slice(b * size, (b + 1) * size)
+            chunks[2 * i + b, :, :width] = query[part]
+            chunks[2 * i + b, :, width:] = keyval[part]
+    x, y = place[0], place[1]
+    for s in range(4):
+        for j in range(4):
+            outs_x[s][j] = chunks[4 * j + (x ^ s), : size // 2, :]
+            outs_y[s][j] = chunks[4 * (y ^ s) + j, size // 2 :, :]
+
+
+def halve_kernel(place, a, b, c, d, own, *outs):
+    for t, out in enumerate([own, *outs]):
+        j = place[0] ^ t
+        total = a[j].astype(F32) + b[j].astype(F32) + c[j].astype(F32) + d[j].astype(F32)
+        out[...] = total.astype(out.dtype)
+
+
+def join_kernel(*refs):
+    out = refs[8]
+    rows = out.shape[0] // 2
+    for side in range(2):
+        total = functools.reduce(
+            jnp.add, [ref[...].astype(F32) for ref in refs[4 * side : 4 * side + 4]]
+        )
+        out[side * rows : (side + 1) * rows, :] = total.astype(BF16)
 
 
 def keys_kernel(a, b, cosine, sine_v, out):
-    total = (a[...].astype(F32) + b[...].astype(F32)).astype(BF16).astype(F32)
+    width = a.shape[1] - HD
+    total = a[:, width:].astype(F32) + b[:, width:].astype(F32)
+    total = total.astype(BF16).astype(F32)
     block = rotate(total, cosine[...], sine_v[...]).astype(BF16)
     for c in range(out.shape[0]):
         out[c] = block
 
 
-def attention_kernel(heads, base, own, got, cosine, sine_v, kv_own, kv_other, out, queries, pair):
+def attention_kernel(
+    heads, base, own, got, cosine, sine_v, kv_own, kv_other, low, high, queries, pair
+):
     per_chunk = own.shape[0]
     half = kv_own.shape[0] // 2
     for side in range(2):
@@ -103,10 +131,32 @@
         totals += jnp.sum(weights, 1, keepdims=True)
         mixed += jnp.dot(weights.astype(BF16), values, preferred_element_type=F32)
     attended = (mixed / totals).astype(BF16)
+    cut = per_chunk // 2
     for h in range(heads):
-        block = attended[h * per_chunk : (h + 1) * per_chunk]
-        for c in range(out.shape[0]):
-            out[c, :, h * HD : (h + 1) * HD] = block
+        cols = slice(h * HD, (h + 1) * HD)
+        low[:, cols] = attended[h * per_chunk : h * per_chunk + cut]
+        high[:, cols] = attended[h * per_chunk + cut : (h + 1) * per_chunk]
+
+
+def stack_kernel(*refs):
+    for s, ref in enumerate(refs[:4]):
+        refs[4][s] = ref[...]
+
+
+def output_kernel(place, *refs):
+    by_y, by_x, weight, kept, sent, chunks = refs[:4], refs[4:8], *refs[8:]
+    x, y = place[0], place[1]
+    rows, width = by_y[0].shape[1:]
+    for side, arrays in enumerate((by_y, by_x)):
+        for t, array in enumerate(arrays):
+            block = array[...].reshape(4 * rows, width)
+            product = jnp.dot(block, weight[...], preferred_element_type=F32).astype(BF16)
+            for s in range(4):
+                k = 4 * (y ^ t) + (x ^ s) if side == 0 else 4 * (y ^ s) + (x ^ t)
+                chunks[k, side * rows : (side + 1) * rows, :] = product[s * rows : (s + 1) * rows]
+    half = kept.shape[0]
+    kept[...] = chunks[:half]
+    sent[...] = chunks[half:]
 
 
 def chip_kernel(kept, got, *outs):
@@ -116,14 +166,18 @@
         out[...] = (kept[part, :].astype(F32) + got[part, :].astype(F32)).astype(BF16)
 
 
-def call(kernel, outs, args, scratch=(), scalars=0):
+def call(kernel, outs, args, specs=(), scratch=()):
+    specs = list(specs) + [VMEM] * (len(args) - len(specs))
     return pl.pallas_call(
         kernel,
-        out_shape=[jax.ShapeDtypeStruct(s, BF16) for s in outs],
-        in_specs=[SMEM] * scalars + [VMEM] * (len(args) - scalars),
+        out_shape=[
+            s if isinstance(s, jax.ShapeDtypeStruct) else jax.ShapeDtypeStruct(s, BF16)
+            for s in outs
+        ],
+        in_specs=specs,
         out_specs=[VMEM] * len(outs),
         scratch_shapes=list(scratch),
-        compiler_params=PARAMS,
+        compiler_params=pltpu.CompilerParams(vmem_limit_bytes=32 * 1024 * 1024),
     )(*args)
 
 
@@ -136,12 +190,13 @@
     half = per_row * Z_LO
     total = half * 2
     per_chunk = total // (Y * X)
+    cut = per_chunk // 2
     width = w_query.shape[1]
     heads = width // HD
+    both = width + HD
 
     mine = [tokens] + [partner(tokens, "zl", s) for s in (1, 2, 3)]
     others = [partner(block, "core", 1) for block in mine]
-    everyone = mine + others
     kv_moves = [(e, 2 * e if e < 4 else 2 * (e - 4) + 1) for e in range(8)]
     w_kv = lax.ppermute(w_keyval, ROW, kv_moves)
 
@@ -154,29 +209,64 @@
     cosine, sine_v = tables((row_start + jnp.arange(per_chunk)).astype(F32), HD)
     key_cos = jnp.where(core == 0, cosine, 1.0)
     key_sin = jnp.where(core == 0, sine_v, 0.0)
-
-    (parts,) = call(
-        projection_kernel, [(Y * X, per_chunk, width + HD)], [*everyone, w_query, w_kv]
-    )
-    parts = lax.all_to_all(parts, PLANE, 0, 0, tiled=True)
-    query, kv = call(sums_kernel, [(per_chunk, width), (per_chunk, HD)], [parts])
-    (kv_block,) = call(
-        keys_kernel, [(Y * X, per_chunk, HD)], [kv, partner(kv, "zh", 1), key_cos, key_sin]
-    )
+    place_xy = jnp.stack([x, y]).astype(jnp.int32)
+    place_yx = jnp.stack([y, x]).astype(jnp.int32)
+
+    parts = call(
+        projection_kernel,
+        [(4, cut, both)] * 8,
+        [place_xy, tokens, *mine[1:], *others, w_query, w_kv],
+        [SMEM, HBM, *[VMEM] * 7, HBM],
+        [
+            pltpu.VMEM((Y * X, per_chunk, both), BF16),
+            pltpu.VMEM(w_query.shape, BF16),
+            pltpu.VMEM(tokens.shape, BF16),
+            pltpu.SemaphoreType.DMA((5,)),
+        ],
+    )
+    summed = []
+    for place, first, second, pieces in (
+        (place_yx, "x", "y", parts[:4]),
+        (place_xy, "y", "x", parts[4:]),
+    ):
+        got = [partner(pieces[s], first, s) for s in (1, 2, 3)]
+        own, *sends = call(
+            halve_kernel,
+            [jax.ShapeDtypeStruct((cut, both), F32), *[(cut, both)] * 3],
+            [place, pieces[0], *got],
+            [SMEM],
+        )
+        summed += [own] + [partner(sends[t - 1], second, t) for t in (1, 2, 3)]
+    (own,) = call(join_kernel, [(per_chunk, both)], summed)
+    got = partner(own, "zh", 1)
+
+    (kv_block,) = call(keys_kernel, [(Y * X, per_chunk, HD)], [own, got, key_cos, key_sin])
     kv_own = lax.all_to_all(kv_block, PLANE, 0, 0, tiled=True).reshape(total, HD)
     kv_other = partner(kv_own, "core", 1)
-    query_got = partner(query, "zh", 1)
-    (attended,) = call(
+    low, high = call(
         functools.partial(attention_kernel, heads),
-        [(Y * X, per_chunk, width)],
-        [base, query, query_got, cosine, sine_v, kv_own, kv_other],
+        [(cut, width)] * 2,
+        [base, own, got, cosine, sine_v, kv_own, kv_other],
+        [SMEM],
         [pltpu.VMEM((heads * per_chunk, HD), BF16), pltpu.VMEM((2, total, HD), BF16)],
-        scalars=1,
-    )
-    attended = lax.all_to_all(attended, PLANE, 0, 0, tiled=True).reshape(total, width)
-
-    sent = jnp.dot(attended[half:], w_output, preferred_element_type=F32).astype(BF16)
-    kept = jnp.dot(attended[:half], w_output, preferred_element_type=F32).astype(BF16)
+    )
+
+    gathered = []
+    for first, second, block in (("x", "y", low), ("y", "x", high)):
+        (line,) = call(
+            stack_kernel,
+            [(4, cut, width)],
+            [block] + [partner(block, first, s) for s in (1, 2, 3)],
+        )
+        gathered += [line] + [partner(line, second, t) for t in (1, 2, 3)]
+    kept, sent = call(
+        output_kernel,
+        [(Y * X // 2, per_chunk, features)] * 2,
+        [place_xy, *gathered, w_output],
+        [SMEM],
+        [pltpu.VMEM((Y * X, per_chunk, features), BF16)],
+    )
+    kept, sent = kept.reshape(half, features), sent.reshape(half, features)
     chip = call(chip_kernel, [(per_row, features)] * 4, [kept, partner(sent, "core", 1)])
     blocks = [chip[0]] + [partner(chip[s], "zl", s) for s in (3, 2, 1)]
     return functools.reduce(jnp.add, [b.astype(F32) for b in blocks]).astype(BF16)

time: 150 us -> 141 us (0.940)
  blocking collectives: 39.5 us -> 12.1 us
  starting transfers between devices: 46.6 us -> 66.7 us
  Pallas kernels: 5.46 us -> 8.53 us
  waiting for transfers between devices: 51.4 us -> 49.8 us
    all_to_all x1 -> x0, waiting for transfers between devices: 33.2 us -> none  [shards(): parts = lax.all_to_all(parts, PLANE, 0, 0, tiled=True)]
    ppermute x14 -> x37, waiting for transfers between devices: 14.4 us -> 46.1 us  [partner(): return lax.ppermute(block, axis, [(i, i ^ step) for i in range(size)])]
    all_to_all x1 -> x0, blocking collectives: 28 us -> none  [shards(): lax.all_to_all(attended, PLANE, 0, 0, tiled=True).reshape(total, width)]
    ppermute x14 -> x37, starting transfers between devices: 37.9 us -> 64.8 us  [partner(): return lax.ppermute(block, axis, [(i, i ^ step) for i in range(size)])]
    all_to_all x1 -> x0, starting transfers between devices: 6.71 us -> none  [shards(): parts = lax.all_to_all(parts, PLANE, 0, 0, tiled=True)]
    pallas_call x5 -> x10, Pallas kernels: 5.46 us -> 8.53 us  [call(): pl.pallas_call(kernel, out_shape=[s if isinstance(s, jax.ShapeDtypeStruct...]
  transfers between devices with their start and end apart: 16 -> 38, of which waited for: 8 -> 18; matrix products, arithmetic and copies ran while one was open for 1% -> 0% of each run, Pallas kernels for 0% -> 1%
where the time goes in v4:
time: 141 us
  starting transfers between devices  66.7 us (47%)
  waiting for transfers between devices  49.8 us (35%)
  blocking collectives  12.1 us (9%)
  Pallas kernels  8.53 us (6%)
  local copies, waits for them, and re-layouts  2.21 us (2%)
    ppermute x37, starting transfers between devices, partner(): return lax.ppermute(block, axis, [(i, i ^ step) for i in range(size)])  64.8 us
    ppermute x37, waiting for transfers between devices, partner(): return lax.ppermute(block, axis, [(i, i ^ step) for i in range(size)])  46.1 us
    all_to_all x1, blocking collectives, shards(): lax.all_to_all(kv_block, PLANE, 0, 0, tiled=True).reshape(total, HD)  12.1 us
    pallas_call x10, Pallas kernels, call(): pl.pallas_call(kernel, out_shape=[s if isinstance(s, jax.ShapeDtypeStruct...  8.53 us
    ppermute x1, waiting for transfers between devices, shards(): w_kv = lax.ppermute(w_keyval, ROW, kv_moves)  3.74 us
  transfers between devices with their start and end apart: 38, of which 18 were waited for; matrix products, arithmetic and copies ran while one was open for 0% of the time, Pallas kernels for 1%

profile of v4, /device:TPU:1, one launch (start us, length us, event | category | flops | bytes accessed | tf_op | source)
XLA Modules:
  0.0 140.8 jit_solution(8104910130278095754)
XLA Ops:
  0.0 2.5 %collective-permute-start = (bf16[128,512]{1,0:T(8,128)(2,1)}, bf16[128,512]{1,0:T(8,128)(2,1)S(1)}, u32[]{:S(2)}, u32[]{:S(2)}) collective-permute-start(bf16[128,512]{1,0:T(8,128)(2,1)} %own.1), channel_id=1, source_target_pairs={{0,64},{64,0},{128,192},{192,128},{1,65},{65,1},{129,193},{193,129... | collective-permute-start | bytes 393224 | tf_op jit(solution)/shard_map/ppermute | solution.py:38
  2.5 3.0 %collective-permute-start.1 = (bf16[128,512]{1,0:T(8,128)(2,1)}, bf16[128,512]{1,0:T(8,128)(2,1)S(1)}, u32[]{:S(2)}, u32[]{:S(2)}) collective-permute-start(bf16[128,512]{1,0:T(8,128)(2,1)} %own.1), channel_id=1, source_target_pairs={{0,128},{64,192},{128,0},{192,64},{1,129},{65,193},{129,1},{193,65... | collective-permute-start | bytes 393224 | tf_op jit(solution)/shard_map/ppermute | solution.py:38
  5.5 2.2 %collective-permute-start.3 = (bf16[128,512]{1,0:T(8,128)(2,1)}, bf16[128,512]{1,0:T(8,128)(2,1)S(1)}, u32[]{:S(2)}, u32[]{:S(2)}) collective-permute-start(bf16[128,512]{1,0:T(8,128)(2,1)} %own.1), channel_id=1, source_target_pairs={{0,32},{32,0},{1,33},{33,1},{2,34},{34,2},{3,35},{35,3},{4,36},{36... | collective-permute-start | bytes 393224 | tf_op jit(solution)/shard_map/ppermute | solution.py:38
  10.4 6.5 %collective-permute-start.5 = (bf16[128,512]{1,0:T(8,128)(2,1)S(1)}, bf16[128,512]{1,0:T(8,128)(2,1)S(1)}, u32[]{:S(2)}, u32[]{:S(2)}) collective-permute-start(bf16[128,512]{1,0:T(8,128)(2,1)S(1)} %collective-permute-done.1.refs_1_), channel_id=1, source_target_pairs={{0,32},{32,0},{1,33},{33,1},{2,34},{34,2},{3,35},{35,3},{4,36},{36... | collective-permute-start | bytes 393224 | tf_op jit(solution)/shard_map/ppermute | solution.py:38
  17.0 3.7 %collective-permute-done.7.refs_8_ = bf16[512,128]{1,0:T(8,128)(2,1)S(1)} collective-permute-done((bf16[512,128]{1,0:T(8,128)(2,1)}, bf16[512,128]{1,0:T(8,128)(2,1)S(1)}, u32[]{:S(2)}, u32[]{:S(2)}) %collective-permute-start.7) | collective-permute-done | bytes 131104 | tf_op jit(solution)/shard_map/ppermute | solution.py:201
  22.9 3.3 %shard_map.46 = (bf16[4,32,1152]{2,1,0:T(8,128)(2,1)S(1)}, bf16[4,32,1152]{2,1,0:T(8,128)(2,1)S(1)}, bf16[4,32,1152]{2,1,0:T(8,128)(2,1)S(1)}, bf16[4,32,1152]{2...) custom-call(s32[2]{0:T(128)S(1)} %pad_add_fusion.place, ...), custom_call_target="tpu_custom_call" | custom-call | tf_op jit(solution)/shard_map/pallas_call | solution.py:171
  27.5 2.6 %collective-permute-start.15 = (bf16[4,32,1152]{2,1,0:T(8,128)(2,1)}, bf16[4,32,1152]{2,1,0:T(8,128)(2,1)S(1)}, u32[]{:S(2)}, u32[]{:S(2)}) collective-permute-start(bf16[4,32,1152]{2,1,0:T(8,128)(2,1)} %get-tuple-element.39), channel_id=1, source_target_pairs={{0,8},{4,12},{8,0},{12,4},{1,9},{5,13},{9,1},{13,5},{2,10},{6,14},... | collective-permute-start | bytes 884744 | tf_op jit(solution)/shard_map/ppermute | solution.py:38
  30.2 2.5 %collective-permute-start.10 = (bf16[4,32,1152]{2,1,0:T(8,128)(2,1)S(1)}, bf16[4,32,1152]{2,1,0:T(8,128)(2,1)S(1)}, u32[]{:S(2)}, u32[]{:S(2)}) collective-permute-start(bf16[4,32,1152]{2,1,0:T(8,128)(2,1)S(1)} %get-tuple-element.32), channel_id=1, source_target_pairs={{0,3},{1,2},{2,1},{3,0},{4,7},{5,6},{6,5},{7,4},{8,11},{9,10},{10,... | collective-permute-start | bytes 884744 | tf_op jit(solution)/shard_map/ppermute | solution.py:38
  32.6 2.7 %collective-permute-done.14.b = bf16[4,32,1152]{2,1,0:T(8,128)(2,1)S(1)} collective-permute-done((bf16[4,32,1152]{2,1,0:T(8,128)(2,1)S(1)}, bf16[4,32,1152]{2,1,0:T(8,128)(2,1)S(1)}, u32[]{:S(2)}, u32[]{:S(2)}) %collective-permute-start.14) | collective-permute-done | bytes 294944 | tf_op jit(solution)/shard_map/ppermute | solution.py:38
  35.4 2.7 %collective-permute-start.9 = (bf16[4,32,1152]{2,1,0:T(8,128)(2,1)S(1)}, bf16[4,32,1152]{2,1,0:T(8,128)(2,1)S(1)}, u32[]{:S(2)}, u32[]{:S(2)}) collective-permute-start(bf16[4,32,1152]{2,1,0:T(8,128)(2,1)S(1)} %get-tuple-element.31), channel_id=1, source_target_pairs={{0,2},{1,3},{2,0},{3,1},{4,6},{5,7},{6,4},{7,5},{8,10},{9,11},{10,... | collective-permute-start | bytes 884744 | tf_op jit(solution)/shard_map/ppermute | solution.py:38
  38.1 4.1 %collective-permute-done.15.c = bf16[4,32,1152]{2,1,0:T(8,128)(2,1)S(1)} collective-permute-done((bf16[4,32,1152]{2,1,0:T(8,128)(2,1)}, bf16[4,32,1152]{2,1,0:T(8,128)(2,1)S(1)}, u32[]{:S(2)}, u32[]{:S(2)}) %collective-permute-start.15) | collective-permute-done | bytes 294944 | tf_op jit(solution)/shard_map/ppermute | solution.py:38
  42.3 3.2 %collective-permute-done.16.d = bf16[4,32,1152]{2,1,0:T(8,128)(2,1)S(1)} collective-permute-done((bf16[4,32,1152]{2,1,0:T(8,128)(2,1)S(1)}, bf16[4,32,1152]{2,1,0:T(8,128)(2,1)S(1)}, u32[]{:S(2)}, u32[]{:S(2)}) %collective-permute-start.16) | collective-permute-done | bytes 294944 | tf_op jit(solution)/shard_map/ppermute | solution.py:38
  47.2 2.7 %collective-permute-start.18 = (bf16[32,1152]{1,0:T(8,128)(2,1)S(1)}, bf16[32,1152]{1,0:T(8,128)(2,1)S(1)}, u32[]{:S(2)}, u32[]{:S(2)}) collective-permute-start(bf16[32,1152]{1,0:T(8,128)(2,1)S(1)} %get-tuple-element.43), channel_id=1, source_target_pairs={{0,2},{1,3},{2,0},{3,1},{4,6},{5,7},{6,4},{7,5},{8,10},{9,11},{10,... | collective-permute-start | bytes 221192 | tf_op jit(solution)/shard_map/ppermute | solution.py:38
  52.0 2.7 %collective-permute-start.13 = (bf16[32,1152]{1,0:T(8,128)(2,1)S(1)}, bf16[32,1152]{1,0:T(8,128)(2,1)S(1)}, u32[]{:S(2)}, u32[]{:S(2)}) collective-permute-start(bf16[32,1152]{1,0:T(8,128)(2,1)S(1)} %get-tuple-element.36), channel_id=1, source_target_pairs={{0,12},{4,8},{8,4},{12,0},{1,13},{5,9},{9,5},{13,1},{2,14},{6,10},... | collective-permute-start | bytes 221192 | tf_op jit(solution)/shard_map/ppermute | solution.py:38
  58.3 5.5 %collective-permute-start.20 = (bf16[64,1152]{1,0:T(8,128)(2,1)S(1)}, bf16[64,1152]{1,0:T(8,128)(2,1)S(1)}, u32[]{:S(2)}, u32[]{:S(2)}) collective-permute-start(bf16[64,1152]{1,0:T(8,128)(2,1)S(1)} %shard_map.49.a.own), channel_id=1, source_target_pairs={{0,16},{16,0},{1,17},{17,1},{2,18},{18,2},{3,19},{19,3},{4,20},{20... | collective-permute-start | bytes 442376 | tf_op jit(solution)/shard_map/ppermute | solution.py:38
  64.1 4.7 %collective-permute-done.20.b.got = bf16[64,1152]{1,0:T(8,128)(2,1)S(1)} collective-permute-done((bf16[64,1152]{1,0:T(8,128)(2,1)S(1)}, bf16[64,1152]{1,0:T(8,128)(2,1)S(1)}, u32[]{:S(2)}, u32[]{:S(2)}) %collective-permute-start.20) | collective-permute-done | bytes 147488 | tf_op jit(solution)/shard_map/ppermute | solution.py:38
  69.0 12.1 %all_to_all.5 = bf16[16,64,128]{2,1,0:T(8,128)(2,1)S(1)} all-to-all(bf16[16,64,128]{2,1,0:T(8,128)(2,1)S(1)} %shard_map.50), channel_id=1, replica_groups=mesh['zl'=4,'core'=2,'zh'=2,'y'=4,'x'=4] {'y','x'}, dimensions={0} | all-to-all | bytes 524288 | tf_op jit(solution)/shard_map/all_to_all | solution.py:244
  81.1 3.6 %collective-permute-start.21 = (bf16[1024,128]{1,0:T(8,128)(2,1)S(1)}, bf16[1024,128]{1,0:T(8,128)(2,1)S(1)}, u32[]{:S(2)}, u32[]{:S(2)}) collective-permute-start(bf16[1024,128]{1,0:T(8,128)(2,1)S(1)} %bitcast.15), channel_id=1, source_target_pairs={{0,32},{32,0},{1,33},{33,1},{2,34},{34,2},{3,35},{35,3},{4,36},{36... | collective-permute-start | bytes 786440 | tf_op jit(solution)/shard_map/ppermute | solution.py:38
  98.6 2.8 %collective-permute-done.22.refs_1_ = bf16[32,1024]{1,0:T(8,128)(2,1)S(1)} collective-permute-done((bf16[32,1024]{1,0:T(8,128)(2,1)S(1)}, bf16[32,1024]{1,0:T(8,128)(2,1)S(1)}, u32[]{:S(2)}, u32[]{:S(2)}) %collective-permute-start.22) | collective-permute-done | bytes 65568 | tf_op jit(solution)/shard_map/ppermute | solution.py:38
  103.2 2.6 %collective-permute-start.26 = (bf16[4,32,1024]{2,1,0:T(8,128)(2,1)S(1)}, bf16[4,32,1024]{2,1,0:T(8,128)(2,1)S(1)}, u32[]{:S(2)}, u32[]{:S(2)}) collective-permute-start(bf16[4,32,1024]{2,1,0:T(8,128)(2,1)S(1)} %shard_map.52.refs_0_), channel_id=1, source_target_pairs={{0,8},{4,12},{8,0},{12,4},{1,9},{5,13},{9,1},{13,5},{2,10},{6,14},... | collective-permute-start | bytes 786440 | tf_op jit(solution)/shard_map/ppermute | solution.py:38
  109.0 6.5 %collective-permute-done.33.refs_7_ = bf16[4,32,1024]{2,1,0:T(8,128)(2,1)S(1)} collective-permute-done((bf16[4,32,1024]{2,1,0:T(8,128)(2,1)S(1)}, bf16[4,32,1024]{2,1,0:T(8,128)(2,1)S(1)}, u32[]{:S(2)}, u32[]{:S(2)}) %collective-permute-start.33) | collective-permute-done | bytes 262176 | tf_op jit(solution)/shard_map/ppermute | solution.py:38
  117.5 6.7 %collective-permute-start.34 = (bf16[512,512]{1,0:T(8,128)(2,1)S(1)}, bf16[512,512]{1,0:T(8,128)(2,1)S(1)}, u32[]{:S(2)}, u32[]{:S(2)}) collective-permute-start(bf16[512,512]{1,0:T(8,128)(2,1)S(1)} %bitcast.18), channel_id=1, source_target_pairs={{0,32},{32,0},{1,33},{33,1},{2,34},{34,2},{3,35},{35,3},{4,36},{36... | collective-permute-start | bytes 1572872 | tf_op jit(solution)/shard_map/ppermute | solution.py:38
  129.5 3.0 %collective-permute-done.35 = bf16[128,512]{1,0:T(8,128)(2,1)S(1)} collective-permute-done((bf16[128,512]{1,0:T(8,128)(2,1)S(1)}, bf16[128,512]{1,0:T(8,128)(2,1)S(1)}, u32[]{:S(2)}, u32[]{:S(2)}) %collective-permute-start.35) | collective-permute-done | bytes 131104 | tf_op jit(solution)/shard_map/ppermute | solution.py:38
  132.5 7.6 %collective-permute-done.36 = bf16[128,512]{1,0:T(8,128)(2,1)S(1)} collective-permute-done((bf16[128,512]{1,0:T(8,128)(2,1)S(1)}, bf16[128,512]{1,0:T(8,128)(2,1)S(1)}, u32[]{:S(2)}, u32[]{:S(2)}) %collective-permute-start.36) | collective-permute-done | bytes 131104 | tf_op jit(solution)/shard_map/ppermute | solution.py:38
  (77 shorter events, 41.0 us)
Async XLA Ops:
  0.0 9.5 %collective-permute-start = (bf16[128,512]{1,0:T(8,128)(2,1)}, bf16[128,512]{1,0:T(8,128)(2,1)S(1)}, u32[]{:S(2)}, u32[]{:S(2)}) collective-permute-start(bf16[128,512]{1,0:T(8,128)(2,1)} %own.1), channel_id=1, source_target_pairs={{0,64},{64,0},{128,192},{192,128},{1,65},{65,1},{129,193},{193,129... | collective-permute-start | bytes 393224 | tf_op jit(solution)/shard_map/ppermute | solution.py:38
  2.5 7.9 %collective-permute-start.1 = (bf16[128,512]{1,0:T(8,128)(2,1)}, bf16[128,512]{1,0:T(8,128)(2,1)S(1)}, u32[]{:S(2)}, u32[]{:S(2)}) collective-permute-start(bf16[128,512]{1,0:T(8,128)(2,1)} %own.1), channel_id=1, source_target_pairs={{0,128},{64,192},{128,0},{192,64},{1,129},{65,193},{129,1},{193,65... | collective-permute-start | bytes 393224 | tf_op jit(solution)/shard_map/ppermute | solution.py:38
  5.5 11.5 %collective-permute-start.2 = (bf16[128,512]{1,0:T(8,128)(2,1)}, bf16[128,512]{1,0:T(8,128)(2,1)S(1)}, u32[]{:S(2)}, u32[]{:S(2)}) collective-permute-start(bf16[128,512]{1,0:T(8,128)(2,1)} %own.1), channel_id=1, source_target_pairs={{0,192},{64,128},{128,64},{192,0},{1,193},{65,129},{129,65},{193,1... | collective-permute-start | bytes 393224 | tf_op jit(solution)/shard_map/ppermute | solution.py:38
  5.5 11.5 %collective-permute-start.3 = (bf16[128,512]{1,0:T(8,128)(2,1)}, bf16[128,512]{1,0:T(8,128)(2,1)S(1)}, u32[]{:S(2)}, u32[]{:S(2)}) collective-permute-start(bf16[128,512]{1,0:T(8,128)(2,1)} %own.1), channel_id=1, source_target_pairs={{0,32},{32,0},{1,33},{33,1},{2,34},{34,2},{3,35},{35,3},{4,36},{36... | collective-permute-start | bytes 393224 | tf_op jit(solution)/shard_map/ppermute | solution.py:38
  7.6 13.1 %collective-permute-start.7 = (bf16[512,128]{1,0:T(8,128)(2,1)}, bf16[512,128]{1,0:T(8,128)(2,1)S(1)}, u32[]{:S(2)}, u32[]{:S(2)}) collective-permute-start(bf16[512,128]{1,0:T(8,128)(2,1)} %param.6), channel_id=1, source_target_pairs={{0,0},{32,64},{64,128},{96,192},{128,32},{160,96},{192,160},{224,2... | collective-permute-start | bytes 393224 | tf_op jit(solution)/shard_map/ppermute | solution.py:201
  9.6 11.2 %collective-permute-start.4 = (bf16[128,512]{1,0:T(8,128)(2,1)S(1)}, bf16[128,512]{1,0:T(8,128)(2,1)S(1)}, u32[]{:S(2)}, u32[]{:S(2)}) collective-permute-start(bf16[128,512]{1,0:T(8,128)(2,1)S(1)} %collective-permute-done.refs_0_), channel_id=1, source_target_pairs={{0,32},{32,0},{1,33},{33,1},{2,34},{34,2},{3,35},{35,3},{4,36},{36... | collective-permute-start | bytes 393224 | tf_op jit(solution)/shard_map/ppermute | solution.py:38
  10.4 10.3 %collective-permute-start.5 = (bf16[128,512]{1,0:T(8,128)(2,1)S(1)}, bf16[128,512]{1,0:T(8,128)(2,1)S(1)}, u32[]{:S(2)}, u32[]{:S(2)}) collective-permute-start(bf16[128,512]{1,0:T(8,128)(2,1)S(1)} %collective-permute-done.1.refs_1_), channel_id=1, source_target_pairs={{0,32},{32,0},{1,33},{33,1},{2,34},{34,2},{3,35},{35,3},{4,36},{36... | collective-permute-start | bytes 393224 | tf_op jit(solution)/shard_map/ppermute | solution.py:38
  26.2 9.2 %collective-permute-start.14 = (bf16[4,32,1152]{2,1,0:T(8,128)(2,1)S(1)}, bf16[4,32,1152]{2,1,0:T(8,128)(2,1)S(1)}, u32[]{:S(2)}, u32[]{:S(2)}) collective-permute-start(bf16[4,32,1152]{2,1,0:T(8,128)(2,1)S(1)} %get-tuple-element.38), channel_id=1, source_target_pairs={{0,4},{4,0},{8,12},{12,8},{1,5},{5,1},{9,13},{13,9},{2,6},{6,2},{1... | collective-permute-start | bytes 884744 | tf_op jit(solution)/shard_map/ppermute | solution.py:38
  27.5 14.7 %collective-permute-start.15 = (bf16[4,32,1152]{2,1,0:T(8,128)(2,1)}, bf16[4,32,1152]{2,1,0:T(8,128)(2,1)S(1)}, u32[]{:S(2)}, u32[]{:S(2)}) collective-permute-start(bf16[4,32,1152]{2,1,0:T(8,128)(2,1)} %get-tuple-element.39), channel_id=1, source_target_pairs={{0,8},{4,12},{8,0},{12,4},{1,9},{5,13},{9,1},{13,5},{2,10},{6,14},... | collective-permute-start | bytes 884744 | tf_op jit(solution)/shard_map/ppermute | solution.py:38
  30.2 15.3 %collective-permute-start.16 = (bf16[4,32,1152]{2,1,0:T(8,128)(2,1)S(1)}, bf16[4,32,1152]{2,1,0:T(8,128)(2,1)S(1)}, u32[]{:S(2)}, u32[]{:S(2)}) collective-permute-start(bf16[4,32,1152]{2,1,0:T(8,128)(2,1)S(1)} %get-tuple-element.40), channel_id=1, source_target_pairs={{0,12},{4,8},{8,4},{12,0},{1,13},{5,9},{9,5},{13,1},{2,14},{6,10},... | collective-permute-start | bytes 884744 | tf_op jit(solution)/shard_map/ppermute | solution.py:38
  30.2 19.8 %collective-permute-start.10 = (bf16[4,32,1152]{2,1,0:T(8,128)(2,1)S(1)}, bf16[4,32,1152]{2,1,0:T(8,128)(2,1)S(1)}, u32[]{:S(2)}, u32[]{:S(2)}) collective-permute-start(bf16[4,32,1152]{2,1,0:T(8,128)(2,1)S(1)} %get-tuple-element.32), channel_id=1, source_target_pairs={{0,3},{1,2},{2,1},{3,0},{4,7},{5,6},{6,5},{7,4},{8,11},{9,10},{10,... | collective-permute-start | bytes 884744 | tf_op jit(solution)/shard_map/ppermute | solution.py:38
  32.6 17.5 %collective-permute-start.8 = (bf16[4,32,1152]{2,1,0:T(8,128)(2,1)S(1)}, bf16[4,32,1152]{2,1,0:T(8,128)(2,1)S(1)}, u32[]{:S(2)}, u32[]{:S(2)}) collective-permute-start(bf16[4,32,1152]{2,1,0:T(8,128)(2,1)S(1)} %get-tuple-element.30), channel_id=1, source_target_pairs={{0,1},{1,0},{2,3},{3,2},{4,5},{5,4},{6,7},{7,6},{8,9},{9,8},{10,11... | collective-permute-start | bytes 884744 | tf_op jit(solution)/shard_map/ppermute | solution.py:38
  35.4 14.8 %collective-permute-start.9 = (bf16[4,32,1152]{2,1,0:T(8,128)(2,1)S(1)}, bf16[4,32,1152]{2,1,0:T(8,128)(2,1)S(1)}, u32[]{:S(2)}, u32[]{:S(2)}) collective-permute-start(bf16[4,32,1152]{2,1,0:T(8,128)(2,1)S(1)} %get-tuple-element.31), channel_id=1, source_target_pairs={{0,2},{1,3},{2,0},{3,1},{4,6},{5,7},{6,4},{7,5},{8,10},{9,11},{10,... | collective-permute-start | bytes 884744 | tf_op jit(solution)/shard_map/ppermute | solution.py:38
  58.3 10.5 %collective-permute-start.20 = (bf16[64,1152]{1,0:T(8,128)(2,1)S(1)}, bf16[64,1152]{1,0:T(8,128)(2,1)S(1)}, u32[]{:S(2)}, u32[]{:S(2)}) collective-permute-start(bf16[64,1152]{1,0:T(8,128)(2,1)S(1)} %shard_map.49.a.own), channel_id=1, source_target_pairs={{0,16},{16,0},{1,17},{17,1},{2,18},{18,2},{3,19},{19,3},{4,20},{20... | collective-permute-start | bytes 442376 | tf_op jit(solution)/shard_map/ppermute | solution.py:38
  93.9 11.9 %collective-permute-start.31 = (bf16[4,32,1024]{2,1,0:T(8,128)(2,1)S(1)}, bf16[4,32,1024]{2,1,0:T(8,128)(2,1)S(1)}, u32[]{:S(2)}, u32[]{:S(2)}) collective-permute-start(bf16[4,32,1024]{2,1,0:T(8,128)(2,1)S(1)} %shard_map.53.refs_4_), channel_id=1, source_target_pairs={{0,1},{1,0},{2,3},{3,2},{4,5},{5,4},{6,7},{7,6},{8,9},{9,8},{10,11... | collective-permute-start | bytes 786440 | tf_op jit(solution)/shard_map/ppermute | solution.py:38
  95.5 7.6 %collective-permute-start.23 = (bf16[32,1024]{1,0:T(8,128)(2,1)S(1)}, bf16[32,1024]{1,0:T(8,128)(2,1)S(1)}, u32[]{:S(2)}, u32[]{:S(2)}) collective-permute-start(bf16[32,1024]{1,0:T(8,128)(2,1)S(1)} %get-tuple-element.45.refs_0_), channel_id=1, source_target_pairs={{0,2},{1,3},{2,0},{3,1},{4,6},{5,7},{6,4},{7,5},{8,10},{9,11},{10,... | collective-permute-start | bytes 196616 | tf_op jit(solution)/shard_map/ppermute | solution.py:38
  98.1 10.9 %collective-permute-start.32 = (bf16[4,32,1024]{2,1,0:T(8,128)(2,1)S(1)}, bf16[4,32,1024]{2,1,0:T(8,128)(2,1)S(1)}, u32[]{:S(2)}, u32[]{:S(2)}) collective-permute-start(bf16[4,32,1024]{2,1,0:T(8,128)(2,1)S(1)} %shard_map.53.refs_4_), channel_id=1, source_target_pairs={{0,2},{1,3},{2,0},{3,1},{4,6},{5,7},{6,4},{7,5},{8,10},{9,11},{10,... | collective-permute-start | bytes 786440 | tf_op jit(solution)/shard_map/ppermute | solution.py:38
  101.4 14.1 %collective-permute-start.33 = (bf16[4,32,1024]{2,1,0:T(8,128)(2,1)S(1)}, bf16[4,32,1024]{2,1,0:T(8,128)(2,1)S(1)}, u32[]{:S(2)}, u32[]{:S(2)}) collective-permute-start(bf16[4,32,1024]{2,1,0:T(8,128)(2,1)S(1)} %shard_map.53.refs_4_), channel_id=1, source_target_pairs={{0,3},{1,2},{2,1},{3,0},{4,7},{5,6},{6,5},{7,4},{8,11},{9,10},{10,... | collective-permute-start | bytes 786440 | tf_op jit(solution)/shard_map/ppermute | solution.py:38
  103.1 12.4 %collective-permute-start.25 = (bf16[4,32,1024]{2,1,0:T(8,128)(2,1)S(1)}, bf16[4,32,1024]{2,1,0:T(8,128)(2,1)S(1)}, u32[]{:S(2)}, u32[]{:S(2)}) collective-permute-start(bf16[4,32,1024]{2,1,0:T(8,128)(2,1)S(1)} %shard_map.52.refs_0_), channel_id=1, source_target_pairs={{0,4},{4,0},{8,12},{12,8},{1,5},{5,1},{9,13},{13,9},{2,6},{6,2},{1... | collective-permute-start | bytes 786440 | tf_op jit(solution)/shard_map/ppermute | solution.py:38
  103.2 12.3 %collective-permute-start.26 = (bf16[4,32,1024]{2,1,0:T(8,128)(2,1)S(1)}, bf16[4,32,1024]{2,1,0:T(8,128)(2,1)S(1)}, u32[]{:S(2)}, u32[]{:S(2)}) collective-permute-start(bf16[4,32,1024]{2,1,0:T(8,128)(2,1)S(1)} %shard_map.52.refs_0_), channel_id=1, source_target_pairs={{0,8},{4,12},{8,0},{12,4},{1,9},{5,13},{9,1},{13,5},{2,10},{6,14},... | collective-permute-start | bytes 786440 | tf_op jit(solution)/shard_map/ppermute | solution.py:38
  105.8 9.7 %collective-permute-start.27 = (bf16[4,32,1024]{2,1,0:T(8,128)(2,1)S(1)}, bf16[4,32,1024]{2,1,0:T(8,128)(2,1)S(1)}, u32[]{:S(2)}, u32[]{:S(2)}) collective-permute-start(bf16[4,32,1024]{2,1,0:T(8,128)(2,1)S(1)} %shard_map.52.refs_0_), channel_id=1, source_target_pairs={{0,12},{4,8},{8,4},{12,0},{1,13},{5,9},{9,5},{13,1},{2,14},{6,10},... | collective-permute-start | bytes 786440 | tf_op jit(solution)/shard_map/ppermute | solution.py:38
  117.5 8.2 %collective-permute-start.34 = (bf16[512,512]{1,0:T(8,128)(2,1)S(1)}, bf16[512,512]{1,0:T(8,128)(2,1)S(1)}, u32[]{:S(2)}, u32[]{:S(2)}) collective-permute-start(bf16[512,512]{1,0:T(8,128)(2,1)S(1)} %bitcast.18), channel_id=1, source_target_pairs={{0,32},{32,0},{1,33},{33,1},{2,34},{34,2},{3,35},{35,3},{4,36},{36... | collective-permute-start | bytes 1572872 | tf_op jit(solution)/shard_map/ppermute | solution.py:38
  127.5 12.6 %collective-permute-start.36 = (bf16[128,512]{1,0:T(8,128)(2,1)S(1)}, bf16[128,512]{1,0:T(8,128)(2,1)S(1)}, u32[]{:S(2)}, u32[]{:S(2)}) collective-permute-start(bf16[128,512]{1,0:T(8,128)(2,1)S(1)} %get-tuple-element.51), channel_id=1, source_target_pairs={{0,128},{64,192},{128,0},{192,64},{1,129},{65,193},{129,1},{193,65... | collective-permute-start | bytes 393224 | tf_op jit(solution)/shard_map/ppermute | solution.py:38
  128.4 11.7 %collective-permute-start.37 = (bf16[128,512]{1,0:T(8,128)(2,1)S(1)}, bf16[128,512]{1,0:T(8,128)(2,1)S(1)}, u32[]{:S(2)}, u32[]{:S(2)}) collective-permute-start(bf16[128,512]{1,0:T(8,128)(2,1)S(1)} %get-tuple-element.52), channel_id=1, source_target_pairs={{0,64},{64,0},{128,192},{192,128},{1,65},{65,1},{129,193},{193,129... | collective-permute-start | bytes 393224 | tf_op jit(solution)/shard_map/ppermute | solution.py:38
  (17 other events, 114.5 us)

commit v5 on v4

--- a/solution.py
+++ b/solution.py
@@ -18,7 +18,6 @@
 F32 = jnp.float32
 VMEM = pl.BlockSpec(memory_space=pltpu.VMEM)
 SMEM = pl.BlockSpec(memory_space=pltpu.SMEM)
-HBM = pl.BlockSpec(memory_space=pltpu.HBM)
 
 
 def tables(positions, width):
@@ -38,56 +37,62 @@
     return lax.ppermute(block, axis, [(i, i ^ step) for i in range(size)])
 
 
-def projection_kernel(place, own, *refs):
-    blocks, w_hbm, w_kv = refs[:7], refs[7], refs[8]
-    outs_x, outs_y = refs[9:13], refs[13:17]
-    chunks, w_query, first, sems = refs[17:]
-    copies = [pltpu.make_async_copy(own, first, sems.at[4])]
-    rows = w_query.shape[0] // 4
-    for i in range(4):
-        part = pl.ds(i * rows, rows)
-        copies.append(pltpu.make_async_copy(w_hbm.at[part], w_query.at[part], sems.at[i]))
-    for copy in copies:
-        copy.start()
-    for copy in copies:
-        copy.wait()
+def project(block, w_query, w_kv, chunks, k):
     size = chunks.shape[1]
     width = w_query.shape[1]
-    for i, block in enumerate([first, *blocks]):
-        query = jnp.dot(block[...], w_query[...], preferred_element_type=F32).astype(BF16)
-        keyval = jnp.dot(block[...], w_kv[...], preferred_element_type=F32).astype(BF16)
-        for b in range(2):
-            part = slice(b * size, (b + 1) * size)
-            chunks[2 * i + b, :, :width] = query[part]
-            chunks[2 * i + b, :, width:] = keyval[part]
+    query = jnp.dot(block[...], w_query[...], preferred_element_type=F32).astype(BF16)
+    keyval = jnp.dot(block[...], w_kv[...], preferred_element_type=F32).astype(BF16)
+    for b in range(2):
+        part = slice(b * size, (b + 1) * size)
+        chunks[k + b, :, :width] = query[part]
+        chunks[k + b, :, width:] = keyval[part]
+
+
+def early_kernel(*refs):
+    blocks, w_query, w_kv, out = refs[:2], *refs[2:]
+    for i, block in enumerate(blocks):
+        project(block, w_query, w_kv, out, 2 * i)
+
+
+def late_kernel(place, *refs):
+    blocks, w_query, w_kv, early = refs[:6], *refs[6:9]
+    outs_x, outs_y, chunks = refs[9:13], refs[13:17], refs[17]
+    for side in range(2):
+        chunks[8 * side] = early[2 * side]
+        chunks[8 * side + 1] = early[2 * side + 1]
+        for i in range(3):
+            project(blocks[3 * side + i], w_query, w_kv, chunks, 8 * side + 2 * i + 2)
+    cut = chunks.shape[1] // 2
     x, y = place[0], place[1]
     for s in range(4):
         for j in range(4):
-            outs_x[s][j] = chunks[4 * j + (x ^ s), : size // 2, :]
-            outs_y[s][j] = chunks[4 * (y ^ s) + j, size // 2 :, :]
-
-
-def halve_kernel(place, a, b, c, d, own, *outs):
-    for t, out in enumerate([own, *outs]):
-        j = place[0] ^ t
-        total = a[j].astype(F32) + b[j].astype(F32) + c[j].astype(F32) + d[j].astype(F32)
-        out[...] = total.astype(out.dtype)
+            outs_x[s][j] = chunks[4 * j + (x ^ s), :cut, :]
+            outs_y[s][j] = chunks[4 * (y ^ s) + j, cut:, :]
+
+
+def halve_kernel(place, *refs):
+    for side in range(2):
+        a, b, c, d = refs[4 * side : 4 * side + 4]
+        for t in range(4):
+            out = refs[8 + 4 * side + t]
+            j = place[1 - side] ^ t
+            total = a[j].astype(F32) + b[j].astype(F32) + c[j].astype(F32) + d[j].astype(F32)
+            out[...] = total.astype(out.dtype)
 
 
 def join_kernel(*refs):
-    out = refs[8]
-    rows = out.shape[0] // 2
+    query, keyval = refs[8:]
+    rows, width = query.shape[0] // 2, query.shape[1]
     for side in range(2):
         total = functools.reduce(
             jnp.add, [ref[...].astype(F32) for ref in refs[4 * side : 4 * side + 4]]
-        )
-        out[side * rows : (side + 1) * rows, :] = total.astype(BF16)
+        ).astype(BF16)
+        query[side * rows : (side + 1) * rows, :] = total[:, :width]
+        keyval[side * rows : (side + 1) * rows, :] = total[:, width:]
 
 
 def keys_kernel(a, b, cosine, sine_v, out):
-    width = a.shape[1] - HD
-    total = a[:, width:].astype(F32) + b[:, width:].astype(F32)
-    total = total.astype(BF16).astype(F32)
+    total = (a[...].astype(F32) + b[...].astype(F32)).astype(BF16).astype(F32)
     block = rotate(total, cosine[...], sine_v[...]).astype(BF16)
     for c in range(out.shape[0]):
         out[c] = block
@@ -97,12 +102,10 @@
     heads, base, own, got, cosine, sine_v, kv_own, kv_other, low, high, queries, pair
 ):
     per_chunk = own.shape[0]
-    half = kv_own.shape[0] // 2
-    for side in range(2):
-        pair[0, side * half : (side + 1) * half, :] = kv_own[side * half : (side + 1) * half, :]
-        pair[1, side * half : (side + 1) * half, :] = kv_other[
-            (1 - side) * half : (2 - side) * half, :
-        ]
+    pair[0] = kv_own[...]
+    for s in range(4):
+        part = slice(s * 2 * HD, (s + 1) * 2 * HD)
+        pair[1, part, :] = kv_other[(s ^ 1) * 2 * HD : ((s ^ 1) + 1) * 2 * HD, :]
     for h in range(heads):
         cols = slice(h * HD, (h + 1) * HD)
         total = own[:, cols].astype(F32) + got[:, cols].astype(F32)
@@ -139,8 +142,9 @@
 
 
 def stack_kernel(*refs):
-    for s, ref in enumerate(refs[:4]):
-        refs[4][s] = ref[...]
+    for side in range(2):
+        for s in range(4):
+            refs[8 + side][s] = refs[4 * side + s][...]
 
 
 def output_kernel(place, *refs):
@@ -196,51 +200,58 @@
     both = width + HD
 
     mine = [tokens] + [partner(tokens, "zl", s) for s in (1, 2, 3)]
-    others = [partner(block, "core", 1) for block in mine]
-    kv_moves = [(e, 2 * e if e < 4 else 2 * (e - 4) + 1) for e in range(8)]
-    w_kv = lax.ppermute(w_keyval, ROW, kv_moves)
-
-    def block_start(index):
-        return (((zl ^ (index & 3)) << 1) + ((index >> 2) ^ core)) * per_row
+
+    def block_start(chip, side, index):
+        return (((chip ^ (index & 3)) << 1) + ((index >> 2) ^ side)) * per_row
 
     chunk = y * X + x
-    row_start = block_start(chunk >> 1) + (chunk & 1) * per_chunk
-    base = jnp.stack([*[block_start(i) for i in range(8)], row_start, core]).astype(jnp.int32)
-    cosine, sine_v = tables((row_start + jnp.arange(per_chunk)).astype(F32), HD)
-    key_cos = jnp.where(core == 0, cosine, 1.0)
-    key_sin = jnp.where(core == 0, sine_v, 0.0)
-    place_xy = jnp.stack([x, y]).astype(jnp.int32)
-    place_yx = jnp.stack([y, x]).astype(jnp.int32)
-
+    offset = (chunk & 1) * per_chunk
+    source_chip, source_core = (zl >> 1) + 2 * core, zl & 1
+    row_start = block_start(zl, core, chunk >> 1) + offset
+    key_start = block_start(source_chip, source_core, chunk >> 1) + offset
+    starts = [block_start(source_chip, source_core, i) for i in range(8)]
+    base = jnp.stack([*starts, row_start, core]).astype(jnp.int32)
+    steps = jnp.arange(per_chunk)
+    cosine, sine_v = tables((row_start + steps).astype(F32), HD)
+    key_cos, key_sin = tables((key_start + steps).astype(F32), HD)
+    key_cos = jnp.where(core == 0, key_cos, 1.0)
+    key_sin = jnp.where(core == 0, key_sin, 0.0)
+    place = jnp.stack([x, y]).astype(jnp.int32)
+
+    near = partner(tokens, "core", 1)
+    (early,) = call(early_kernel, [(4, per_chunk, both)], [tokens, near, w_query, w_keyval])
+    *far, early = lax.optimization_barrier((*mine[1:], early))
     parts = call(
-        projection_kernel,
+        late_kernel,
         [(4, cut, both)] * 8,
-        [place_xy, tokens, *mine[1:], *others, w_query, w_kv],
-        [SMEM, HBM, *[VMEM] * 7, HBM],
-        [
-            pltpu.VMEM((Y * X, per_chunk, both), BF16),
-            pltpu.VMEM(w_query.shape, BF16),
-            pltpu.VMEM(tokens.shape, BF16),
-            pltpu.SemaphoreType.DMA((5,)),
-        ],
-    )
-    summed = []
-    for place, first, second, pieces in (
-        (place_yx, "x", "y", parts[:4]),
-        (place_xy, "y", "x", parts[4:]),
-    ):
-        got = [partner(pieces[s], first, s) for s in (1, 2, 3)]
-        own, *sends = call(
-            halve_kernel,
-            [jax.ShapeDtypeStruct((cut, both), F32), *[(cut, both)] * 3],
-            [place, pieces[0], *got],
-            [SMEM],
-        )
-        summed += [own] + [partner(sends[t - 1], second, t) for t in (1, 2, 3)]
-    (own,) = call(join_kernel, [(per_chunk, both)], summed)
+        [place, *far, *[partner(block, "core", 1) for block in far], w_query, w_keyval, early],
+        [SMEM],
+        [pltpu.VMEM((Y * X, per_chunk, both), BF16)],
+    )
+    got_x = [partner(parts[s], "x", s) for s in (1, 2, 3)]
+    got_y = [partner(parts[4 + s], "y", s) for s in (1, 2, 3)]
+    kept_f32 = jax.ShapeDtypeStruct((cut, both), F32)
+    halves = call(
+        halve_kernel,
+        [kept_f32, *[(cut, both)] * 3] * 2,
+        [place, parts[0], *got_x, parts[4], *got_y],
+        [SMEM],
+    )
+    got_y = [partner(halves[t], "y", t) for t in (1, 2, 3)]
+    got_x = [partner(halves[4 + t], "x", t) for t in (1, 2, 3)]
+    own, kv = call(
+        join_kernel,
+        [(per_chunk, width), (per_chunk, HD)],
+        [halves[0], *got_y, halves[4], *got_x],
+    )
     got = partner(own, "zh", 1)
 
-    (kv_block,) = call(keys_kernel, [(Y * X, per_chunk, HD)], [own, got, key_cos, key_sin])
+    moves = [(e, 2 * (e % 4) + e // 4) for e in range(8)]
+    here = lax.ppermute(kv, ROW, moves)
+    across = lax.ppermute(
+        kv, (*ROW, "zh"), [(2 * e + h, 2 * r + 1 - h) for e, r in moves for h in range(2)]
+    )
+    (kv_block,) = call(keys_kernel, [(Y * X, per_chunk, HD)], [here, across, key_cos, key_sin])
     kv_own = lax.all_to_all(kv_block, PLANE, 0, 0, tiled=True).reshape(total, HD)
     kv_other = partner(kv_own, "core", 1)
     low, high = call(
@@ -251,18 +262,24 @@
         [pltpu.VMEM((heads * per_chunk, HD), BF16), pltpu.VMEM((2, total, HD), BF16)],
     )
 
-    gathered = []
-    for first, second, block in (("x", "y", low), ("y", "x", high)):
-        (line,) = call(
-            stack_kernel,
-            [(4, cut, width)],
-            [block] + [partner(block, first, s) for s in (1, 2, 3)],
-        )
-        gathered += [line] + [partner(line, second, t) for t in (1, 2, 3)]
+    lines = call(
+        stack_kernel,
+        [(4, cut, width)] * 2,
+        [low]
+        + [partner(low, "x", s) for s in (1, 2, 3)]
+        + [high]
+        + [partner(high, "y", s) for s in (1, 2, 3)],
+    )
+    gathered = (
+        [lines[0]]
+        + [partner(lines[0], "y", t) for t in (1, 2, 3)]
+        + [lines[1]]
+        + [partner(lines[1], "x", t) for t in (1, 2, 3)]
+    )
     kept, sent = call(
         output_kernel,
         [(Y * X // 2, per_chunk, features)] * 2,
-        [place_xy, *gathered, w_output],
+        [place, *gathered, w_output],
         [SMEM],
         [pltpu.VMEM((Y * X, per_chunk, features), BF16)],
     )

time: 141 us -> 148 us (1.050)
  starting transfers between devices: 66.7 us -> 75.7 us
  waiting for transfers between devices: 49.8 us -> 47.7 us
    ppermute x1 -> x2, starting transfers between devices: 1.91 us -> 14 us  [the longest x1 8.67 us: shards(): here = lax.ppermute(kv, ROW, moves)]
    ppermute x37, starting transfers between devices: 64.8 us -> 61.7 us  [partner(): return lax.ppermute(block, axis, [(i, i ^ step) for i in range(size)])]
    ppermute x1 -> x2, waiting for transfers between devices: 3.74 us -> 0.77 us  [the longest x1 0.77 us: shards(): lax.ppermute(kv, (*ROW, 'zh'), [(2 * e + h, 2 * r + 1 - h) for e, r in mo...]
    unnamed x6 -> x12, local copies, waits for them, and re-layouts: 2.13 us -> 3.05 us
    pallas_call x10 -> x9, Pallas kernels: 8.53 us -> 8.11 us  [call(): pl.pallas_call(kernel, out_shape=[s if isinstance(s, jax.ShapeDtypeStruct...]
  transfers between devices with their start and end apart: 38 -> 39, of which waited for: 18 -> 22; matrix products, arithmetic and copies ran while one was open for 0% -> 0% of each run, Pallas kernels for 1% -> 0%
where the time goes in v5:
time: 148 us
  starting transfers between devices  75.7 us (51%)
  waiting for transfers between devices  47.7 us (32%)
  blocking collectives  11.9 us (8%)
  Pallas kernels  8.11 us (5%)
  local copies, waits for them, and re-layouts  3.13 us (2%)
    ppermute x37, starting transfers between devices, partner(): return lax.ppermute(block, axis, [(i, i ^ step) for i in range(size)])  61.7 us
    ppermute x37, waiting for transfers between devices, partner(): return lax.ppermute(block, axis, [(i, i ^ step) for i in range(size)])  46.9 us
    all_to_all x1, blocking collectives, shards(): lax.all_to_all(kv_block, PLANE, 0, 0, tiled=True).reshape(total, HD)  11.9 us
    ppermute x1, starting transfers between devices, shards(): here = lax.ppermute(kv, ROW, moves)  8.67 us
    pallas_call x9, Pallas kernels, call(): pl.pallas_call(kernel, out_shape=[s if isinstance(s, jax.ShapeDtypeStruct...  8.11 us
    ppermute x1, starting transfers between devices, shards(): lax.ppermute(kv, (*ROW, 'zh'), [(2 * e + h, 2 * r + 1 - h) for e, r in mo...  5.34 us
    unnamed x12, local copies, waits for them, and re-layouts  3.05 us
  transfers between devices with their start and end apart: 39, of which 22 were waited for; matrix products, arithmetic and copies ran while one was open for 0% of the time, Pallas kernels for 0%

profile of v5, /device:TPU:1, one launch (start us, length us, event | category | flops | bytes accessed | tf_op | source)
XLA Modules:
  0.0 148.0 jit_solution(15649454203568340857)
XLA Ops:
  0.0 3.2 %collective-permute-start.3 = (bf16[128,512]{1,0:T(8,128)(2,1)}, bf16[128,512]{1,0:T(8,128)(2,1)S(1)}, u32[]{:S(2)}, u32[]{:S(2)}) collective-permute-start(bf16[128,512]{1,0:T(8,128)(2,1)} %refs_0_.1), channel_id=1, source_target_pairs={{0,32},{32,0},{1,33},{33,1},{2,34},{34,2},{3,35},{35,3},{4,36},{36... | collective-permute-start | bytes 393224 | tf_op jit(solution)/shard_map/ppermute | solution.py:37
  3.2 2.9 %collective-permute-start.1 = (bf16[128,512]{1,0:T(8,128)(2,1)}, bf16[128,512]{1,0:T(8,128)(2,1)S(1)}, u32[]{:S(2)}, u32[]{:S(2)}) collective-permute-start(bf16[128,512]{1,0:T(8,128)(2,1)} %refs_0_.1), channel_id=1, source_target_pairs={{0,128},{64,192},{128,0},{192,64},{1,129},{65,193},{129,1},{193,65... | collective-permute-start | bytes 393224 | tf_op jit(solution)/shard_map/ppermute | solution.py:37
  11.1 4.4 %collective-permute-done.2.refs_2_ = bf16[128,512]{1,0:T(8,128)(2,1)S(1)} collective-permute-done((bf16[128,512]{1,0:T(8,128)(2,1)}, bf16[128,512]{1,0:T(8,128)(2,1)S(1)}, u32[]{:S(2)}, u32[]{:S(2)}) %collective-permute-start.2) | collective-permute-done | bytes 131104 | tf_op jit(solution)/shard_map/ppermute | solution.py:37
  18.4 2.9 %shard_map.47 = (bf16[4,32,1152]{2,1,0:T(8,128)(2,1)S(1)}, bf16[4,32,1152]{2,1,0:T(8,128)(2,1)}, bf16[4,32,1152]{2,1,0:T(8,128)(2,1)}, bf16[4,32,1152]{2,1,0:T(8...) custom-call(s32[2]{0:T(128)S(1)} %pad_add_fusion.place, ...), custom_call_target="tpu_custom_call" | custom-call | tf_op jit(solution)/shard_map/pallas_call | solution.py:175
  22.6 2.6 %collective-permute-start.11 = (bf16[4,32,1152]{2,1,0:T(8,128)(2,1)}, bf16[4,32,1152]{2,1,0:T(8,128)(2,1)S(1)}, u32[]{:S(2)}, u32[]{:S(2)}) collective-permute-start(bf16[4,32,1152]{2,1,0:T(8,128)(2,1)} %get-tuple-element.47), channel_id=1, source_target_pairs={{0,8},{4,12},{8,0},{12,4},{1,9},{5,13},{9,1},{13,5},{2,10},{6,14},... | collective-permute-start | bytes 884744 | tf_op jit(solution)/shard_map/ppermute | solution.py:37
  26.4 2.5 %collective-permute-start.8 = (bf16[4,32,1152]{2,1,0:T(8,128)(2,1)}, bf16[4,32,1152]{2,1,0:T(8,128)(2,1)S(1)}, u32[]{:S(2)}, u32[]{:S(2)}) collective-permute-start(bf16[4,32,1152]{2,1,0:T(8,128)(2,1)} %get-tuple-element.43), channel_id=1, source_target_pairs={{0,2},{1,3},{2,0},{3,1},{4,6},{5,7},{6,4},{7,5},{8,10},{9,11},{10,... | collective-permute-start | bytes 884744 | tf_op jit(solution)/shard_map/ppermute | solution.py:37
  29.6 2.4 %collective-permute-start.9 = (bf16[4,32,1152]{2,1,0:T(8,128)(2,1)S(1)}, bf16[4,32,1152]{2,1,0:T(8,128)(2,1)S(1)}, u32[]{:S(2)}, u32[]{:S(2)}) collective-permute-start(bf16[4,32,1152]{2,1,0:T(8,128)(2,1)S(1)} %get-tuple-element.44), channel_id=1, source_target_pairs={{0,3},{1,2},{2,1},{3,0},{4,7},{5,6},{6,5},{7,4},{8,11},{9,10},{10,... | collective-permute-start | bytes 884744 | tf_op jit(solution)/shard_map/ppermute | solution.py:37
  32.0 6.3 %collective-permute-done.11.refs_6_ = bf16[4,32,1152]{2,1,0:T(8,128)(2,1)S(1)} collective-permute-done((bf16[4,32,1152]{2,1,0:T(8,128)(2,1)}, bf16[4,32,1152]{2,1,0:T(8,128)(2,1)S(1)}, u32[]{:S(2)}, u32[]{:S(2)}) %collective-permute-start.11) | collective-permute-done | bytes 294944 | tf_op jit(solution)/shard_map/ppermute | solution.py:37
  41.4 2.8 %collective-permute-done.9.refs_3_ = bf16[4,32,1152]{2,1,0:T(8,128)(2,1)S(1)} collective-permute-done((bf16[4,32,1152]{2,1,0:T(8,128)(2,1)S(1)}, bf16[4,32,1152]{2,1,0:T(8,128)(2,1)S(1)}, u32[]{:S(2)}, u32[]{:S(2)}) %collective-permute-start.9) | collective-permute-done | bytes 294944 | tf_op jit(solution)/shard_map/ppermute | solution.py:37
  49.5 3.4 %collective-permute-start.17 = (bf16[32,1152]{1,0:T(8,128)(2,1)S(1)}, bf16[32,1152]{1,0:T(8,128)(2,1)S(1)}, u32[]{:S(2)}, u32[]{:S(2)}) collective-permute-start(bf16[32,1152]{1,0:T(8,128)(2,1)S(1)} %get-tuple-element.55), channel_id=1, source_target_pairs={{0,2},{1,3},{2,0},{3,1},{4,6},{5,7},{6,4},{7,5},{8,10},{9,11},{10,... | collective-permute-start | bytes 221192 | tf_op jit(solution)/shard_map/ppermute | solution.py:37
  57.4 8.7 %collective-permute-start.20 = (bf16[64,128]{1,0:T(8,128)(2,1)S(1)}, bf16[64,128]{1,0:T(8,128)(2,1)S(1)}, u32[]{:S(2)}, u32[]{:S(2)}) collective-permute-start(bf16[64,128]{1,0:T(8,128)(2,1)S(1)} %get-tuple-element.58), channel_id=1, source_target_pairs={{0,0},{32,64},{64,128},{96,192},{128,32},{160,96},{192,160},{224,2... | collective-permute-start | bytes 49160 | tf_op jit(solution)/shard_map/ppermute | solution.py:250
  66.1 5.3 %collective-permute-start.21 = (bf16[64,128]{1,0:T(8,128)(2,1)S(1)}, bf16[64,128]{1,0:T(8,128)(2,1)S(1)}, u32[]{:S(2)}, u32[]{:S(2)}) collective-permute-start(bf16[64,128]{1,0:T(8,128)(2,1)S(1)} %get-tuple-element.58), channel_id=1, source_target_pairs={{0,16},{16,0},{32,80},{48,64},{64,144},{80,128},{96,208},{112,192}... | collective-permute-start | bytes 49160 | tf_op jit(solution)/shard_map/ppermute | solution.py:251
  72.4 11.9 %all_to_all.5 = bf16[16,64,128]{2,1,0:T(8,128)(2,1)S(1)} all-to-all(bf16[16,64,128]{2,1,0:T(8,128)(2,1)S(1)} %shard_map.50), channel_id=1, replica_groups=mesh['zl'=4,'core'=2,'zh'=2,'y'=4,'x'=4] {'y','x'}, dimensions={0} | all-to-all | bytes 524288 | tf_op jit(solution)/shard_map/all_to_all | solution.py:255
  84.3 5.9 %collective-permute-start.19 = (bf16[64,1024]{1,0:T(8,128)(2,1)S(1)}, bf16[64,1024]{1,0:T(8,128)(2,1)S(1)}, u32[]{:S(2)}, u32[]{:S(2)}) collective-permute-start(bf16[64,1024]{1,0:T(8,128)(2,1)S(1)} %get-tuple-element.57.own), channel_id=1, source_target_pairs={{0,16},{16,0},{1,17},{17,1},{2,18},{18,2},{3,19},{19,3},{4,20},{20... | collective-permute-start | bytes 393224 | tf_op jit(solution)/shard_map/ppermute | solution.py:37
  90.4 3.6 %collective-permute-done.19.got = bf16[64,1024]{1,0:T(8,128)(2,1)S(1)} collective-permute-done((bf16[64,1024]{1,0:T(8,128)(2,1)S(1)}, bf16[64,1024]{1,0:T(8,128)(2,1)S(1)}, u32[]{:S(2)}, u32[]{:S(2)}) %collective-permute-start.19) | collective-permute-done | bytes 131104 | tf_op jit(solution)/shard_map/ppermute | solution.py:37
  96.5 3.0 %collective-permute-start.25 = (bf16[32,1024]{1,0:T(8,128)(2,1)S(1)}, bf16[32,1024]{1,0:T(8,128)(2,1)S(1)}, u32[]{:S(2)}, u32[]{:S(2)}) collective-permute-start(bf16[32,1024]{1,0:T(8,128)(2,1)S(1)} %get-tuple-element.59.refs_0_), channel_id=1, source_target_pairs={{0,3},{1,2},{2,1},{3,0},{4,7},{5,6},{6,5},{7,4},{8,11},{9,10},{10,... | collective-permute-start | bytes 196616 | tf_op jit(solution)/shard_map/ppermute | solution.py:37
  105.9 3.1 %collective-permute-start.30 = (bf16[4,32,1024]{2,1,0:T(8,128)(2,1)S(1)}, bf16[4,32,1024]{2,1,0:T(8,128)(2,1)S(1)}, u32[]{:S(2)}, u32[]{:S(2)}) collective-permute-start(bf16[4,32,1024]{2,1,0:T(8,128)(2,1)S(1)} %get-tuple-element.61.refs_0_), channel_id=1, source_target_pairs={{0,8},{4,12},{8,0},{12,4},{1,9},{5,13},{9,1},{13,5},{2,10},{6,14},... | collective-permute-start | bytes 786440 | tf_op jit(solution)/shard_map/ppermute | solution.py:37
  111.2 2.2 %collective-permute-start.34 = (bf16[4,32,1024]{2,1,0:T(8,128)(2,1)S(1)}, bf16[4,32,1024]{2,1,0:T(8,128)(2,1)S(1)}, u32[]{:S(2)}, u32[]{:S(2)}) collective-permute-start(bf16[4,32,1024]{2,1,0:T(8,128)(2,1)S(1)} %get-tuple-element.62.refs_4_), channel_id=1, source_target_pairs={{0,3},{1,2},{2,1},{3,0},{4,7},{5,6},{6,5},{7,4},{8,11},{9,10},{10,... | collective-permute-start | bytes 786440 | tf_op jit(solution)/shard_map/ppermute | solution.py:37
  113.5 2.2 %collective-permute-done.30.refs_2_ = bf16[4,32,1024]{2,1,0:T(8,128)(2,1)S(1)} collective-permute-done((bf16[4,32,1024]{2,1,0:T(8,128)(2,1)S(1)}, bf16[4,32,1024]{2,1,0:T(8,128)(2,1)S(1)}, u32[]{:S(2)}, u32[]{:S(2)}) %collective-permute-start.30) | collective-permute-done | bytes 262176 | tf_op jit(solution)/shard_map/ppermute | solution.py:37
  115.7 2.6 %collective-permute-done.31.refs_3_ = bf16[4,32,1024]{2,1,0:T(8,128)(2,1)S(1)} collective-permute-done((bf16[4,32,1024]{2,1,0:T(8,128)(2,1)S(1)}, bf16[4,32,1024]{2,1,0:T(8,128)(2,1)S(1)}, u32[]{:S(2)}, u32[]{:S(2)}) %collective-permute-start.31) | collective-permute-done | bytes 262176 | tf_op jit(solution)/shard_map/ppermute | solution.py:37
  118.3 2.5 %collective-permute-done.34.refs_7_ = bf16[4,32,1024]{2,1,0:T(8,128)(2,1)S(1)} collective-permute-done((bf16[4,32,1024]{2,1,0:T(8,128)(2,1)S(1)}, bf16[4,32,1024]{2,1,0:T(8,128)(2,1)S(1)}, u32[]{:S(2)}, u32[]{:S(2)}) %collective-permute-start.34) | collective-permute-done | bytes 262176 | tf_op jit(solution)/shard_map/ppermute | solution.py:37
  122.8 7.4 %collective-permute-start.35 = (bf16[512,512]{1,0:T(8,128)(2,1)S(1)}, bf16[512,512]{1,0:T(8,128)(2,1)S(1)}, u32[]{:S(2)}, u32[]{:S(2)}) collective-permute-start(bf16[512,512]{1,0:T(8,128)(2,1)S(1)} %bitcast.18), channel_id=1, source_target_pairs={{0,32},{32,0},{1,33},{33,1},{2,34},{34,2},{3,35},{35,3},{4,36},{36... | collective-permute-start | bytes 1572872 | tf_op jit(solution)/shard_map/ppermute | solution.py:37
  132.4 5.1 %collective-permute-start.37 = (bf16[128,512]{1,0:T(8,128)(2,1)S(1)}, bf16[128,512]{1,0:T(8,128)(2,1)S(1)}, u32[]{:S(2)}, u32[]{:S(2)}) collective-permute-start(bf16[128,512]{1,0:T(8,128)(2,1)S(1)} %get-tuple-element.67), channel_id=1, source_target_pairs={{0,128},{64,192},{128,0},{192,64},{1,129},{65,193},{129,1},{193,65... | collective-permute-start | bytes 393224 | tf_op jit(solution)/shard_map/ppermute | solution.py:37
  138.4 8.8 %collective-permute-done.37 = bf16[128,512]{1,0:T(8,128)(2,1)S(1)} collective-permute-done((bf16[128,512]{1,0:T(8,128)(2,1)S(1)}, bf16[128,512]{1,0:T(8,128)(2,1)S(1)}, u32[]{:S(2)}, u32[]{:S(2)}) %collective-permute-start.37) | collective-permute-done | bytes 131104 | tf_op jit(solution)/shard_map/ppermute | solution.py:37
  (85 shorter events, 41.9 us)
Async XLA Ops:
  0.0 6.8 %collective-permute-start.3 = (bf16[128,512]{1,0:T(8,128)(2,1)}, bf16[128,512]{1,0:T(8,128)(2,1)S(1)}, u32[]{:S(2)}, u32[]{:S(2)}) collective-permute-start(bf16[128,512]{1,0:T(8,128)(2,1)} %refs_0_.1), channel_id=1, source_target_pairs={{0,32},{32,0},{1,33},{33,1},{2,34},{34,2},{3,35},{35,3},{4,36},{36... | collective-permute-start | bytes 393224 | tf_op jit(solution)/shard_map/ppermute | solution.py:37
  3.2 7.8 %collective-permute-start = (bf16[128,512]{1,0:T(8,128)(2,1)}, bf16[128,512]{1,0:T(8,128)(2,1)S(1)}, u32[]{:S(2)}, u32[]{:S(2)}) collective-permute-start(bf16[128,512]{1,0:T(8,128)(2,1)} %refs_0_.1), channel_id=1, source_target_pairs={{0,64},{64,0},{128,192},{192,128},{1,65},{65,1},{129,193},{193,129... | collective-permute-start | bytes 393224 | tf_op jit(solution)/shard_map/ppermute | solution.py:37
  3.2 7.8 %collective-permute-start.1 = (bf16[128,512]{1,0:T(8,128)(2,1)}, bf16[128,512]{1,0:T(8,128)(2,1)S(1)}, u32[]{:S(2)}, u32[]{:S(2)}) collective-permute-start(bf16[128,512]{1,0:T(8,128)(2,1)} %refs_0_.1), channel_id=1, source_target_pairs={{0,128},{64,192},{128,0},{192,64},{1,129},{65,193},{129,1},{193,65... | collective-permute-start | bytes 393224 | tf_op jit(solution)/shard_map/ppermute | solution.py:37
  6.1 9.3 %collective-permute-start.2 = (bf16[128,512]{1,0:T(8,128)(2,1)}, bf16[128,512]{1,0:T(8,128)(2,1)S(1)}, u32[]{:S(2)}, u32[]{:S(2)}) collective-permute-start(bf16[128,512]{1,0:T(8,128)(2,1)} %refs_0_.1), channel_id=1, source_target_pairs={{0,192},{64,128},{128,64},{192,0},{1,193},{65,129},{129,65},{193,1... | collective-permute-start | bytes 393224 | tf_op jit(solution)/shard_map/ppermute | solution.py:37
  21.3 8.3 %collective-permute-start.10 = (bf16[4,32,1152]{2,1,0:T(8,128)(2,1)S(1)}, bf16[4,32,1152]{2,1,0:T(8,128)(2,1)S(1)}, u32[]{:S(2)}, u32[]{:S(2)}) collective-permute-start(bf16[4,32,1152]{2,1,0:T(8,128)(2,1)S(1)} %get-tuple-element.46), channel_id=1, source_target_pairs={{0,4},{4,0},{8,12},{12,8},{1,5},{5,1},{9,13},{13,9},{2,6},{6,2},{1... | collective-permute-start | bytes 884744 | tf_op jit(solution)/shard_map/ppermute | solution.py:37
  22.6 15.8 %collective-permute-start.11 = (bf16[4,32,1152]{2,1,0:T(8,128)(2,1)}, bf16[4,32,1152]{2,1,0:T(8,128)(2,1)S(1)}, u32[]{:S(2)}, u32[]{:S(2)}) collective-permute-start(bf16[4,32,1152]{2,1,0:T(8,128)(2,1)} %get-tuple-element.47), channel_id=1, source_target_pairs={{0,8},{4,12},{8,0},{12,4},{1,9},{5,13},{9,1},{13,5},{2,10},{6,14},... | collective-permute-start | bytes 884744 | tf_op jit(solution)/shard_map/ppermute | solution.py:37
  25.2 15.4 %collective-permute-start.12 = (bf16[4,32,1152]{2,1,0:T(8,128)(2,1)}, bf16[4,32,1152]{2,1,0:T(8,128)(2,1)S(1)}, u32[]{:S(2)}, u32[]{:S(2)}) collective-permute-start(bf16[4,32,1152]{2,1,0:T(8,128)(2,1)} %get-tuple-element.48), channel_id=1, source_target_pairs={{0,12},{4,8},{8,4},{12,0},{1,13},{5,9},{9,5},{13,1},{2,14},{6,10},... | collective-permute-start | bytes 884744 | tf_op jit(solution)/shard_map/ppermute | solution.py:37
  25.2 15.4 %collective-permute-start.7 = (bf16[4,32,1152]{2,1,0:T(8,128)(2,1)}, bf16[4,32,1152]{2,1,0:T(8,128)(2,1)S(1)}, u32[]{:S(2)}, u32[]{:S(2)}) collective-permute-start(bf16[4,32,1152]{2,1,0:T(8,128)(2,1)} %get-tuple-element.42), channel_id=1, source_target_pairs={{0,1},{1,0},{2,3},{3,2},{4,5},{5,4},{6,7},{7,6},{8,9},{9,8},{10,11... | collective-permute-start | bytes 884744 | tf_op jit(solution)/shard_map/ppermute | solution.py:37
  26.4 15.0 %collective-permute-start.8 = (bf16[4,32,1152]{2,1,0:T(8,128)(2,1)}, bf16[4,32,1152]{2,1,0:T(8,128)(2,1)S(1)}, u32[]{:S(2)}, u32[]{:S(2)}) collective-permute-start(bf16[4,32,1152]{2,1,0:T(8,128)(2,1)} %get-tuple-element.43), channel_id=1, source_target_pairs={{0,2},{1,3},{2,0},{3,1},{4,6},{5,7},{6,4},{7,5},{8,10},{9,11},{10,... | collective-permute-start | bytes 884744 | tf_op jit(solution)/shard_map/ppermute | solution.py:37
  29.6 14.6 %collective-permute-start.9 = (bf16[4,32,1152]{2,1,0:T(8,128)(2,1)S(1)}, bf16[4,32,1152]{2,1,0:T(8,128)(2,1)S(1)}, u32[]{:S(2)}, u32[]{:S(2)}) collective-permute-start(bf16[4,32,1152]{2,1,0:T(8,128)(2,1)S(1)} %get-tuple-element.44), channel_id=1, source_target_pairs={{0,3},{1,2},{2,1},{3,0},{4,7},{5,6},{6,5},{7,4},{8,11},{9,10},{10,... | collective-permute-start | bytes 884744 | tf_op jit(solution)/shard_map/ppermute | solution.py:37
  45.0 8.0 %collective-permute-start.13 = (bf16[32,1152]{1,0:T(8,128)(2,1)S(1)}, bf16[32,1152]{1,0:T(8,128)(2,1)S(1)}, u32[]{:S(2)}, u32[]{:S(2)}) collective-permute-start(bf16[32,1152]{1,0:T(8,128)(2,1)S(1)} %get-tuple-element.50), channel_id=1, source_target_pairs={{0,4},{4,0},{8,12},{12,8},{1,5},{5,1},{9,13},{13,9},{2,6},{6,2},{1... | collective-permute-start | bytes 221192 | tf_op jit(solution)/shard_map/ppermute | solution.py:37
  57.4 14.1 %collective-permute-start.20 = (bf16[64,128]{1,0:T(8,128)(2,1)S(1)}, bf16[64,128]{1,0:T(8,128)(2,1)S(1)}, u32[]{:S(2)}, u32[]{:S(2)}) collective-permute-start(bf16[64,128]{1,0:T(8,128)(2,1)S(1)} %get-tuple-element.58), channel_id=1, source_target_pairs={{0,0},{32,64},{64,128},{96,192},{128,32},{160,96},{192,160},{224,2... | collective-permute-start | bytes 49160 | tf_op jit(solution)/shard_map/ppermute | solution.py:250
  84.3 9.7 %collective-permute-start.22 = (bf16[1024,128]{1,0:T(8,128)(2,1)S(1)}, bf16[1024,128]{1,0:T(8,128)(2,1)S(1)}, u32[]{:S(2)}, u32[]{:S(2)}) collective-permute-start(bf16[1024,128]{1,0:T(8,128)(2,1)S(1)} %bitcast.15), channel_id=1, source_target_pairs={{0,32},{32,0},{1,33},{33,1},{2,34},{34,2},{3,35},{35,3},{4,36},{36... | collective-permute-start | bytes 786440 | tf_op jit(solution)/shard_map/ppermute | solution.py:37
  84.3 9.7 %collective-permute-start.19 = (bf16[64,1024]{1,0:T(8,128)(2,1)S(1)}, bf16[64,1024]{1,0:T(8,128)(2,1)S(1)}, u32[]{:S(2)}, u32[]{:S(2)}) collective-permute-start(bf16[64,1024]{1,0:T(8,128)(2,1)S(1)} %get-tuple-element.57.own), channel_id=1, source_target_pairs={{0,16},{16,0},{1,17},{17,1},{2,18},{18,2},{3,19},{19,3},{4,20},{20... | collective-permute-start | bytes 393224 | tf_op jit(solution)/shard_map/ppermute | solution.py:37
  95.9 7.4 %collective-permute-start.24 = (bf16[32,1024]{1,0:T(8,128)(2,1)S(1)}, bf16[32,1024]{1,0:T(8,128)(2,1)S(1)}, u32[]{:S(2)}, u32[]{:S(2)}) collective-permute-start(bf16[32,1024]{1,0:T(8,128)(2,1)S(1)} %get-tuple-element.59.refs_0_), channel_id=1, source_target_pairs={{0,2},{1,3},{2,0},{3,1},{4,6},{5,7},{6,4},{7,5},{8,10},{9,11},{10,... | collective-permute-start | bytes 196616 | tf_op jit(solution)/shard_map/ppermute | solution.py:37
  96.5 6.9 %collective-permute-start.25 = (bf16[32,1024]{1,0:T(8,128)(2,1)S(1)}, bf16[32,1024]{1,0:T(8,128)(2,1)S(1)}, u32[]{:S(2)}, u32[]{:S(2)}) collective-permute-start(bf16[32,1024]{1,0:T(8,128)(2,1)S(1)} %get-tuple-element.59.refs_0_), channel_id=1, source_target_pairs={{0,3},{1,2},{2,1},{3,0},{4,7},{5,6},{6,5},{7,4},{8,11},{9,10},{10,... | collective-permute-start | bytes 196616 | tf_op jit(solution)/shard_map/ppermute | solution.py:37
  105.9 9.8 %collective-permute-start.30 = (bf16[4,32,1024]{2,1,0:T(8,128)(2,1)S(1)}, bf16[4,32,1024]{2,1,0:T(8,128)(2,1)S(1)}, u32[]{:S(2)}, u32[]{:S(2)}) collective-permute-start(bf16[4,32,1024]{2,1,0:T(8,128)(2,1)S(1)} %get-tuple-element.61.refs_0_), channel_id=1, source_target_pairs={{0,8},{4,12},{8,0},{12,4},{1,9},{5,13},{9,1},{13,5},{2,10},{6,14},... | collective-permute-start | bytes 786440 | tf_op jit(solution)/shard_map/ppermute | solution.py:37
  109.0 9.2 %collective-permute-start.31 = (bf16[4,32,1024]{2,1,0:T(8,128)(2,1)S(1)}, bf16[4,32,1024]{2,1,0:T(8,128)(2,1)S(1)}, u32[]{:S(2)}, u32[]{:S(2)}) collective-permute-start(bf16[4,32,1024]{2,1,0:T(8,128)(2,1)S(1)} %get-tuple-element.61.refs_0_), channel_id=1, source_target_pairs={{0,12},{4,8},{8,4},{12,0},{1,13},{5,9},{9,5},{13,1},{2,14},{6,10},... | collective-permute-start | bytes 786440 | tf_op jit(solution)/shard_map/ppermute | solution.py:37
  109.6 8.7 %collective-permute-start.32 = (bf16[4,32,1024]{2,1,0:T(8,128)(2,1)S(1)}, bf16[4,32,1024]{2,1,0:T(8,128)(2,1)S(1)}, u32[]{:S(2)}, u32[]{:S(2)}) collective-permute-start(bf16[4,32,1024]{2,1,0:T(8,128)(2,1)S(1)} %get-tuple-element.62.refs_4_), channel_id=1, source_target_pairs={{0,1},{1,0},{2,3},{3,2},{4,5},{5,4},{6,7},{7,6},{8,9},{9,8},{10,11... | collective-permute-start | bytes 786440 | tf_op jit(solution)/shard_map/ppermute | solution.py:37
  109.6 8.7 %collective-permute-start.33 = (bf16[4,32,1024]{2,1,0:T(8,128)(2,1)S(1)}, bf16[4,32,1024]{2,1,0:T(8,128)(2,1)S(1)}, u32[]{:S(2)}, u32[]{:S(2)}) collective-permute-start(bf16[4,32,1024]{2,1,0:T(8,128)(2,1)S(1)} %get-tuple-element.62.refs_4_), channel_id=1, source_target_pairs={{0,2},{1,3},{2,0},{3,1},{4,6},{5,7},{6,4},{7,5},{8,10},{9,11},{10,... | collective-permute-start | bytes 786440 | tf_op jit(solution)/shard_map/ppermute | solution.py:37
  111.2 9.5 %collective-permute-start.34 = (bf16[4,32,1024]{2,1,0:T(8,128)(2,1)S(1)}, bf16[4,32,1024]{2,1,0:T(8,128)(2,1)S(1)}, u32[]{:S(2)}, u32[]{:S(2)}) collective-permute-start(bf16[4,32,1024]{2,1,0:T(8,128)(2,1)S(1)} %get-tuple-element.62.refs_4_), channel_id=1, source_target_pairs={{0,3},{1,2},{2,1},{3,0},{4,7},{5,6},{6,5},{7,4},{8,11},{9,10},{10,... | collective-permute-start | bytes 786440 | tf_op jit(solution)/shard_map/ppermute | solution.py:37
  122.8 8.9 %collective-permute-start.35 = (bf16[512,512]{1,0:T(8,128)(2,1)S(1)}, bf16[512,512]{1,0:T(8,128)(2,1)S(1)}, u32[]{:S(2)}, u32[]{:S(2)}) collective-permute-start(bf16[512,512]{1,0:T(8,128)(2,1)S(1)} %bitcast.18), channel_id=1, source_target_pairs={{0,32},{32,0},{1,33},{33,1},{2,34},{34,2},{3,35},{35,3},{4,36},{36... | collective-permute-start | bytes 1572872 | tf_op jit(solution)/shard_map/ppermute | solution.py:37
  132.4 14.8 %collective-permute-start.37 = (bf16[128,512]{1,0:T(8,128)(2,1)S(1)}, bf16[128,512]{1,0:T(8,128)(2,1)S(1)}, u32[]{:S(2)}, u32[]{:S(2)}) collective-permute-start(bf16[128,512]{1,0:T(8,128)(2,1)S(1)} %get-tuple-element.67), channel_id=1, source_target_pairs={{0,128},{64,192},{128,0},{192,64},{1,129},{65,193},{129,1},{193,65... | collective-permute-start | bytes 393224 | tf_op jit(solution)/shard_map/ppermute | solution.py:37
  137.6 9.7 %collective-permute-start.38 = (bf16[128,512]{1,0:T(8,128)(2,1)S(1)}, bf16[128,512]{1,0:T(8,128)(2,1)S(1)}, u32[]{:S(2)}, u32[]{:S(2)}) collective-permute-start(bf16[128,512]{1,0:T(8,128)(2,1)S(1)} %get-tuple-element.68), channel_id=1, source_target_pairs={{0,64},{64,0},{128,192},{192,128},{1,65},{65,1},{129,193},{193,129... | collective-permute-start | bytes 393224 | tf_op jit(solution)/shard_map/ppermute | solution.py:37
  (21 other events, 137.0 us)

commit v6 on v5

--- a/solution.py
+++ b/solution.py
@@ -37,6 +37,17 @@
     return lax.ppermute(block, axis, [(i, i ^ step) for i in range(size)])
 
 
+def across_plane(block, step, second):
+    pairs = []
+    for c in range(CORE):
+        for y in range(Y):
+            for x in range(X):
+                along_x = (c == 0) != second
+                to_y, to_x = (y, x ^ step) if along_x else (y ^ step, x)
+                pairs.append(((c * Y + y) * X + x, (c * Y + to_y) * X + to_x))
+    return lax.ppermute(block, ("core", *PLANE), pairs)
+
+
 def project(block, w_query, w_kv, chunks, k):
     size = chunks.shape[1]
     width = w_query.shape[1]
@@ -56,39 +67,33 @@
 
 def late_kernel(place, *refs):
     blocks, w_query, w_kv, early = refs[:6], *refs[6:9]
-    outs_x, outs_y, chunks = refs[9:13], refs[13:17], refs[17]
+    outs, chunks = refs[9:13], refs[13]
     for side in range(2):
         chunks[8 * side] = early[2 * side]
         chunks[8 * side + 1] = early[2 * side + 1]
         for i in range(3):
             project(blocks[3 * side + i], w_query, w_kv, chunks, 8 * side + 2 * i + 2)
-    cut = chunks.shape[1] // 2
-    x, y = place[0], place[1]
     for s in range(4):
         for j in range(4):
-            outs_x[s][j] = chunks[4 * j + (x ^ s), :cut, :]
-            outs_y[s][j] = chunks[4 * (y ^ s) + j, cut:, :]
-
-
-def halve_kernel(place, *refs):
-    for side in range(2):
-        a, b, c, d = refs[4 * side : 4 * side + 4]
-        for t in range(4):
-            out = refs[8 + 4 * side + t]
-            j = place[1 - side] ^ t
-            total = a[j].astype(F32) + b[j].astype(F32) + c[j].astype(F32) + d[j].astype(F32)
-            out[...] = total.astype(out.dtype)
-
-
-def join_kernel(*refs):
-    query, keyval = refs[8:]
-    rows, width = query.shape[0] // 2, query.shape[1]
-    for side in range(2):
-        total = functools.reduce(
-            jnp.add, [ref[...].astype(F32) for ref in refs[4 * side : 4 * side + 4]]
-        ).astype(BF16)
-        query[side * rows : (side + 1) * rows, :] = total[:, :width]
-        keyval[side * rows : (side + 1) * rows, :] = total[:, width:]
+            outs[s][j] = chunks[chunk_at(place, place[0] ^ s, j)]
+
+
+def chunk_at(place, first, second):
+    return first * place[2] + second * place[3]
+
+
+def halve_kernel(place, a, b, c, d, *outs):
+    for t, out in enumerate(outs):
+        j = place[1] ^ t
+        total = a[j].astype(F32) + b[j].astype(F32) + c[j].astype(F32) + d[j].astype(F32)
+        out[...] = total.astype(out.dtype)
+
+
+def join_kernel(a, b, c, d, query, keyval):
+    width = query.shape[1]
+    total = a[...] + b[...].astype(F32) + c[...].astype(F32) + d[...].astype(F32)
+    query[...] = total[:, :width].astype(BF16)
+    keyval[...] = total[:, width:].astype(BF16)
 
 
 def keys_kernel(a, b, cosine, sine_v, out):
@@ -99,7 +104,7 @@
 
 
 def attention_kernel(
-    heads, base, own, got, cosine, sine_v, kv_own, kv_other, low, high, queries, pair
+    heads, base, own, got, cosine, sine_v, kv_own, kv_other, out, queries, pair
 ):
     per_chunk = own.shape[0]
     pair[0] = kv_own[...]
@@ -134,30 +139,24 @@
         totals += jnp.sum(weights, 1, keepdims=True)
         mixed += jnp.dot(weights.astype(BF16), values, preferred_element_type=F32)
     attended = (mixed / totals).astype(BF16)
-    cut = per_chunk // 2
     for h in range(heads):
-        cols = slice(h * HD, (h + 1) * HD)
-        low[:, cols] = attended[h * per_chunk : h * per_chunk + cut]
-        high[:, cols] = attended[h * per_chunk + cut : (h + 1) * per_chunk]
+        out[:, h * HD : (h + 1) * HD] = attended[h * per_chunk : (h + 1) * per_chunk]
 
 
 def stack_kernel(*refs):
-    for side in range(2):
+    for s, ref in enumerate(refs[:4]):
+        refs[4][s] = ref[...]
+
+
+def output_kernel(place, *refs):
+    lines, weight, kept, sent, chunks = refs[:4], *refs[4:]
+    rows, width = lines[0].shape[1:]
+    for t, line in enumerate(lines):
+        block = line[...].reshape(4 * rows, width)
+        product = jnp.dot(block, weight[...], preferred_element_type=F32).astype(BF16)
         for s in range(4):
-            refs[8 + side][s] = refs[4 * side + s][...]
-
-
-def output_kernel(place, *refs):
-    by_y, by_x, weight, kept, sent, chunks = refs[:4], refs[4:8], *refs[8:]
-    x, y = place[0], place[1]
-    rows, width = by_y[0].shape[1:]
-    for side, arrays in enumerate((by_y, by_x)):
-        for t, array in enumerate(arrays):
-            block = array[...].reshape(4 * rows, width)
-            product = jnp.dot(block, weight[...], preferred_element_type=F32).astype(BF16)
-            for s in range(4):
-                k = 4 * (y ^ t) + (x ^ s) if side == 0 else 4 * (y ^ s) + (x ^ t)
-                chunks[k, side * rows : (side + 1) * rows, :] = product[s * rows : (s + 1) * rows]
+            k = chunk_at(place, place[0] ^ s, place[1] ^ t)
+            chunks[k] = product[s * rows : (s + 1) * rows]
     half = kept.shape[0]
     kept[...] = chunks[:half]
     sent[...] = chunks[half:]
@@ -194,7 +193,6 @@
     half = per_row * Z_LO
     total = half * 2
     per_chunk = total // (Y * X)
-    cut = per_chunk // 2
     width = w_query.shape[1]
     heads = width // HD
     both = width + HD
@@ -216,34 +214,28 @@
     key_cos, key_sin = tables((key_start + steps).astype(F32), HD)
     key_cos = jnp.where(core == 0, key_cos, 1.0)
     key_sin = jnp.where(core == 0, key_sin, 0.0)
-    place = jnp.stack([x, y]).astype(jnp.int32)
+    first, second = jnp.where(core == 0, x, y), jnp.where(core == 0, y, x)
+    place = jnp.stack([first, second, 1 + 3 * core, 4 - 3 * core]).astype(jnp.int32)
 
     near = partner(tokens, "core", 1)
     (early,) = call(early_kernel, [(4, per_chunk, both)], [tokens, near, w_query, w_keyval])
     *far, early = lax.optimization_barrier((*mine[1:], early))
     parts = call(
         late_kernel,
-        [(4, cut, both)] * 8,
+        [(4, per_chunk, both)] * 4,
         [place, *far, *[partner(block, "core", 1) for block in far], w_query, w_keyval, early],
         [SMEM],
         [pltpu.VMEM((Y * X, per_chunk, both), BF16)],
     )
-    got_x = [partner(parts[s], "x", s) for s in (1, 2, 3)]
-    got_y = [partner(parts[4 + s], "y", s) for s in (1, 2, 3)]
-    kept_f32 = jax.ShapeDtypeStruct((cut, both), F32)
+    got = [across_plane(parts[s], s, False) for s in (1, 2, 3)]
     halves = call(
         halve_kernel,
-        [kept_f32, *[(cut, both)] * 3] * 2,
-        [place, parts[0], *got_x, parts[4], *got_y],
-        [SMEM],
-    )
-    got_y = [partner(halves[t], "y", t) for t in (1, 2, 3)]
-    got_x = [partner(halves[4 + t], "x", t) for t in (1, 2, 3)]
-    own, kv = call(
-        join_kernel,
-        [(per_chunk, width), (per_chunk, HD)],
-        [halves[0], *got_y, halves[4], *got_x],
-    )
+        [jax.ShapeDtypeStruct((per_chunk, both), F32), *[(per_chunk, both)] * 3],
+        [place, parts[0], *got],
+        [SMEM],
+    )
+    got = [across_plane(halves[t], t, True) for t in (1, 2, 3)]
+    own, kv = call(join_kernel, [(per_chunk, width), (per_chunk, HD)], [halves[0], *got])
     got = partner(own, "zh", 1)
 
     moves = [(e, 2 * (e % 4) + e // 4) for e in range(8)]
@@ -251,31 +243,24 @@
     across = lax.ppermute(
         kv, (*ROW, "zh"), [(2 * e + h, 2 * r + 1 - h) for e, r in moves for h in range(2)]
     )
+    here, across, got = lax.optimization_barrier((here, across, got))
     (kv_block,) = call(keys_kernel, [(Y * X, per_chunk, HD)], [here, across, key_cos, key_sin])
     kv_own = lax.all_to_all(kv_block, PLANE, 0, 0, tiled=True).reshape(total, HD)
     kv_other = partner(kv_own, "core", 1)
-    low, high = call(
+    (attended,) = call(
         functools.partial(attention_kernel, heads),
-        [(cut, width)] * 2,
+        [(per_chunk, width)],
         [base, own, got, cosine, sine_v, kv_own, kv_other],
         [SMEM],
         [pltpu.VMEM((heads * per_chunk, HD), BF16), pltpu.VMEM((2, total, HD), BF16)],
     )
 
-    lines = call(
+    (line,) = call(
         stack_kernel,
-        [(4, cut, width)] * 2,
-        [low]
-        + [partner(low, "x", s) for s in (1, 2, 3)]
-        + [high]
-        + [partner(high, "y", s) for s in (1, 2, 3)],
-    )
-    gathered = (
-        [lines[0]]
-        + [partner(lines[0], "y", t) for t in (1, 2, 3)]
-        + [lines[1]]
-        + [partner(lines[1], "x", t) for t in (1, 2, 3)]
-    )
+        [(4, per_chunk, width)],
+        [attended] + [across_plane(attended, s, False) for s in (1, 2, 3)],
+    )
+    gathered = [line] + [across_plane(line, t, True) for t in (1, 2, 3)]
     kept, sent = call(
         output_kernel,
         [(Y * X // 2, per_chunk, features)] * 2,

time: 148 us -> 133 us (0.90)
  starting transfers between devices: 75.7 us -> 45.8 us
  waiting for transfers between devices: 47.7 us -> 62.8 us
    ppermute x37 -> x13, starting transfers between devices: 61.7 us -> 22.3 us  [partner(): return lax.ppermute(block, axis, [(i, i ^ step) for i in range(size)])]
    ppermute x0 -> x12, waiting for transfers between devices: none -> 38.8 us  [across_plane(): return lax.ppermute(block, ('core', *PLANE), pairs)]
    ppermute x37 -> x13, waiting for transfers between devices: 46.9 us -> 19.1 us  [partner(): return lax.ppermute(block, axis, [(i, i ^ step) for i in range(size)])]
    ppermute x0 -> x12, starting transfers between devices: none -> 15.7 us  [across_plane(): return lax.ppermute(block, ('core', *PLANE), pairs)]
    ppermute x1, starting transfers between devices: 5.34 us -> 0.39 us  [shards(): lax.ppermute(kv, (*ROW, 'zh'), [(2 * e + h, 2 * r + 1 - h) for e, r in mo...]
    ppermute x1, waiting for transfers between devices: 0.77 us -> 3.48 us  [shards(): lax.ppermute(kv, (*ROW, 'zh'), [(2 * e + h, 2 * r + 1 - h) for e, r in mo...]
  transfers between devices with their start and end apart: 39 -> 27, of which waited for: 22 -> 23; matrix products, arithmetic and copies ran while one was open for 0% -> 0% of each run, Pallas kernels for 0% -> 0%
where the time goes in v6:
time: 133 us; the launch traced here: 132 us
  waiting for transfers between devices  62.8 us (47%)
  starting transfers between devices  45.8 us (34%)
  blocking collectives  11.2 us (8%)
  Pallas kernels  8.08 us (6%)
  local copies, waits for them, and re-layouts  3.13 us (2%)
    ppermute x12, waiting for transfers between devices, across_plane(): return lax.ppermute(block, ('core', *PLANE), pairs)  38.8 us
    ppermute x13, starting transfers between devices, partner(): return lax.ppermute(block, axis, [(i, i ^ step) for i in range(size)])  22.3 us
    ppermute x13, waiting for transfers between devices, partner(): return lax.ppermute(block, axis, [(i, i ^ step) for i in range(size)])  19.1 us
    ppermute x12, starting transfers between devices, across_plane(): return lax.ppermute(block, ('core', *PLANE), pairs)  15.7 us
    all_to_all x1, blocking collectives, shards(): lax.all_to_all(kv_block, PLANE, 0, 0, tiled=True).reshape(total, HD)  11.2 us
    pallas_call x9, Pallas kernels, call(): pl.pallas_call(kernel, out_shape=[s if isinstance(s, jax.ShapeDtypeStruct...  8.08 us
    ppermute x1, starting transfers between devices, shards(): here = lax.ppermute(kv, ROW, moves)  7.42 us
    ppermute x1, waiting for transfers between devices, shards(): lax.ppermute(kv, (*ROW, 'zh'), [(2 * e + h, 2 * r + 1 - h) for e, r in mo...  3.48 us
  transfers between devices with their start and end apart: 27, of which 23 were waited for; matrix products, arithmetic and copies ran while one was open for 0% of the time, Pallas kernels for 0%

profile of v6, /device:TPU:1, one launch (start us, length us, event | category | flops | bytes accessed | tf_op | source)
XLA Modules:
  0.0 132.4 jit_solution(2212267173303441851)
XLA Ops:
  0.0 3.2 %collective-permute-start.3 = (bf16[128,512]{1,0:T(8,128)(2,1)}, bf16[128,512]{1,0:T(8,128)(2,1)S(1)}, u32[]{:S(2)}, u32[]{:S(2)}) collective-permute-start(bf16[128,512]{1,0:T(8,128)(2,1)} %refs_0_.1), channel_id=1, source_target_pairs={{0,32},{32,0},{1,33},{33,1},{2,34},{34,2},{3,35},{35,3},{4,36},{36... | collective-permute-start | bytes 393224 | tf_op jit(solution)/shard_map/ppermute | solution.py:37
  3.2 2.9 %collective-permute-start.1 = (bf16[128,512]{1,0:T(8,128)(2,1)}, bf16[128,512]{1,0:T(8,128)(2,1)S(1)}, u32[]{:S(2)}, u32[]{:S(2)}) collective-permute-start(bf16[128,512]{1,0:T(8,128)(2,1)} %refs_0_.1), channel_id=1, source_target_pairs={{0,128},{64,192},{128,0},{192,64},{1,129},{65,193},{129,1},{193,65... | collective-permute-start | bytes 393224 | tf_op jit(solution)/shard_map/ppermute | solution.py:37
  11.1 4.4 %collective-permute-done.2.refs_2_ = bf16[128,512]{1,0:T(8,128)(2,1)S(1)} collective-permute-done((bf16[128,512]{1,0:T(8,128)(2,1)}, bf16[128,512]{1,0:T(8,128)(2,1)S(1)}, u32[]{:S(2)}, u32[]{:S(2)}) %collective-permute-start.2) | collective-permute-done | bytes 131104 | tf_op jit(solution)/shard_map/ppermute | solution.py:37
  18.4 3.0 %shard_map.47 = (bf16[4,64,1152]{2,1,0:T(8,128)(2,1)S(1)}, bf16[4,64,1152]{2,1,0:T(8,128)(2,1)}, bf16[4,64,1152]{2,1,0:T(8,128)(2,1)}, bf16[4,64,1152]{2,1,0:T(8,128)(2,1)}) custom-call(s32[4]{0:T(128)S(1)} %pad_add_fusion.place, bf16[128,512]{1,0:T(8,128)(2,1)S(1)} %collective-permute-done.refs_0_, bf16[128,512]{1,0:T(8,128)(2,1)S(1)} %collective-permute-done.1.refs_1_, ...), custom_call_target="tpu_custom_call" | custom-call | tf_op jit(solution)/shard_map/pallas_call | solution.py:174
  22.7 2.6 %collective-permute-start.8 = (bf16[4,64,1152]{2,1,0:T(8,128)(2,1)}, bf16[4,64,1152]{2,1,0:T(8,128)(2,1)S(1)}, u32[]{:S(2)}, u32[]{:S(2)}) collective-permute-start(bf16[4,64,1152]{2,1,0:T(8,128)(2,1)} %get-tuple-element.34), channel_id=1, source_target_pairs={{0,2},{1,3},{2,0},{3,1},{4,6},{5,7},{6,4},{7,5},{8,10},{9,11},{10,... | collective-permute-start | bytes 1769480 | tf_op jit(solution)/shard_map/ppermute | solution.py:48
  25.3 5.4 %collective-permute-done.7.b = bf16[4,64,1152]{2,1,0:T(8,128)(2,1)S(1)} collective-permute-done((bf16[4,64,1152]{2,1,0:T(8,128)(2,1)}, bf16[4,64,1152]{2,1,0:T(8,128)(2,1)S(1)}, u32[]{:S(2)}, u32[]{:S(2)}) %collective-permute-start.7) | collective-permute-done | bytes 589856 | tf_op jit(solution)/shard_map/ppermute | solution.py:48
  30.7 8.8 %collective-permute-done.8.c = bf16[4,64,1152]{2,1,0:T(8,128)(2,1)S(1)} collective-permute-done((bf16[4,64,1152]{2,1,0:T(8,128)(2,1)}, bf16[4,64,1152]{2,1,0:T(8,128)(2,1)S(1)}, u32[]{:S(2)}, u32[]{:S(2)}) %collective-permute-start.8) | collective-permute-done | bytes 589856 | tf_op jit(solution)/shard_map/ppermute | solution.py:48
  39.4 2.6 %collective-permute-done.9.d = bf16[4,64,1152]{2,1,0:T(8,128)(2,1)S(1)} collective-permute-done((bf16[4,64,1152]{2,1,0:T(8,128)(2,1)}, bf16[4,64,1152]{2,1,0:T(8,128)(2,1)S(1)}, u32[]{:S(2)}, u32[]{:S(2)}) %collective-permute-start.9) | collective-permute-done | bytes 589856 | tf_op jit(solution)/shard_map/ppermute | solution.py:48
  43.9 2.4 %collective-permute-start.11 = (bf16[64,1152]{1,0:T(8,128)(2,1)S(1)}, bf16[64,1152]{1,0:T(8,128)(2,1)S(1)}, u32[]{:S(2)}, u32[]{:S(2)}) collective-permute-start(bf16[64,1152]{1,0:T(8,128)(2,1)S(1)} %get-tuple-element.38), channel_id=1, source_target_pairs={{0,8},{1,9},{2,10},{3,11},{4,12},{5,13},{6,14},{7,15},{8,0},{9,1},... | collective-permute-start | bytes 442376 | tf_op jit(solution)/shard_map/ppermute | solution.py:48
  47.0 3.5 %collective-permute-done.11.c = bf16[64,1152]{1,0:T(8,128)(2,1)S(1)} collective-permute-done((bf16[64,1152]{1,0:T(8,128)(2,1)S(1)}, bf16[64,1152]{1,0:T(8,128)(2,1)S(1)}, u32[]{:S(2)}, u32[]{:S(2)}) %collective-permute-start.11) | collective-permute-done | bytes 147488 | tf_op jit(solution)/shard_map/ppermute | solution.py:48
  52.4 5.8 %collective-permute-start.15 = (bf16[64,1024]{1,0:T(8,128)(2,1)S(1)}, bf16[64,1024]{1,0:T(8,128)(2,1)S(1)}, u32[]{:S(2)}, u32[]{:S(2)}) collective-permute-start(bf16[64,1024]{1,0:T(8,128)(2,1)S(1)} %get-tuple-element.40.own), channel_id=1, source_target_pairs={{0,16},{16,0},{1,17},{17,1},{2,18},{18,2},{3,19},{19,3},{4,20},{20... | collective-permute-start | bytes 393224 | tf_op jit(solution)/shard_map/ppermute | solution.py:37
  58.5 7.4 %collective-permute-start.13 = (bf16[64,128]{1,0:T(8,128)(2,1)S(1)}, bf16[64,128]{1,0:T(8,128)(2,1)S(1)}, u32[]{:S(2)}, u32[]{:S(2)}) collective-permute-start(bf16[64,128]{1,0:T(8,128)(2,1)S(1)} %get-tuple-element.41), channel_id=1, source_target_pairs={{0,0},{32,64},{64,128},{96,192},{128,32},{160,96},{192,160},{224,2... | collective-permute-start | bytes 49160 | tf_op jit(solution)/shard_map/ppermute | solution.py:242
  67.8 3.5 %collective-permute-done.14.b = bf16[64,128]{1,0:T(8,128)(2,1)S(1)} collective-permute-done((bf16[64,128]{1,0:T(8,128)(2,1)S(1)}, bf16[64,128]{1,0:T(8,128)(2,1)S(1)}, u32[]{:S(2)}, u32[]{:S(2)}) %collective-permute-start.14) | collective-permute-done | bytes 16416 | tf_op jit(solution)/shard_map/ppermute | solution.py:243
  71.4 11.2 %all_to_all.5 = bf16[16,64,128]{2,1,0:T(8,128)(2,1)S(1)} all-to-all(bf16[16,64,128]{2,1,0:T(8,128)(2,1)S(1)} %shard_map.50), channel_id=1, replica_groups=mesh['zl'=4,'core'=2,'zh'=2,'y'=4,'x'=4] {'y','x'}, dimensions={0} | all-to-all | bytes 524288 | tf_op jit(solution)/shard_map/all_to_all | solution.py:248
  88.2 2.1 %collective-permute-start.19 = (bf16[64,1024]{1,0:T(8,128)(2,1)S(1)}, bf16[64,1024]{1,0:T(8,128)(2,1)S(1)}, u32[]{:S(2)}, u32[]{:S(2)}) collective-permute-start(bf16[64,1024]{1,0:T(8,128)(2,1)S(1)} %shard_map.51.refs_0_), channel_id=1, source_target_pairs={{0,3},{1,2},{2,1},{3,0},{4,7},{5,6},{6,5},{7,4},{8,11},{9,10},{10,... | collective-permute-start | bytes 393224 | tf_op jit(solution)/shard_map/ppermute | solution.py:48
  95.7 2.0 %collective-permute-start.22 = (bf16[4,64,1024]{2,1,0:T(8,128)(2,1)S(1)}, bf16[4,64,1024]{2,1,0:T(8,128)(2,1)S(1)}, u32[]{:S(2)}, u32[]{:S(2)}) collective-permute-start(bf16[4,64,1024]{2,1,0:T(8,128)(2,1)S(1)} %shard_map.52.refs_0_), channel_id=1, source_target_pairs={{0,12},{1,13},{2,14},{3,15},{4,8},{5,9},{6,10},{7,11},{8,4},{9,5},... | collective-permute-start | bytes 1572872 | tf_op jit(solution)/shard_map/ppermute | solution.py:48
  97.6 4.5 %collective-permute-done.20.refs_1_ = bf16[4,64,1024]{2,1,0:T(8,128)(2,1)S(1)} collective-permute-done((bf16[4,64,1024]{2,1,0:T(8,128)(2,1)S(1)}, bf16[4,64,1024]{2,1,0:T(8,128)(2,1)S(1)}, u32[]{:S(2)}, u32[]{:S(2)}) %collective-permute-start.20) | collective-permute-done | bytes 524320 | tf_op jit(solution)/shard_map/ppermute | solution.py:48
  102.1 6.1 %collective-permute-done.21.refs_2_ = bf16[4,64,1024]{2,1,0:T(8,128)(2,1)S(1)} collective-permute-done((bf16[4,64,1024]{2,1,0:T(8,128)(2,1)S(1)}, bf16[4,64,1024]{2,1,0:T(8,128)(2,1)S(1)}, u32[]{:S(2)}, u32[]{:S(2)}) %collective-permute-start.21) | collective-permute-done | bytes 524320 | tf_op jit(solution)/shard_map/ppermute | solution.py:48
  108.2 2.6 %collective-permute-done.22.refs_3_ = bf16[4,64,1024]{2,1,0:T(8,128)(2,1)S(1)} collective-permute-done((bf16[4,64,1024]{2,1,0:T(8,128)(2,1)S(1)}, bf16[4,64,1024]{2,1,0:T(8,128)(2,1)S(1)}, u32[]{:S(2)}, u32[]{:S(2)}) %collective-permute-start.22) | collective-permute-done | bytes 524320 | tf_op jit(solution)/shard_map/ppermute | solution.py:48
  110.8 1.9 %shard_map.53 = (bf16[8,64,512]{2,1,0:T(8,128)(2,1)S(1)}, bf16[8,64,512]{2,1,0:T(8,128)(2,1)S(1)}) custom-call(s32[4]{0:T(128)S(1)} %pad_add_fusion.place, bf16[4,64,1024]{2,1,0:T(8,128)(2,1)S(1)} %shard_map.52.refs_0_, bf16[4,64,1024]{2,1,0:T(8,128)(2,1)S(1)} %collective-permute-done.20.refs_1_, bf16[4,64,1024]{2,1,0:T(8,128)(2,1)S(1)} %collective-permute-done.21.refs_2_, ...), custom_call_target="tpu_custom_call" | custom-call | tf_op jit(solution)/shard_map/pallas_call | solution.py:174
  112.7 3.2 %collective-permute-start.23 = (bf16[512,512]{1,0:T(8,128)(2,1)S(1)}, bf16[512,512]{1,0:T(8,128)(2,1)S(1)}, u32[]{:S(2)}, u32[]{:S(2)}) collective-permute-start(bf16[512,512]{1,0:T(8,128)(2,1)S(1)} %bitcast.20), channel_id=1, source_target_pairs={{0,32},{32,0},{1,33},{33,1},{2,34},{34,2},{3,35},{35,3},{4,36},{36... | collective-permute-start | bytes 1572872 | tf_op jit(solution)/shard_map/ppermute | solution.py:37
  117.6 2.4 %collective-permute-start.25 = (bf16[128,512]{1,0:T(8,128)(2,1)S(1)}, bf16[128,512]{1,0:T(8,128)(2,1)S(1)}, u32[]{:S(2)}, u32[]{:S(2)}) collective-permute-start(bf16[128,512]{1,0:T(8,128)(2,1)S(1)} %get-tuple-element.49), channel_id=1, source_target_pairs={{0,128},{64,192},{128,0},{192,64},{1,129},{65,193},{129,1},{193,65... | collective-permute-start | bytes 393224 | tf_op jit(solution)/shard_map/ppermute | solution.py:37
  121.1 3.0 %collective-permute-done.24 = bf16[128,512]{1,0:T(8,128)(2,1)S(1)} collective-permute-done((bf16[128,512]{1,0:T(8,128)(2,1)S(1)}, bf16[128,512]{1,0:T(8,128)(2,1)S(1)}, u32[]{:S(2)}, u32[]{:S(2)}) %collective-permute-start.24) | collective-permute-done | bytes 131104 | tf_op jit(solution)/shard_map/ppermute | solution.py:37
  124.1 7.5 %collective-permute-done.25 = bf16[128,512]{1,0:T(8,128)(2,1)S(1)} collective-permute-done((bf16[128,512]{1,0:T(8,128)(2,1)S(1)}, bf16[128,512]{1,0:T(8,128)(2,1)S(1)}, u32[]{:S(2)}, u32[]{:S(2)}) %collective-permute-start.25) | collective-permute-done | bytes 131104 | tf_op jit(solution)/shard_map/ppermute | solution.py:37
  (61 shorter events, 30.2 us)
Async XLA Ops:
  0.0 6.8 %collective-permute-start.3 = (bf16[128,512]{1,0:T(8,128)(2,1)}, bf16[128,512]{1,0:T(8,128)(2,1)S(1)}, u32[]{:S(2)}, u32[]{:S(2)}) collective-permute-start(bf16[128,512]{1,0:T(8,128)(2,1)} %refs_0_.1), channel_id=1, source_target_pairs={{0,32},{32,0},{1,33},{33,1},{2,34},{34,2},{3,35},{35,3},{4,36},{36... | collective-permute-start | bytes 393224 | tf_op jit(solution)/shard_map/ppermute | solution.py:37
  3.2 7.8 %collective-permute-start = (bf16[128,512]{1,0:T(8,128)(2,1)}, bf16[128,512]{1,0:T(8,128)(2,1)S(1)}, u32[]{:S(2)}, u32[]{:S(2)}) collective-permute-start(bf16[128,512]{1,0:T(8,128)(2,1)} %refs_0_.1), channel_id=1, source_target_pairs={{0,64},{64,0},{128,192},{192,128},{1,65},{65,1},{129,193},{193,129... | collective-permute-start | bytes 393224 | tf_op jit(solution)/shard_map/ppermute | solution.py:37
  3.2 7.8 %collective-permute-start.1 = (bf16[128,512]{1,0:T(8,128)(2,1)}, bf16[128,512]{1,0:T(8,128)(2,1)S(1)}, u32[]{:S(2)}, u32[]{:S(2)}) collective-permute-start(bf16[128,512]{1,0:T(8,128)(2,1)} %refs_0_.1), channel_id=1, source_target_pairs={{0,128},{64,192},{128,0},{192,64},{1,129},{65,193},{129,1},{193,65... | collective-permute-start | bytes 393224 | tf_op jit(solution)/shard_map/ppermute | solution.py:37
  6.1 9.3 %collective-permute-start.2 = (bf16[128,512]{1,0:T(8,128)(2,1)}, bf16[128,512]{1,0:T(8,128)(2,1)S(1)}, u32[]{:S(2)}, u32[]{:S(2)}) collective-permute-start(bf16[128,512]{1,0:T(8,128)(2,1)} %refs_0_.1), channel_id=1, source_target_pairs={{0,192},{64,128},{128,64},{192,0},{1,193},{65,129},{129,65},{193,1... | collective-permute-start | bytes 393224 | tf_op jit(solution)/shard_map/ppermute | solution.py:37
  15.5 2.4 %collective-permute-start.4 = (bf16[128,512]{1,0:T(8,128)(2,1)S(1)}, bf16[128,512]{1,0:T(8,128)(2,1)S(1)}, u32[]{:S(2)}, u32[]{:S(2)}) collective-permute-start(bf16[128,512]{1,0:T(8,128)(2,1)S(1)} %collective-permute-done.refs_0_), channel_id=1, source_target_pairs={{0,32},{32,0},{1,33},{33,1},{2,34},{34,2},{3,35},{35,3},{4,36},{36... | collective-permute-start | bytes 393224 | tf_op jit(solution)/shard_map/ppermute | solution.py:37
  21.4 9.2 %collective-permute-start.7 = (bf16[4,64,1152]{2,1,0:T(8,128)(2,1)}, bf16[4,64,1152]{2,1,0:T(8,128)(2,1)S(1)}, u32[]{:S(2)}, u32[]{:S(2)}) collective-permute-start(bf16[4,64,1152]{2,1,0:T(8,128)(2,1)} %get-tuple-element.33), channel_id=1, source_target_pairs={{0,1},{1,0},{2,3},{3,2},{4,5},{5,4},{6,7},{7,6},{8,9},{9,8},{10,11... | collective-permute-start | bytes 1769480 | tf_op jit(solution)/shard_map/ppermute | solution.py:48
  22.7 16.8 %collective-permute-start.8 = (bf16[4,64,1152]{2,1,0:T(8,128)(2,1)}, bf16[4,64,1152]{2,1,0:T(8,128)(2,1)S(1)}, u32[]{:S(2)}, u32[]{:S(2)}) collective-permute-start(bf16[4,64,1152]{2,1,0:T(8,128)(2,1)} %get-tuple-element.34), channel_id=1, source_target_pairs={{0,2},{1,3},{2,0},{3,1},{4,6},{5,7},{6,4},{7,5},{8,10},{9,11},{10,... | collective-permute-start | bytes 1769480 | tf_op jit(solution)/shard_map/ppermute | solution.py:48
  25.3 16.8 %collective-permute-start.9 = (bf16[4,64,1152]{2,1,0:T(8,128)(2,1)}, bf16[4,64,1152]{2,1,0:T(8,128)(2,1)S(1)}, u32[]{:S(2)}, u32[]{:S(2)}) collective-permute-start(bf16[4,64,1152]{2,1,0:T(8,128)(2,1)} %get-tuple-element.35), channel_id=1, source_target_pairs={{0,3},{1,2},{2,1},{3,0},{4,7},{5,6},{6,5},{7,4},{8,11},{9,10},{10,... | collective-permute-start | bytes 1769480 | tf_op jit(solution)/shard_map/ppermute | solution.py:48
  42.9 4.1 %collective-permute-start.10 = (bf16[64,1152]{1,0:T(8,128)(2,1)S(1)}, bf16[64,1152]{1,0:T(8,128)(2,1)S(1)}, u32[]{:S(2)}, u32[]{:S(2)}) collective-permute-start(bf16[64,1152]{1,0:T(8,128)(2,1)S(1)} %get-tuple-element.37), channel_id=1, source_target_pairs={{0,4},{1,5},{2,6},{3,7},{4,0},{5,1},{6,2},{7,3},{8,12},{9,13},{10,... | collective-permute-start | bytes 442376 | tf_op jit(solution)/shard_map/ppermute | solution.py:48
  43.9 6.6 %collective-permute-start.11 = (bf16[64,1152]{1,0:T(8,128)(2,1)S(1)}, bf16[64,1152]{1,0:T(8,128)(2,1)S(1)}, u32[]{:S(2)}, u32[]{:S(2)}) collective-permute-start(bf16[64,1152]{1,0:T(8,128)(2,1)S(1)} %get-tuple-element.38), channel_id=1, source_target_pairs={{0,8},{1,9},{2,10},{3,11},{4,12},{5,13},{6,14},{7,15},{8,0},{9,1},... | collective-permute-start | bytes 442376 | tf_op jit(solution)/shard_map/ppermute | solution.py:48
  46.4 6.0 %collective-permute-start.12 = (bf16[64,1152]{1,0:T(8,128)(2,1)S(1)}, bf16[64,1152]{1,0:T(8,128)(2,1)S(1)}, u32[]{:S(2)}, u32[]{:S(2)}) collective-permute-start(bf16[64,1152]{1,0:T(8,128)(2,1)S(1)} %get-tuple-element.39), channel_id=1, source_target_pairs={{0,12},{1,13},{2,14},{3,15},{4,8},{5,9},{6,10},{7,11},{8,4},{9,5},... | collective-permute-start | bytes 442376 | tf_op jit(solution)/shard_map/ppermute | solution.py:48
  52.4 18.9 %collective-permute-start.15 = (bf16[64,1024]{1,0:T(8,128)(2,1)S(1)}, bf16[64,1024]{1,0:T(8,128)(2,1)S(1)}, u32[]{:S(2)}, u32[]{:S(2)}) collective-permute-start(bf16[64,1024]{1,0:T(8,128)(2,1)S(1)} %get-tuple-element.40.own), channel_id=1, source_target_pairs={{0,16},{16,0},{1,17},{17,1},{2,18},{18,2},{3,19},{19,3},{4,20},{20... | collective-permute-start | bytes 393224 | tf_op jit(solution)/shard_map/ppermute | solution.py:37
  58.5 9.3 %collective-permute-start.13 = (bf16[64,128]{1,0:T(8,128)(2,1)S(1)}, bf16[64,128]{1,0:T(8,128)(2,1)S(1)}, u32[]{:S(2)}, u32[]{:S(2)}) collective-permute-start(bf16[64,128]{1,0:T(8,128)(2,1)S(1)} %get-tuple-element.41), channel_id=1, source_target_pairs={{0,0},{32,64},{64,128},{96,192},{128,32},{160,96},{192,160},{224,2... | collective-permute-start | bytes 49160 | tf_op jit(solution)/shard_map/ppermute | solution.py:242
  65.9 5.3 %collective-permute-start.14 = (bf16[64,128]{1,0:T(8,128)(2,1)S(1)}, bf16[64,128]{1,0:T(8,128)(2,1)S(1)}, u32[]{:S(2)}, u32[]{:S(2)}) collective-permute-start(bf16[64,128]{1,0:T(8,128)(2,1)S(1)} %get-tuple-element.41), channel_id=1, source_target_pairs={{0,16},{16,0},{32,80},{48,64},{64,144},{80,128},{96,208},{112,192}... | collective-permute-start | bytes 49160 | tf_op jit(solution)/shard_map/ppermute | solution.py:243
  86.4 4.2 %collective-permute-start.17 = (bf16[64,1024]{1,0:T(8,128)(2,1)S(1)}, bf16[64,1024]{1,0:T(8,128)(2,1)S(1)}, u32[]{:S(2)}, u32[]{:S(2)}) collective-permute-start(bf16[64,1024]{1,0:T(8,128)(2,1)S(1)} %shard_map.51.refs_0_), channel_id=1, source_target_pairs={{0,1},{1,0},{2,3},{3,2},{4,5},{5,4},{6,7},{7,6},{8,9},{9,8},{10,11... | collective-permute-start | bytes 393224 | tf_op jit(solution)/shard_map/ppermute | solution.py:48
  86.5 5.8 %collective-permute-start.18 = (bf16[64,1024]{1,0:T(8,128)(2,1)S(1)}, bf16[64,1024]{1,0:T(8,128)(2,1)S(1)}, u32[]{:S(2)}, u32[]{:S(2)}) collective-permute-start(bf16[64,1024]{1,0:T(8,128)(2,1)S(1)} %shard_map.51.refs_0_), channel_id=1, source_target_pairs={{0,2},{1,3},{2,0},{3,1},{4,6},{5,7},{6,4},{7,5},{8,10},{9,11},{10,... | collective-permute-start | bytes 393224 | tf_op jit(solution)/shard_map/ppermute | solution.py:48
  88.2 5.5 %collective-permute-start.19 = (bf16[64,1024]{1,0:T(8,128)(2,1)S(1)}, bf16[64,1024]{1,0:T(8,128)(2,1)S(1)}, u32[]{:S(2)}, u32[]{:S(2)}) collective-permute-start(bf16[64,1024]{1,0:T(8,128)(2,1)S(1)} %shard_map.51.refs_0_), channel_id=1, source_target_pairs={{0,3},{1,2},{2,1},{3,0},{4,7},{5,6},{6,5},{7,4},{8,11},{9,10},{10,... | collective-permute-start | bytes 393224 | tf_op jit(solution)/shard_map/ppermute | solution.py:48
  93.7 8.4 %collective-permute-start.20 = (bf16[4,64,1024]{2,1,0:T(8,128)(2,1)S(1)}, bf16[4,64,1024]{2,1,0:T(8,128)(2,1)S(1)}, u32[]{:S(2)}, u32[]{:S(2)}) collective-permute-start(bf16[4,64,1024]{2,1,0:T(8,128)(2,1)S(1)} %shard_map.52.refs_0_), channel_id=1, source_target_pairs={{0,4},{1,5},{2,6},{3,7},{4,0},{5,1},{6,2},{7,3},{8,12},{9,13},{10,... | collective-permute-start | bytes 1572872 | tf_op jit(solution)/shard_map/ppermute | solution.py:48
  93.9 14.3 %collective-permute-start.21 = (bf16[4,64,1024]{2,1,0:T(8,128)(2,1)S(1)}, bf16[4,64,1024]{2,1,0:T(8,128)(2,1)S(1)}, u32[]{:S(2)}, u32[]{:S(2)}) collective-permute-start(bf16[4,64,1024]{2,1,0:T(8,128)(2,1)S(1)} %shard_map.52.refs_0_), channel_id=1, source_target_pairs={{0,8},{1,9},{2,10},{3,11},{4,12},{5,13},{6,14},{7,15},{8,0},{9,1},... | collective-permute-start | bytes 1572872 | tf_op jit(solution)/shard_map/ppermute | solution.py:48
  95.7 15.2 %collective-permute-start.22 = (bf16[4,64,1024]{2,1,0:T(8,128)(2,1)S(1)}, bf16[4,64,1024]{2,1,0:T(8,128)(2,1)S(1)}, u32[]{:S(2)}, u32[]{:S(2)}) collective-permute-start(bf16[4,64,1024]{2,1,0:T(8,128)(2,1)S(1)} %shard_map.52.refs_0_), channel_id=1, source_target_pairs={{0,12},{1,13},{2,14},{3,15},{4,8},{5,9},{6,10},{7,11},{8,4},{9,5},... | collective-permute-start | bytes 1572872 | tf_op jit(solution)/shard_map/ppermute | solution.py:48
  112.7 4.7 %collective-permute-start.23 = (bf16[512,512]{1,0:T(8,128)(2,1)S(1)}, bf16[512,512]{1,0:T(8,128)(2,1)S(1)}, u32[]{:S(2)}, u32[]{:S(2)}) collective-permute-start(bf16[512,512]{1,0:T(8,128)(2,1)S(1)} %bitcast.20), channel_id=1, source_target_pairs={{0,32},{32,0},{1,33},{33,1},{2,34},{34,2},{3,35},{35,3},{4,36},{36... | collective-permute-start | bytes 1572872 | tf_op jit(solution)/shard_map/ppermute | solution.py:37
  117.5 6.6 %collective-permute-start.24 = (bf16[128,512]{1,0:T(8,128)(2,1)S(1)}, bf16[128,512]{1,0:T(8,128)(2,1)S(1)}, u32[]{:S(2)}, u32[]{:S(2)}) collective-permute-start(bf16[128,512]{1,0:T(8,128)(2,1)S(1)} %get-tuple-element.48), channel_id=1, source_target_pairs={{0,192},{64,128},{128,64},{192,0},{1,193},{65,129},{129,65},{193,1... | collective-permute-start | bytes 393224 | tf_op jit(solution)/shard_map/ppermute | solution.py:37
  117.6 14.1 %collective-permute-start.25 = (bf16[128,512]{1,0:T(8,128)(2,1)S(1)}, bf16[128,512]{1,0:T(8,128)(2,1)S(1)}, u32[]{:S(2)}, u32[]{:S(2)}) collective-permute-start(bf16[128,512]{1,0:T(8,128)(2,1)S(1)} %get-tuple-element.49), channel_id=1, source_target_pairs={{0,128},{64,192},{128,0},{192,64},{1,129},{65,193},{129,1},{193,65... | collective-permute-start | bytes 393224 | tf_op jit(solution)/shard_map/ppermute | solution.py:37
  120.0 11.7 %collective-permute-start.26 = (bf16[128,512]{1,0:T(8,128)(2,1)S(1)}, bf16[128,512]{1,0:T(8,128)(2,1)S(1)}, u32[]{:S(2)}, u32[]{:S(2)}) collective-permute-start(bf16[128,512]{1,0:T(8,128)(2,1)S(1)} %get-tuple-element.50), channel_id=1, source_target_pairs={{0,64},{64,0},{128,192},{192,128},{1,65},{65,1},{129,193},{193,129... | collective-permute-start | bytes 393224 | tf_op jit(solution)/shard_map/ppermute | solution.py:37
  (9 other events, 52.3 us)

commit v7 on v6

--- a/solution.py
+++ b/solution.py
@@ -75,11 +75,7 @@
             project(blocks[3 * side + i], w_query, w_kv, chunks, 8 * side + 2 * i + 2)
     for s in range(4):
         for j in range(4):
-            outs[s][j] = chunks[chunk_at(place, place[0] ^ s, j)]
-
-
-def chunk_at(place, first, second):
-    return first * place[2] + second * place[3]
+            outs[s][j] = chunks[(place[0] ^ s) + 4 * j]
 
 
 def halve_kernel(place, a, b, c, d, *outs):
@@ -98,19 +94,18 @@
 
 def keys_kernel(a, b, cosine, sine_v, out):
     total = (a[...].astype(F32) + b[...].astype(F32)).astype(BF16).astype(F32)
-    block = rotate(total, cosine[...], sine_v[...]).astype(BF16)
-    for c in range(out.shape[0]):
-        out[c] = block
-
-
-def attention_kernel(
-    heads, base, own, got, cosine, sine_v, kv_own, kv_other, out, queries, pair
-):
+    out[...] = rotate(total, cosine[...], sine_v[...]).astype(BF16)
+
+
+def attention_kernel(heads, base, own, got, cosine, sine_v, *refs):
+    kv_own, kv_other, out, queries, pair = refs[:4], refs[4:8], *refs[8:]
     per_chunk = own.shape[0]
-    pair[0] = kv_own[...]
-    for s in range(4):
-        part = slice(s * 2 * HD, (s + 1) * 2 * HD)
-        pair[1, part, :] = kv_other[(s ^ 1) * 2 * HD : ((s ^ 1) + 1) * 2 * HD, :]
+    first, second, by_first, by_second = base[10], base[11], base[12], base[13]
+    for t in range(4):
+        for s in range(4):
+            pair[0, by_first * (first ^ s) + by_second * (second ^ t)] = kv_own[t][s]
+            k = by_second * (second ^ s) + by_first * (first ^ t)
+            pair[1, k ^ 4] = kv_other[t][s]
     for h in range(heads):
         cols = slice(h * HD, (h + 1) * HD)
         total = own[:, cols].astype(F32) + got[:, cols].astype(F32)
@@ -126,8 +121,8 @@
     totals = jnp.zeros((rows, 1), F32)
     mixed = jnp.zeros((rows, HD), F32)
     for s in range(4):
-        part = slice(s * 2 * HD, (s + 1) * 2 * HD)
-        keys, values = pair[core, part, :], pair[1 - core, part, :]
+        keys = pair[core, 4 * s : 4 * s + 4].reshape(4 * per_chunk, HD)
+        values = pair[1 - core, 4 * s : 4 * s + 4].reshape(4 * per_chunk, HD)
         scores = (
             lax.dot_general(query, keys, (((1,), (1,)), ((), ())), preferred_element_type=F32)
             * score_scale
@@ -155,8 +150,7 @@
         block = line[...].reshape(4 * rows, width)
         product = jnp.dot(block, weight[...], preferred_element_type=F32).astype(BF16)
         for s in range(4):
-            k = chunk_at(place, place[0] ^ s, place[1] ^ t)
-            chunks[k] = product[s * rows : (s + 1) * rows]
+            chunks[(place[0] ^ s) + 4 * (place[1] ^ t)] = product[s * rows : (s + 1) * rows]
     half = kept.shape[0]
     kept[...] = chunks[:half]
     sent[...] = chunks[half:]
@@ -202,20 +196,24 @@
     def block_start(chip, side, index):
         return (((chip ^ (index & 3)) << 1) + ((index >> 2) ^ side)) * per_row
 
-    chunk = y * X + x
-    offset = (chunk & 1) * per_chunk
+    first, second = jnp.where(core == 0, x, y), jnp.where(core == 0, y, x)
     source_chip, source_core = (zl >> 1) + 2 * core, zl & 1
-    row_start = block_start(zl, core, chunk >> 1) + offset
-    key_start = block_start(source_chip, source_core, chunk >> 1) + offset
+    by_first = jnp.where(source_core == core, 1, 4)
+    by_second = 5 - by_first
+    chunk = first + 4 * second
+    key_chunk = by_first * first + by_second * second
+    row_start = block_start(zl, core, chunk >> 1) + (chunk & 1) * per_chunk
+    key_start = block_start(source_chip, source_core, key_chunk >> 1) + (key_chunk & 1) * per_chunk
     starts = [block_start(source_chip, source_core, i) for i in range(8)]
-    base = jnp.stack([*starts, row_start, core]).astype(jnp.int32)
+    base = jnp.stack([*starts, row_start, core, first, second, by_first, by_second]).astype(
+        jnp.int32
+    )
     steps = jnp.arange(per_chunk)
     cosine, sine_v = tables((row_start + steps).astype(F32), HD)
     key_cos, key_sin = tables((key_start + steps).astype(F32), HD)
     key_cos = jnp.where(core == 0, key_cos, 1.0)
     key_sin = jnp.where(core == 0, key_sin, 0.0)
-    first, second = jnp.where(core == 0, x, y), jnp.where(core == 0, y, x)
-    place = jnp.stack([first, second, 1 + 3 * core, 4 - 3 * core]).astype(jnp.int32)
+    place = jnp.stack([first, second]).astype(jnp.int32)
 
     near = partner(tokens, "core", 1)
     (early,) = call(early_kernel, [(4, per_chunk, both)], [tokens, near, w_query, w_keyval])
@@ -236,23 +234,29 @@
     )
     got = [across_plane(halves[t], t, True) for t in (1, 2, 3)]
     own, kv = call(join_kernel, [(per_chunk, width), (per_chunk, HD)], [halves[0], *got])
-    got = partner(own, "zh", 1)
-
     moves = [(e, 2 * (e % 4) + e // 4) for e in range(8)]
     here = lax.ppermute(kv, ROW, moves)
     across = lax.ppermute(
         kv, (*ROW, "zh"), [(2 * e + h, 2 * r + 1 - h) for e, r in moves for h in range(2)]
     )
-    here, across, got = lax.optimization_barrier((here, across, got))
-    (kv_block,) = call(keys_kernel, [(Y * X, per_chunk, HD)], [here, across, key_cos, key_sin])
-    kv_own = lax.all_to_all(kv_block, PLANE, 0, 0, tiled=True).reshape(total, HD)
-    kv_other = partner(kv_own, "core", 1)
+    got = partner(own, "zh", 1)
+    (kv_block,) = call(keys_kernel, [(per_chunk, HD)], [here, across, key_cos, key_sin])
+    (kv_line,) = call(
+        stack_kernel,
+        [(4, per_chunk, HD)],
+        [kv_block] + [across_plane(kv_block, s, False) for s in (1, 2, 3)],
+    )
+    kv_own = [kv_line] + [across_plane(kv_line, t, True) for t in (1, 2, 3)]
+    kv_other = [partner(lines, "core", 1) for lines in kv_own]
     (attended,) = call(
         functools.partial(attention_kernel, heads),
         [(per_chunk, width)],
-        [base, own, got, cosine, sine_v, kv_own, kv_other],
-        [SMEM],
-        [pltpu.VMEM((heads * per_chunk, HD), BF16), pltpu.VMEM((2, total, HD), BF16)],
+        [base, own, got, cosine, sine_v, *kv_own, *kv_other],
+        [SMEM],
+        [
+            pltpu.VMEM((heads * per_chunk, HD), BF16),
+            pltpu.VMEM((2, Y * X, per_chunk, HD), BF16),
+        ],
     )
 
     (line,) = call(

time: 133 us -> 137 us (1.030)
  starting transfers between devices: 45.8 us -> 60.6 us
  blocking collectives: 11.2 us -> 0 us
    all_to_all x1 -> x0, blocking collectives: 11.2 us -> none  [shards(): lax.all_to_all(kv_block, PLANE, 0, 0, tiled=True).reshape(total, HD)]
    ppermute x12 -> x18, starting transfers between devices: 15.7 us -> 23.4 us  [across_plane(): return lax.ppermute(block, ('core', *PLANE), pairs)]
    ppermute x1, starting transfers between devices: 0.39 us -> 5.32 us  [shards(): lax.ppermute(kv, (*ROW, 'zh'), [(2 * e + h, 2 * r + 1 - h) for e, r in mo...]
    ppermute x13 -> x16, waiting for transfers between devices: 19.1 us -> 22.7 us  [partner(): return lax.ppermute(block, axis, [(i, i ^ step) for i in range(size)])]
    ppermute x1, waiting for transfers between devices: 3.48 us -> 0.77 us  [shards(): lax.ppermute(kv, (*ROW, 'zh'), [(2 * e + h, 2 * r + 1 - h) for e, r in mo...]
    ppermute x13 -> x16, starting transfers between devices: 22.3 us -> 24.4 us  [partner(): return lax.ppermute(block, axis, [(i, i ^ step) for i in range(size)])]
    ppermute x1, waiting for transfers between devices: 1.39 us -> 0.01 us  [shards(): here = lax.ppermute(kv, ROW, moves)]
    ppermute x12 -> x18, waiting for transfers between devices: 38.8 us -> 40.1 us  [across_plane(): return lax.ppermute(block, ('core', *PLANE), pairs)]
  transfers between devices with their start and end apart: 27 -> 36, of which waited for: 23 -> 24; matrix products, arithmetic and copies ran while one was open for 0% -> 0% of each run, Pallas kernels for 0% -> 0%
where the time goes in v7:
time: 137 us
  waiting for transfers between devices  63.6 us (46%)
  starting transfers between devices  60.6 us (44%)
  Pallas kernels  8.07 us (6%)
  local copies, waits for them, and re-layouts  3.13 us (2%)
    ppermute x18, waiting for transfers between devices, across_plane(): return lax.ppermute(block, ('core', *PLANE), pairs)  40.1 us
    ppermute x16, starting transfers between devices, partner(): return lax.ppermute(block, axis, [(i, i ^ step) for i in range(size)])  24.4 us
    ppermute x18, starting transfers between devices, across_plane(): return lax.ppermute(block, ('core', *PLANE), pairs)  23.4 us
    ppermute x16, waiting for transfers between devices, partner(): return lax.ppermute(block, axis, [(i, i ^ step) for i in range(size)])  22.7 us
    pallas_call x10, Pallas kernels, call(): pl.pallas_call(kernel, out_shape=[s if isinstance(s, jax.ShapeDtypeStruct...  8.07 us
    ppermute x1, starting transfers between devices, shards(): here = lax.ppermute(kv, ROW, moves)  7.47 us
    ppermute x1, starting transfers between devices, shards(): lax.ppermute(kv, (*ROW, 'zh'), [(2 * e + h, 2 * r + 1 - h) for e, r in mo...  5.32 us
    unnamed x12, local copies, waits for them, and re-layouts  3.05 us
  transfers between devices with their start and end apart: 36, of which 24 were waited for; matrix products, arithmetic and copies ran while one was open for 0% of the time, Pallas kernels for 0%

profile of v7, /device:TPU:1, one launch (start us, length us, event | category | flops | bytes accessed | tf_op | source)
XLA Modules:
  0.0 136.8 jit_solution(10739993483336614930)
XLA Ops:
  0.0 3.2 %collective-permute-start.3 = (bf16[128,512]{1,0:T(8,128)(2,1)}, bf16[128,512]{1,0:T(8,128)(2,1)S(1)}, u32[]{:S(2)}, u32[]{:S(2)}) collective-permute-start(bf16[128,512]{1,0:T(8,128)(2,1)} %refs_0_.1), channel_id=1, source_target_pairs={{0,32},{32,0},{1,33},{33,1},{2,34},{34,2},{3,35},{35,3},{4,36},{36... | collective-permute-start | bytes 393224 | tf_op jit(solution)/shard_map/ppermute | solution.py:37
  3.2 2.9 %collective-permute-start.1 = (bf16[128,512]{1,0:T(8,128)(2,1)}, bf16[128,512]{1,0:T(8,128)(2,1)S(1)}, u32[]{:S(2)}, u32[]{:S(2)}) collective-permute-start(bf16[128,512]{1,0:T(8,128)(2,1)} %refs_0_.1), channel_id=1, source_target_pairs={{0,128},{64,192},{128,0},{192,64},{1,129},{65,193},{129,1},{193,65... | collective-permute-start | bytes 393224 | tf_op jit(solution)/shard_map/ppermute | solution.py:37
  11.1 4.4 %collective-permute-done.2.refs_2_ = bf16[128,512]{1,0:T(8,128)(2,1)S(1)} collective-permute-done((bf16[128,512]{1,0:T(8,128)(2,1)}, bf16[128,512]{1,0:T(8,128)(2,1)S(1)}, u32[]{:S(2)}, u32[]{:S(2)}) %collective-permute-start.2) | collective-permute-done | bytes 131104 | tf_op jit(solution)/shard_map/ppermute | solution.py:37
  18.4 3.0 %shard_map.47 = (bf16[4,64,1152]{2,1,0:T(8,128)(2,1)S(1)}, bf16[4,64,1152]{2,1,0:T(8,128)(2,1)}, bf16[4,64,1152]{2,1,0:T(8,128)(2,1)}, bf16[4,64,1152]{2,1,0:T(8,128)(2,1)}) custom-call(s32[2]{0:T(128)S(1)} %pad_add_fusion.place, bf16[128,512]{1,0:T(8,128)(2,1)S(1)} %collective-permute-done.refs_0_, bf16[128,512]{1,0:T(8,128)(2,1)S(1)} %collective-permute-done.1.refs_1_, ...), custom_call_target="tpu_custom_call" | custom-call | tf_op jit(solution)/shard_map/pallas_call | solution.py:168
  22.7 2.6 %collective-permute-start.8 = (bf16[4,64,1152]{2,1,0:T(8,128)(2,1)}, bf16[4,64,1152]{2,1,0:T(8,128)(2,1)S(1)}, u32[]{:S(2)}, u32[]{:S(2)}) collective-permute-start(bf16[4,64,1152]{2,1,0:T(8,128)(2,1)} %get-tuple-element.31), channel_id=1, source_target_pairs={{0,2},{1,3},{2,0},{3,1},{4,6},{5,7},{6,4},{7,5},{8,10},{9,11},{10,... | collective-permute-start | bytes 1769480 | tf_op jit(solution)/shard_map/ppermute | solution.py:48
  25.3 5.3 %collective-permute-done.7.b = bf16[4,64,1152]{2,1,0:T(8,128)(2,1)S(1)} collective-permute-done((bf16[4,64,1152]{2,1,0:T(8,128)(2,1)}, bf16[4,64,1152]{2,1,0:T(8,128)(2,1)S(1)}, u32[]{:S(2)}, u32[]{:S(2)}) %collective-permute-start.7) | collective-permute-done | bytes 589856 | tf_op jit(solution)/shard_map/ppermute | solution.py:48
  30.6 8.8 %collective-permute-done.8.c = bf16[4,64,1152]{2,1,0:T(8,128)(2,1)S(1)} collective-permute-done((bf16[4,64,1152]{2,1,0:T(8,128)(2,1)}, bf16[4,64,1152]{2,1,0:T(8,128)(2,1)S(1)}, u32[]{:S(2)}, u32[]{:S(2)}) %collective-permute-start.8) | collective-permute-done | bytes 589856 | tf_op jit(solution)/shard_map/ppermute | solution.py:48
  39.4 2.6 %collective-permute-done.9.d = bf16[4,64,1152]{2,1,0:T(8,128)(2,1)S(1)} collective-permute-done((bf16[4,64,1152]{2,1,0:T(8,128)(2,1)}, bf16[4,64,1152]{2,1,0:T(8,128)(2,1)S(1)}, u32[]{:S(2)}, u32[]{:S(2)}) %collective-permute-start.9) | collective-permute-done | bytes 589856 | tf_op jit(solution)/shard_map/ppermute | solution.py:48
  43.9 2.4 %collective-permute-start.11 = (bf16[64,1152]{1,0:T(8,128)(2,1)S(1)}, bf16[64,1152]{1,0:T(8,128)(2,1)S(1)}, u32[]{:S(2)}, u32[]{:S(2)}) collective-permute-start(bf16[64,1152]{1,0:T(8,128)(2,1)S(1)} %get-tuple-element.35), channel_id=1, source_target_pairs={{0,8},{1,9},{2,10},{3,11},{4,12},{5,13},{6,14},{7,15},{8,0},{9,1},... | collective-permute-start | bytes 442376 | tf_op jit(solution)/shard_map/ppermute | solution.py:48
  47.2 3.3 %collective-permute-done.11.c = bf16[64,1152]{1,0:T(8,128)(2,1)S(1)} collective-permute-done((bf16[64,1152]{1,0:T(8,128)(2,1)S(1)}, bf16[64,1152]{1,0:T(8,128)(2,1)S(1)}, u32[]{:S(2)}, u32[]{:S(2)}) %collective-permute-start.11) | collective-permute-done | bytes 147488 | tf_op jit(solution)/shard_map/ppermute | solution.py:48
  52.4 7.5 %collective-permute-start.14 = (bf16[64,128]{1,0:T(8,128)(2,1)S(1)}, bf16[64,128]{1,0:T(8,128)(2,1)S(1)}, u32[]{:S(2)}, u32[]{:S(2)}) collective-permute-start(bf16[64,128]{1,0:T(8,128)(2,1)S(1)} %get-tuple-element.38), channel_id=1, source_target_pairs={{0,0},{32,64},{64,128},{96,192},{128,32},{160,96},{192,160},{224,2... | collective-permute-start | bytes 49160 | tf_op jit(solution)/shard_map/ppermute | solution.py:238
  59.9 5.3 %collective-permute-start.15 = (bf16[64,128]{1,0:T(8,128)(2,1)S(1)}, bf16[64,128]{1,0:T(8,128)(2,1)S(1)}, u32[]{:S(2)}, u32[]{:S(2)}) collective-permute-start(bf16[64,128]{1,0:T(8,128)(2,1)S(1)} %get-tuple-element.38), channel_id=1, source_target_pairs={{0,16},{16,0},{32,80},{48,64},{64,144},{80,128},{96,208},{112,192}... | collective-permute-start | bytes 49160 | tf_op jit(solution)/shard_map/ppermute | solution.py:239
  73.4 2.5 %collective-permute-start.21 = (bf16[4,64,128]{2,1,0:T(8,128)(2,1)S(1)}, bf16[4,64,128]{2,1,0:T(8,128)(2,1)S(1)}, u32[]{:S(2)}, u32[]{:S(2)}) collective-permute-start(bf16[4,64,128]{2,1,0:T(8,128)(2,1)S(1)} %shard_map.51.refs_0_), channel_id=1, source_target_pairs={{0,12},{1,13},{2,14},{3,15},{4,8},{5,9},{6,10},{7,11},{8,4},{9,5},... | collective-permute-start | bytes 196616 | tf_op jit(solution)/shard_map/ppermute | solution.py:48
  75.9 4.6 %collective-permute-start.13 = (bf16[64,1024]{1,0:T(8,128)(2,1)S(1)}, bf16[64,1024]{1,0:T(8,128)(2,1)S(1)}, u32[]{:S(2)}, u32[]{:S(2)}) collective-permute-start(bf16[64,1024]{1,0:T(8,128)(2,1)S(1)} %get-tuple-element.37.own), channel_id=1, source_target_pairs={{0,16},{16,0},{1,17},{17,1},{2,18},{18,2},{3,19},{19,3},{4,20},{20... | collective-permute-start | bytes 393224 | tf_op jit(solution)/shard_map/ppermute | solution.py:37
  82.5 4.1 %collective-permute-done.13.got = bf16[64,1024]{1,0:T(8,128)(2,1)S(1)} collective-permute-done((bf16[64,1024]{1,0:T(8,128)(2,1)S(1)}, bf16[64,1024]{1,0:T(8,128)(2,1)S(1)}, u32[]{:S(2)}, u32[]{:S(2)}) %collective-permute-start.13) | collective-permute-done | bytes 131104 | tf_op jit(solution)/shard_map/ppermute | solution.py:37
  88.3 2.1 %collective-permute-start.27 = (bf16[64,1024]{1,0:T(8,128)(2,1)S(1)}, bf16[64,1024]{1,0:T(8,128)(2,1)S(1)}, u32[]{:S(2)}, u32[]{:S(2)}) collective-permute-start(bf16[64,1024]{1,0:T(8,128)(2,1)S(1)} %shard_map.52.refs_0_), channel_id=1, source_target_pairs={{0,2},{1,3},{2,0},{3,1},{4,6},{5,7},{6,4},{7,5},{8,10},{9,11},{10,... | collective-permute-start | bytes 393224 | tf_op jit(solution)/shard_map/ppermute | solution.py:48
  96.2 3.6 %collective-permute-start.31 = (bf16[4,64,1024]{2,1,0:T(8,128)(2,1)S(1)}, bf16[4,64,1024]{2,1,0:T(8,128)(2,1)S(1)}, u32[]{:S(2)}, u32[]{:S(2)}) collective-permute-start(bf16[4,64,1024]{2,1,0:T(8,128)(2,1)S(1)} %shard_map.53.refs_0_), channel_id=1, source_target_pairs={{0,12},{1,13},{2,14},{3,15},{4,8},{5,9},{6,10},{7,11},{8,4},{9,5},... | collective-permute-start | bytes 1572872 | tf_op jit(solution)/shard_map/ppermute | solution.py:48
  99.9 4.5 %collective-permute-done.29.refs_1_ = bf16[4,64,1024]{2,1,0:T(8,128)(2,1)S(1)} collective-permute-done((bf16[4,64,1024]{2,1,0:T(8,128)(2,1)S(1)}, bf16[4,64,1024]{2,1,0:T(8,128)(2,1)S(1)}, u32[]{:S(2)}, u32[]{:S(2)}) %collective-permute-start.29) | collective-permute-done | bytes 524320 | tf_op jit(solution)/shard_map/ppermute | solution.py:48
  104.4 4.3 %collective-permute-done.30.refs_2_ = bf16[4,64,1024]{2,1,0:T(8,128)(2,1)S(1)} collective-permute-done((bf16[4,64,1024]{2,1,0:T(8,128)(2,1)S(1)}, bf16[4,64,1024]{2,1,0:T(8,128)(2,1)S(1)}, u32[]{:S(2)}, u32[]{:S(2)}) %collective-permute-start.30) | collective-permute-done | bytes 524320 | tf_op jit(solution)/shard_map/ppermute | solution.py:48
  108.7 3.7 %collective-permute-done.31.refs_3_ = bf16[4,64,1024]{2,1,0:T(8,128)(2,1)S(1)} collective-permute-done((bf16[4,64,1024]{2,1,0:T(8,128)(2,1)S(1)}, bf16[4,64,1024]{2,1,0:T(8,128)(2,1)S(1)}, u32[]{:S(2)}, u32[]{:S(2)}) %collective-permute-start.31) | collective-permute-done | bytes 524320 | tf_op jit(solution)/shard_map/ppermute | solution.py:48
  114.2 4.5 %collective-permute-start.32 = (bf16[512,512]{1,0:T(8,128)(2,1)S(1)}, bf16[512,512]{1,0:T(8,128)(2,1)S(1)}, u32[]{:S(2)}, u32[]{:S(2)}) collective-permute-start(bf16[512,512]{1,0:T(8,128)(2,1)S(1)} %bitcast.17), channel_id=1, source_target_pairs={{0,32},{32,0},{1,33},{33,1},{2,34},{34,2},{3,35},{35,3},{4,36},{36... | collective-permute-start | bytes 1572872 | tf_op jit(solution)/shard_map/ppermute | solution.py:37
  120.4 2.9 %collective-permute-start.33 = (bf16[128,512]{1,0:T(8,128)(2,1)S(1)}, bf16[128,512]{1,0:T(8,128)(2,1)S(1)}, u32[]{:S(2)}, u32[]{:S(2)}) collective-permute-start(bf16[128,512]{1,0:T(8,128)(2,1)S(1)} %get-tuple-element.42), channel_id=1, source_target_pairs={{0,192},{64,128},{128,64},{192,0},{1,193},{65,129},{129,65},{193,1... | collective-permute-start | bytes 393224 | tf_op jit(solution)/shard_map/ppermute | solution.py:37
  123.2 2.1 %collective-permute-start.34 = (bf16[128,512]{1,0:T(8,128)(2,1)S(1)}, bf16[128,512]{1,0:T(8,128)(2,1)S(1)}, u32[]{:S(2)}, u32[]{:S(2)}) collective-permute-start(bf16[128,512]{1,0:T(8,128)(2,1)S(1)} %get-tuple-element.43), channel_id=1, source_target_pairs={{0,128},{64,192},{128,0},{192,64},{1,129},{65,193},{129,1},{193,65... | collective-permute-start | bytes 393224 | tf_op jit(solution)/shard_map/ppermute | solution.py:37
  127.0 9.2 %collective-permute-done.34 = bf16[128,512]{1,0:T(8,128)(2,1)S(1)} collective-permute-done((bf16[128,512]{1,0:T(8,128)(2,1)S(1)}, bf16[128,512]{1,0:T(8,128)(2,1)S(1)}, u32[]{:S(2)}, u32[]{:S(2)}) %collective-permute-start.34) | collective-permute-done | bytes 131104 | tf_op jit(solution)/shard_map/ppermute | solution.py:37
  (79 shorter events, 37.2 us)
Async XLA Ops:
  0.0 6.8 %collective-permute-start.3 = (bf16[128,512]{1,0:T(8,128)(2,1)}, bf16[128,512]{1,0:T(8,128)(2,1)S(1)}, u32[]{:S(2)}, u32[]{:S(2)}) collective-permute-start(bf16[128,512]{1,0:T(8,128)(2,1)} %refs_0_.1), channel_id=1, source_target_pairs={{0,32},{32,0},{1,33},{33,1},{2,34},{34,2},{3,35},{35,3},{4,36},{36... | collective-permute-start | bytes 393224 | tf_op jit(solution)/shard_map/ppermute | solution.py:37
  3.2 7.8 %collective-permute-start = (bf16[128,512]{1,0:T(8,128)(2,1)}, bf16[128,512]{1,0:T(8,128)(2,1)S(1)}, u32[]{:S(2)}, u32[]{:S(2)}) collective-permute-start(bf16[128,512]{1,0:T(8,128)(2,1)} %refs_0_.1), channel_id=1, source_target_pairs={{0,64},{64,0},{128,192},{192,128},{1,65},{65,1},{129,193},{193,129... | collective-permute-start | bytes 393224 | tf_op jit(solution)/shard_map/ppermute | solution.py:37
  3.2 7.8 %collective-permute-start.1 = (bf16[128,512]{1,0:T(8,128)(2,1)}, bf16[128,512]{1,0:T(8,128)(2,1)S(1)}, u32[]{:S(2)}, u32[]{:S(2)}) collective-permute-start(bf16[128,512]{1,0:T(8,128)(2,1)} %refs_0_.1), channel_id=1, source_target_pairs={{0,128},{64,192},{128,0},{192,64},{1,129},{65,193},{129,1},{193,65... | collective-permute-start | bytes 393224 | tf_op jit(solution)/shard_map/ppermute | solution.py:37
  6.1 9.3 %collective-permute-start.2 = (bf16[128,512]{1,0:T(8,128)(2,1)}, bf16[128,512]{1,0:T(8,128)(2,1)S(1)}, u32[]{:S(2)}, u32[]{:S(2)}) collective-permute-start(bf16[128,512]{1,0:T(8,128)(2,1)} %refs_0_.1), channel_id=1, source_target_pairs={{0,192},{64,128},{128,64},{192,0},{1,193},{65,129},{129,65},{193,1... | collective-permute-start | bytes 393224 | tf_op jit(solution)/shard_map/ppermute | solution.py:37
  21.4 9.2 %collective-permute-start.7 = (bf16[4,64,1152]{2,1,0:T(8,128)(2,1)}, bf16[4,64,1152]{2,1,0:T(8,128)(2,1)S(1)}, u32[]{:S(2)}, u32[]{:S(2)}) collective-permute-start(bf16[4,64,1152]{2,1,0:T(8,128)(2,1)} %get-tuple-element.30), channel_id=1, source_target_pairs={{0,1},{1,0},{2,3},{3,2},{4,5},{5,4},{6,7},{7,6},{8,9},{9,8},{10,11... | collective-permute-start | bytes 1769480 | tf_op jit(solution)/shard_map/ppermute | solution.py:48
  22.7 16.8 %collective-permute-start.8 = (bf16[4,64,1152]{2,1,0:T(8,128)(2,1)}, bf16[4,64,1152]{2,1,0:T(8,128)(2,1)S(1)}, u32[]{:S(2)}, u32[]{:S(2)}) collective-permute-start(bf16[4,64,1152]{2,1,0:T(8,128)(2,1)} %get-tuple-element.31), channel_id=1, source_target_pairs={{0,2},{1,3},{2,0},{3,1},{4,6},{5,7},{6,4},{7,5},{8,10},{9,11},{10,... | collective-permute-start | bytes 1769480 | tf_op jit(solution)/shard_map/ppermute | solution.py:48
  25.3 16.8 %collective-permute-start.9 = (bf16[4,64,1152]{2,1,0:T(8,128)(2,1)}, bf16[4,64,1152]{2,1,0:T(8,128)(2,1)S(1)}, u32[]{:S(2)}, u32[]{:S(2)}) collective-permute-start(bf16[4,64,1152]{2,1,0:T(8,128)(2,1)} %get-tuple-element.32), channel_id=1, source_target_pairs={{0,3},{1,2},{2,1},{3,0},{4,7},{5,6},{6,5},{7,4},{8,11},{9,10},{10,... | collective-permute-start | bytes 1769480 | tf_op jit(solution)/shard_map/ppermute | solution.py:48
  43.9 6.6 %collective-permute-start.11 = (bf16[64,1152]{1,0:T(8,128)(2,1)S(1)}, bf16[64,1152]{1,0:T(8,128)(2,1)S(1)}, u32[]{:S(2)}, u32[]{:S(2)}) collective-permute-start(bf16[64,1152]{1,0:T(8,128)(2,1)S(1)} %get-tuple-element.35), channel_id=1, source_target_pairs={{0,8},{1,9},{2,10},{3,11},{4,12},{5,13},{6,14},{7,15},{8,0},{9,1},... | collective-permute-start | bytes 442376 | tf_op jit(solution)/shard_map/ppermute | solution.py:48
  46.3 6.0 %collective-permute-start.12 = (bf16[64,1152]{1,0:T(8,128)(2,1)S(1)}, bf16[64,1152]{1,0:T(8,128)(2,1)S(1)}, u32[]{:S(2)}, u32[]{:S(2)}) collective-permute-start(bf16[64,1152]{1,0:T(8,128)(2,1)S(1)} %get-tuple-element.36), channel_id=1, source_target_pairs={{0,12},{1,13},{2,14},{3,15},{4,8},{5,9},{6,10},{7,11},{8,4},{9,5},... | collective-permute-start | bytes 442376 | tf_op jit(solution)/shard_map/ppermute | solution.py:48
  52.4 12.9 %collective-permute-start.14 = (bf16[64,128]{1,0:T(8,128)(2,1)S(1)}, bf16[64,128]{1,0:T(8,128)(2,1)S(1)}, u32[]{:S(2)}, u32[]{:S(2)}) collective-permute-start(bf16[64,128]{1,0:T(8,128)(2,1)S(1)} %get-tuple-element.38), channel_id=1, source_target_pairs={{0,0},{32,64},{64,128},{96,192},{128,32},{160,96},{192,160},{224,2... | collective-permute-start | bytes 49160 | tf_op jit(solution)/shard_map/ppermute | solution.py:238
  59.9 6.2 %collective-permute-start.15 = (bf16[64,128]{1,0:T(8,128)(2,1)S(1)}, bf16[64,128]{1,0:T(8,128)(2,1)S(1)}, u32[]{:S(2)}, u32[]{:S(2)}) collective-permute-start(bf16[64,128]{1,0:T(8,128)(2,1)S(1)} %get-tuple-element.38), channel_id=1, source_target_pairs={{0,16},{16,0},{32,80},{48,64},{64,144},{80,128},{96,208},{112,192}... | collective-permute-start | bytes 49160 | tf_op jit(solution)/shard_map/ppermute | solution.py:239
  72.0 9.6 %collective-permute-start.19 = (bf16[4,64,128]{2,1,0:T(8,128)(2,1)S(1)}, bf16[4,64,128]{2,1,0:T(8,128)(2,1)S(1)}, u32[]{:S(2)}, u32[]{:S(2)}) collective-permute-start(bf16[4,64,128]{2,1,0:T(8,128)(2,1)S(1)} %shard_map.51.refs_0_), channel_id=1, source_target_pairs={{0,4},{1,5},{2,6},{3,7},{4,0},{5,1},{6,2},{7,3},{8,12},{9,13},{10,... | collective-permute-start | bytes 196616 | tf_op jit(solution)/shard_map/ppermute | solution.py:48
  72.0 9.7 %collective-permute-start.20 = (bf16[4,64,128]{2,1,0:T(8,128)(2,1)S(1)}, bf16[4,64,128]{2,1,0:T(8,128)(2,1)S(1)}, u32[]{:S(2)}, u32[]{:S(2)}) collective-permute-start(bf16[4,64,128]{2,1,0:T(8,128)(2,1)S(1)} %shard_map.51.refs_0_), channel_id=1, source_target_pairs={{0,8},{1,9},{2,10},{3,11},{4,12},{5,13},{6,14},{7,15},{8,0},{9,1},... | collective-permute-start | bytes 196616 | tf_op jit(solution)/shard_map/ppermute | solution.py:48
  73.4 8.7 %collective-permute-start.21 = (bf16[4,64,128]{2,1,0:T(8,128)(2,1)S(1)}, bf16[4,64,128]{2,1,0:T(8,128)(2,1)S(1)}, u32[]{:S(2)}, u32[]{:S(2)}) collective-permute-start(bf16[4,64,128]{2,1,0:T(8,128)(2,1)S(1)} %shard_map.51.refs_0_), channel_id=1, source_target_pairs={{0,12},{1,13},{2,14},{3,15},{4,8},{5,9},{6,10},{7,11},{8,4},{9,5},... | collective-permute-start | bytes 196616 | tf_op jit(solution)/shard_map/ppermute | solution.py:48
  75.9 10.7 %collective-permute-start.13 = (bf16[64,1024]{1,0:T(8,128)(2,1)S(1)}, bf16[64,1024]{1,0:T(8,128)(2,1)S(1)}, u32[]{:S(2)}, u32[]{:S(2)}) collective-permute-start(bf16[64,1024]{1,0:T(8,128)(2,1)S(1)} %get-tuple-element.37.own), channel_id=1, source_target_pairs={{0,16},{16,0},{1,17},{17,1},{2,18},{18,2},{3,19},{19,3},{4,20},{20... | collective-permute-start | bytes 393224 | tf_op jit(solution)/shard_map/ppermute | solution.py:37
  88.3 6.2 %collective-permute-start.27 = (bf16[64,1024]{1,0:T(8,128)(2,1)S(1)}, bf16[64,1024]{1,0:T(8,128)(2,1)S(1)}, u32[]{:S(2)}, u32[]{:S(2)}) collective-permute-start(bf16[64,1024]{1,0:T(8,128)(2,1)S(1)} %shard_map.52.refs_0_), channel_id=1, source_target_pairs={{0,2},{1,3},{2,0},{3,1},{4,6},{5,7},{6,4},{7,5},{8,10},{9,11},{10,... | collective-permute-start | bytes 393224 | tf_op jit(solution)/shard_map/ppermute | solution.py:48
  90.4 5.5 %collective-permute-start.28 = (bf16[64,1024]{1,0:T(8,128)(2,1)S(1)}, bf16[64,1024]{1,0:T(8,128)(2,1)S(1)}, u32[]{:S(2)}, u32[]{:S(2)}) collective-permute-start(bf16[64,1024]{1,0:T(8,128)(2,1)S(1)} %shard_map.52.refs_0_), channel_id=1, source_target_pairs={{0,3},{1,2},{2,1},{3,0},{4,7},{5,6},{6,5},{7,4},{8,11},{9,10},{10,... | collective-permute-start | bytes 393224 | tf_op jit(solution)/shard_map/ppermute | solution.py:48
  95.9 8.4 %collective-permute-start.29 = (bf16[4,64,1024]{2,1,0:T(8,128)(2,1)S(1)}, bf16[4,64,1024]{2,1,0:T(8,128)(2,1)S(1)}, u32[]{:S(2)}, u32[]{:S(2)}) collective-permute-start(bf16[4,64,1024]{2,1,0:T(8,128)(2,1)S(1)} %shard_map.53.refs_0_), channel_id=1, source_target_pairs={{0,4},{1,5},{2,6},{3,7},{4,0},{5,1},{6,2},{7,3},{8,12},{9,13},{10,... | collective-permute-start | bytes 1572872 | tf_op jit(solution)/shard_map/ppermute | solution.py:48
  96.0 12.6 %collective-permute-start.30 = (bf16[4,64,1024]{2,1,0:T(8,128)(2,1)S(1)}, bf16[4,64,1024]{2,1,0:T(8,128)(2,1)S(1)}, u32[]{:S(2)}, u32[]{:S(2)}) collective-permute-start(bf16[4,64,1024]{2,1,0:T(8,128)(2,1)S(1)} %shard_map.53.refs_0_), channel_id=1, source_target_pairs={{0,8},{1,9},{2,10},{3,11},{4,12},{5,13},{6,14},{7,15},{8,0},{9,1},... | collective-permute-start | bytes 1572872 | tf_op jit(solution)/shard_map/ppermute | solution.py:48
  96.2 16.1 %collective-permute-start.31 = (bf16[4,64,1024]{2,1,0:T(8,128)(2,1)S(1)}, bf16[4,64,1024]{2,1,0:T(8,128)(2,1)S(1)}, u32[]{:S(2)}, u32[]{:S(2)}) collective-permute-start(bf16[4,64,1024]{2,1,0:T(8,128)(2,1)S(1)} %shard_map.53.refs_0_), channel_id=1, source_target_pairs={{0,12},{1,13},{2,14},{3,15},{4,8},{5,9},{6,10},{7,11},{8,4},{9,5},... | collective-permute-start | bytes 1572872 | tf_op jit(solution)/shard_map/ppermute | solution.py:48
  114.2 6.0 %collective-permute-start.32 = (bf16[512,512]{1,0:T(8,128)(2,1)S(1)}, bf16[512,512]{1,0:T(8,128)(2,1)S(1)}, u32[]{:S(2)}, u32[]{:S(2)}) collective-permute-start(bf16[512,512]{1,0:T(8,128)(2,1)S(1)} %bitcast.17), channel_id=1, source_target_pairs={{0,32},{32,0},{1,33},{33,1},{2,34},{34,2},{3,35},{35,3},{4,36},{36... | collective-permute-start | bytes 1572872 | tf_op jit(solution)/shard_map/ppermute | solution.py:37
  120.4 6.6 %collective-permute-start.33 = (bf16[128,512]{1,0:T(8,128)(2,1)S(1)}, bf16[128,512]{1,0:T(8,128)(2,1)S(1)}, u32[]{:S(2)}, u32[]{:S(2)}) collective-permute-start(bf16[128,512]{1,0:T(8,128)(2,1)S(1)} %get-tuple-element.42), channel_id=1, source_target_pairs={{0,192},{64,128},{128,64},{192,0},{1,193},{65,129},{129,65},{193,1... | collective-permute-start | bytes 393224 | tf_op jit(solution)/shard_map/ppermute | solution.py:37
  123.2 12.9 %collective-permute-start.34 = (bf16[128,512]{1,0:T(8,128)(2,1)S(1)}, bf16[128,512]{1,0:T(8,128)(2,1)S(1)}, u32[]{:S(2)}, u32[]{:S(2)}) collective-permute-start(bf16[128,512]{1,0:T(8,128)(2,1)S(1)} %get-tuple-element.43), channel_id=1, source_target_pairs={{0,128},{64,192},{128,0},{192,64},{1,129},{65,193},{129,1},{193,65... | collective-permute-start | bytes 393224 | tf_op jit(solution)/shard_map/ppermute | solution.py:37
  125.3 10.8 %collective-permute-start.35 = (bf16[128,512]{1,0:T(8,128)(2,1)S(1)}, bf16[128,512]{1,0:T(8,128)(2,1)S(1)}, u32[]{:S(2)}, u32[]{:S(2)}) collective-permute-start(bf16[128,512]{1,0:T(8,128)(2,1)S(1)} %get-tuple-element.44), channel_id=1, source_target_pairs={{0,64},{64,0},{128,192},{192,128},{1,65},{65,1},{129,193},{193,129... | collective-permute-start | bytes 393224 | tf_op jit(solution)/shard_map/ppermute | solution.py:37
  (18 other events, 92.2 us)

commit v8 on v6

--- a/solution.py
+++ b/solution.py
@@ -67,15 +67,26 @@
 
 def late_kernel(place, *refs):
     blocks, w_query, w_kv, early = refs[:6], *refs[6:9]
-    outs, chunks = refs[9:13], refs[13]
+    outs, late = refs[9:13], refs[13]
+    in_y = place[2] == 4
+
+    def put(k, source, row):
+        first = jnp.where(in_y, k >> 2, k & 3)
+        second = jnp.where(in_y, k & 3, k >> 2)
+        for s, out in enumerate(outs):
+
+            @pl.when((first ^ place[0]) == s)
+            def _():
+                out[second] = source[row]
+
     for side in range(2):
-        chunks[8 * side] = early[2 * side]
-        chunks[8 * side + 1] = early[2 * side + 1]
+        for b in range(2):
+            put(8 * side + b, early, 2 * side + b)
         for i in range(3):
-            project(blocks[3 * side + i], w_query, w_kv, chunks, 8 * side + 2 * i + 2)
-    for s in range(4):
-        for j in range(4):
-            outs[s][j] = chunks[chunk_at(place, place[0] ^ s, j)]
+            row = 6 * side + 2 * i
+            project(blocks[3 * side + i], w_query, w_kv, late, row)
+            for b in range(2):
+                put(8 * side + 2 * i + 2 + b, late, row + b)
 
 
 def chunk_at(place, first, second):
@@ -148,15 +159,20 @@
         refs[4][s] = ref[...]
 
 
+def line_kernel(line, weight, out):
+    rows, width = line.shape[1:]
+    block = line[...].reshape(4 * rows, width)
+    product = jnp.dot(block, weight[...], preferred_element_type=F32).astype(BF16)
+    for s in range(4):
+        out[s] = product[s * rows : (s + 1) * rows]
+
+
 def output_kernel(place, *refs):
-    lines, weight, kept, sent, chunks = refs[:4], *refs[4:]
-    rows, width = lines[0].shape[1:]
-    for t, line in enumerate(lines):
-        block = line[...].reshape(4 * rows, width)
-        product = jnp.dot(block, weight[...], preferred_element_type=F32).astype(BF16)
+    early, line, weight, kept, sent, last, chunks = refs[:3], *refs[3:]
+    line_kernel(line, weight, last)
+    for t, part in enumerate([*early, last]):
         for s in range(4):
-            k = chunk_at(place, place[0] ^ s, place[1] ^ t)
-            chunks[k] = product[s * rows : (s + 1) * rows]
+            chunks[chunk_at(place, place[0] ^ s, place[1] ^ t)] = part[s]
     half = kept.shape[0]
     kept[...] = chunks[:half]
     sent[...] = chunks[half:]
@@ -225,7 +241,7 @@
         [(4, per_chunk, both)] * 4,
         [place, *far, *[partner(block, "core", 1) for block in far], w_query, w_keyval, early],
         [SMEM],
-        [pltpu.VMEM((Y * X, per_chunk, both), BF16)],
+        [pltpu.VMEM((12, per_chunk, both), BF16)],
     )
     got = [across_plane(parts[s], s, False) for s in (1, 2, 3)]
     halves = call(
@@ -260,13 +276,21 @@
         [(4, per_chunk, width)],
         [attended] + [across_plane(attended, s, False) for s in (1, 2, 3)],
     )
-    gathered = [line] + [across_plane(line, t, True) for t in (1, 2, 3)]
+    gathered = [across_plane(line, t, True) for t in (1, 2, 3)]
+    early = []
+    for t in range(3):
+        (done,) = call(line_kernel, [(4, per_chunk, features)], [line, w_output])
+        line, done = lax.optimization_barrier((gathered[t], done))
+        early.append(done)
     kept, sent = call(
         output_kernel,
         [(Y * X // 2, per_chunk, features)] * 2,
-        [place, *gathered, w_output],
+        [place, *early, line, w_output],
         [SMEM],
-        [pltpu.VMEM((Y * X, per_chunk, features), BF16)],
+        [
+            pltpu.VMEM((4, per_chunk, features), BF16),
+            pltpu.VMEM((Y * X, per_chunk, features), BF16),
+        ],
     )
     kept, sent = kept.reshape(half, features), sent.reshape(half, features)
     chip = call(chip_kernel, [(per_row, features)] * 4, [kept, partner(sent, "core", 1)])

time: 133 us -> 133 us (level)
  Pallas kernels: 8.08 us -> 10 us
  waiting for transfers between devices: 62.8 us -> 61.4 us
    pallas_call x9 -> x12, Pallas kernels: 8.08 us -> 10 us  [call(): pl.pallas_call(kernel, out_shape=[s if isinstance(s, jax.ShapeDtypeStruct...]
  transfers between devices with their start and end apart: 27 -> 27, of which waited for: 23 -> 23; matrix products, arithmetic and copies ran while one was open for 0% -> 0% of each run, Pallas kernels for 0% -> 1%
where the time goes in v8:
time: 133 us
  waiting for transfers between devices  61.4 us (46%)
  starting transfers between devices  45.5 us (34%)
  blocking collectives  11.7 us (9%)
  Pallas kernels  10 us (8%)
  local copies, waits for them, and re-layouts  3.13 us (2%)
    ppermute x12, waiting for transfers between devices, across_plane(): return lax.ppermute(block, ('core', *PLANE), pairs)  37.4 us
    ppermute x13, starting transfers between devices, partner(): return lax.ppermute(block, axis, [(i, i ^ step) for i in range(size)])  21.8 us
    ppermute x13, waiting for transfers between devices, partner(): return lax.ppermute(block, axis, [(i, i ^ step) for i in range(size)])  19.1 us
    ppermute x12, starting transfers between devices, across_plane(): return lax.ppermute(block, ('core', *PLANE), pairs)  15.7 us
    all_to_all x1, blocking collectives, shards(): lax.all_to_all(kv_block, PLANE, 0, 0, tiled=True).reshape(total, HD)  11.7 us
    pallas_call x12, Pallas kernels, call(): pl.pallas_call(kernel, out_shape=[s if isinstance(s, jax.ShapeDtypeStruct...  10 us
    ppermute x1, starting transfers between devices, shards(): here = lax.ppermute(kv, ROW, moves)  7.42 us
    ppermute x1, waiting for transfers between devices, shards(): lax.ppermute(kv, (*ROW, 'zh'), [(2 * e + h, 2 * r + 1 - h) for e, r in mo...  3.66 us
  transfers between devices with their start and end apart: 27, of which 23 were waited for; matrix products, arithmetic and copies ran while one was open for 0% of the time, Pallas kernels for 1%

profile of v8, /device:TPU:1, one launch (start us, length us, event | category | flops | bytes accessed | tf_op | source)
XLA Modules:
  0.0 133.3 jit_solution(3987461029486199661)
XLA Ops:
  0.0 3.2 %collective-permute-start.3 = (bf16[128,512]{1,0:T(8,128)(2,1)}, bf16[128,512]{1,0:T(8,128)(2,1)S(1)}, u32[]{:S(2)}, u32[]{:S(2)}) collective-permute-start(bf16[128,512]{1,0:T(8,128)(2,1)} %refs_0_.1), channel_id=1, source_target_pairs={{0,32},{32,0},{1,33},{33,1},{2,34},{34,2},{3,35},{35,3},{4,36},{36... | collective-permute-start | bytes 393224 | tf_op jit(solution)/shard_map/ppermute | solution.py:37
  3.2 2.9 %collective-permute-start.1 = (bf16[128,512]{1,0:T(8,128)(2,1)}, bf16[128,512]{1,0:T(8,128)(2,1)S(1)}, u32[]{:S(2)}, u32[]{:S(2)}) collective-permute-start(bf16[128,512]{1,0:T(8,128)(2,1)} %refs_0_.1), channel_id=1, source_target_pairs={{0,128},{64,192},{128,0},{192,64},{1,129},{65,193},{129,1},{193,65... | collective-permute-start | bytes 393224 | tf_op jit(solution)/shard_map/ppermute | solution.py:37
  11.1 4.4 %collective-permute-done.2.refs_2_ = bf16[128,512]{1,0:T(8,128)(2,1)S(1)} collective-permute-done((bf16[128,512]{1,0:T(8,128)(2,1)}, bf16[128,512]{1,0:T(8,128)(2,1)S(1)}, u32[]{:S(2)}, u32[]{:S(2)}) %collective-permute-start.2) | collective-permute-done | bytes 131104 | tf_op jit(solution)/shard_map/ppermute | solution.py:37
  18.4 4.5 %shard_map.47 = (bf16[4,64,1152]{2,1,0:T(8,128)(2,1)S(1)}, bf16[4,64,1152]{2,1,0:T(8,128)(2,1)}, bf16[4,64,1152]{2,1,0:T(8,128)(2,1)}, bf16[4,64,1152]{2,1,0:T(8,128)(2,1)}) custom-call(s32[4]{0:T(128)S(1)} %pad_add_fusion.place, bf16[128,512]{1,0:T(8,128)(2,1)S(1)} %collective-permute-done.refs_0_, bf16[128,512]{1,0:T(8,128)(2,1)S(1)} %collective-permute-done.1.refs_1_, ...), custom_call_target="tpu_custom_call" | custom-call | tf_op jit(solution)/shard_map/pallas_call | solution.py:190
  24.2 2.6 %collective-permute-start.8 = (bf16[4,64,1152]{2,1,0:T(8,128)(2,1)}, bf16[4,64,1152]{2,1,0:T(8,128)(2,1)S(1)}, u32[]{:S(2)}, u32[]{:S(2)}) collective-permute-start(bf16[4,64,1152]{2,1,0:T(8,128)(2,1)} %get-tuple-element.40), channel_id=1, source_target_pairs={{0,2},{1,3},{2,0},{3,1},{4,6},{5,7},{6,4},{7,5},{8,10},{9,11},{10,... | collective-permute-start | bytes 1769480 | tf_op jit(solution)/shard_map/ppermute | solution.py:48
  26.8 5.4 %collective-permute-done.7.b = bf16[4,64,1152]{2,1,0:T(8,128)(2,1)S(1)} collective-permute-done((bf16[4,64,1152]{2,1,0:T(8,128)(2,1)}, bf16[4,64,1152]{2,1,0:T(8,128)(2,1)S(1)}, u32[]{:S(2)}, u32[]{:S(2)}) %collective-permute-start.7) | collective-permute-done | bytes 589856 | tf_op jit(solution)/shard_map/ppermute | solution.py:48
  32.1 8.8 %collective-permute-done.8.c = bf16[4,64,1152]{2,1,0:T(8,128)(2,1)S(1)} collective-permute-done((bf16[4,64,1152]{2,1,0:T(8,128)(2,1)}, bf16[4,64,1152]{2,1,0:T(8,128)(2,1)S(1)}, u32[]{:S(2)}, u32[]{:S(2)}) %collective-permute-start.8) | collective-permute-done | bytes 589856 | tf_op jit(solution)/shard_map/ppermute | solution.py:48
  40.9 2.6 %collective-permute-done.9.d = bf16[4,64,1152]{2,1,0:T(8,128)(2,1)S(1)} collective-permute-done((bf16[4,64,1152]{2,1,0:T(8,128)(2,1)}, bf16[4,64,1152]{2,1,0:T(8,128)(2,1)S(1)}, u32[]{:S(2)}, u32[]{:S(2)}) %collective-permute-start.9) | collective-permute-done | bytes 589856 | tf_op jit(solution)/shard_map/ppermute | solution.py:48
  45.4 2.4 %collective-permute-start.11 = (bf16[64,1152]{1,0:T(8,128)(2,1)S(1)}, bf16[64,1152]{1,0:T(8,128)(2,1)S(1)}, u32[]{:S(2)}, u32[]{:S(2)}) collective-permute-start(bf16[64,1152]{1,0:T(8,128)(2,1)S(1)} %get-tuple-element.44), channel_id=1, source_target_pairs={{0,8},{1,9},{2,10},{3,11},{4,12},{5,13},{6,14},{7,15},{8,0},{9,1},... | collective-permute-start | bytes 442376 | tf_op jit(solution)/shard_map/ppermute | solution.py:48
  48.5 3.5 %collective-permute-done.11.c = bf16[64,1152]{1,0:T(8,128)(2,1)S(1)} collective-permute-done((bf16[64,1152]{1,0:T(8,128)(2,1)S(1)}, bf16[64,1152]{1,0:T(8,128)(2,1)S(1)}, u32[]{:S(2)}, u32[]{:S(2)}) %collective-permute-start.11) | collective-permute-done | bytes 147488 | tf_op jit(solution)/shard_map/ppermute | solution.py:48
  52.0 1.8 %collective-permute-done.12.d = bf16[64,1152]{1,0:T(8,128)(2,1)S(1)} collective-permute-done((bf16[64,1152]{1,0:T(8,128)(2,1)S(1)}, bf16[64,1152]{1,0:T(8,128)(2,1)S(1)}, u32[]{:S(2)}, u32[]{:S(2)}) %collective-permute-start.12) | collective-permute-done | bytes 147488 | tf_op jit(solution)/shard_map/ppermute | solution.py:48
  53.9 5.8 %collective-permute-start.15 = (bf16[64,1024]{1,0:T(8,128)(2,1)S(1)}, bf16[64,1024]{1,0:T(8,128)(2,1)S(1)}, u32[]{:S(2)}, u32[]{:S(2)}) collective-permute-start(bf16[64,1024]{1,0:T(8,128)(2,1)S(1)} %get-tuple-element.46.own), channel_id=1, source_target_pairs={{0,16},{16,0},{1,17},{17,1},{2,18},{18,2},{3,19},{19,3},{4,20},{20... | collective-permute-start | bytes 393224 | tf_op jit(solution)/shard_map/ppermute | solution.py:37
  60.0 7.4 %collective-permute-start.13 = (bf16[64,128]{1,0:T(8,128)(2,1)S(1)}, bf16[64,128]{1,0:T(8,128)(2,1)S(1)}, u32[]{:S(2)}, u32[]{:S(2)}) collective-permute-start(bf16[64,128]{1,0:T(8,128)(2,1)S(1)} %get-tuple-element.47), channel_id=1, source_target_pairs={{0,0},{32,64},{64,128},{96,192},{128,32},{160,96},{192,160},{224,2... | collective-permute-start | bytes 49160 | tf_op jit(solution)/shard_map/ppermute | solution.py:258
  69.3 3.7 %collective-permute-done.14.b = bf16[64,128]{1,0:T(8,128)(2,1)S(1)} collective-permute-done((bf16[64,128]{1,0:T(8,128)(2,1)S(1)}, bf16[64,128]{1,0:T(8,128)(2,1)S(1)}, u32[]{:S(2)}, u32[]{:S(2)}) %collective-permute-start.14) | collective-permute-done | bytes 16416 | tf_op jit(solution)/shard_map/ppermute | solution.py:259
  73.1 11.7 %all_to_all.5 = bf16[16,64,128]{2,1,0:T(8,128)(2,1)S(1)} all-to-all(bf16[16,64,128]{2,1,0:T(8,128)(2,1)S(1)} %shard_map.50), channel_id=1, replica_groups=mesh['zl'=4,'core'=2,'zh'=2,'y'=4,'x'=4] {'y','x'}, dimensions={0} | all-to-all | bytes 524288 | tf_op jit(solution)/shard_map/all_to_all | solution.py:264
  89.8 2.1 %collective-permute-start.19 = (bf16[64,1024]{1,0:T(8,128)(2,1)S(1)}, bf16[64,1024]{1,0:T(8,128)(2,1)S(1)}, u32[]{:S(2)}, u32[]{:S(2)}) collective-permute-start(bf16[64,1024]{1,0:T(8,128)(2,1)S(1)} %shard_map.51.refs_0_), channel_id=1, source_target_pairs={{0,3},{1,2},{2,1},{3,0},{4,7},{5,6},{6,5},{7,4},{8,11},{9,10},{10,... | collective-permute-start | bytes 393224 | tf_op jit(solution)/shard_map/ppermute | solution.py:48
  97.3 2.0 %collective-permute-start.22 = (bf16[4,64,1024]{2,1,0:T(8,128)(2,1)S(1)}, bf16[4,64,1024]{2,1,0:T(8,128)(2,1)S(1)}, u32[]{:S(2)}, u32[]{:S(2)}) collective-permute-start(bf16[4,64,1024]{2,1,0:T(8,128)(2,1)S(1)} %shard_map.52.line), channel_id=1, source_target_pairs={{0,12},{1,13},{2,14},{3,15},{4,8},{5,9},{6,10},{7,11},{8,4},{9,5},... | collective-permute-start | bytes 1572872 | tf_op jit(solution)/shard_map/ppermute | solution.py:48
  99.7 4.0 %collective-permute-done.20.line = bf16[4,64,1024]{2,1,0:T(8,128)(2,1)S(1)} collective-permute-done((bf16[4,64,1024]{2,1,0:T(8,128)(2,1)S(1)}, bf16[4,64,1024]{2,1,0:T(8,128)(2,1)S(1)}, u32[]{:S(2)}, u32[]{:S(2)}) %collective-permute-start.20) | collective-permute-done | bytes 524320 | tf_op jit(solution)/shard_map/ppermute | solution.py:48
  104.2 5.7 %collective-permute-done.21.line = bf16[4,64,1024]{2,1,0:T(8,128)(2,1)S(1)} collective-permute-done((bf16[4,64,1024]{2,1,0:T(8,128)(2,1)S(1)}, bf16[4,64,1024]{2,1,0:T(8,128)(2,1)S(1)}, u32[]{:S(2)}, u32[]{:S(2)}) %collective-permute-start.21) | collective-permute-done | bytes 524320 | tf_op jit(solution)/shard_map/ppermute | solution.py:48
  110.3 2.2 %collective-permute-done.22.refs_3_ = bf16[4,64,1024]{2,1,0:T(8,128)(2,1)S(1)} collective-permute-done((bf16[4,64,1024]{2,1,0:T(8,128)(2,1)S(1)}, bf16[4,64,1024]{2,1,0:T(8,128)(2,1)S(1)}, u32[]{:S(2)}, u32[]{:S(2)}) %collective-permute-start.22) | collective-permute-done | bytes 524320 | tf_op jit(solution)/shard_map/ppermute | solution.py:48
  113.5 3.2 %collective-permute-start.23 = (bf16[512,512]{1,0:T(8,128)(2,1)S(1)}, bf16[512,512]{1,0:T(8,128)(2,1)S(1)}, u32[]{:S(2)}, u32[]{:S(2)}) collective-permute-start(bf16[512,512]{1,0:T(8,128)(2,1)S(1)} %bitcast.20), channel_id=1, source_target_pairs={{0,32},{32,0},{1,33},{33,1},{2,34},{34,2},{3,35},{35,3},{4,36},{36... | collective-permute-start | bytes 1572872 | tf_op jit(solution)/shard_map/ppermute | solution.py:37
  118.4 2.4 %collective-permute-start.25 = (bf16[128,512]{1,0:T(8,128)(2,1)S(1)}, bf16[128,512]{1,0:T(8,128)(2,1)S(1)}, u32[]{:S(2)}, u32[]{:S(2)}) collective-permute-start(bf16[128,512]{1,0:T(8,128)(2,1)S(1)} %get-tuple-element.61), channel_id=1, source_target_pairs={{0,128},{64,192},{128,0},{192,64},{1,129},{65,193},{129,1},{193,65... | collective-permute-start | bytes 393224 | tf_op jit(solution)/shard_map/ppermute | solution.py:37
  122.0 3.0 %collective-permute-done.24 = bf16[128,512]{1,0:T(8,128)(2,1)S(1)} collective-permute-done((bf16[128,512]{1,0:T(8,128)(2,1)S(1)}, bf16[128,512]{1,0:T(8,128)(2,1)S(1)}, u32[]{:S(2)}, u32[]{:S(2)}) %collective-permute-start.24) | collective-permute-done | bytes 131104 | tf_op jit(solution)/shard_map/ppermute | solution.py:37
  125.0 7.5 %collective-permute-done.25 = bf16[128,512]{1,0:T(8,128)(2,1)S(1)} collective-permute-done((bf16[128,512]{1,0:T(8,128)(2,1)S(1)}, bf16[128,512]{1,0:T(8,128)(2,1)S(1)}, u32[]{:S(2)}, u32[]{:S(2)}) %collective-permute-start.25) | collective-permute-done | bytes 131104 | tf_op jit(solution)/shard_map/ppermute | solution.py:37
  (64 shorter events, 30.3 us)
Async XLA Ops:
  0.0 6.8 %collective-permute-start.3 = (bf16[128,512]{1,0:T(8,128)(2,1)}, bf16[128,512]{1,0:T(8,128)(2,1)S(1)}, u32[]{:S(2)}, u32[]{:S(2)}) collective-permute-start(bf16[128,512]{1,0:T(8,128)(2,1)} %refs_0_.1), channel_id=1, source_target_pairs={{0,32},{32,0},{1,33},{33,1},{2,34},{34,2},{3,35},{35,3},{4,36},{36... | collective-permute-start | bytes 393224 | tf_op jit(solution)/shard_map/ppermute | solution.py:37
  3.2 7.8 %collective-permute-start = (bf16[128,512]{1,0:T(8,128)(2,1)}, bf16[128,512]{1,0:T(8,128)(2,1)S(1)}, u32[]{:S(2)}, u32[]{:S(2)}) collective-permute-start(bf16[128,512]{1,0:T(8,128)(2,1)} %refs_0_.1), channel_id=1, source_target_pairs={{0,64},{64,0},{128,192},{192,128},{1,65},{65,1},{129,193},{193,129... | collective-permute-start | bytes 393224 | tf_op jit(solution)/shard_map/ppermute | solution.py:37
  3.2 7.8 %collective-permute-start.1 = (bf16[128,512]{1,0:T(8,128)(2,1)}, bf16[128,512]{1,0:T(8,128)(2,1)S(1)}, u32[]{:S(2)}, u32[]{:S(2)}) collective-permute-start(bf16[128,512]{1,0:T(8,128)(2,1)} %refs_0_.1), channel_id=1, source_target_pairs={{0,128},{64,192},{128,0},{192,64},{1,129},{65,193},{129,1},{193,65... | collective-permute-start | bytes 393224 | tf_op jit(solution)/shard_map/ppermute | solution.py:37
  6.1 9.3 %collective-permute-start.2 = (bf16[128,512]{1,0:T(8,128)(2,1)}, bf16[128,512]{1,0:T(8,128)(2,1)S(1)}, u32[]{:S(2)}, u32[]{:S(2)}) collective-permute-start(bf16[128,512]{1,0:T(8,128)(2,1)} %refs_0_.1), channel_id=1, source_target_pairs={{0,192},{64,128},{128,64},{192,0},{1,193},{65,129},{129,65},{193,1... | collective-permute-start | bytes 393224 | tf_op jit(solution)/shard_map/ppermute | solution.py:37
  15.5 2.4 %collective-permute-start.4 = (bf16[128,512]{1,0:T(8,128)(2,1)S(1)}, bf16[128,512]{1,0:T(8,128)(2,1)S(1)}, u32[]{:S(2)}, u32[]{:S(2)}) collective-permute-start(bf16[128,512]{1,0:T(8,128)(2,1)S(1)} %collective-permute-done.refs_0_), channel_id=1, source_target_pairs={{0,32},{32,0},{1,33},{33,1},{2,34},{34,2},{3,35},{35,3},{4,36},{36... | collective-permute-start | bytes 393224 | tf_op jit(solution)/shard_map/ppermute | solution.py:37
  22.9 9.2 %collective-permute-start.7 = (bf16[4,64,1152]{2,1,0:T(8,128)(2,1)}, bf16[4,64,1152]{2,1,0:T(8,128)(2,1)S(1)}, u32[]{:S(2)}, u32[]{:S(2)}) collective-permute-start(bf16[4,64,1152]{2,1,0:T(8,128)(2,1)} %get-tuple-element.39), channel_id=1, source_target_pairs={{0,1},{1,0},{2,3},{3,2},{4,5},{5,4},{6,7},{7,6},{8,9},{9,8},{10,11... | collective-permute-start | bytes 1769480 | tf_op jit(solution)/shard_map/ppermute | solution.py:48
  24.2 16.7 %collective-permute-start.8 = (bf16[4,64,1152]{2,1,0:T(8,128)(2,1)}, bf16[4,64,1152]{2,1,0:T(8,128)(2,1)S(1)}, u32[]{:S(2)}, u32[]{:S(2)}) collective-permute-start(bf16[4,64,1152]{2,1,0:T(8,128)(2,1)} %get-tuple-element.40), channel_id=1, source_target_pairs={{0,2},{1,3},{2,0},{3,1},{4,6},{5,7},{6,4},{7,5},{8,10},{9,11},{10,... | collective-permute-start | bytes 1769480 | tf_op jit(solution)/shard_map/ppermute | solution.py:48
  26.8 16.8 %collective-permute-start.9 = (bf16[4,64,1152]{2,1,0:T(8,128)(2,1)}, bf16[4,64,1152]{2,1,0:T(8,128)(2,1)S(1)}, u32[]{:S(2)}, u32[]{:S(2)}) collective-permute-start(bf16[4,64,1152]{2,1,0:T(8,128)(2,1)} %get-tuple-element.41), channel_id=1, source_target_pairs={{0,3},{1,2},{2,1},{3,0},{4,7},{5,6},{6,5},{7,4},{8,11},{9,10},{10,... | collective-permute-start | bytes 1769480 | tf_op jit(solution)/shard_map/ppermute | solution.py:48
  44.4 4.1 %collective-permute-start.10 = (bf16[64,1152]{1,0:T(8,128)(2,1)S(1)}, bf16[64,1152]{1,0:T(8,128)(2,1)S(1)}, u32[]{:S(2)}, u32[]{:S(2)}) collective-permute-start(bf16[64,1152]{1,0:T(8,128)(2,1)S(1)} %get-tuple-element.43), channel_id=1, source_target_pairs={{0,4},{1,5},{2,6},{3,7},{4,0},{5,1},{6,2},{7,3},{8,12},{9,13},{10,... | collective-permute-start | bytes 442376 | tf_op jit(solution)/shard_map/ppermute | solution.py:48
  45.4 6.6 %collective-permute-start.11 = (bf16[64,1152]{1,0:T(8,128)(2,1)S(1)}, bf16[64,1152]{1,0:T(8,128)(2,1)S(1)}, u32[]{:S(2)}, u32[]{:S(2)}) collective-permute-start(bf16[64,1152]{1,0:T(8,128)(2,1)S(1)} %get-tuple-element.44), channel_id=1, source_target_pairs={{0,8},{1,9},{2,10},{3,11},{4,12},{5,13},{6,14},{7,15},{8,0},{9,1},... | collective-permute-start | bytes 442376 | tf_op jit(solution)/shard_map/ppermute | solution.py:48
  47.8 6.0 %collective-permute-start.12 = (bf16[64,1152]{1,0:T(8,128)(2,1)S(1)}, bf16[64,1152]{1,0:T(8,128)(2,1)S(1)}, u32[]{:S(2)}, u32[]{:S(2)}) collective-permute-start(bf16[64,1152]{1,0:T(8,128)(2,1)S(1)} %get-tuple-element.45), channel_id=1, source_target_pairs={{0,12},{1,13},{2,14},{3,15},{4,8},{5,9},{6,10},{7,11},{8,4},{9,5},... | collective-permute-start | bytes 442376 | tf_op jit(solution)/shard_map/ppermute | solution.py:48
  53.9 19.1 %collective-permute-start.15 = (bf16[64,1024]{1,0:T(8,128)(2,1)S(1)}, bf16[64,1024]{1,0:T(8,128)(2,1)S(1)}, u32[]{:S(2)}, u32[]{:S(2)}) collective-permute-start(bf16[64,1024]{1,0:T(8,128)(2,1)S(1)} %get-tuple-element.46.own), channel_id=1, source_target_pairs={{0,16},{16,0},{1,17},{17,1},{2,18},{18,2},{3,19},{19,3},{4,20},{20... | collective-permute-start | bytes 393224 | tf_op jit(solution)/shard_map/ppermute | solution.py:37
  60.0 9.3 %collective-permute-start.13 = (bf16[64,128]{1,0:T(8,128)(2,1)S(1)}, bf16[64,128]{1,0:T(8,128)(2,1)S(1)}, u32[]{:S(2)}, u32[]{:S(2)}) collective-permute-start(bf16[64,128]{1,0:T(8,128)(2,1)S(1)} %get-tuple-element.47), channel_id=1, source_target_pairs={{0,0},{32,64},{64,128},{96,192},{128,32},{160,96},{192,160},{224,2... | collective-permute-start | bytes 49160 | tf_op jit(solution)/shard_map/ppermute | solution.py:258
  67.4 5.5 %collective-permute-start.14 = (bf16[64,128]{1,0:T(8,128)(2,1)S(1)}, bf16[64,128]{1,0:T(8,128)(2,1)S(1)}, u32[]{:S(2)}, u32[]{:S(2)}) collective-permute-start(bf16[64,128]{1,0:T(8,128)(2,1)S(1)} %get-tuple-element.47), channel_id=1, source_target_pairs={{0,16},{16,0},{32,80},{48,64},{64,144},{80,128},{96,208},{112,192}... | collective-permute-start | bytes 49160 | tf_op jit(solution)/shard_map/ppermute | solution.py:259
  88.0 4.2 %collective-permute-start.17 = (bf16[64,1024]{1,0:T(8,128)(2,1)S(1)}, bf16[64,1024]{1,0:T(8,128)(2,1)S(1)}, u32[]{:S(2)}, u32[]{:S(2)}) collective-permute-start(bf16[64,1024]{1,0:T(8,128)(2,1)S(1)} %shard_map.51.refs_0_), channel_id=1, source_target_pairs={{0,1},{1,0},{2,3},{3,2},{4,5},{5,4},{6,7},{7,6},{8,9},{9,8},{10,11... | collective-permute-start | bytes 393224 | tf_op jit(solution)/shard_map/ppermute | solution.py:48
  88.1 5.8 %collective-permute-start.18 = (bf16[64,1024]{1,0:T(8,128)(2,1)S(1)}, bf16[64,1024]{1,0:T(8,128)(2,1)S(1)}, u32[]{:S(2)}, u32[]{:S(2)}) collective-permute-start(bf16[64,1024]{1,0:T(8,128)(2,1)S(1)} %shard_map.51.refs_0_), channel_id=1, source_target_pairs={{0,2},{1,3},{2,0},{3,1},{4,6},{5,7},{6,4},{7,5},{8,10},{9,11},{10,... | collective-permute-start | bytes 393224 | tf_op jit(solution)/shard_map/ppermute | solution.py:48
  89.8 5.5 %collective-permute-start.19 = (bf16[64,1024]{1,0:T(8,128)(2,1)S(1)}, bf16[64,1024]{1,0:T(8,128)(2,1)S(1)}, u32[]{:S(2)}, u32[]{:S(2)}) collective-permute-start(bf16[64,1024]{1,0:T(8,128)(2,1)S(1)} %shard_map.51.refs_0_), channel_id=1, source_target_pairs={{0,3},{1,2},{2,1},{3,0},{4,7},{5,6},{6,5},{7,4},{8,11},{9,10},{10,... | collective-permute-start | bytes 393224 | tf_op jit(solution)/shard_map/ppermute | solution.py:48
  95.3 8.4 %collective-permute-start.20 = (bf16[4,64,1024]{2,1,0:T(8,128)(2,1)S(1)}, bf16[4,64,1024]{2,1,0:T(8,128)(2,1)S(1)}, u32[]{:S(2)}, u32[]{:S(2)}) collective-permute-start(bf16[4,64,1024]{2,1,0:T(8,128)(2,1)S(1)} %shard_map.52.line), channel_id=1, source_target_pairs={{0,4},{1,5},{2,6},{3,7},{4,0},{5,1},{6,2},{7,3},{8,12},{9,13},{10,... | collective-permute-start | bytes 1572872 | tf_op jit(solution)/shard_map/ppermute | solution.py:48
  95.6 14.3 %collective-permute-start.21 = (bf16[4,64,1024]{2,1,0:T(8,128)(2,1)S(1)}, bf16[4,64,1024]{2,1,0:T(8,128)(2,1)S(1)}, u32[]{:S(2)}, u32[]{:S(2)}) collective-permute-start(bf16[4,64,1024]{2,1,0:T(8,128)(2,1)S(1)} %shard_map.52.line), channel_id=1, source_target_pairs={{0,8},{1,9},{2,10},{3,11},{4,12},{5,13},{6,14},{7,15},{8,0},{9,1},... | collective-permute-start | bytes 1572872 | tf_op jit(solution)/shard_map/ppermute | solution.py:48
  97.3 15.2 %collective-permute-start.22 = (bf16[4,64,1024]{2,1,0:T(8,128)(2,1)S(1)}, bf16[4,64,1024]{2,1,0:T(8,128)(2,1)S(1)}, u32[]{:S(2)}, u32[]{:S(2)}) collective-permute-start(bf16[4,64,1024]{2,1,0:T(8,128)(2,1)S(1)} %shard_map.52.line), channel_id=1, source_target_pairs={{0,12},{1,13},{2,14},{3,15},{4,8},{5,9},{6,10},{7,11},{8,4},{9,5},... | collective-permute-start | bytes 1572872 | tf_op jit(solution)/shard_map/ppermute | solution.py:48
  113.5 4.7 %collective-permute-start.23 = (bf16[512,512]{1,0:T(8,128)(2,1)S(1)}, bf16[512,512]{1,0:T(8,128)(2,1)S(1)}, u32[]{:S(2)}, u32[]{:S(2)}) collective-permute-start(bf16[512,512]{1,0:T(8,128)(2,1)S(1)} %bitcast.20), channel_id=1, source_target_pairs={{0,32},{32,0},{1,33},{33,1},{2,34},{34,2},{3,35},{35,3},{4,36},{36... | collective-permute-start | bytes 1572872 | tf_op jit(solution)/shard_map/ppermute | solution.py:37
  118.3 6.6 %collective-permute-start.24 = (bf16[128,512]{1,0:T(8,128)(2,1)S(1)}, bf16[128,512]{1,0:T(8,128)(2,1)S(1)}, u32[]{:S(2)}, u32[]{:S(2)}) collective-permute-start(bf16[128,512]{1,0:T(8,128)(2,1)S(1)} %get-tuple-element.60), channel_id=1, source_target_pairs={{0,192},{64,128},{128,64},{192,0},{1,193},{65,129},{129,65},{193,1... | collective-permute-start | bytes 393224 | tf_op jit(solution)/shard_map/ppermute | solution.py:37
  118.4 14.1 %collective-permute-start.25 = (bf16[128,512]{1,0:T(8,128)(2,1)S(1)}, bf16[128,512]{1,0:T(8,128)(2,1)S(1)}, u32[]{:S(2)}, u32[]{:S(2)}) collective-permute-start(bf16[128,512]{1,0:T(8,128)(2,1)S(1)} %get-tuple-element.61), channel_id=1, source_target_pairs={{0,128},{64,192},{128,0},{192,64},{1,129},{65,193},{129,1},{193,65... | collective-permute-start | bytes 393224 | tf_op jit(solution)/shard_map/ppermute | solution.py:37
  120.9 11.7 %collective-permute-start.26 = (bf16[128,512]{1,0:T(8,128)(2,1)S(1)}, bf16[128,512]{1,0:T(8,128)(2,1)S(1)}, u32[]{:S(2)}, u32[]{:S(2)}) collective-permute-start(bf16[128,512]{1,0:T(8,128)(2,1)S(1)} %get-tuple-element.62), channel_id=1, source_target_pairs={{0,64},{64,0},{128,192},{192,128},{1,65},{65,1},{129,193},{193,129... | collective-permute-start | bytes 393224 | tf_op jit(solution)/shard_map/ppermute | solution.py:37
  (9 other events, 38.6 us)

commit v9 on v8

--- a/solution.py
+++ b/solution.py
@@ -14,6 +14,8 @@
 ROW = ("zl", "core")
 COL = ("zh", "y", "x")
 PLANE = ("y", "x")
+STEPS = (0, 1, 3, 2)
+FAR = (2, 3, 1)
 BF16 = jnp.bfloat16
 F32 = jnp.float32
 VMEM = pl.BlockSpec(memory_space=pltpu.VMEM)
@@ -67,26 +69,15 @@
 
 def late_kernel(place, *refs):
     blocks, w_query, w_kv, early = refs[:6], *refs[6:9]
-    outs, late = refs[9:13], refs[13]
-    in_y = place[2] == 4
-
-    def put(k, source, row):
-        first = jnp.where(in_y, k >> 2, k & 3)
-        second = jnp.where(in_y, k & 3, k >> 2)
-        for s, out in enumerate(outs):
-
-            @pl.when((first ^ place[0]) == s)
-            def _():
-                out[second] = source[row]
-
+    outs, chunks = refs[9:13], refs[13]
     for side in range(2):
-        for b in range(2):
-            put(8 * side + b, early, 2 * side + b)
+        chunks[8 * side] = early[2 * side]
+        chunks[8 * side + 1] = early[2 * side + 1]
         for i in range(3):
-            row = 6 * side + 2 * i
-            project(blocks[3 * side + i], w_query, w_kv, late, row)
-            for b in range(2):
-                put(8 * side + 2 * i + 2 + b, late, row + b)
+            project(blocks[3 * side + i], w_query, w_kv, chunks, 8 * side + 2 * FAR[i])
+    for s in range(4):
+        for j in range(4):
+            outs[s][j] = chunks[chunk_at(place, place[0] ^ s, j)]
 
 
 def chunk_at(place, first, second):
@@ -155,7 +146,7 @@
 
 
 def stack_kernel(*refs):
-    for s, ref in enumerate(refs[:4]):
+    for s, ref in zip(STEPS, refs[:4]):
         refs[4][s] = ref[...]
 
 
@@ -170,7 +161,7 @@
 def output_kernel(place, *refs):
     early, line, weight, kept, sent, last, chunks = refs[:3], *refs[3:]
     line_kernel(line, weight, last)
-    for t, part in enumerate([*early, last]):
+    for t, part in zip(STEPS, [*early, last]):
         for s in range(4):
             chunks[chunk_at(place, place[0] ^ s, place[1] ^ t)] = part[s]
     half = kept.shape[0]
@@ -213,7 +204,7 @@
     heads = width // HD
     both = width + HD
 
-    mine = [tokens] + [partner(tokens, "zl", s) for s in (1, 2, 3)]
+    far = [partner(tokens, "zl", s) for s in FAR]
 
     def block_start(chip, side, index):
         return (((chip ^ (index & 3)) << 1) + ((index >> 2) ^ side)) * per_row
@@ -235,22 +226,22 @@
 
     near = partner(tokens, "core", 1)
     (early,) = call(early_kernel, [(4, per_chunk, both)], [tokens, near, w_query, w_keyval])
-    *far, early = lax.optimization_barrier((*mine[1:], early))
+    *far, early = lax.optimization_barrier((*far, early))
     parts = call(
         late_kernel,
         [(4, per_chunk, both)] * 4,
         [place, *far, *[partner(block, "core", 1) for block in far], w_query, w_keyval, early],
         [SMEM],
-        [pltpu.VMEM((12, per_chunk, both), BF16)],
-    )
-    got = [across_plane(parts[s], s, False) for s in (1, 2, 3)]
+        [pltpu.VMEM((Y * X, per_chunk, both), BF16)],
+    )
+    got = [across_plane(parts[s], s, False) for s in STEPS[1:]]
     halves = call(
         halve_kernel,
         [jax.ShapeDtypeStruct((per_chunk, both), F32), *[(per_chunk, both)] * 3],
         [place, parts[0], *got],
         [SMEM],
     )
-    got = [across_plane(halves[t], t, True) for t in (1, 2, 3)]
+    got = [across_plane(halves[t], t, True) for t in STEPS[1:]]
     own, kv = call(join_kernel, [(per_chunk, width), (per_chunk, HD)], [halves[0], *got])
     got = partner(own, "zh", 1)
 
@@ -274,13 +265,13 @@
     (line,) = call(
         stack_kernel,
         [(4, per_chunk, width)],
-        [attended] + [across_plane(attended, s, False) for s in (1, 2, 3)],
-    )
-    gathered = [across_plane(line, t, True) for t in (1, 2, 3)]
+        [attended] + [across_plane(attended, s, False) for s in STEPS[1:]],
+    )
+    gathered = [across_plane(line, t, True) for t in STEPS[1:]]
     early = []
-    for t in range(3):
+    for block in gathered:
         (done,) = call(line_kernel, [(4, per_chunk, features)], [line, w_output])
-        line, done = lax.optimization_barrier((gathered[t], done))
+        line, done = lax.optimization_barrier((block, done))
         early.append(done)
     kept, sent = call(
         output_kernel,

time: 133 us -> 128 us (0.962)
  waiting for transfers between devices: 61.4 us -> 58.7 us
  starting transfers between devices: 45.5 us -> 43.6 us
  Pallas kernels: 10 us -> 8.57 us
    ppermute x12, waiting for transfers between devices: 37.4 us -> 33.2 us  [across_plane(): return lax.ppermute(block, ('core', *PLANE), pairs)]
    ppermute x12, starting transfers between devices: 15.7 us -> 13.4 us  [across_plane(): return lax.ppermute(block, ('core', *PLANE), pairs)]
    ppermute x13, waiting for transfers between devices: 19.1 us -> 20.9 us  [partner(): return lax.ppermute(block, axis, [(i, i ^ step) for i in range(size)])]
    pallas_call x12, Pallas kernels: 10 us -> 8.57 us  [call(): pl.pallas_call(kernel, out_shape=[s if isinstance(s, jax.ShapeDtypeStruct...]
  transfers between devices with their start and end apart: 27 -> 27, of which waited for: 23 -> 21; matrix products, arithmetic and copies ran while one was open for 0% -> 1% of each run, Pallas kernels for 1% -> 1%
where the time goes in v9:
time: 128 us; the launch traced here: 127 us
  waiting for transfers between devices  58.7 us (46%)
  starting transfers between devices  43.6 us (34%)
  blocking collectives  11.9 us (9%)
  Pallas kernels  8.57 us (7%)
  local copies, waits for them, and re-layouts  3.13 us (2%)
  other arithmetic  1.29 us (1%)
    ppermute x12, waiting for transfers between devices, across_plane(): return lax.ppermute(block, ('core', *PLANE), pairs)  33.2 us
    ppermute x13, starting transfers between devices, partner(): return lax.ppermute(block, axis, [(i, i ^ step) for i in range(size)])  22.2 us
    ppermute x13, waiting for transfers between devices, partner(): return lax.ppermute(block, axis, [(i, i ^ step) for i in range(size)])  20.9 us
    ppermute x12, starting transfers between devices, across_plane(): return lax.ppermute(block, ('core', *PLANE), pairs)  13.4 us
    all_to_all x1, blocking collectives, shards(): lax.all_to_all(kv_block, PLANE, 0, 0, tiled=True).reshape(total, HD)  11.9 us
    pallas_call x12, Pallas kernels, call(): pl.pallas_call(kernel, out_shape=[s if isinstance(s, jax.ShapeDtypeStruct...  8.57 us
    ppermute x1, starting transfers between devices, shards(): here = lax.ppermute(kv, ROW, moves)  7.39 us
    ppermute x1, waiting for transfers between devices, shards(): lax.ppermute(kv, (*ROW, 'zh'), [(2 * e + h, 2 * r + 1 - h) for e, r in mo...  3.47 us
  transfers between devices with their start and end apart: 27, of which 21 were waited for; matrix products, arithmetic and copies ran while one was open for 1% of the time, Pallas kernels for 1%

profile of v9, /device:TPU:1, one launch (start us, length us, event | category | flops | bytes accessed | tf_op | source)
XLA Modules:
  0.0 127.4 jit_solution(5786845630612628088)
XLA Ops:
  0.0 3.2 %collective-permute-start.3 = (bf16[128,512]{1,0:T(8,128)(2,1)}, bf16[128,512]{1,0:T(8,128)(2,1)S(1)}, u32[]{:S(2)}, u32[]{:S(2)}) collective-permute-start(bf16[128,512]{1,0:T(8,128)(2,1)} %refs_0_.1), channel_id=1, source_target_pairs={{0,32},{32,0},{1,33},{33,1},{2,34},{34,2},{3,35},{35,3},{4,36},{36... | collective-permute-start | bytes 393224 | tf_op jit(solution)/shard_map/ppermute | solution.py:39
  9.7 5.5 %collective-permute-done.refs_0_ = bf16[128,512]{1,0:T(8,128)(2,1)S(1)} collective-permute-done((bf16[128,512]{1,0:T(8,128)(2,1)}, bf16[128,512]{1,0:T(8,128)(2,1)S(1)}, u32[]{:S(2)}, u32[]{:S(2)}) %collective-permute-start) | collective-permute-done | bytes 131104 | tf_op jit(solution)/shard_map/ppermute | solution.py:39
  18.8 3.0 %shard_map.47 = (bf16[4,64,1152]{2,1,0:T(8,128)(2,1)S(1)}, bf16[4,64,1152]{2,1,0:T(8,128)(2,1)}, bf16[4,64,1152]{2,1,0:T(8,128)(2,1)}, bf16[4,64,1152]{2,1,0:T(8,128)(2,1)}) custom-call(s32[4]{0:T(128)S(1)} %pad_add_fusion.place, bf16[128,512]{1,0:T(8,128)(2,1)S(1)} %collective-permute-done.refs_0_, bf16[128,512]{1,0:T(8,128)(2,1)S(1)} %collective-permute-done.1.refs_1_, ...), custom_call_target="tpu_custom_call" | custom-call | tf_op jit(solution)/shard_map/pallas_call | solution.py:181
  22.0 1.9 %collective-permute-start.8 = (bf16[4,64,1152]{2,1,0:T(8,128)(2,1)}, bf16[4,64,1152]{2,1,0:T(8,128)(2,1)S(1)}, u32[]{:S(2)}, u32[]{:S(2)}) collective-permute-start(bf16[4,64,1152]{2,1,0:T(8,128)(2,1)} %get-tuple-element.40), channel_id=1, source_target_pairs={{0,3},{1,2},{2,1},{3,0},{4,7},{5,6},{6,5},{7,4},{8,11},{9,10},{10,... | collective-permute-start | bytes 1769480 | tf_op jit(solution)/shard_map/ppermute | solution.py:50
  25.1 6.0 %collective-permute-done.7.b = bf16[4,64,1152]{2,1,0:T(8,128)(2,1)S(1)} collective-permute-done((bf16[4,64,1152]{2,1,0:T(8,128)(2,1)}, bf16[4,64,1152]{2,1,0:T(8,128)(2,1)S(1)}, u32[]{:S(2)}, u32[]{:S(2)}) %collective-permute-start.7) | collective-permute-done | bytes 589856 | tf_op jit(solution)/shard_map/ppermute | solution.py:50
  31.0 6.3 %collective-permute-done.8.c = bf16[4,64,1152]{2,1,0:T(8,128)(2,1)S(1)} collective-permute-done((bf16[4,64,1152]{2,1,0:T(8,128)(2,1)}, bf16[4,64,1152]{2,1,0:T(8,128)(2,1)S(1)}, u32[]{:S(2)}, u32[]{:S(2)}) %collective-permute-start.8) | collective-permute-done | bytes 589856 | tf_op jit(solution)/shard_map/ppermute | solution.py:50
  40.6 1.8 %collective-permute-start.11 = (bf16[64,1152]{1,0:T(8,128)(2,1)S(1)}, bf16[64,1152]{1,0:T(8,128)(2,1)S(1)}, u32[]{:S(2)}, u32[]{:S(2)}) collective-permute-start(bf16[64,1152]{1,0:T(8,128)(2,1)S(1)} %get-tuple-element.44), channel_id=1, source_target_pairs={{0,12},{1,13},{2,14},{3,15},{4,8},{5,9},{6,10},{7,11},{8,4},{9,5},... | collective-permute-start | bytes 442376 | tf_op jit(solution)/shard_map/ppermute | solution.py:50
  43.6 2.5 %collective-permute-done.11.c = bf16[64,1152]{1,0:T(8,128)(2,1)S(1)} collective-permute-done((bf16[64,1152]{1,0:T(8,128)(2,1)S(1)}, bf16[64,1152]{1,0:T(8,128)(2,1)S(1)}, u32[]{:S(2)}, u32[]{:S(2)}) %collective-permute-start.11) | collective-permute-done | bytes 147488 | tf_op jit(solution)/shard_map/ppermute | solution.py:50
  46.1 1.8 %collective-permute-done.12.d = bf16[64,1152]{1,0:T(8,128)(2,1)S(1)} collective-permute-done((bf16[64,1152]{1,0:T(8,128)(2,1)S(1)}, bf16[64,1152]{1,0:T(8,128)(2,1)S(1)}, u32[]{:S(2)}, u32[]{:S(2)}) %collective-permute-start.12) | collective-permute-done | bytes 147488 | tf_op jit(solution)/shard_map/ppermute | solution.py:50
  48.0 6.4 %collective-permute-start.15 = (bf16[64,1024]{1,0:T(8,128)(2,1)S(1)}, bf16[64,1024]{1,0:T(8,128)(2,1)S(1)}, u32[]{:S(2)}, u32[]{:S(2)}) collective-permute-start(bf16[64,1024]{1,0:T(8,128)(2,1)S(1)} %get-tuple-element.46.own), channel_id=1, source_target_pairs={{0,16},{16,0},{1,17},{17,1},{2,18},{18,2},{3,19},{19,3},{4,20},{20... | collective-permute-start | bytes 393224 | tf_op jit(solution)/shard_map/ppermute | solution.py:39
  54.7 7.4 %collective-permute-start.13 = (bf16[64,128]{1,0:T(8,128)(2,1)S(1)}, bf16[64,128]{1,0:T(8,128)(2,1)S(1)}, u32[]{:S(2)}, u32[]{:S(2)}) collective-permute-start(bf16[64,128]{1,0:T(8,128)(2,1)S(1)} %get-tuple-element.47), channel_id=1, source_target_pairs={{0,0},{32,64},{64,128},{96,192},{128,32},{160,96},{192,160},{224,2... | collective-permute-start | bytes 49160 | tf_op jit(solution)/shard_map/ppermute | solution.py:249
  63.9 3.5 %collective-permute-done.14.b = bf16[64,128]{1,0:T(8,128)(2,1)S(1)} collective-permute-done((bf16[64,128]{1,0:T(8,128)(2,1)S(1)}, bf16[64,128]{1,0:T(8,128)(2,1)S(1)}, u32[]{:S(2)}, u32[]{:S(2)}) %collective-permute-start.14) | collective-permute-done | bytes 16416 | tf_op jit(solution)/shard_map/ppermute | solution.py:250
  67.5 11.9 %all_to_all.5 = bf16[16,64,128]{2,1,0:T(8,128)(2,1)S(1)} all-to-all(bf16[16,64,128]{2,1,0:T(8,128)(2,1)S(1)} %shard_map.50), channel_id=1, replica_groups=mesh['zl'=4,'core'=2,'zh'=2,'y'=4,'x'=4] {'y','x'}, dimensions={0} | all-to-all | bytes 524288 | tf_op jit(solution)/shard_map/all_to_all | solution.py:255
  82.0 1.6 %shard_map.51.refs_0_ = bf16[64,1024]{1,0:T(8,128)(2,1)S(1)} custom-call(s32[10]{0:T(128)S(1)} %stack.63.base, bf16[64,1024]{1,0:T(8,128)(2,1)S(1)} %get-tuple-element.46.own, bf16[64,1024]{1,0:T(8,128)(2,1)S(1)} %collective-permute-done.15.got, f32[64,128]{1,0:T(8,128)S(1)} %get-tuple-element.74.cosine, f32[64,128]{1,0:T(8,128)S(1)} %get-tuple-element.75.sine_v, ...), custom_call_target="tpu_custom_call" | custom-call | tf_op jit(solution)/shard_map/pallas_call | solution.py:181
  84.5 2.4 %collective-permute-start.19 = (bf16[64,1024]{1,0:T(8,128)(2,1)S(1)}, bf16[64,1024]{1,0:T(8,128)(2,1)S(1)}, u32[]{:S(2)}, u32[]{:S(2)}) collective-permute-start(bf16[64,1024]{1,0:T(8,128)(2,1)S(1)} %shard_map.51.refs_0_), channel_id=1, source_target_pairs={{0,2},{1,3},{2,0},{3,1},{4,6},{5,7},{6,4},{7,5},{8,10},{9,11},{10,... | collective-permute-start | bytes 393224 | tf_op jit(solution)/shard_map/ppermute | solution.py:50
  87.8 2.7 %collective-permute-done.18.refs_2_ = bf16[64,1024]{1,0:T(8,128)(2,1)S(1)} collective-permute-done((bf16[64,1024]{1,0:T(8,128)(2,1)S(1)}, bf16[64,1024]{1,0:T(8,128)(2,1)S(1)}, u32[]{:S(2)}, u32[]{:S(2)}) %collective-permute-start.18) | collective-permute-done | bytes 131104 | tf_op jit(solution)/shard_map/ppermute | solution.py:50
  91.5 2.4 %collective-permute-start.22 = (bf16[4,64,1024]{2,1,0:T(8,128)(2,1)S(1)}, bf16[4,64,1024]{2,1,0:T(8,128)(2,1)S(1)}, u32[]{:S(2)}, u32[]{:S(2)}) collective-permute-start(bf16[4,64,1024]{2,1,0:T(8,128)(2,1)S(1)} %shard_map.52.line), channel_id=1, source_target_pairs={{0,8},{1,9},{2,10},{3,11},{4,12},{5,13},{6,14},{7,15},{8,0},{9,1},... | collective-permute-start | bytes 1572872 | tf_op jit(solution)/shard_map/ppermute | solution.py:50
  94.3 4.6 %collective-permute-done.20.line = bf16[4,64,1024]{2,1,0:T(8,128)(2,1)S(1)} collective-permute-done((bf16[4,64,1024]{2,1,0:T(8,128)(2,1)S(1)}, bf16[4,64,1024]{2,1,0:T(8,128)(2,1)S(1)}, u32[]{:S(2)}, u32[]{:S(2)}) %collective-permute-start.20) | collective-permute-done | bytes 524320 | tf_op jit(solution)/shard_map/ppermute | solution.py:50
  99.4 6.5 %collective-permute-done.21.line = bf16[4,64,1024]{2,1,0:T(8,128)(2,1)S(1)} collective-permute-done((bf16[4,64,1024]{2,1,0:T(8,128)(2,1)S(1)}, bf16[4,64,1024]{2,1,0:T(8,128)(2,1)S(1)}, u32[]{:S(2)}, u32[]{:S(2)}) %collective-permute-start.21) | collective-permute-done | bytes 524320 | tf_op jit(solution)/shard_map/ppermute | solution.py:50
  107.4 2.9 %collective-permute-start.23 = (bf16[512,512]{1,0:T(8,128)(2,1)S(1)}, bf16[512,512]{1,0:T(8,128)(2,1)S(1)}, u32[]{:S(2)}, u32[]{:S(2)}) collective-permute-start(bf16[512,512]{1,0:T(8,128)(2,1)S(1)} %bitcast.20), channel_id=1, source_target_pairs={{0,32},{32,0},{1,33},{33,1},{2,34},{34,2},{3,35},{35,3},{4,36},{36... | collective-permute-start | bytes 1572872 | tf_op jit(solution)/shard_map/ppermute | solution.py:39
  110.3 1.5 %collective-permute-done.23.got = bf16[512,512]{1,0:T(8,128)(2,1)S(1)} collective-permute-done((bf16[512,512]{1,0:T(8,128)(2,1)S(1)}, bf16[512,512]{1,0:T(8,128)(2,1)S(1)}, u32[]{:S(2)}, u32[]{:S(2)}) %collective-permute-start.23) | collective-permute-done | bytes 524320 | tf_op jit(solution)/shard_map/ppermute | solution.py:39
  112.1 2.7 %collective-permute-start.25 = (bf16[128,512]{1,0:T(8,128)(2,1)S(1)}, bf16[128,512]{1,0:T(8,128)(2,1)S(1)}, u32[]{:S(2)}, u32[]{:S(2)}) collective-permute-start(bf16[128,512]{1,0:T(8,128)(2,1)S(1)} %get-tuple-element.61), channel_id=1, source_target_pairs={{0,128},{64,192},{128,0},{192,64},{1,129},{65,193},{129,1},{193,65... | collective-permute-start | bytes 393224 | tf_op jit(solution)/shard_map/ppermute | solution.py:39
  115.6 3.0 %collective-permute-done.24 = bf16[128,512]{1,0:T(8,128)(2,1)S(1)} collective-permute-done((bf16[128,512]{1,0:T(8,128)(2,1)S(1)}, bf16[128,512]{1,0:T(8,128)(2,1)S(1)}, u32[]{:S(2)}, u32[]{:S(2)}) %collective-permute-start.24) | collective-permute-done | bytes 131104 | tf_op jit(solution)/shard_map/ppermute | solution.py:39
  118.6 8.1 %collective-permute-done.25 = bf16[128,512]{1,0:T(8,128)(2,1)S(1)} collective-permute-done((bf16[128,512]{1,0:T(8,128)(2,1)S(1)}, bf16[128,512]{1,0:T(8,128)(2,1)S(1)}, u32[]{:S(2)}, u32[]{:S(2)}) %collective-permute-start.25) | collective-permute-done | bytes 131104 | tf_op jit(solution)/shard_map/ppermute | solution.py:39
  (64 shorter events, 27.6 us)
Async XLA Ops:
  0.0 6.1 %collective-permute-start.3 = (bf16[128,512]{1,0:T(8,128)(2,1)}, bf16[128,512]{1,0:T(8,128)(2,1)S(1)}, u32[]{:S(2)}, u32[]{:S(2)}) collective-permute-start(bf16[128,512]{1,0:T(8,128)(2,1)} %refs_0_.1), channel_id=1, source_target_pairs={{0,32},{32,0},{1,33},{33,1},{2,34},{34,2},{3,35},{35,3},{4,36},{36... | collective-permute-start | bytes 393224 | tf_op jit(solution)/shard_map/ppermute | solution.py:39
  3.2 11.9 %collective-permute-start = (bf16[128,512]{1,0:T(8,128)(2,1)}, bf16[128,512]{1,0:T(8,128)(2,1)S(1)}, u32[]{:S(2)}, u32[]{:S(2)}) collective-permute-start(bf16[128,512]{1,0:T(8,128)(2,1)} %refs_0_.1), channel_id=1, source_target_pairs={{0,128},{64,192},{128,0},{192,64},{1,129},{65,193},{129,1},{193,65... | collective-permute-start | bytes 393224 | tf_op jit(solution)/shard_map/ppermute | solution.py:39
  4.5 10.7 %collective-permute-start.1 = (bf16[128,512]{1,0:T(8,128)(2,1)}, bf16[128,512]{1,0:T(8,128)(2,1)S(1)}, u32[]{:S(2)}, u32[]{:S(2)}) collective-permute-start(bf16[128,512]{1,0:T(8,128)(2,1)} %refs_0_.1), channel_id=1, source_target_pairs={{0,192},{64,128},{128,64},{192,0},{1,193},{65,129},{129,65},{193,1... | collective-permute-start | bytes 393224 | tf_op jit(solution)/shard_map/ppermute | solution.py:39
  5.9 10.2 %collective-permute-start.2 = (bf16[128,512]{1,0:T(8,128)(2,1)}, bf16[128,512]{1,0:T(8,128)(2,1)S(1)}, u32[]{:S(2)}, u32[]{:S(2)}) collective-permute-start(bf16[128,512]{1,0:T(8,128)(2,1)} %refs_0_.1), channel_id=1, source_target_pairs={{0,64},{64,0},{128,192},{192,128},{1,65},{65,1},{129,193},{193,129... | collective-permute-start | bytes 393224 | tf_op jit(solution)/shard_map/ppermute | solution.py:39
  21.8 9.2 %collective-permute-start.7 = (bf16[4,64,1152]{2,1,0:T(8,128)(2,1)}, bf16[4,64,1152]{2,1,0:T(8,128)(2,1)S(1)}, u32[]{:S(2)}, u32[]{:S(2)}) collective-permute-start(bf16[4,64,1152]{2,1,0:T(8,128)(2,1)} %get-tuple-element.39), channel_id=1, source_target_pairs={{0,1},{1,0},{2,3},{3,2},{4,5},{5,4},{6,7},{7,6},{8,9},{9,8},{10,11... | collective-permute-start | bytes 1769480 | tf_op jit(solution)/shard_map/ppermute | solution.py:50
  22.0 15.4 %collective-permute-start.8 = (bf16[4,64,1152]{2,1,0:T(8,128)(2,1)}, bf16[4,64,1152]{2,1,0:T(8,128)(2,1)S(1)}, u32[]{:S(2)}, u32[]{:S(2)}) collective-permute-start(bf16[4,64,1152]{2,1,0:T(8,128)(2,1)} %get-tuple-element.40), channel_id=1, source_target_pairs={{0,3},{1,2},{2,1},{3,0},{4,7},{5,6},{6,5},{7,4},{8,11},{9,10},{10,... | collective-permute-start | bytes 1769480 | tf_op jit(solution)/shard_map/ppermute | solution.py:50
  23.9 14.8 %collective-permute-start.9 = (bf16[4,64,1152]{2,1,0:T(8,128)(2,1)}, bf16[4,64,1152]{2,1,0:T(8,128)(2,1)S(1)}, u32[]{:S(2)}, u32[]{:S(2)}) collective-permute-start(bf16[4,64,1152]{2,1,0:T(8,128)(2,1)} %get-tuple-element.41), channel_id=1, source_target_pairs={{0,2},{1,3},{2,0},{3,1},{4,6},{5,7},{6,4},{7,5},{8,10},{9,11},{10,... | collective-permute-start | bytes 1769480 | tf_op jit(solution)/shard_map/ppermute | solution.py:50
  39.5 4.1 %collective-permute-start.10 = (bf16[64,1152]{1,0:T(8,128)(2,1)S(1)}, bf16[64,1152]{1,0:T(8,128)(2,1)S(1)}, u32[]{:S(2)}, u32[]{:S(2)}) collective-permute-start(bf16[64,1152]{1,0:T(8,128)(2,1)S(1)} %get-tuple-element.43), channel_id=1, source_target_pairs={{0,4},{1,5},{2,6},{3,7},{4,0},{5,1},{6,2},{7,3},{8,12},{9,13},{10,... | collective-permute-start | bytes 442376 | tf_op jit(solution)/shard_map/ppermute | solution.py:50
  40.6 5.5 %collective-permute-start.11 = (bf16[64,1152]{1,0:T(8,128)(2,1)S(1)}, bf16[64,1152]{1,0:T(8,128)(2,1)S(1)}, u32[]{:S(2)}, u32[]{:S(2)}) collective-permute-start(bf16[64,1152]{1,0:T(8,128)(2,1)S(1)} %get-tuple-element.44), channel_id=1, source_target_pairs={{0,12},{1,13},{2,14},{3,15},{4,8},{5,9},{6,10},{7,11},{8,4},{9,5},... | collective-permute-start | bytes 442376 | tf_op jit(solution)/shard_map/ppermute | solution.py:50
  42.4 5.5 %collective-permute-start.12 = (bf16[64,1152]{1,0:T(8,128)(2,1)S(1)}, bf16[64,1152]{1,0:T(8,128)(2,1)S(1)}, u32[]{:S(2)}, u32[]{:S(2)}) collective-permute-start(bf16[64,1152]{1,0:T(8,128)(2,1)S(1)} %get-tuple-element.45), channel_id=1, source_target_pairs={{0,8},{1,9},{2,10},{3,11},{4,12},{5,13},{6,14},{7,15},{8,0},{9,1},... | collective-permute-start | bytes 442376 | tf_op jit(solution)/shard_map/ppermute | solution.py:50
  48.0 19.4 %collective-permute-start.15 = (bf16[64,1024]{1,0:T(8,128)(2,1)S(1)}, bf16[64,1024]{1,0:T(8,128)(2,1)S(1)}, u32[]{:S(2)}, u32[]{:S(2)}) collective-permute-start(bf16[64,1024]{1,0:T(8,128)(2,1)S(1)} %get-tuple-element.46.own), channel_id=1, source_target_pairs={{0,16},{16,0},{1,17},{17,1},{2,18},{18,2},{3,19},{19,3},{4,20},{20... | collective-permute-start | bytes 393224 | tf_op jit(solution)/shard_map/ppermute | solution.py:39
  54.7 9.3 %collective-permute-start.13 = (bf16[64,128]{1,0:T(8,128)(2,1)S(1)}, bf16[64,128]{1,0:T(8,128)(2,1)S(1)}, u32[]{:S(2)}, u32[]{:S(2)}) collective-permute-start(bf16[64,128]{1,0:T(8,128)(2,1)S(1)} %get-tuple-element.47), channel_id=1, source_target_pairs={{0,0},{32,64},{64,128},{96,192},{128,32},{160,96},{192,160},{224,2... | collective-permute-start | bytes 49160 | tf_op jit(solution)/shard_map/ppermute | solution.py:249
  62.1 5.3 %collective-permute-start.14 = (bf16[64,128]{1,0:T(8,128)(2,1)S(1)}, bf16[64,128]{1,0:T(8,128)(2,1)S(1)}, u32[]{:S(2)}, u32[]{:S(2)}) collective-permute-start(bf16[64,128]{1,0:T(8,128)(2,1)S(1)} %get-tuple-element.47), channel_id=1, source_target_pairs={{0,16},{16,0},{32,80},{48,64},{64,144},{80,128},{96,208},{112,192}... | collective-permute-start | bytes 49160 | tf_op jit(solution)/shard_map/ppermute | solution.py:250
  79.4 2.6 %collective-permute-start.16 = (bf16[1024,128]{1,0:T(8,128)(2,1)S(1)}, bf16[1024,128]{1,0:T(8,128)(2,1)S(1)}, u32[]{:S(2)}, u32[]{:S(2)}) collective-permute-start(bf16[1024,128]{1,0:T(8,128)(2,1)S(1)} %bitcast.17), channel_id=1, source_target_pairs={{0,32},{32,0},{1,33},{33,1},{2,34},{34,2},{3,35},{35,3},{4,36},{36... | collective-permute-start | bytes 786440 | tf_op jit(solution)/shard_map/ppermute | solution.py:39
  83.6 4.2 %collective-permute-start.17 = (bf16[64,1024]{1,0:T(8,128)(2,1)S(1)}, bf16[64,1024]{1,0:T(8,128)(2,1)S(1)}, u32[]{:S(2)}, u32[]{:S(2)}) collective-permute-start(bf16[64,1024]{1,0:T(8,128)(2,1)S(1)} %shard_map.51.refs_0_), channel_id=1, source_target_pairs={{0,1},{1,0},{2,3},{3,2},{4,5},{5,4},{6,7},{7,6},{8,9},{9,8},{10,11... | collective-permute-start | bytes 393224 | tf_op jit(solution)/shard_map/ppermute | solution.py:50
  83.7 6.8 %collective-permute-start.18 = (bf16[64,1024]{1,0:T(8,128)(2,1)S(1)}, bf16[64,1024]{1,0:T(8,128)(2,1)S(1)}, u32[]{:S(2)}, u32[]{:S(2)}) collective-permute-start(bf16[64,1024]{1,0:T(8,128)(2,1)S(1)} %shard_map.51.refs_0_), channel_id=1, source_target_pairs={{0,3},{1,2},{2,1},{3,0},{4,7},{5,6},{6,5},{7,4},{8,11},{9,10},{10,... | collective-permute-start | bytes 393224 | tf_op jit(solution)/shard_map/ppermute | solution.py:50
  84.5 6.0 %collective-permute-start.19 = (bf16[64,1024]{1,0:T(8,128)(2,1)S(1)}, bf16[64,1024]{1,0:T(8,128)(2,1)S(1)}, u32[]{:S(2)}, u32[]{:S(2)}) collective-permute-start(bf16[64,1024]{1,0:T(8,128)(2,1)S(1)} %shard_map.51.refs_0_), channel_id=1, source_target_pairs={{0,2},{1,3},{2,0},{3,1},{4,6},{5,7},{6,4},{7,5},{8,10},{9,11},{10,... | collective-permute-start | bytes 393224 | tf_op jit(solution)/shard_map/ppermute | solution.py:50
  90.6 8.4 %collective-permute-start.20 = (bf16[4,64,1024]{2,1,0:T(8,128)(2,1)S(1)}, bf16[4,64,1024]{2,1,0:T(8,128)(2,1)S(1)}, u32[]{:S(2)}, u32[]{:S(2)}) collective-permute-start(bf16[4,64,1024]{2,1,0:T(8,128)(2,1)S(1)} %shard_map.52.line), channel_id=1, source_target_pairs={{0,4},{1,5},{2,6},{3,7},{4,0},{5,1},{6,2},{7,3},{8,12},{9,13},{10,... | collective-permute-start | bytes 1572872 | tf_op jit(solution)/shard_map/ppermute | solution.py:50
  90.8 15.2 %collective-permute-start.21 = (bf16[4,64,1024]{2,1,0:T(8,128)(2,1)S(1)}, bf16[4,64,1024]{2,1,0:T(8,128)(2,1)S(1)}, u32[]{:S(2)}, u32[]{:S(2)}) collective-permute-start(bf16[4,64,1024]{2,1,0:T(8,128)(2,1)S(1)} %shard_map.52.line), channel_id=1, source_target_pairs={{0,12},{1,13},{2,14},{3,15},{4,8},{5,9},{6,10},{7,11},{8,4},{9,5},... | collective-permute-start | bytes 1572872 | tf_op jit(solution)/shard_map/ppermute | solution.py:50
  91.5 14.9 %collective-permute-start.22 = (bf16[4,64,1024]{2,1,0:T(8,128)(2,1)S(1)}, bf16[4,64,1024]{2,1,0:T(8,128)(2,1)S(1)}, u32[]{:S(2)}, u32[]{:S(2)}) collective-permute-start(bf16[4,64,1024]{2,1,0:T(8,128)(2,1)S(1)} %shard_map.52.line), channel_id=1, source_target_pairs={{0,8},{1,9},{2,10},{3,11},{4,12},{5,13},{6,14},{7,15},{8,0},{9,1},... | collective-permute-start | bytes 1572872 | tf_op jit(solution)/shard_map/ppermute | solution.py:50
  107.4 4.4 %collective-permute-start.23 = (bf16[512,512]{1,0:T(8,128)(2,1)S(1)}, bf16[512,512]{1,0:T(8,128)(2,1)S(1)}, u32[]{:S(2)}, u32[]{:S(2)}) collective-permute-start(bf16[512,512]{1,0:T(8,128)(2,1)S(1)} %bitcast.20), channel_id=1, source_target_pairs={{0,32},{32,0},{1,33},{33,1},{2,34},{34,2},{3,35},{35,3},{4,36},{36... | collective-permute-start | bytes 1572872 | tf_op jit(solution)/shard_map/ppermute | solution.py:39
  112.0 6.6 %collective-permute-start.24 = (bf16[128,512]{1,0:T(8,128)(2,1)S(1)}, bf16[128,512]{1,0:T(8,128)(2,1)S(1)}, u32[]{:S(2)}, u32[]{:S(2)}) collective-permute-start(bf16[128,512]{1,0:T(8,128)(2,1)S(1)} %get-tuple-element.60), channel_id=1, source_target_pairs={{0,192},{64,128},{128,64},{192,0},{1,193},{65,129},{129,65},{193,1... | collective-permute-start | bytes 393224 | tf_op jit(solution)/shard_map/ppermute | solution.py:39
  112.1 14.6 %collective-permute-start.25 = (bf16[128,512]{1,0:T(8,128)(2,1)S(1)}, bf16[128,512]{1,0:T(8,128)(2,1)S(1)}, u32[]{:S(2)}, u32[]{:S(2)}) collective-permute-start(bf16[128,512]{1,0:T(8,128)(2,1)S(1)} %get-tuple-element.61), channel_id=1, source_target_pairs={{0,128},{64,192},{128,0},{192,64},{1,129},{65,193},{129,1},{193,65... | collective-permute-start | bytes 393224 | tf_op jit(solution)/shard_map/ppermute | solution.py:39
  114.8 11.9 %collective-permute-start.26 = (bf16[128,512]{1,0:T(8,128)(2,1)S(1)}, bf16[128,512]{1,0:T(8,128)(2,1)S(1)}, u32[]{:S(2)}, u32[]{:S(2)}) collective-permute-start(bf16[128,512]{1,0:T(8,128)(2,1)S(1)} %get-tuple-element.62), channel_id=1, source_target_pairs={{0,64},{64,0},{128,192},{192,128},{1,65},{65,1},{129,193},{193,129... | collective-permute-start | bytes 393224 | tf_op jit(solution)/shard_map/ppermute | solution.py:39
  (9 other events, 40.2 us)

commit v10 on v9

--- a/solution.py
+++ b/solution.py
@@ -50,31 +50,33 @@
     return lax.ppermute(block, ("core", *PLANE), pairs)
 
 
-def project(block, w_query, w_kv, chunks, k):
+def project(block, w_query, w_kv, chunks, keyvals, k):
     size = chunks.shape[1]
-    width = w_query.shape[1]
     query = jnp.dot(block[...], w_query[...], preferred_element_type=F32).astype(BF16)
     keyval = jnp.dot(block[...], w_kv[...], preferred_element_type=F32).astype(BF16)
     for b in range(2):
         part = slice(b * size, (b + 1) * size)
-        chunks[k + b, :, :width] = query[part]
-        chunks[k + b, :, width:] = keyval[part]
+        chunks[k + b] = query[part]
+        keyvals[k + b] = keyval[part]
 
 
 def early_kernel(*refs):
-    blocks, w_query, w_kv, out = refs[:2], *refs[2:]
+    blocks, w_query, w_kv, out, keyvals = refs[:2], *refs[2:]
     for i, block in enumerate(blocks):
-        project(block, w_query, w_kv, out, 2 * i)
+        project(block, w_query, w_kv, out, keyvals, 2 * i)
 
 
 def late_kernel(place, *refs):
-    blocks, w_query, w_kv, early = refs[:6], *refs[6:9]
-    outs, chunks = refs[9:13], refs[13]
+    blocks, w_query, w_kv, early, early_kv = refs[:6], *refs[6:10]
+    outs, keyvals, chunks = refs[10:14], refs[14], refs[15]
     for side in range(2):
-        chunks[8 * side] = early[2 * side]
-        chunks[8 * side + 1] = early[2 * side + 1]
+        for b in range(2):
+            chunks[8 * side + b] = early[2 * side + b]
+            keyvals[8 * side + b] = early_kv[2 * side + b]
         for i in range(3):
-            project(blocks[3 * side + i], w_query, w_kv, chunks, 8 * side + 2 * FAR[i])
+            project(
+                blocks[3 * side + i], w_query, w_kv, chunks, keyvals, 8 * side + 2 * FAR[i]
+            )
     for s in range(4):
         for j in range(4):
             outs[s][j] = chunks[chunk_at(place, place[0] ^ s, j)]
@@ -91,11 +93,16 @@
         out[...] = total.astype(out.dtype)
 
 
-def join_kernel(a, b, c, d, query, keyval):
-    width = query.shape[1]
+def join_kernel(a, b, c, d, out):
     total = a[...] + b[...].astype(F32) + c[...].astype(F32) + d[...].astype(F32)
-    query[...] = total[:, :width].astype(BF16)
-    keyval[...] = total[:, width:].astype(BF16)
+    out[...] = total.astype(BF16)
+
+
+def sum_kernel(parts, out):
+    total = parts[0].astype(F32)
+    for c in range(1, parts.shape[0]):
+        total += parts[c].astype(F32)
+    out[...] = total.astype(BF16)
 
 
 def keys_kernel(a, b, cosine, sine_v, out):
@@ -202,7 +209,6 @@
     per_chunk = total // (Y * X)
     width = w_query.shape[1]
     heads = width // HD
-    both = width + HD
 
     far = [partner(tokens, "zl", s) for s in FAR]
 
@@ -225,35 +231,50 @@
     place = jnp.stack([first, second, 1 + 3 * core, 4 - 3 * core]).astype(jnp.int32)
 
     near = partner(tokens, "core", 1)
-    (early,) = call(early_kernel, [(4, per_chunk, both)], [tokens, near, w_query, w_keyval])
+    early, early_kv = call(
+        early_kernel,
+        [(4, per_chunk, width), (4, per_chunk, HD)],
+        [tokens, near, w_query, w_keyval],
+    )
     *far, early = lax.optimization_barrier((*far, early))
-    parts = call(
+    *parts, kv_parts = call(
         late_kernel,
-        [(4, per_chunk, both)] * 4,
-        [place, *far, *[partner(block, "core", 1) for block in far], w_query, w_keyval, early],
+        [(4, per_chunk, width)] * 4 + [(Y * X, per_chunk, HD)],
+        [
+            place,
+            *far,
+            *[partner(block, "core", 1) for block in far],
+            w_query,
+            w_keyval,
+            early,
+            early_kv,
+        ],
         [SMEM],
-        [pltpu.VMEM((Y * X, per_chunk, both), BF16)],
-    )
-    got = [across_plane(parts[s], s, False) for s in STEPS[1:]]
-    halves = call(
-        halve_kernel,
-        [jax.ShapeDtypeStruct((per_chunk, both), F32), *[(per_chunk, both)] * 3],
-        [place, parts[0], *got],
-        [SMEM],
-    )
-    got = [across_plane(halves[t], t, True) for t in STEPS[1:]]
-    own, kv = call(join_kernel, [(per_chunk, width), (per_chunk, HD)], [halves[0], *got])
-    got = partner(own, "zh", 1)
+        [pltpu.VMEM((Y * X, per_chunk, width), BF16)],
+    )
+    kv_parts = lax.all_to_all(kv_parts, PLANE, 0, 0, tiled=True)
+    (kv,) = call(sum_kernel, [(per_chunk, HD)], [kv_parts])
 
     moves = [(e, 2 * (e % 4) + e // 4) for e in range(8)]
     here = lax.ppermute(kv, ROW, moves)
     across = lax.ppermute(
         kv, (*ROW, "zh"), [(2 * e + h, 2 * r + 1 - h) for e, r in moves for h in range(2)]
     )
-    here, across, got = lax.optimization_barrier((here, across, got))
     (kv_block,) = call(keys_kernel, [(Y * X, per_chunk, HD)], [here, across, key_cos, key_sin])
     kv_own = lax.all_to_all(kv_block, PLANE, 0, 0, tiled=True).reshape(total, HD)
     kv_other = partner(kv_own, "core", 1)
+
+    got = [across_plane(parts[s], s, False) for s in STEPS[1:]]
+    halves = call(
+        halve_kernel,
+        [jax.ShapeDtypeStruct((per_chunk, width), F32), *[(per_chunk, width)] * 3],
+        [place, parts[0], *got],
+        [SMEM],
+    )
+    got = [across_plane(halves[t], t, True) for t in STEPS[1:]]
+    (own,) = call(join_kernel, [(per_chunk, width)], [halves[0], *got])
+    got = partner(own, "zh", 1)
+
     (attended,) = call(
         functools.partial(attention_kernel, heads),
         [(per_chunk, width)],

time: 128 us -> 124 us (0.969); the launches traced: 127 us -> 122 us
  starting transfers between devices: 43.6 us -> 59.4 us
  waiting for transfers between devices: 58.7 us -> 46.6 us
  blocking collectives: 11.9 us -> 0 us
  local copies, waits for them, and re-layouts: 3.13 us -> 5.58 us
    ppermute x12, waiting for transfers between devices: 33.2 us -> 17.8 us  [across_plane(): return lax.ppermute(block, ('core', *PLANE), pairs)]
    all_to_all x1 -> x0, blocking collectives: 11.9 us -> none  [shards(): lax.all_to_all(kv_block, PLANE, 0, 0, tiled=True).reshape(total, HD)]
    all_to_all x0 -> x2, starting transfers between devices: none -> 9.3 us  [the longest x1 5.77 us: shards(): kv_parts = lax.all_to_all(kv_parts, PLANE, 0, 0, tiled=True)]
    all_to_all x0 -> x2, waiting for transfers between devices: none -> 7.22 us  [the longest x1 3.99 us: shards(): kv_parts = lax.all_to_all(kv_parts, PLANE, 0, 0, tiled=True)]
    ppermute x1, starting transfers between devices: 0.64 us -> 5.95 us  [shards(): lax.ppermute(kv, (*ROW, 'zh'), [(2 * e + h, 2 * r + 1 - h) for e, r in mo...]
    ppermute x1, waiting for transfers between devices: 3.47 us -> 0.77 us  [shards(): lax.ppermute(kv, (*ROW, 'zh'), [(2 * e + h, 2 * r + 1 - h) for e, r in mo...]
    unnamed x12 -> x20, local copies, waits for them, and re-layouts: 3.05 us -> 5.49 us
    ppermute x1, starting transfers between devices: 7.39 us -> 5.31 us  [shards(): here = lax.ppermute(kv, ROW, moves)]
  transfers between devices with their start and end apart: 27 -> 29, of which waited for: 21 -> 17; matrix products, arithmetic and copies ran while one was open for 1% -> 1% of each run, Pallas kernels for 1% -> 3%
where the time goes in v10:
time: 124 us; the launch traced here: 122 us
  starting transfers between devices  59.4 us (48%)
  waiting for transfers between devices  46.6 us (38%)
  Pallas kernels  8.89 us (7%)
  local copies, waits for them, and re-layouts  5.58 us (4%)
  other arithmetic  1.29 us (1%)
    ppermute x13, starting transfers between devices, partner(): return lax.ppermute(block, axis, [(i, i ^ step) for i in range(size)])  23.5 us
    ppermute x13, waiting for transfers between devices, partner(): return lax.ppermute(block, axis, [(i, i ^ step) for i in range(size)])  20.8 us
    ppermute x12, waiting for transfers between devices, across_plane(): return lax.ppermute(block, ('core', *PLANE), pairs)  17.8 us
    ppermute x12, starting transfers between devices, across_plane(): return lax.ppermute(block, ('core', *PLANE), pairs)  15.3 us
    pallas_call x13, Pallas kernels, call(): pl.pallas_call(kernel, out_shape=[s if isinstance(s, jax.ShapeDtypeStruct...  8.89 us
    ppermute x1, starting transfers between devices, shards(): lax.ppermute(kv, (*ROW, 'zh'), [(2 * e + h, 2 * r + 1 - h) for e, r in mo...  5.95 us
    all_to_all x1, starting transfers between devices, shards(): kv_parts = lax.all_to_all(kv_parts, PLANE, 0, 0, tiled=True)  5.77 us
    unnamed x20, local copies, waits for them, and re-layouts  5.49 us
  transfers between devices with their start and end apart: 29, of which 17 were waited for; matrix products, arithmetic and copies ran while one was open for 1% of the time, Pallas kernels for 3%

profile of v10, /device:TPU:1, one launch (start us, length us, event | category | flops | bytes accessed | tf_op | source)
XLA Modules:
  0.0 122.0 jit_solution(9950634379872555155)
XLA Ops:
  0.0 3.2 %collective-permute-start.3 = (bf16[128,512]{1,0:T(8,128)(2,1)}, bf16[128,512]{1,0:T(8,128)(2,1)S(1)}, u32[]{:S(2)}, u32[]{:S(2)}) collective-permute-start(bf16[128,512]{1,0:T(8,128)(2,1)} %refs_0_.1), channel_id=1, source_target_pairs={{0,32},{32,0},{1,33},{33,1},{2,34},{34,2},{3,35},{35,3},{4,36},{36... | collective-permute-start | bytes 393224 | tf_op jit(solution)/shard_map/ppermute | solution.py:39
  9.7 5.4 %collective-permute-done.refs_0_ = bf16[128,512]{1,0:T(8,128)(2,1)S(1)} collective-permute-done((bf16[128,512]{1,0:T(8,128)(2,1)}, bf16[128,512]{1,0:T(8,128)(2,1)S(1)}, u32[]{:S(2)}, u32[]{:S(2)}) %collective-permute-start) | collective-permute-done | bytes 131104 | tf_op jit(solution)/shard_map/ppermute | solution.py:39
  18.8 2.6 %shard_map.47 = (bf16[4,64,1024]{2,1,0:T(8,128)(2,1)S(1)}, bf16[4,64,1024]{2,1,0:T(8,128)(2,1)S(1)}, bf16[4,64,1024]{2,1,0:T(8,128)(2,1)S(1)}, bf16[4,64,1024]{2,1,0:T(8,128)(2,1)S(1)}, bf16[16,64,128]{2,1,0:T(8,128)(2,1)}) custom-call(s32[4]{0:T(128)S(1)} %pad_add_fusion.place, bf16[128,512]{1,0:T(8,128)(2,1)S(1)} %collective-permute-done.refs_0_, ...), custom_call_target="tpu_custom_call" | custom-call | tf_op jit(solution)/shard_map/pallas_call | solution.py:188
  23.8 5.8 %all-to-all-start = ((bf16[16,64,128]{2,1,0:T(8,128)(2,1)}), bf16[16,64,128]{2,1,0:T(8,128)(2,1)S(1)}, u32[]{:S(2)}, u32[]{:S(2)}) async-start(bf16[16,64,128]{2,1,0:T(8,128)(2,1)} %get-tuple-element.46), calls=%async_computation | async-start | bytes 524288 | tf_op jit(solution)/shard_map/all_to_all | solution.py:255
  31.1 1.8 %collective-permute-start.8 = (bf16[4,64,1024]{2,1,0:T(8,128)(2,1)}, bf16[4,64,1024]{2,1,0:T(8,128)(2,1)S(1)}, u32[]{:S(2)}, u32[]{:S(2)}) collective-permute-start(bf16[4,64,1024]{2,1,0:T(8,128)(2,1)} %copy-done.8), channel_id=1, source_target_pairs={{0,3},{1,2},{2,1},{3,0},{4,7},{5,6},{6,5},{7,4},{8,11},{9,10},{10,... | collective-permute-start | bytes 1572872 | tf_op jit(solution)/shard_map/ppermute | solution.py:50
  33.8 4.0 %all-to-all-done.parts = bf16[16,64,128]{2,1,0:T(8,128)(2,1)S(1)} async-done(((bf16[16,64,128]{2,1,0:T(8,128)(2,1)}), bf16[16,64,128]{2,1,0:T(8,128)(2,1)S(1)}, u32[]{:S(2)}, u32[]{:S(2)}) %all-to-all-start) | async-done | bytes 262176 | tf_op jit(solution)/shard_map/all_to_all | solution.py:255
  37.8 5.3 %collective-permute-start.14 = (bf16[64,128]{1,0:T(8,128)(2,1)S(1)}, bf16[64,128]{1,0:T(8,128)(2,1)S(1)}, u32[]{:S(2)}, u32[]{:S(2)}) collective-permute-start(bf16[64,128]{1,0:T(8,128)(2,1)S(1)} %shard_map.50), channel_id=1, source_target_pairs={{0,0},{32,64},{64,128},{96,192},{128,32},{160,96},{192,160},{224,2... | collective-permute-start | bytes 49160 | tf_op jit(solution)/shard_map/ppermute | solution.py:259
  43.2 6.0 %collective-permute-start.15 = (bf16[64,128]{1,0:T(8,128)(2,1)S(1)}, bf16[64,128]{1,0:T(8,128)(2,1)S(1)}, u32[]{:S(2)}, u32[]{:S(2)}) collective-permute-start(bf16[64,128]{1,0:T(8,128)(2,1)S(1)} %shard_map.50), channel_id=1, source_target_pairs={{0,16},{16,0},{32,80},{48,64},{64,144},{80,128},{96,208},{112,192}... | collective-permute-start | bytes 49160 | tf_op jit(solution)/shard_map/ppermute | solution.py:260
  50.8 3.5 %all-to-all-start.1 = ((bf16[16,64,128]{2,1,0:T(8,128)(2,1)}), bf16[16,64,128]{2,1,0:T(8,128)(2,1)S(1)}, u32[]{:S(2)}, u32[]{:S(2)}) async-start(bf16[16,64,128]{2,1,0:T(8,128)(2,1)} %shard_map.51), calls=%async_computation.1 | async-start | bytes 524288 | tf_op jit(solution)/shard_map/all_to_all | solution.py:264
  56.5 1.8 %collective-permute-start.11 = (bf16[64,1024]{1,0:T(8,128)(2,1)S(1)}, bf16[64,1024]{1,0:T(8,128)(2,1)S(1)}, u32[]{:S(2)}, u32[]{:S(2)}) collective-permute-start(bf16[64,1024]{1,0:T(8,128)(2,1)S(1)} %get-tuple-element.44), channel_id=1, source_target_pairs={{0,12},{1,13},{2,14},{3,15},{4,8},{5,9},{6,10},{7,11},{8,4},{9,5},... | collective-permute-start | bytes 393224 | tf_op jit(solution)/shard_map/ppermute | solution.py:50
  58.9 3.2 %all-to-all-done.1 = bf16[16,64,128]{2,1,0:T(8,128)(2,1)S(1)} async-done(((bf16[16,64,128]{2,1,0:T(8,128)(2,1)}), bf16[16,64,128]{2,1,0:T(8,128)(2,1)S(1)}, u32[]{:S(2)}, u32[]{:S(2)}) %all-to-all-start.1) | async-done | bytes 262176 | tf_op jit(solution)/shard_map/all_to_all | solution.py:264
  62.1 1.7 %collective-permute-done.12.d = bf16[64,1024]{1,0:T(8,128)(2,1)S(1)} collective-permute-done((bf16[64,1024]{1,0:T(8,128)(2,1)S(1)}, bf16[64,1024]{1,0:T(8,128)(2,1)S(1)}, u32[]{:S(2)}, u32[]{:S(2)}) %collective-permute-start.12) | collective-permute-done | bytes 131104 | tf_op jit(solution)/shard_map/ppermute | solution.py:50
  63.9 5.1 %collective-permute-start.13 = (bf16[64,1024]{1,0:T(8,128)(2,1)S(1)}, bf16[64,1024]{1,0:T(8,128)(2,1)S(1)}, u32[]{:S(2)}, u32[]{:S(2)}) collective-permute-start(bf16[64,1024]{1,0:T(8,128)(2,1)S(1)} %shard_map.49.own), channel_id=1, source_target_pairs={{0,16},{16,0},{1,17},{17,1},{2,18},{18,2},{3,19},{19,3},{4,20},{20... | collective-permute-start | bytes 393224 | tf_op jit(solution)/shard_map/ppermute | solution.py:39
  69.2 3.0 %collective-permute-done.13.got = bf16[64,1024]{1,0:T(8,128)(2,1)S(1)} collective-permute-done((bf16[64,1024]{1,0:T(8,128)(2,1)S(1)}, bf16[64,1024]{1,0:T(8,128)(2,1)S(1)}, u32[]{:S(2)}, u32[]{:S(2)}) %collective-permute-start.13) | collective-permute-done | bytes 131104 | tf_op jit(solution)/shard_map/ppermute | solution.py:39
  72.3 1.6 %shard_map.52.refs_0_ = bf16[64,1024]{1,0:T(8,128)(2,1)S(1)} custom-call(s32[10]{0:T(128)S(1)} %stack.63.base, bf16[64,1024]{1,0:T(8,128)(2,1)S(1)} %shard_map.49.own, bf16[64,1024]{1,0:T(8,128)(2,1)S(1)} %collective-permute-done.13.got, f32[64,128]{1,0:T(8,128)S(1)} %get-tuple-element.70.cosine, f32[64,128]{1,0:T(8,128)S(1)} %get-tuple-element.71.sine_v, ...), custom_call_target="tpu_custom_call" | custom-call | tf_op jit(solution)/shard_map/pallas_call | solution.py:188
  73.8 2.1 %collective-permute-start.17 = (bf16[64,1024]{1,0:T(8,128)(2,1)S(1)}, bf16[64,1024]{1,0:T(8,128)(2,1)S(1)}, u32[]{:S(2)}, u32[]{:S(2)}) collective-permute-start(bf16[64,1024]{1,0:T(8,128)(2,1)S(1)} %shard_map.52.refs_0_), channel_id=1, source_target_pairs={{0,1},{1,0},{2,3},{3,2},{4,5},{5,4},{6,7},{7,6},{8,9},{9,8},{10,11... | collective-permute-start | bytes 393224 | tf_op jit(solution)/shard_map/ppermute | solution.py:50
  78.3 2.7 %collective-permute-done.18.refs_2_ = bf16[64,1024]{1,0:T(8,128)(2,1)S(1)} collective-permute-done((bf16[64,1024]{1,0:T(8,128)(2,1)S(1)}, bf16[64,1024]{1,0:T(8,128)(2,1)S(1)}, u32[]{:S(2)}, u32[]{:S(2)}) %collective-permute-start.18) | collective-permute-done | bytes 131104 | tf_op jit(solution)/shard_map/ppermute | solution.py:50
  81.0 1.5 %collective-permute-done.19.refs_3_ = bf16[64,1024]{1,0:T(8,128)(2,1)S(1)} collective-permute-done((bf16[64,1024]{1,0:T(8,128)(2,1)S(1)}, bf16[64,1024]{1,0:T(8,128)(2,1)S(1)}, u32[]{:S(2)}, u32[]{:S(2)}) %collective-permute-start.19) | collective-permute-done | bytes 131104 | tf_op jit(solution)/shard_map/ppermute | solution.py:50
  86.3 4.6 %collective-permute-done.20.line = bf16[4,64,1024]{2,1,0:T(8,128)(2,1)S(1)} collective-permute-done((bf16[4,64,1024]{2,1,0:T(8,128)(2,1)S(1)}, bf16[4,64,1024]{2,1,0:T(8,128)(2,1)S(1)}, u32[]{:S(2)}, u32[]{:S(2)}) %collective-permute-start.20) | collective-permute-done | bytes 524320 | tf_op jit(solution)/shard_map/ppermute | solution.py:50
  91.4 7.2 %collective-permute-done.21.line = bf16[4,64,1024]{2,1,0:T(8,128)(2,1)S(1)} collective-permute-done((bf16[4,64,1024]{2,1,0:T(8,128)(2,1)S(1)}, bf16[4,64,1024]{2,1,0:T(8,128)(2,1)S(1)}, u32[]{:S(2)}, u32[]{:S(2)}) %collective-permute-start.21) | collective-permute-done | bytes 524320 | tf_op jit(solution)/shard_map/ppermute | solution.py:50
  100.0 4.5 %collective-permute-start.23 = (bf16[512,512]{1,0:T(8,128)(2,1)S(1)}, bf16[512,512]{1,0:T(8,128)(2,1)S(1)}, u32[]{:S(2)}, u32[]{:S(2)}) collective-permute-start(bf16[512,512]{1,0:T(8,128)(2,1)S(1)} %bitcast.20), channel_id=1, source_target_pairs={{0,32},{32,0},{1,33},{33,1},{2,34},{34,2},{3,35},{35,3},{4,36},{36... | collective-permute-start | bytes 1572872 | tf_op jit(solution)/shard_map/ppermute | solution.py:39
  104.5 1.5 %collective-permute-done.23.got = bf16[512,512]{1,0:T(8,128)(2,1)S(1)} collective-permute-done((bf16[512,512]{1,0:T(8,128)(2,1)S(1)}, bf16[512,512]{1,0:T(8,128)(2,1)S(1)}, u32[]{:S(2)}, u32[]{:S(2)}) %collective-permute-start.23) | collective-permute-done | bytes 524320 | tf_op jit(solution)/shard_map/ppermute | solution.py:39
  106.2 3.9 %collective-permute-start.26 = (bf16[128,512]{1,0:T(8,128)(2,1)S(1)}, bf16[128,512]{1,0:T(8,128)(2,1)S(1)}, u32[]{:S(2)}, u32[]{:S(2)}) collective-permute-start(bf16[128,512]{1,0:T(8,128)(2,1)S(1)} %get-tuple-element.58), channel_id=1, source_target_pairs={{0,64},{64,0},{128,192},{192,128},{1,65},{65,1},{129,193},{193,129... | collective-permute-start | bytes 393224 | tf_op jit(solution)/shard_map/ppermute | solution.py:39
  113.6 7.6 %collective-permute-done.25 = bf16[128,512]{1,0:T(8,128)(2,1)S(1)} collective-permute-done((bf16[128,512]{1,0:T(8,128)(2,1)S(1)}, bf16[128,512]{1,0:T(8,128)(2,1)S(1)}, u32[]{:S(2)}, u32[]{:S(2)}) %collective-permute-start.25) | collective-permute-done | bytes 131104 | tf_op jit(solution)/shard_map/ppermute | solution.py:39
  (76 shorter events, 32.1 us)
Async XLA Ops:
  0.0 6.1 %collective-permute-start.3 = (bf16[128,512]{1,0:T(8,128)(2,1)}, bf16[128,512]{1,0:T(8,128)(2,1)S(1)}, u32[]{:S(2)}, u32[]{:S(2)}) collective-permute-start(bf16[128,512]{1,0:T(8,128)(2,1)} %refs_0_.1), channel_id=1, source_target_pairs={{0,32},{32,0},{1,33},{33,1},{2,34},{34,2},{3,35},{35,3},{4,36},{36... | collective-permute-start | bytes 393224 | tf_op jit(solution)/shard_map/ppermute | solution.py:39
  3.2 11.9 %collective-permute-start = (bf16[128,512]{1,0:T(8,128)(2,1)}, bf16[128,512]{1,0:T(8,128)(2,1)S(1)}, u32[]{:S(2)}, u32[]{:S(2)}) collective-permute-start(bf16[128,512]{1,0:T(8,128)(2,1)} %refs_0_.1), channel_id=1, source_target_pairs={{0,128},{64,192},{128,0},{192,64},{1,129},{65,193},{129,1},{193,65... | collective-permute-start | bytes 393224 | tf_op jit(solution)/shard_map/ppermute | solution.py:39
  4.5 10.7 %collective-permute-start.1 = (bf16[128,512]{1,0:T(8,128)(2,1)}, bf16[128,512]{1,0:T(8,128)(2,1)S(1)}, u32[]{:S(2)}, u32[]{:S(2)}) collective-permute-start(bf16[128,512]{1,0:T(8,128)(2,1)} %refs_0_.1), channel_id=1, source_target_pairs={{0,192},{64,128},{128,64},{192,0},{1,193},{65,129},{129,65},{193,1... | collective-permute-start | bytes 393224 | tf_op jit(solution)/shard_map/ppermute | solution.py:39
  5.9 10.2 %collective-permute-start.2 = (bf16[128,512]{1,0:T(8,128)(2,1)}, bf16[128,512]{1,0:T(8,128)(2,1)S(1)}, u32[]{:S(2)}, u32[]{:S(2)}) collective-permute-start(bf16[128,512]{1,0:T(8,128)(2,1)} %refs_0_.1), channel_id=1, source_target_pairs={{0,64},{64,0},{128,192},{192,128},{1,65},{65,1},{129,193},{193,129... | collective-permute-start | bytes 393224 | tf_op jit(solution)/shard_map/ppermute | solution.py:39
  23.8 13.9 %all-to-all-start = ((bf16[16,64,128]{2,1,0:T(8,128)(2,1)}), bf16[16,64,128]{2,1,0:T(8,128)(2,1)S(1)}, u32[]{:S(2)}, u32[]{:S(2)}) async-start(bf16[16,64,128]{2,1,0:T(8,128)(2,1)} %get-tuple-element.46), calls=%async_computation | async-start | bytes 524288 | tf_op jit(solution)/shard_map/all_to_all | solution.py:255
  29.6 24.7 %collective-permute-start.7 = (bf16[4,64,1024]{2,1,0:T(8,128)(2,1)}, bf16[4,64,1024]{2,1,0:T(8,128)(2,1)S(1)}, u32[]{:S(2)}, u32[]{:S(2)}) collective-permute-start(bf16[4,64,1024]{2,1,0:T(8,128)(2,1)} %copy-done.9), channel_id=1, source_target_pairs={{0,1},{1,0},{2,3},{3,2},{4,5},{5,4},{6,7},{7,6},{8,9},{9,8},{10,11... | collective-permute-start | bytes 1572872 | tf_op jit(solution)/shard_map/ppermute | solution.py:50
  31.1 23.2 %collective-permute-start.8 = (bf16[4,64,1024]{2,1,0:T(8,128)(2,1)}, bf16[4,64,1024]{2,1,0:T(8,128)(2,1)S(1)}, u32[]{:S(2)}, u32[]{:S(2)}) collective-permute-start(bf16[4,64,1024]{2,1,0:T(8,128)(2,1)} %copy-done.8), channel_id=1, source_target_pairs={{0,3},{1,2},{2,1},{3,0},{4,7},{5,6},{6,5},{7,4},{8,11},{9,10},{10,... | collective-permute-start | bytes 1572872 | tf_op jit(solution)/shard_map/ppermute | solution.py:50
  32.9 21.5 %collective-permute-start.9 = (bf16[4,64,1024]{2,1,0:T(8,128)(2,1)S(1)}, bf16[4,64,1024]{2,1,0:T(8,128)(2,1)S(1)}, u32[]{:S(2)}, u32[]{:S(2)}) collective-permute-start(bf16[4,64,1024]{2,1,0:T(8,128)(2,1)S(1)} %copy-done.7), channel_id=1, source_target_pairs={{0,2},{1,3},{2,0},{3,1},{4,6},{5,7},{6,4},{7,5},{8,10},{9,11},{10,... | collective-permute-start | bytes 1572872 | tf_op jit(solution)/shard_map/ppermute | solution.py:50
  37.8 11.4 %collective-permute-start.14 = (bf16[64,128]{1,0:T(8,128)(2,1)S(1)}, bf16[64,128]{1,0:T(8,128)(2,1)S(1)}, u32[]{:S(2)}, u32[]{:S(2)}) collective-permute-start(bf16[64,128]{1,0:T(8,128)(2,1)S(1)} %shard_map.50), channel_id=1, source_target_pairs={{0,0},{32,64},{64,128},{96,192},{128,32},{160,96},{192,160},{224,2... | collective-permute-start | bytes 49160 | tf_op jit(solution)/shard_map/ppermute | solution.py:259
  43.2 6.8 %collective-permute-start.15 = (bf16[64,128]{1,0:T(8,128)(2,1)S(1)}, bf16[64,128]{1,0:T(8,128)(2,1)S(1)}, u32[]{:S(2)}, u32[]{:S(2)}) collective-permute-start(bf16[64,128]{1,0:T(8,128)(2,1)S(1)} %shard_map.50), channel_id=1, source_target_pairs={{0,16},{16,0},{32,80},{48,64},{64,144},{80,128},{96,208},{112,192}... | collective-permute-start | bytes 49160 | tf_op jit(solution)/shard_map/ppermute | solution.py:260
  50.8 11.3 %all-to-all-start.1 = ((bf16[16,64,128]{2,1,0:T(8,128)(2,1)}), bf16[16,64,128]{2,1,0:T(8,128)(2,1)S(1)}, u32[]{:S(2)}, u32[]{:S(2)}) async-start(bf16[16,64,128]{2,1,0:T(8,128)(2,1)} %shard_map.51), calls=%async_computation.1 | async-start | bytes 524288 | tf_op jit(solution)/shard_map/all_to_all | solution.py:264
  55.2 7.0 %collective-permute-start.10 = (bf16[64,1024]{1,0:T(8,128)(2,1)S(1)}, bf16[64,1024]{1,0:T(8,128)(2,1)S(1)}, u32[]{:S(2)}, u32[]{:S(2)}) collective-permute-start(bf16[64,1024]{1,0:T(8,128)(2,1)S(1)} %get-tuple-element.43), channel_id=1, source_target_pairs={{0,4},{1,5},{2,6},{3,7},{4,0},{5,1},{6,2},{7,3},{8,12},{9,13},{10,... | collective-permute-start | bytes 393224 | tf_op jit(solution)/shard_map/ppermute | solution.py:50
  56.5 5.7 %collective-permute-start.11 = (bf16[64,1024]{1,0:T(8,128)(2,1)S(1)}, bf16[64,1024]{1,0:T(8,128)(2,1)S(1)}, u32[]{:S(2)}, u32[]{:S(2)}) collective-permute-start(bf16[64,1024]{1,0:T(8,128)(2,1)S(1)} %get-tuple-element.44), channel_id=1, source_target_pairs={{0,12},{1,13},{2,14},{3,15},{4,8},{5,9},{6,10},{7,11},{8,4},{9,5},... | collective-permute-start | bytes 393224 | tf_op jit(solution)/shard_map/ppermute | solution.py:50
  58.3 5.6 %collective-permute-start.12 = (bf16[64,1024]{1,0:T(8,128)(2,1)S(1)}, bf16[64,1024]{1,0:T(8,128)(2,1)S(1)}, u32[]{:S(2)}, u32[]{:S(2)}) collective-permute-start(bf16[64,1024]{1,0:T(8,128)(2,1)S(1)} %get-tuple-element.45), channel_id=1, source_target_pairs={{0,8},{1,9},{2,10},{3,11},{4,12},{5,13},{6,14},{7,15},{8,0},{9,1},... | collective-permute-start | bytes 393224 | tf_op jit(solution)/shard_map/ppermute | solution.py:50
  62.1 7.1 %collective-permute-start.16 = (bf16[1024,128]{1,0:T(8,128)(2,1)S(1)}, bf16[1024,128]{1,0:T(8,128)(2,1)S(1)}, u32[]{:S(2)}, u32[]{:S(2)}) collective-permute-start(bf16[1024,128]{1,0:T(8,128)(2,1)S(1)} %bitcast.17), channel_id=1, source_target_pairs={{0,32},{32,0},{1,33},{33,1},{2,34},{34,2},{3,35},{35,3},{4,36},{36... | collective-permute-start | bytes 786440 | tf_op jit(solution)/shard_map/ppermute | solution.py:39
  63.9 8.3 %collective-permute-start.13 = (bf16[64,1024]{1,0:T(8,128)(2,1)S(1)}, bf16[64,1024]{1,0:T(8,128)(2,1)S(1)}, u32[]{:S(2)}, u32[]{:S(2)}) collective-permute-start(bf16[64,1024]{1,0:T(8,128)(2,1)S(1)} %shard_map.49.own), channel_id=1, source_target_pairs={{0,16},{16,0},{1,17},{17,1},{2,18},{18,2},{3,19},{19,3},{4,20},{20... | collective-permute-start | bytes 393224 | tf_op jit(solution)/shard_map/ppermute | solution.py:39
  77.2 5.3 %collective-permute-start.19 = (bf16[64,1024]{1,0:T(8,128)(2,1)S(1)}, bf16[64,1024]{1,0:T(8,128)(2,1)S(1)}, u32[]{:S(2)}, u32[]{:S(2)}) collective-permute-start(bf16[64,1024]{1,0:T(8,128)(2,1)S(1)} %shard_map.52.refs_0_), channel_id=1, source_target_pairs={{0,2},{1,3},{2,0},{3,1},{4,6},{5,7},{6,4},{7,5},{8,10},{9,11},{10,... | collective-permute-start | bytes 393224 | tf_op jit(solution)/shard_map/ppermute | solution.py:50
  82.5 8.4 %collective-permute-start.20 = (bf16[4,64,1024]{2,1,0:T(8,128)(2,1)S(1)}, bf16[4,64,1024]{2,1,0:T(8,128)(2,1)S(1)}, u32[]{:S(2)}, u32[]{:S(2)}) collective-permute-start(bf16[4,64,1024]{2,1,0:T(8,128)(2,1)S(1)} %shard_map.53.line), channel_id=1, source_target_pairs={{0,4},{1,5},{2,6},{3,7},{4,0},{5,1},{6,2},{7,3},{8,12},{9,13},{10,... | collective-permute-start | bytes 1572872 | tf_op jit(solution)/shard_map/ppermute | solution.py:50
  83.4 15.2 %collective-permute-start.21 = (bf16[4,64,1024]{2,1,0:T(8,128)(2,1)S(1)}, bf16[4,64,1024]{2,1,0:T(8,128)(2,1)S(1)}, u32[]{:S(2)}, u32[]{:S(2)}) collective-permute-start(bf16[4,64,1024]{2,1,0:T(8,128)(2,1)S(1)} %shard_map.53.line), channel_id=1, source_target_pairs={{0,12},{1,13},{2,14},{3,15},{4,8},{5,9},{6,10},{7,11},{8,4},{9,5},... | collective-permute-start | bytes 1572872 | tf_op jit(solution)/shard_map/ppermute | solution.py:50
  84.6 14.4 %collective-permute-start.22 = (bf16[4,64,1024]{2,1,0:T(8,128)(2,1)S(1)}, bf16[4,64,1024]{2,1,0:T(8,128)(2,1)S(1)}, u32[]{:S(2)}, u32[]{:S(2)}) collective-permute-start(bf16[4,64,1024]{2,1,0:T(8,128)(2,1)S(1)} %shard_map.53.line), channel_id=1, source_target_pairs={{0,8},{1,9},{2,10},{3,11},{4,12},{5,13},{6,14},{7,15},{8,0},{9,1},... | collective-permute-start | bytes 1572872 | tf_op jit(solution)/shard_map/ppermute | solution.py:50
  100.0 6.0 %collective-permute-start.23 = (bf16[512,512]{1,0:T(8,128)(2,1)S(1)}, bf16[512,512]{1,0:T(8,128)(2,1)S(1)}, u32[]{:S(2)}, u32[]{:S(2)}) collective-permute-start(bf16[512,512]{1,0:T(8,128)(2,1)S(1)} %bitcast.20), channel_id=1, source_target_pairs={{0,32},{32,0},{1,33},{33,1},{2,34},{34,2},{3,35},{35,3},{4,36},{36... | collective-permute-start | bytes 1572872 | tf_op jit(solution)/shard_map/ppermute | solution.py:39
  106.2 7.4 %collective-permute-start.26 = (bf16[128,512]{1,0:T(8,128)(2,1)S(1)}, bf16[128,512]{1,0:T(8,128)(2,1)S(1)}, u32[]{:S(2)}, u32[]{:S(2)}) collective-permute-start(bf16[128,512]{1,0:T(8,128)(2,1)S(1)} %get-tuple-element.58), channel_id=1, source_target_pairs={{0,64},{64,0},{128,192},{192,128},{1,65},{65,1},{129,193},{193,129... | collective-permute-start | bytes 393224 | tf_op jit(solution)/shard_map/ppermute | solution.py:39
  110.1 11.2 %collective-permute-start.25 = (bf16[128,512]{1,0:T(8,128)(2,1)S(1)}, bf16[128,512]{1,0:T(8,128)(2,1)S(1)}, u32[]{:S(2)}, u32[]{:S(2)}) collective-permute-start(bf16[128,512]{1,0:T(8,128)(2,1)S(1)} %get-tuple-element.57), channel_id=1, source_target_pairs={{0,128},{64,192},{128,0},{192,64},{1,129},{65,193},{129,1},{193,65... | collective-permute-start | bytes 393224 | tf_op jit(solution)/shard_map/ppermute | solution.py:39
  111.0 10.2 %collective-permute-start.24 = (bf16[128,512]{1,0:T(8,128)(2,1)S(1)}, bf16[128,512]{1,0:T(8,128)(2,1)S(1)}, u32[]{:S(2)}, u32[]{:S(2)}) collective-permute-start(bf16[128,512]{1,0:T(8,128)(2,1)S(1)} %get-tuple-element.56), channel_id=1, source_target_pairs={{0,192},{64,128},{128,64},{192,0},{1,193},{65,129},{129,65},{193,1... | collective-permute-start | bytes 393224 | tf_op jit(solution)/shard_map/ppermute | solution.py:39
  (15 other events, 64.9 us)

commit v11 on v10

--- a/solution.py
+++ b/solution.py
@@ -50,33 +50,35 @@
     return lax.ppermute(block, ("core", *PLANE), pairs)
 
 
-def project(block, w_query, w_kv, chunks, keyvals, k):
+def project(block, weight, chunks, k):
     size = chunks.shape[1]
-    query = jnp.dot(block[...], w_query[...], preferred_element_type=F32).astype(BF16)
-    keyval = jnp.dot(block[...], w_kv[...], preferred_element_type=F32).astype(BF16)
+    product = jnp.dot(block[...], weight[...], preferred_element_type=F32).astype(BF16)
     for b in range(2):
-        part = slice(b * size, (b + 1) * size)
-        chunks[k + b] = query[part]
-        keyvals[k + b] = keyval[part]
+        chunks[k + b] = product[b * size : (b + 1) * size]
 
 
 def early_kernel(*refs):
     blocks, w_query, w_kv, out, keyvals = refs[:2], *refs[2:]
     for i, block in enumerate(blocks):
-        project(block, w_query, w_kv, out, keyvals, 2 * i)
-
-
-def late_kernel(place, *refs):
-    blocks, w_query, w_kv, early, early_kv = refs[:6], *refs[6:10]
-    outs, keyvals, chunks = refs[10:14], refs[14], refs[15]
+        project(block, w_query, out, 2 * i)
+        project(block, w_kv, keyvals, 2 * i)
+
+
+def fill(blocks, weight, early, chunks):
     for side in range(2):
         for b in range(2):
             chunks[8 * side + b] = early[2 * side + b]
-            keyvals[8 * side + b] = early_kv[2 * side + b]
         for i in range(3):
-            project(
-                blocks[3 * side + i], w_query, w_kv, chunks, keyvals, 8 * side + 2 * FAR[i]
-            )
+            project(blocks[3 * side + i], weight, chunks, 8 * side + 2 * FAR[i])
+
+
+def keyval_kernel(*refs):
+    fill(refs[:6], *refs[6:])
+
+
+def query_kernel(place, *refs):
+    outs, chunks = refs[8:12], refs[12]
+    fill(refs[:6], refs[6], refs[7], chunks)
     for s in range(4):
         for j in range(4):
             outs[s][j] = chunks[chunk_at(place, place[0] ^ s, j)]
@@ -95,6 +97,11 @@
 
 def join_kernel(a, b, c, d, out):
     total = a[...] + b[...].astype(F32) + c[...].astype(F32) + d[...].astype(F32)
+    out[...] = total.astype(BF16)
+
+
+def total_kernel(a, b, c, d, out):
+    total = a[...].astype(F32) + b[...].astype(F32) + c[...].astype(F32) + d[...].astype(F32)
     out[...] = total.astype(BF16)
 
 
@@ -237,18 +244,14 @@
         [tokens, near, w_query, w_keyval],
     )
     *far, early = lax.optimization_barrier((*far, early))
-    *parts, kv_parts = call(
-        late_kernel,
-        [(4, per_chunk, width)] * 4 + [(Y * X, per_chunk, HD)],
-        [
-            place,
-            *far,
-            *[partner(block, "core", 1) for block in far],
-            w_query,
-            w_keyval,
-            early,
-            early_kv,
-        ],
+    far += [partner(block, "core", 1) for block in far]
+    (kv_parts,) = call(
+        keyval_kernel, [(Y * X, per_chunk, HD)], [*far, w_keyval, early_kv]
+    )
+    parts = call(
+        query_kernel,
+        [(4, per_chunk, width)] * 4,
+        [place, *far, w_query, early],
         [SMEM],
         [pltpu.VMEM((Y * X, per_chunk, width), BF16)],
     )
@@ -261,9 +264,6 @@
         kv, (*ROW, "zh"), [(2 * e + h, 2 * r + 1 - h) for e, r in moves for h in range(2)]
     )
     (kv_block,) = call(keys_kernel, [(Y * X, per_chunk, HD)], [here, across, key_cos, key_sin])
-    kv_own = lax.all_to_all(kv_block, PLANE, 0, 0, tiled=True).reshape(total, HD)
-    kv_other = partner(kv_own, "core", 1)
-
     got = [across_plane(parts[s], s, False) for s in STEPS[1:]]
     halves = call(
         halve_kernel,
@@ -272,6 +272,8 @@
         [SMEM],
     )
     got = [across_plane(halves[t], t, True) for t in STEPS[1:]]
+    kv_own = lax.all_to_all(kv_block, PLANE, 0, 0, tiled=True).reshape(total, HD)
+    kv_other = partner(kv_own, "core", 1)
     (own,) = call(join_kernel, [(per_chunk, width)], [halves[0], *got])
     got = partner(own, "zh", 1)
 
@@ -306,8 +308,9 @@
     )
     kept, sent = kept.reshape(half, features), sent.reshape(half, features)
     chip = call(chip_kernel, [(per_row, features)] * 4, [kept, partner(sent, "core", 1)])
-    blocks = [chip[0]] + [partner(chip[s], "zl", s) for s in (3, 2, 1)]
-    return functools.reduce(jnp.add, [b.astype(F32) for b in blocks]).astype(BF16)
+    blocks = [chip[0]] + [partner(chip[s], "zl", s) for s in FAR]
+    (result,) = call(total_kernel, [(per_row, features)], blocks)
+    return result
 
 
 def solution(mesh):

time: 124 us -> 119 us (0.960)
  waiting for transfers between devices: 46.6 us -> 41.4 us
  local copies, waits for them, and re-layouts: 5.58 us -> 3.13 us
  starting transfers between devices: 59.4 us -> 61.7 us
  Pallas kernels: 8.89 us -> 10.8 us
    all_to_all x1, waiting for transfers between devices: 3.99 us -> 1.27 us  [shards(): kv_parts = lax.all_to_all(kv_parts, PLANE, 0, 0, tiled=True)]
    unnamed x20 -> x12, local copies, waits for them, and re-layouts: 5.49 us -> 3.05 us
    ppermute x13, waiting for transfers between devices: 20.8 us -> 18.5 us  [partner(): return lax.ppermute(block, axis, [(i, i ^ step) for i in range(size)])]
    pallas_call x13 -> x15, Pallas kernels: 8.89 us -> 10.8 us  [call(): pl.pallas_call(kernel, out_shape=[s if isinstance(s, jax.ShapeDtypeStruct...]
    all_to_all x1, starting transfers between devices: 3.53 us -> 5.13 us  [shards(): lax.all_to_all(kv_block, PLANE, 0, 0, tiled=True).reshape(total, HD)]
  transfers between devices with their start and end apart: 29 -> 29, of which waited for: 17 -> 18; matrix products, arithmetic and copies ran while one was open for 1% -> 1% of each run, Pallas kernels for 3% -> 5%
where the time goes in v11:
time: 119 us; the launch traced here: 118 us
  starting transfers between devices  61.7 us (52%)
  waiting for transfers between devices  41.4 us (35%)
  Pallas kernels  10.8 us (9%)
  local copies, waits for them, and re-layouts  3.13 us (3%)
    ppermute x13, starting transfers between devices, partner(): return lax.ppermute(block, axis, [(i, i ^ step) for i in range(size)])  23.8 us
    ppermute x13, waiting for transfers between devices, partner(): return lax.ppermute(block, axis, [(i, i ^ step) for i in range(size)])  18.5 us
    ppermute x12, waiting for transfers between devices, across_plane(): return lax.ppermute(block, ('core', *PLANE), pairs)  17.4 us
    ppermute x12, starting transfers between devices, across_plane(): return lax.ppermute(block, ('core', *PLANE), pairs)  15.9 us
    pallas_call x15, Pallas kernels, call(): pl.pallas_call(kernel, out_shape=[s if isinstance(s, jax.ShapeDtypeStruct...  10.8 us
    ppermute x1, starting transfers between devices, shards(): lax.ppermute(kv, (*ROW, 'zh'), [(2 * e + h, 2 * r + 1 - h) for e, r in mo...  5.95 us
    all_to_all x1, starting transfers between devices, shards(): kv_parts = lax.all_to_all(kv_parts, PLANE, 0, 0, tiled=True)  5.65 us
    ppermute x1, starting transfers between devices, shards(): here = lax.ppermute(kv, ROW, moves)  5.31 us
  transfers between devices with their start and end apart: 29, of which 18 were waited for; matrix products, arithmetic and copies ran while one was open for 1% of the time, Pallas kernels for 5%

profile of v11, /device:TPU:1, one launch (start us, length us, event | category | flops | bytes accessed | tf_op | source)
XLA Modules:
  0.0 117.7 jit_solution(12307152045472748915)
XLA Ops:
  0.0 3.2 %collective-permute-start.3 = (bf16[128,512]{1,0:T(8,128)(2,1)}, bf16[128,512]{1,0:T(8,128)(2,1)S(1)}, u32[]{:S(2)}, u32[]{:S(2)}) collective-permute-start(bf16[128,512]{1,0:T(8,128)(2,1)} %refs_0_.1), channel_id=1, source_target_pairs={{0,32},{32,0},{1,33},{33,1},{2,34},{34,2},{3,35},{35,3},{4,36},{36... | collective-permute-start | bytes 393224 | tf_op jit(solution)/shard_map/ppermute | solution.py:39
  9.7 5.5 %collective-permute-done.refs_0_ = bf16[128,512]{1,0:T(8,128)(2,1)S(1)} collective-permute-done((bf16[128,512]{1,0:T(8,128)(2,1)}, bf16[128,512]{1,0:T(8,128)(2,1)S(1)}, u32[]{:S(2)}, u32[]{:S(2)}) %collective-permute-start) | collective-permute-done | bytes 131104 | tf_op jit(solution)/shard_map/ppermute | solution.py:39
  19.8 5.6 %all-to-all-start = ((bf16[16,64,128]{2,1,0:T(8,128)(2,1)}), bf16[16,64,128]{2,1,0:T(8,128)(2,1)S(1)}, u32[]{:S(2)}, u32[]{:S(2)}) async-start(bf16[16,64,128]{2,1,0:T(8,128)(2,1)} %shard_map.50), calls=%async_computation | async-start | bytes 524288 | tf_op jit(solution)/shard_map/all_to_all | solution.py:258
  25.6 2.7 %shard_map.47 = (bf16[4,64,1024]{2,1,0:T(8,128)(2,1)S(1)}, bf16[4,64,1024]{2,1,0:T(8,128)(2,1)}, bf16[4,64,1024]{2,1,0:T(8,128)(2,1)}, bf16[4,64,1024]{2,1,0:T(8,128)(2,1)}) custom-call(s32[4]{0:T(128)S(1)} %pad_add_fusion.place, bf16[128,512]{1,0:T(8,128)(2,1)S(1)} %collective-permute-done.refs_0_, bf16[128,512]{1,0:T(8,128)(2,1)S(1)} %collective-permute-done.1.refs_1_, ...), custom_call_target="tpu_custom_call" | custom-call | tf_op jit(solution)/shard_map/pallas_call | solution.py:195
  29.7 1.8 %collective-permute-start.8 = (bf16[4,64,1024]{2,1,0:T(8,128)(2,1)}, bf16[4,64,1024]{2,1,0:T(8,128)(2,1)S(1)}, u32[]{:S(2)}, u32[]{:S(2)}) collective-permute-start(bf16[4,64,1024]{2,1,0:T(8,128)(2,1)} %get-tuple-element.38), channel_id=1, source_target_pairs={{0,3},{1,2},{2,1},{3,0},{4,7},{5,6},{6,5},{7,4},{8,11},{9,10},{10,... | collective-permute-start | bytes 1572872 | tf_op jit(solution)/shard_map/ppermute | solution.py:50
  33.7 5.3 %collective-permute-start.14 = (bf16[64,128]{1,0:T(8,128)(2,1)S(1)}, bf16[64,128]{1,0:T(8,128)(2,1)S(1)}, u32[]{:S(2)}, u32[]{:S(2)}) collective-permute-start(bf16[64,128]{1,0:T(8,128)(2,1)S(1)} %shard_map.51), channel_id=1, source_target_pairs={{0,0},{32,64},{64,128},{96,192},{128,32},{160,96},{192,160},{224,2... | collective-permute-start | bytes 49160 | tf_op jit(solution)/shard_map/ppermute | solution.py:262
  39.0 5.9 %collective-permute-start.15 = (bf16[64,128]{1,0:T(8,128)(2,1)S(1)}, bf16[64,128]{1,0:T(8,128)(2,1)S(1)}, u32[]{:S(2)}, u32[]{:S(2)}) collective-permute-start(bf16[64,128]{1,0:T(8,128)(2,1)S(1)} %shard_map.51), channel_id=1, source_target_pairs={{0,16},{16,0},{32,80},{48,64},{64,144},{80,128},{96,208},{112,192}... | collective-permute-start | bytes 49160 | tf_op jit(solution)/shard_map/ppermute | solution.py:263
  46.6 5.1 %all-to-all-start.1 = ((bf16[16,64,128]{2,1,0:T(8,128)(2,1)}), bf16[16,64,128]{2,1,0:T(8,128)(2,1)S(1)}, u32[]{:S(2)}, u32[]{:S(2)}) async-start(bf16[16,64,128]{2,1,0:T(8,128)(2,1)} %shard_map.52), calls=%async_computation.1 | async-start | bytes 524288 | tf_op jit(solution)/shard_map/all_to_all | solution.py:275
  54.1 1.8 %collective-permute-start.11 = (bf16[64,1024]{1,0:T(8,128)(2,1)S(1)}, bf16[64,1024]{1,0:T(8,128)(2,1)S(1)}, u32[]{:S(2)}, u32[]{:S(2)}) collective-permute-start(bf16[64,1024]{1,0:T(8,128)(2,1)S(1)} %get-tuple-element.42), channel_id=1, source_target_pairs={{0,12},{1,13},{2,14},{3,15},{4,8},{5,9},{6,10},{7,11},{8,4},{9,5},... | collective-permute-start | bytes 393224 | tf_op jit(solution)/shard_map/ppermute | solution.py:50
  56.5 3.4 %all-to-all-done.1 = bf16[16,64,128]{2,1,0:T(8,128)(2,1)S(1)} async-done(((bf16[16,64,128]{2,1,0:T(8,128)(2,1)}), bf16[16,64,128]{2,1,0:T(8,128)(2,1)S(1)}, u32[]{:S(2)}, u32[]{:S(2)}) %all-to-all-start.1) | async-done | bytes 262176 | tf_op jit(solution)/shard_map/all_to_all | solution.py:275
  59.9 1.6 %collective-permute-done.12.d = bf16[64,1024]{1,0:T(8,128)(2,1)S(1)} collective-permute-done((bf16[64,1024]{1,0:T(8,128)(2,1)S(1)}, bf16[64,1024]{1,0:T(8,128)(2,1)S(1)}, u32[]{:S(2)}, u32[]{:S(2)}) %collective-permute-start.12) | collective-permute-done | bytes 131104 | tf_op jit(solution)/shard_map/ppermute | solution.py:50
  61.5 5.1 %collective-permute-start.13 = (bf16[64,1024]{1,0:T(8,128)(2,1)S(1)}, bf16[64,1024]{1,0:T(8,128)(2,1)S(1)}, u32[]{:S(2)}, u32[]{:S(2)}) collective-permute-start(bf16[64,1024]{1,0:T(8,128)(2,1)S(1)} %shard_map.49.own), channel_id=1, source_target_pairs={{0,16},{16,0},{1,17},{17,1},{2,18},{18,2},{3,19},{19,3},{4,20},{20... | collective-permute-start | bytes 393224 | tf_op jit(solution)/shard_map/ppermute | solution.py:39
  66.8 2.8 %collective-permute-done.13.got = bf16[64,1024]{1,0:T(8,128)(2,1)S(1)} collective-permute-done((bf16[64,1024]{1,0:T(8,128)(2,1)S(1)}, bf16[64,1024]{1,0:T(8,128)(2,1)S(1)}, u32[]{:S(2)}, u32[]{:S(2)}) %collective-permute-start.13) | collective-permute-done | bytes 131104 | tf_op jit(solution)/shard_map/ppermute | solution.py:39
  69.6 1.6 %shard_map.53.refs_0_ = bf16[64,1024]{1,0:T(8,128)(2,1)S(1)} custom-call(s32[10]{0:T(128)S(1)} %stack.63.base, bf16[64,1024]{1,0:T(8,128)(2,1)S(1)} %shard_map.49.own, bf16[64,1024]{1,0:T(8,128)(2,1)S(1)} %collective-permute-done.13.got, f32[64,128]{1,0:T(8,128)S(1)} %get-tuple-element.68.cosine, f32[64,128]{1,0:T(8,128)S(1)} %get-tuple-element.69.sine_v, ...), custom_call_target="tpu_custom_call" | custom-call | tf_op jit(solution)/shard_map/pallas_call | solution.py:195
  71.2 2.2 %collective-permute-start.17 = (bf16[64,1024]{1,0:T(8,128)(2,1)S(1)}, bf16[64,1024]{1,0:T(8,128)(2,1)S(1)}, u32[]{:S(2)}, u32[]{:S(2)}) collective-permute-start(bf16[64,1024]{1,0:T(8,128)(2,1)S(1)} %shard_map.53.refs_0_), channel_id=1, source_target_pairs={{0,1},{1,0},{2,3},{3,2},{4,5},{5,4},{6,7},{7,6},{8,9},{9,8},{10,11... | collective-permute-start | bytes 393224 | tf_op jit(solution)/shard_map/ppermute | solution.py:50
  73.4 1.6 %collective-permute-start.18 = (bf16[64,1024]{1,0:T(8,128)(2,1)S(1)}, bf16[64,1024]{1,0:T(8,128)(2,1)S(1)}, u32[]{:S(2)}, u32[]{:S(2)}) collective-permute-start(bf16[64,1024]{1,0:T(8,128)(2,1)S(1)} %shard_map.53.refs_0_), channel_id=1, source_target_pairs={{0,3},{1,2},{2,1},{3,0},{4,7},{5,6},{6,5},{7,4},{8,11},{9,10},{10,... | collective-permute-start | bytes 393224 | tf_op jit(solution)/shard_map/ppermute | solution.py:50
  76.1 2.3 %collective-permute-done.18.refs_2_ = bf16[64,1024]{1,0:T(8,128)(2,1)S(1)} collective-permute-done((bf16[64,1024]{1,0:T(8,128)(2,1)S(1)}, bf16[64,1024]{1,0:T(8,128)(2,1)S(1)}, u32[]{:S(2)}, u32[]{:S(2)}) %collective-permute-start.18) | collective-permute-done | bytes 131104 | tf_op jit(solution)/shard_map/ppermute | solution.py:50
  78.4 1.9 %collective-permute-done.19.refs_3_ = bf16[64,1024]{1,0:T(8,128)(2,1)S(1)} collective-permute-done((bf16[64,1024]{1,0:T(8,128)(2,1)S(1)}, bf16[64,1024]{1,0:T(8,128)(2,1)S(1)}, u32[]{:S(2)}, u32[]{:S(2)}) %collective-permute-start.19) | collective-permute-done | bytes 131104 | tf_op jit(solution)/shard_map/ppermute | solution.py:50
  84.2 4.6 %collective-permute-done.20.line = bf16[4,64,1024]{2,1,0:T(8,128)(2,1)S(1)} collective-permute-done((bf16[4,64,1024]{2,1,0:T(8,128)(2,1)S(1)}, bf16[4,64,1024]{2,1,0:T(8,128)(2,1)S(1)}, u32[]{:S(2)}, u32[]{:S(2)}) %collective-permute-start.20) | collective-permute-done | bytes 524320 | tf_op jit(solution)/shard_map/ppermute | solution.py:50
  89.2 7.0 %collective-permute-done.21.line = bf16[4,64,1024]{2,1,0:T(8,128)(2,1)S(1)} collective-permute-done((bf16[4,64,1024]{2,1,0:T(8,128)(2,1)S(1)}, bf16[4,64,1024]{2,1,0:T(8,128)(2,1)S(1)}, u32[]{:S(2)}, u32[]{:S(2)}) %collective-permute-start.21) | collective-permute-done | bytes 524320 | tf_op jit(solution)/shard_map/ppermute | solution.py:50
  97.7 5.2 %collective-permute-start.23 = (bf16[512,512]{1,0:T(8,128)(2,1)S(1)}, bf16[512,512]{1,0:T(8,128)(2,1)S(1)}, u32[]{:S(2)}, u32[]{:S(2)}) collective-permute-start(bf16[512,512]{1,0:T(8,128)(2,1)S(1)} %bitcast.20), channel_id=1, source_target_pairs={{0,32},{32,0},{1,33},{33,1},{2,34},{34,2},{3,35},{35,3},{4,36},{36... | collective-permute-start | bytes 1572872 | tf_op jit(solution)/shard_map/ppermute | solution.py:39
  104.5 2.6 %collective-permute-start.24 = (bf16[128,512]{1,0:T(8,128)(2,1)S(1)}, bf16[128,512]{1,0:T(8,128)(2,1)S(1)}, u32[]{:S(2)}, u32[]{:S(2)}) collective-permute-start(bf16[128,512]{1,0:T(8,128)(2,1)S(1)} %get-tuple-element.54), channel_id=1, source_target_pairs={{0,128},{64,192},{128,0},{192,64},{1,129},{65,193},{129,1},{193,65... | collective-permute-start | bytes 393224 | tf_op jit(solution)/shard_map/ppermute | solution.py:39
  107.1 3.1 %collective-permute-start.25 = (bf16[128,512]{1,0:T(8,128)(2,1)S(1)}, bf16[128,512]{1,0:T(8,128)(2,1)S(1)}, u32[]{:S(2)}, u32[]{:S(2)}) collective-permute-start(bf16[128,512]{1,0:T(8,128)(2,1)S(1)} %get-tuple-element.55), channel_id=1, source_target_pairs={{0,192},{64,128},{128,64},{192,0},{1,193},{65,129},{129,65},{193,1... | collective-permute-start | bytes 393224 | tf_op jit(solution)/shard_map/ppermute | solution.py:39
  110.5 5.8 %collective-permute-done.25.c = bf16[128,512]{1,0:T(8,128)(2,1)S(1)} collective-permute-done((bf16[128,512]{1,0:T(8,128)(2,1)S(1)}, bf16[128,512]{1,0:T(8,128)(2,1)S(1)}, u32[]{:S(2)}, u32[]{:S(2)}) %collective-permute-start.25) | collective-permute-done | bytes 131104 | tf_op jit(solution)/shard_map/ppermute | solution.py:39
  (69 shorter events, 29.7 us)
Async XLA Ops:
  0.0 6.1 %collective-permute-start.3 = (bf16[128,512]{1,0:T(8,128)(2,1)}, bf16[128,512]{1,0:T(8,128)(2,1)S(1)}, u32[]{:S(2)}, u32[]{:S(2)}) collective-permute-start(bf16[128,512]{1,0:T(8,128)(2,1)} %refs_0_.1), channel_id=1, source_target_pairs={{0,32},{32,0},{1,33},{33,1},{2,34},{34,2},{3,35},{35,3},{4,36},{36... | collective-permute-start | bytes 393224 | tf_op jit(solution)/shard_map/ppermute | solution.py:39
  3.2 11.9 %collective-permute-start = (bf16[128,512]{1,0:T(8,128)(2,1)}, bf16[128,512]{1,0:T(8,128)(2,1)S(1)}, u32[]{:S(2)}, u32[]{:S(2)}) collective-permute-start(bf16[128,512]{1,0:T(8,128)(2,1)} %refs_0_.1), channel_id=1, source_target_pairs={{0,128},{64,192},{128,0},{192,64},{1,129},{65,193},{129,1},{193,65... | collective-permute-start | bytes 393224 | tf_op jit(solution)/shard_map/ppermute | solution.py:39
  4.5 10.7 %collective-permute-start.1 = (bf16[128,512]{1,0:T(8,128)(2,1)}, bf16[128,512]{1,0:T(8,128)(2,1)S(1)}, u32[]{:S(2)}, u32[]{:S(2)}) collective-permute-start(bf16[128,512]{1,0:T(8,128)(2,1)} %refs_0_.1), channel_id=1, source_target_pairs={{0,192},{64,128},{128,64},{192,0},{1,193},{65,129},{129,65},{193,1... | collective-permute-start | bytes 393224 | tf_op jit(solution)/shard_map/ppermute | solution.py:39
  5.9 10.2 %collective-permute-start.2 = (bf16[128,512]{1,0:T(8,128)(2,1)}, bf16[128,512]{1,0:T(8,128)(2,1)S(1)}, u32[]{:S(2)}, u32[]{:S(2)}) collective-permute-start(bf16[128,512]{1,0:T(8,128)(2,1)} %refs_0_.1), channel_id=1, source_target_pairs={{0,64},{64,0},{128,192},{192,128},{1,65},{65,1},{129,193},{193,129... | collective-permute-start | bytes 393224 | tf_op jit(solution)/shard_map/ppermute | solution.py:39
  19.8 13.8 %all-to-all-start = ((bf16[16,64,128]{2,1,0:T(8,128)(2,1)}), bf16[16,64,128]{2,1,0:T(8,128)(2,1)S(1)}, u32[]{:S(2)}, u32[]{:S(2)}) async-start(bf16[16,64,128]{2,1,0:T(8,128)(2,1)} %shard_map.50), calls=%async_computation | async-start | bytes 524288 | tf_op jit(solution)/shard_map/all_to_all | solution.py:258
  28.3 23.4 %collective-permute-start.7 = (bf16[4,64,1024]{2,1,0:T(8,128)(2,1)}, bf16[4,64,1024]{2,1,0:T(8,128)(2,1)S(1)}, u32[]{:S(2)}, u32[]{:S(2)}) collective-permute-start(bf16[4,64,1024]{2,1,0:T(8,128)(2,1)} %get-tuple-element.37), channel_id=1, source_target_pairs={{0,1},{1,0},{2,3},{3,2},{4,5},{5,4},{6,7},{7,6},{8,9},{9,8},{10,11... | collective-permute-start | bytes 1572872 | tf_op jit(solution)/shard_map/ppermute | solution.py:50
  29.7 22.1 %collective-permute-start.8 = (bf16[4,64,1024]{2,1,0:T(8,128)(2,1)}, bf16[4,64,1024]{2,1,0:T(8,128)(2,1)S(1)}, u32[]{:S(2)}, u32[]{:S(2)}) collective-permute-start(bf16[4,64,1024]{2,1,0:T(8,128)(2,1)} %get-tuple-element.38), channel_id=1, source_target_pairs={{0,3},{1,2},{2,1},{3,0},{4,7},{5,6},{6,5},{7,4},{8,11},{9,10},{10,... | collective-permute-start | bytes 1572872 | tf_op jit(solution)/shard_map/ppermute | solution.py:50
  31.5 20.3 %collective-permute-start.9 = (bf16[4,64,1024]{2,1,0:T(8,128)(2,1)}, bf16[4,64,1024]{2,1,0:T(8,128)(2,1)S(1)}, u32[]{:S(2)}, u32[]{:S(2)}) collective-permute-start(bf16[4,64,1024]{2,1,0:T(8,128)(2,1)} %get-tuple-element.39), channel_id=1, source_target_pairs={{0,2},{1,3},{2,0},{3,1},{4,6},{5,7},{6,4},{7,5},{8,10},{9,11},{10,... | collective-permute-start | bytes 1572872 | tf_op jit(solution)/shard_map/ppermute | solution.py:50
  33.7 11.4 %collective-permute-start.14 = (bf16[64,128]{1,0:T(8,128)(2,1)S(1)}, bf16[64,128]{1,0:T(8,128)(2,1)S(1)}, u32[]{:S(2)}, u32[]{:S(2)}) collective-permute-start(bf16[64,128]{1,0:T(8,128)(2,1)S(1)} %shard_map.51), channel_id=1, source_target_pairs={{0,0},{32,64},{64,128},{96,192},{128,32},{160,96},{192,160},{224,2... | collective-permute-start | bytes 49160 | tf_op jit(solution)/shard_map/ppermute | solution.py:262
  39.0 6.8 %collective-permute-start.15 = (bf16[64,128]{1,0:T(8,128)(2,1)S(1)}, bf16[64,128]{1,0:T(8,128)(2,1)S(1)}, u32[]{:S(2)}, u32[]{:S(2)}) collective-permute-start(bf16[64,128]{1,0:T(8,128)(2,1)S(1)} %shard_map.51), channel_id=1, source_target_pairs={{0,16},{16,0},{32,80},{48,64},{64,144},{80,128},{96,208},{112,192}... | collective-permute-start | bytes 49160 | tf_op jit(solution)/shard_map/ppermute | solution.py:263
  46.6 13.2 %all-to-all-start.1 = ((bf16[16,64,128]{2,1,0:T(8,128)(2,1)}), bf16[16,64,128]{2,1,0:T(8,128)(2,1)S(1)}, u32[]{:S(2)}, u32[]{:S(2)}) async-start(bf16[16,64,128]{2,1,0:T(8,128)(2,1)} %shard_map.52), calls=%async_computation.1 | async-start | bytes 524288 | tf_op jit(solution)/shard_map/all_to_all | solution.py:275
  52.6 7.3 %collective-permute-start.10 = (bf16[64,1024]{1,0:T(8,128)(2,1)S(1)}, bf16[64,1024]{1,0:T(8,128)(2,1)S(1)}, u32[]{:S(2)}, u32[]{:S(2)}) collective-permute-start(bf16[64,1024]{1,0:T(8,128)(2,1)S(1)} %get-tuple-element.41), channel_id=1, source_target_pairs={{0,4},{1,5},{2,6},{3,7},{4,0},{5,1},{6,2},{7,3},{8,12},{9,13},{10,... | collective-permute-start | bytes 393224 | tf_op jit(solution)/shard_map/ppermute | solution.py:50
  54.1 5.8 %collective-permute-start.11 = (bf16[64,1024]{1,0:T(8,128)(2,1)S(1)}, bf16[64,1024]{1,0:T(8,128)(2,1)S(1)}, u32[]{:S(2)}, u32[]{:S(2)}) collective-permute-start(bf16[64,1024]{1,0:T(8,128)(2,1)S(1)} %get-tuple-element.42), channel_id=1, source_target_pairs={{0,12},{1,13},{2,14},{3,15},{4,8},{5,9},{6,10},{7,11},{8,4},{9,5},... | collective-permute-start | bytes 393224 | tf_op jit(solution)/shard_map/ppermute | solution.py:50
  55.8 5.6 %collective-permute-start.12 = (bf16[64,1024]{1,0:T(8,128)(2,1)S(1)}, bf16[64,1024]{1,0:T(8,128)(2,1)S(1)}, u32[]{:S(2)}, u32[]{:S(2)}) collective-permute-start(bf16[64,1024]{1,0:T(8,128)(2,1)S(1)} %get-tuple-element.43), channel_id=1, source_target_pairs={{0,8},{1,9},{2,10},{3,11},{4,12},{5,13},{6,14},{7,15},{8,0},{9,1},... | collective-permute-start | bytes 393224 | tf_op jit(solution)/shard_map/ppermute | solution.py:50
  59.9 6.9 %collective-permute-start.16 = (bf16[1024,128]{1,0:T(8,128)(2,1)S(1)}, bf16[1024,128]{1,0:T(8,128)(2,1)S(1)}, u32[]{:S(2)}, u32[]{:S(2)}) collective-permute-start(bf16[1024,128]{1,0:T(8,128)(2,1)S(1)} %bitcast.17), channel_id=1, source_target_pairs={{0,32},{32,0},{1,33},{33,1},{2,34},{34,2},{3,35},{35,3},{4,36},{36... | collective-permute-start | bytes 786440 | tf_op jit(solution)/shard_map/ppermute | solution.py:39
  61.5 8.1 %collective-permute-start.13 = (bf16[64,1024]{1,0:T(8,128)(2,1)S(1)}, bf16[64,1024]{1,0:T(8,128)(2,1)S(1)}, u32[]{:S(2)}, u32[]{:S(2)}) collective-permute-start(bf16[64,1024]{1,0:T(8,128)(2,1)S(1)} %shard_map.49.own), channel_id=1, source_target_pairs={{0,16},{16,0},{1,17},{17,1},{2,18},{18,2},{3,19},{19,3},{4,20},{20... | collective-permute-start | bytes 393224 | tf_op jit(solution)/shard_map/ppermute | solution.py:39
  75.0 5.3 %collective-permute-start.19 = (bf16[64,1024]{1,0:T(8,128)(2,1)S(1)}, bf16[64,1024]{1,0:T(8,128)(2,1)S(1)}, u32[]{:S(2)}, u32[]{:S(2)}) collective-permute-start(bf16[64,1024]{1,0:T(8,128)(2,1)S(1)} %shard_map.53.refs_0_), channel_id=1, source_target_pairs={{0,2},{1,3},{2,0},{3,1},{4,6},{5,7},{6,4},{7,5},{8,10},{9,11},{10,... | collective-permute-start | bytes 393224 | tf_op jit(solution)/shard_map/ppermute | solution.py:50
  80.4 8.4 %collective-permute-start.20 = (bf16[4,64,1024]{2,1,0:T(8,128)(2,1)S(1)}, bf16[4,64,1024]{2,1,0:T(8,128)(2,1)S(1)}, u32[]{:S(2)}, u32[]{:S(2)}) collective-permute-start(bf16[4,64,1024]{2,1,0:T(8,128)(2,1)S(1)} %shard_map.54.line), channel_id=1, source_target_pairs={{0,4},{1,5},{2,6},{3,7},{4,0},{5,1},{6,2},{7,3},{8,12},{9,13},{10,... | collective-permute-start | bytes 1572872 | tf_op jit(solution)/shard_map/ppermute | solution.py:50
  81.0 15.2 %collective-permute-start.21 = (bf16[4,64,1024]{2,1,0:T(8,128)(2,1)S(1)}, bf16[4,64,1024]{2,1,0:T(8,128)(2,1)S(1)}, u32[]{:S(2)}, u32[]{:S(2)}) collective-permute-start(bf16[4,64,1024]{2,1,0:T(8,128)(2,1)S(1)} %shard_map.54.line), channel_id=1, source_target_pairs={{0,12},{1,13},{2,14},{3,15},{4,8},{5,9},{6,10},{7,11},{8,4},{9,5},... | collective-permute-start | bytes 1572872 | tf_op jit(solution)/shard_map/ppermute | solution.py:50
  82.2 14.4 %collective-permute-start.22 = (bf16[4,64,1024]{2,1,0:T(8,128)(2,1)S(1)}, bf16[4,64,1024]{2,1,0:T(8,128)(2,1)S(1)}, u32[]{:S(2)}, u32[]{:S(2)}) collective-permute-start(bf16[4,64,1024]{2,1,0:T(8,128)(2,1)S(1)} %shard_map.54.line), channel_id=1, source_target_pairs={{0,8},{1,9},{2,10},{3,11},{4,12},{5,13},{6,14},{7,15},{8,0},{9,1},... | collective-permute-start | bytes 1572872 | tf_op jit(solution)/shard_map/ppermute | solution.py:50
  97.7 6.7 %collective-permute-start.23 = (bf16[512,512]{1,0:T(8,128)(2,1)S(1)}, bf16[512,512]{1,0:T(8,128)(2,1)S(1)}, u32[]{:S(2)}, u32[]{:S(2)}) collective-permute-start(bf16[512,512]{1,0:T(8,128)(2,1)S(1)} %bitcast.20), channel_id=1, source_target_pairs={{0,32},{32,0},{1,33},{33,1},{2,34},{34,2},{3,35},{35,3},{4,36},{36... | collective-permute-start | bytes 1572872 | tf_op jit(solution)/shard_map/ppermute | solution.py:39
  104.5 6.0 %collective-permute-start.24 = (bf16[128,512]{1,0:T(8,128)(2,1)S(1)}, bf16[128,512]{1,0:T(8,128)(2,1)S(1)}, u32[]{:S(2)}, u32[]{:S(2)}) collective-permute-start(bf16[128,512]{1,0:T(8,128)(2,1)S(1)} %get-tuple-element.54), channel_id=1, source_target_pairs={{0,128},{64,192},{128,0},{192,64},{1,129},{65,193},{129,1},{193,65... | collective-permute-start | bytes 393224 | tf_op jit(solution)/shard_map/ppermute | solution.py:39
  107.1 9.2 %collective-permute-start.25 = (bf16[128,512]{1,0:T(8,128)(2,1)S(1)}, bf16[128,512]{1,0:T(8,128)(2,1)S(1)}, u32[]{:S(2)}, u32[]{:S(2)}) collective-permute-start(bf16[128,512]{1,0:T(8,128)(2,1)S(1)} %get-tuple-element.55), channel_id=1, source_target_pairs={{0,192},{64,128},{128,64},{192,0},{1,193},{65,129},{129,65},{193,1... | collective-permute-start | bytes 393224 | tf_op jit(solution)/shard_map/ppermute | solution.py:39
  110.2 6.8 %collective-permute-start.26 = (bf16[128,512]{1,0:T(8,128)(2,1)S(1)}, bf16[128,512]{1,0:T(8,128)(2,1)S(1)}, u32[]{:S(2)}, u32[]{:S(2)}) collective-permute-start(bf16[128,512]{1,0:T(8,128)(2,1)S(1)} %get-tuple-element.56), channel_id=1, source_target_pairs={{0,64},{64,0},{128,192},{192,128},{1,65},{65,1},{129,193},{193,129... | collective-permute-start | bytes 393224 | tf_op jit(solution)/shard_map/ppermute | solution.py:39
  (11 other events, 60.5 us)

commit v12 on v11

--- a/solution.py
+++ b/solution.py
@@ -160,24 +160,24 @@
 
 
 def stack_kernel(*refs):
-    for s, ref in zip(STEPS, refs[:4]):
-        refs[4][s] = ref[...]
-
-
-def line_kernel(line, weight, out):
-    rows, width = line.shape[1:]
-    block = line[...].reshape(4 * rows, width)
-    product = jnp.dot(block, weight[...], preferred_element_type=F32).astype(BF16)
-    for s in range(4):
-        out[s] = product[s * rows : (s + 1) * rows]
+    for i, ref in enumerate(refs[:3]):
+        refs[3][i] = ref[...]
+
+
+def line_kernel(block, line, weight, out):
+    rows, width = block.shape
+    blocks = jnp.concatenate([block[...][None], line[...]], 0).reshape(4 * rows, width)
+    product = jnp.dot(blocks, weight[...], preferred_element_type=F32).astype(BF16)
+    for i in range(4):
+        out[i] = product[i * rows : (i + 1) * rows]
 
 
 def output_kernel(place, *refs):
-    early, line, weight, kept, sent, last, chunks = refs[:3], *refs[3:]
-    line_kernel(line, weight, last)
+    early, block, line, weight, kept, sent, last, chunks = refs[:3], *refs[3:]
+    line_kernel(block, line, weight, last)
     for t, part in zip(STEPS, [*early, last]):
-        for s in range(4):
-            chunks[chunk_at(place, place[0] ^ s, place[1] ^ t)] = part[s]
+        for i, s in enumerate(STEPS):
+            chunks[chunk_at(place, place[0] ^ s, place[1] ^ t)] = part[i]
     half = kept.shape[0]
     kept[...] = chunks[:half]
     sent[...] = chunks[half:]
@@ -285,21 +285,21 @@
         [pltpu.VMEM((heads * per_chunk, HD), BF16), pltpu.VMEM((2, total, HD), BF16)],
     )
 
-    (line,) = call(
-        stack_kernel,
-        [(4, per_chunk, width)],
-        [attended] + [across_plane(attended, s, False) for s in STEPS[1:]],
-    )
+    around = [across_plane(attended, s, False) for s in STEPS[1:]]
+    direct = [across_plane(attended, t, True) for t in STEPS[1:]]
+    around, direct = lax.optimization_barrier((around, direct))
+    (line,) = call(stack_kernel, [(3, per_chunk, width)], around)
     gathered = [across_plane(line, t, True) for t in STEPS[1:]]
-    early = []
-    for block in gathered:
-        (done,) = call(line_kernel, [(4, per_chunk, features)], [line, w_output])
-        line, done = lax.optimization_barrier((block, done))
+    early, block = [], attended
+    for t in range(3):
+        (done,) = call(line_kernel, [(4, per_chunk, features)], [block, line, w_output])
+        line, done = lax.optimization_barrier((gathered[t], done))
+        block = direct[t]
         early.append(done)
     kept, sent = call(
         output_kernel,
         [(Y * X // 2, per_chunk, features)] * 2,
-        [place, *early, line, w_output],
+        [place, *early, block, line, w_output],
         [SMEM],
         [
             pltpu.VMEM((4, per_chunk, features), BF16),

time: 119 us -> 120 us (level)
    ppermute x12 -> x15, starting transfers between devices: 15.9 us -> 19.1 us  [across_plane(): return lax.ppermute(block, ('core', *PLANE), pairs)]
    ppermute x13, starting transfers between devices: 23.8 us -> 21.5 us  [partner(): return lax.ppermute(block, axis, [(i, i ^ step) for i in range(size)])]
    ppermute x13, waiting for transfers between devices: 18.5 us -> 20.2 us  [partner(): return lax.ppermute(block, axis, [(i, i ^ step) for i in range(size)])]
    ppermute x12 -> x15, waiting for transfers between devices: 17.4 us -> 15.8 us  [across_plane(): return lax.ppermute(block, ('core', *PLANE), pairs)]
  transfers between devices with their start and end apart: 29 -> 32, of which waited for: 18 -> 16; matrix products, arithmetic and copies ran while one was open for 1% -> 1% of each run, Pallas kernels for 5% -> 5%
where the time goes in v12:
time: 120 us; the launch traced here: 119 us
  starting transfers between devices  62.6 us (52%)
  waiting for transfers between devices  41.5 us (35%)
  Pallas kernels  10.8 us (9%)
  local copies, waits for them, and re-layouts  3.13 us (3%)
    ppermute x13, starting transfers between devices, partner(): return lax.ppermute(block, axis, [(i, i ^ step) for i in range(size)])  21.5 us
    ppermute x13, waiting for transfers between devices, partner(): return lax.ppermute(block, axis, [(i, i ^ step) for i in range(size)])  20.2 us
    ppermute x15, starting transfers between devices, across_plane(): return lax.ppermute(block, ('core', *PLANE), pairs)  19.1 us
    ppermute x15, waiting for transfers between devices, across_plane(): return lax.ppermute(block, ('core', *PLANE), pairs)  15.8 us
    pallas_call x15, Pallas kernels, call(): pl.pallas_call(kernel, out_shape=[s if isinstance(s, jax.ShapeDtypeStruct...  10.8 us
    ppermute x1, starting transfers between devices, shards(): lax.ppermute(kv, (*ROW, 'zh'), [(2 * e + h, 2 * r + 1 - h) for e, r in mo...  5.95 us
    all_to_all x1, starting transfers between devices, shards(): kv_parts = lax.all_to_all(kv_parts, PLANE, 0, 0, tiled=True)  5.65 us
    ppermute x1, starting transfers between devices, shards(): here = lax.ppermute(kv, ROW, moves)  5.3 us
  transfers between devices with their start and end apart: 32, of which 16 were waited for; matrix products, arithmetic and copies ran while one was open for 1% of the time, Pallas kernels for 5%

profile of v12, /device:TPU:1, one launch (start us, length us, event | category | flops | bytes accessed | tf_op | source)
XLA Modules:
  0.0 118.8 jit_solution(16841994625094989540)
XLA Ops:
  0.0 3.2 %collective-permute-start.3 = (bf16[128,512]{1,0:T(8,128)(2,1)}, bf16[128,512]{1,0:T(8,128)(2,1)S(1)}, u32[]{:S(2)}, u32[]{:S(2)}) collective-permute-start(bf16[128,512]{1,0:T(8,128)(2,1)} %refs_0_.1), channel_id=1, source_target_pairs={{0,32},{32,0},{1,33},{33,1},{2,34},{34,2},{3,35},{35,3},{4,36},{36... | collective-permute-start | bytes 393224 | tf_op jit(solution)/shard_map/ppermute | solution.py:39
  9.7 5.5 %collective-permute-done.refs_0_ = bf16[128,512]{1,0:T(8,128)(2,1)S(1)} collective-permute-done((bf16[128,512]{1,0:T(8,128)(2,1)}, bf16[128,512]{1,0:T(8,128)(2,1)S(1)}, u32[]{:S(2)}, u32[]{:S(2)}) %collective-permute-start) | collective-permute-done | bytes 131104 | tf_op jit(solution)/shard_map/ppermute | solution.py:39
  19.9 5.6 %all-to-all-start = ((bf16[16,64,128]{2,1,0:T(8,128)(2,1)}), bf16[16,64,128]{2,1,0:T(8,128)(2,1)S(1)}, u32[]{:S(2)}, u32[]{:S(2)}) async-start(bf16[16,64,128]{2,1,0:T(8,128)(2,1)} %shard_map.50), calls=%async_computation | async-start | bytes 524288 | tf_op jit(solution)/shard_map/all_to_all | solution.py:258
  25.6 2.7 %shard_map.47 = (bf16[4,64,1024]{2,1,0:T(8,128)(2,1)S(1)}, bf16[4,64,1024]{2,1,0:T(8,128)(2,1)}, bf16[4,64,1024]{2,1,0:T(8,128)(2,1)}, bf16[4,64,1024]{2,1,0:T(8,128)(2,1)}) custom-call(s32[4]{0:T(128)S(1)} %pad_add_fusion.place, bf16[128,512]{1,0:T(8,128)(2,1)S(1)} %collective-permute-done.refs_0_, bf16[128,512]{1,0:T(8,128)(2,1)S(1)} %collective-permute-done.1.refs_1_, ...), custom_call_target="tpu_custom_call" | custom-call | tf_op jit(solution)/shard_map/pallas_call | solution.py:195
  29.7 1.8 %collective-permute-start.8 = (bf16[4,64,1024]{2,1,0:T(8,128)(2,1)}, bf16[4,64,1024]{2,1,0:T(8,128)(2,1)S(1)}, u32[]{:S(2)}, u32[]{:S(2)}) collective-permute-start(bf16[4,64,1024]{2,1,0:T(8,128)(2,1)} %get-tuple-element.44), channel_id=1, source_target_pairs={{0,3},{1,2},{2,1},{3,0},{4,7},{5,6},{6,5},{7,4},{8,11},{9,10},{10,... | collective-permute-start | bytes 1572872 | tf_op jit(solution)/shard_map/ppermute | solution.py:50
  33.7 5.3 %collective-permute-start.14 = (bf16[64,128]{1,0:T(8,128)(2,1)S(1)}, bf16[64,128]{1,0:T(8,128)(2,1)S(1)}, u32[]{:S(2)}, u32[]{:S(2)}) collective-permute-start(bf16[64,128]{1,0:T(8,128)(2,1)S(1)} %shard_map.51), channel_id=1, source_target_pairs={{0,0},{32,64},{64,128},{96,192},{128,32},{160,96},{192,160},{224,2... | collective-permute-start | bytes 49160 | tf_op jit(solution)/shard_map/ppermute | solution.py:262
  39.0 5.9 %collective-permute-start.15 = (bf16[64,128]{1,0:T(8,128)(2,1)S(1)}, bf16[64,128]{1,0:T(8,128)(2,1)S(1)}, u32[]{:S(2)}, u32[]{:S(2)}) collective-permute-start(bf16[64,128]{1,0:T(8,128)(2,1)S(1)} %shard_map.51), channel_id=1, source_target_pairs={{0,16},{16,0},{32,80},{48,64},{64,144},{80,128},{96,208},{112,192}... | collective-permute-start | bytes 49160 | tf_op jit(solution)/shard_map/ppermute | solution.py:263
  46.7 5.1 %all-to-all-start.1 = ((bf16[16,64,128]{2,1,0:T(8,128)(2,1)}), bf16[16,64,128]{2,1,0:T(8,128)(2,1)S(1)}, u32[]{:S(2)}, u32[]{:S(2)}) async-start(bf16[16,64,128]{2,1,0:T(8,128)(2,1)} %shard_map.52), calls=%async_computation.1 | async-start | bytes 524288 | tf_op jit(solution)/shard_map/all_to_all | solution.py:275
  54.1 1.8 %collective-permute-start.11 = (bf16[64,1024]{1,0:T(8,128)(2,1)S(1)}, bf16[64,1024]{1,0:T(8,128)(2,1)S(1)}, u32[]{:S(2)}, u32[]{:S(2)}) collective-permute-start(bf16[64,1024]{1,0:T(8,128)(2,1)S(1)} %get-tuple-element.48), channel_id=1, source_target_pairs={{0,12},{1,13},{2,14},{3,15},{4,8},{5,9},{6,10},{7,11},{8,4},{9,5},... | collective-permute-start | bytes 393224 | tf_op jit(solution)/shard_map/ppermute | solution.py:50
  56.5 3.4 %all-to-all-done.1 = bf16[16,64,128]{2,1,0:T(8,128)(2,1)S(1)} async-done(((bf16[16,64,128]{2,1,0:T(8,128)(2,1)}), bf16[16,64,128]{2,1,0:T(8,128)(2,1)S(1)}, u32[]{:S(2)}, u32[]{:S(2)}) %all-to-all-start.1) | async-done | bytes 262176 | tf_op jit(solution)/shard_map/all_to_all | solution.py:275
  59.9 1.6 %collective-permute-done.12.d = bf16[64,1024]{1,0:T(8,128)(2,1)S(1)} collective-permute-done((bf16[64,1024]{1,0:T(8,128)(2,1)S(1)}, bf16[64,1024]{1,0:T(8,128)(2,1)S(1)}, u32[]{:S(2)}, u32[]{:S(2)}) %collective-permute-start.12) | collective-permute-done | bytes 131104 | tf_op jit(solution)/shard_map/ppermute | solution.py:50
  61.6 5.1 %collective-permute-start.13 = (bf16[64,1024]{1,0:T(8,128)(2,1)S(1)}, bf16[64,1024]{1,0:T(8,128)(2,1)S(1)}, u32[]{:S(2)}, u32[]{:S(2)}) collective-permute-start(bf16[64,1024]{1,0:T(8,128)(2,1)S(1)} %shard_map.49.own), channel_id=1, source_target_pairs={{0,16},{16,0},{1,17},{17,1},{2,18},{18,2},{3,19},{19,3},{4,20},{20... | collective-permute-start | bytes 393224 | tf_op jit(solution)/shard_map/ppermute | solution.py:39
  66.8 2.8 %collective-permute-done.13.got = bf16[64,1024]{1,0:T(8,128)(2,1)S(1)} collective-permute-done((bf16[64,1024]{1,0:T(8,128)(2,1)S(1)}, bf16[64,1024]{1,0:T(8,128)(2,1)S(1)}, u32[]{:S(2)}, u32[]{:S(2)}) %collective-permute-start.13) | collective-permute-done | bytes 131104 | tf_op jit(solution)/shard_map/ppermute | solution.py:39
  69.7 1.6 %shard_map.53.block = bf16[64,1024]{1,0:T(8,128)(2,1)S(1)} custom-call(s32[10]{0:T(128)S(1)} %stack.63.base, bf16[64,1024]{1,0:T(8,128)(2,1)S(1)} %shard_map.49.own, bf16[64,1024]{1,0:T(8,128)(2,1)S(1)} %collective-permute-done.13.got, f32[64,128]{1,0:T(8,128)S(1)} %get-tuple-element.80.cosine, f32[64,128]{1,0:T(8,128)S(1)} %get-tuple-element.81.sine_v, ...), custom_call_target="tpu_custom_call" | custom-call | tf_op jit(solution)/shard_map/pallas_call | solution.py:195
  71.2 2.2 %collective-permute-start.17 = (bf16[64,1024]{1,0:T(8,128)(2,1)S(1)}, bf16[64,1024]{1,0:T(8,128)(2,1)S(1)}, u32[]{:S(2)}, u32[]{:S(2)}) collective-permute-start(bf16[64,1024]{1,0:T(8,128)(2,1)S(1)} %shard_map.53.block), channel_id=1, source_target_pairs={{0,1},{1,0},{2,3},{3,2},{4,5},{5,4},{6,7},{7,6},{8,9},{9,8},{10,11... | collective-permute-start | bytes 393224 | tf_op jit(solution)/shard_map/ppermute | solution.py:50
  73.4 1.6 %collective-permute-start.18 = (bf16[64,1024]{1,0:T(8,128)(2,1)S(1)}, bf16[64,1024]{1,0:T(8,128)(2,1)S(1)}, u32[]{:S(2)}, u32[]{:S(2)}) collective-permute-start(bf16[64,1024]{1,0:T(8,128)(2,1)S(1)} %shard_map.53.block), channel_id=1, source_target_pairs={{0,3},{1,2},{2,1},{3,0},{4,7},{5,6},{6,5},{7,4},{8,11},{9,10},{10,... | collective-permute-start | bytes 393224 | tf_op jit(solution)/shard_map/ppermute | solution.py:50
  76.7 2.7 %collective-permute-start.22 = (bf16[64,1024]{1,0:T(8,128)(2,1)S(1)}, bf16[64,1024]{1,0:T(8,128)(2,1)S(1)}, u32[]{:S(2)}, u32[]{:S(2)}) collective-permute-start(bf16[64,1024]{1,0:T(8,128)(2,1)S(1)} %shard_map.53.block), channel_id=1, source_target_pairs={{0,8},{1,9},{2,10},{3,11},{4,12},{5,13},{6,14},{7,15},{8,0},{9,1},... | collective-permute-start | bytes 393224 | tf_op jit(solution)/shard_map/ppermute | solution.py:50
  80.4 4.9 %collective-permute-done.21.block = bf16[64,1024]{1,0:T(8,128)(2,1)S(1)} collective-permute-done((bf16[64,1024]{1,0:T(8,128)(2,1)S(1)}, bf16[64,1024]{1,0:T(8,128)(2,1)S(1)}, u32[]{:S(2)}, u32[]{:S(2)}) %collective-permute-start.21) | collective-permute-done | bytes 131104 | tf_op jit(solution)/shard_map/ppermute | solution.py:50
  86.5 2.2 %collective-permute-start.25 = (bf16[3,64,1024]{2,1,0:T(8,128)(2,1)S(1)}, bf16[3,64,1024]{2,1,0:T(8,128)(2,1)S(1)}, u32[]{:S(2)}, u32[]{:S(2)}) collective-permute-start(bf16[3,64,1024]{2,1,0:T(8,128)(2,1)S(1)} %shard_map.54.line), channel_id=1, source_target_pairs={{0,8},{1,9},{2,10},{3,11},{4,12},{5,13},{6,14},{7,15},{8,0},{9,1},... | collective-permute-start | bytes 1179656 | tf_op jit(solution)/shard_map/ppermute | solution.py:50
  89.1 3.2 %collective-permute-done.23.line = bf16[3,64,1024]{2,1,0:T(8,128)(2,1)S(1)} collective-permute-done((bf16[3,64,1024]{2,1,0:T(8,128)(2,1)S(1)}, bf16[3,64,1024]{2,1,0:T(8,128)(2,1)S(1)}, u32[]{:S(2)}, u32[]{:S(2)}) %collective-permute-start.23) | collective-permute-done | bytes 393248 | tf_op jit(solution)/shard_map/ppermute | solution.py:50
  92.8 5.1 %collective-permute-done.24.line = bf16[3,64,1024]{2,1,0:T(8,128)(2,1)S(1)} collective-permute-done((bf16[3,64,1024]{2,1,0:T(8,128)(2,1)S(1)}, bf16[3,64,1024]{2,1,0:T(8,128)(2,1)S(1)}, u32[]{:S(2)}, u32[]{:S(2)}) %collective-permute-start.24) | collective-permute-done | bytes 393248 | tf_op jit(solution)/shard_map/ppermute | solution.py:50
  99.4 4.3 %collective-permute-start.26 = (bf16[512,512]{1,0:T(8,128)(2,1)S(1)}, bf16[512,512]{1,0:T(8,128)(2,1)S(1)}, u32[]{:S(2)}, u32[]{:S(2)}) collective-permute-start(bf16[512,512]{1,0:T(8,128)(2,1)S(1)} %bitcast.20), channel_id=1, source_target_pairs={{0,32},{32,0},{1,33},{33,1},{2,34},{34,2},{3,35},{35,3},{4,36},{36... | collective-permute-start | bytes 1572872 | tf_op jit(solution)/shard_map/ppermute | solution.py:39
  105.3 3.6 %collective-permute-start.27 = (bf16[128,512]{1,0:T(8,128)(2,1)S(1)}, bf16[128,512]{1,0:T(8,128)(2,1)S(1)}, u32[]{:S(2)}, u32[]{:S(2)}) collective-permute-start(bf16[128,512]{1,0:T(8,128)(2,1)S(1)} %get-tuple-element.66), channel_id=1, source_target_pairs={{0,128},{64,192},{128,0},{192,64},{1,129},{65,193},{129,1},{193,65... | collective-permute-start | bytes 393224 | tf_op jit(solution)/shard_map/ppermute | solution.py:39
  109.6 8.5 %collective-permute-done.27.b = bf16[128,512]{1,0:T(8,128)(2,1)S(1)} collective-permute-done((bf16[128,512]{1,0:T(8,128)(2,1)S(1)}, bf16[128,512]{1,0:T(8,128)(2,1)S(1)}, u32[]{:S(2)}, u32[]{:S(2)}) %collective-permute-start.27) | collective-permute-done | bytes 131104 | tf_op jit(solution)/shard_map/ppermute | solution.py:39
  (75 shorter events, 28.8 us)
Async XLA Ops:
  0.0 6.1 %collective-permute-start.3 = (bf16[128,512]{1,0:T(8,128)(2,1)}, bf16[128,512]{1,0:T(8,128)(2,1)S(1)}, u32[]{:S(2)}, u32[]{:S(2)}) collective-permute-start(bf16[128,512]{1,0:T(8,128)(2,1)} %refs_0_.1), channel_id=1, source_target_pairs={{0,32},{32,0},{1,33},{33,1},{2,34},{34,2},{3,35},{35,3},{4,36},{36... | collective-permute-start | bytes 393224 | tf_op jit(solution)/shard_map/ppermute | solution.py:39
  3.2 11.9 %collective-permute-start = (bf16[128,512]{1,0:T(8,128)(2,1)}, bf16[128,512]{1,0:T(8,128)(2,1)S(1)}, u32[]{:S(2)}, u32[]{:S(2)}) collective-permute-start(bf16[128,512]{1,0:T(8,128)(2,1)} %refs_0_.1), channel_id=1, source_target_pairs={{0,128},{64,192},{128,0},{192,64},{1,129},{65,193},{129,1},{193,65... | collective-permute-start | bytes 393224 | tf_op jit(solution)/shard_map/ppermute | solution.py:39
  4.5 10.7 %collective-permute-start.1 = (bf16[128,512]{1,0:T(8,128)(2,1)}, bf16[128,512]{1,0:T(8,128)(2,1)S(1)}, u32[]{:S(2)}, u32[]{:S(2)}) collective-permute-start(bf16[128,512]{1,0:T(8,128)(2,1)} %refs_0_.1), channel_id=1, source_target_pairs={{0,192},{64,128},{128,64},{192,0},{1,193},{65,129},{129,65},{193,1... | collective-permute-start | bytes 393224 | tf_op jit(solution)/shard_map/ppermute | solution.py:39
  5.9 10.2 %collective-permute-start.2 = (bf16[128,512]{1,0:T(8,128)(2,1)}, bf16[128,512]{1,0:T(8,128)(2,1)S(1)}, u32[]{:S(2)}, u32[]{:S(2)}) collective-permute-start(bf16[128,512]{1,0:T(8,128)(2,1)} %refs_0_.1), channel_id=1, source_target_pairs={{0,64},{64,0},{128,192},{192,128},{1,65},{65,1},{129,193},{193,129... | collective-permute-start | bytes 393224 | tf_op jit(solution)/shard_map/ppermute | solution.py:39
  19.9 13.8 %all-to-all-start = ((bf16[16,64,128]{2,1,0:T(8,128)(2,1)}), bf16[16,64,128]{2,1,0:T(8,128)(2,1)S(1)}, u32[]{:S(2)}, u32[]{:S(2)}) async-start(bf16[16,64,128]{2,1,0:T(8,128)(2,1)} %shard_map.50), calls=%async_computation | async-start | bytes 524288 | tf_op jit(solution)/shard_map/all_to_all | solution.py:258
  28.3 23.5 %collective-permute-start.7 = (bf16[4,64,1024]{2,1,0:T(8,128)(2,1)}, bf16[4,64,1024]{2,1,0:T(8,128)(2,1)S(1)}, u32[]{:S(2)}, u32[]{:S(2)}) collective-permute-start(bf16[4,64,1024]{2,1,0:T(8,128)(2,1)} %get-tuple-element.43), channel_id=1, source_target_pairs={{0,1},{1,0},{2,3},{3,2},{4,5},{5,4},{6,7},{7,6},{8,9},{9,8},{10,11... | collective-permute-start | bytes 1572872 | tf_op jit(solution)/shard_map/ppermute | solution.py:50
  29.7 22.1 %collective-permute-start.8 = (bf16[4,64,1024]{2,1,0:T(8,128)(2,1)}, bf16[4,64,1024]{2,1,0:T(8,128)(2,1)S(1)}, u32[]{:S(2)}, u32[]{:S(2)}) collective-permute-start(bf16[4,64,1024]{2,1,0:T(8,128)(2,1)} %get-tuple-element.44), channel_id=1, source_target_pairs={{0,3},{1,2},{2,1},{3,0},{4,7},{5,6},{6,5},{7,4},{8,11},{9,10},{10,... | collective-permute-start | bytes 1572872 | tf_op jit(solution)/shard_map/ppermute | solution.py:50
  31.5 20.3 %collective-permute-start.9 = (bf16[4,64,1024]{2,1,0:T(8,128)(2,1)}, bf16[4,64,1024]{2,1,0:T(8,128)(2,1)S(1)}, u32[]{:S(2)}, u32[]{:S(2)}) collective-permute-start(bf16[4,64,1024]{2,1,0:T(8,128)(2,1)} %get-tuple-element.45), channel_id=1, source_target_pairs={{0,2},{1,3},{2,0},{3,1},{4,6},{5,7},{6,4},{7,5},{8,10},{9,11},{10,... | collective-permute-start | bytes 1572872 | tf_op jit(solution)/shard_map/ppermute | solution.py:50
  33.7 11.4 %collective-permute-start.14 = (bf16[64,128]{1,0:T(8,128)(2,1)S(1)}, bf16[64,128]{1,0:T(8,128)(2,1)S(1)}, u32[]{:S(2)}, u32[]{:S(2)}) collective-permute-start(bf16[64,128]{1,0:T(8,128)(2,1)S(1)} %shard_map.51), channel_id=1, source_target_pairs={{0,0},{32,64},{64,128},{96,192},{128,32},{160,96},{192,160},{224,2... | collective-permute-start | bytes 49160 | tf_op jit(solution)/shard_map/ppermute | solution.py:262
  39.0 6.8 %collective-permute-start.15 = (bf16[64,128]{1,0:T(8,128)(2,1)S(1)}, bf16[64,128]{1,0:T(8,128)(2,1)S(1)}, u32[]{:S(2)}, u32[]{:S(2)}) collective-permute-start(bf16[64,128]{1,0:T(8,128)(2,1)S(1)} %shard_map.51), channel_id=1, source_target_pairs={{0,16},{16,0},{32,80},{48,64},{64,144},{80,128},{96,208},{112,192}... | collective-permute-start | bytes 49160 | tf_op jit(solution)/shard_map/ppermute | solution.py:263
  46.7 13.2 %all-to-all-start.1 = ((bf16[16,64,128]{2,1,0:T(8,128)(2,1)}), bf16[16,64,128]{2,1,0:T(8,128)(2,1)S(1)}, u32[]{:S(2)}, u32[]{:S(2)}) async-start(bf16[16,64,128]{2,1,0:T(8,128)(2,1)} %shard_map.52), calls=%async_computation.1 | async-start | bytes 524288 | tf_op jit(solution)/shard_map/all_to_all | solution.py:275
  52.6 7.3 %collective-permute-start.10 = (bf16[64,1024]{1,0:T(8,128)(2,1)S(1)}, bf16[64,1024]{1,0:T(8,128)(2,1)S(1)}, u32[]{:S(2)}, u32[]{:S(2)}) collective-permute-start(bf16[64,1024]{1,0:T(8,128)(2,1)S(1)} %get-tuple-element.47), channel_id=1, source_target_pairs={{0,4},{1,5},{2,6},{3,7},{4,0},{5,1},{6,2},{7,3},{8,12},{9,13},{10,... | collective-permute-start | bytes 393224 | tf_op jit(solution)/shard_map/ppermute | solution.py:50
  54.1 5.8 %collective-permute-start.11 = (bf16[64,1024]{1,0:T(8,128)(2,1)S(1)}, bf16[64,1024]{1,0:T(8,128)(2,1)S(1)}, u32[]{:S(2)}, u32[]{:S(2)}) collective-permute-start(bf16[64,1024]{1,0:T(8,128)(2,1)S(1)} %get-tuple-element.48), channel_id=1, source_target_pairs={{0,12},{1,13},{2,14},{3,15},{4,8},{5,9},{6,10},{7,11},{8,4},{9,5},... | collective-permute-start | bytes 393224 | tf_op jit(solution)/shard_map/ppermute | solution.py:50
  59.9 6.9 %collective-permute-start.16 = (bf16[1024,128]{1,0:T(8,128)(2,1)S(1)}, bf16[1024,128]{1,0:T(8,128)(2,1)S(1)}, u32[]{:S(2)}, u32[]{:S(2)}) collective-permute-start(bf16[1024,128]{1,0:T(8,128)(2,1)S(1)} %bitcast.17), channel_id=1, source_target_pairs={{0,32},{32,0},{1,33},{33,1},{2,34},{34,2},{3,35},{35,3},{4,36},{36... | collective-permute-start | bytes 786440 | tf_op jit(solution)/shard_map/ppermute | solution.py:39
  61.6 8.1 %collective-permute-start.13 = (bf16[64,1024]{1,0:T(8,128)(2,1)S(1)}, bf16[64,1024]{1,0:T(8,128)(2,1)S(1)}, u32[]{:S(2)}, u32[]{:S(2)}) collective-permute-start(bf16[64,1024]{1,0:T(8,128)(2,1)S(1)} %shard_map.49.own), channel_id=1, source_target_pairs={{0,16},{16,0},{1,17},{17,1},{2,18},{18,2},{3,19},{19,3},{4,20},{20... | collective-permute-start | bytes 393224 | tf_op jit(solution)/shard_map/ppermute | solution.py:39
  73.4 6.0 %collective-permute-start.18 = (bf16[64,1024]{1,0:T(8,128)(2,1)S(1)}, bf16[64,1024]{1,0:T(8,128)(2,1)S(1)}, u32[]{:S(2)}, u32[]{:S(2)}) collective-permute-start(bf16[64,1024]{1,0:T(8,128)(2,1)S(1)} %shard_map.53.block), channel_id=1, source_target_pairs={{0,3},{1,2},{2,1},{3,0},{4,7},{5,6},{6,5},{7,4},{8,11},{9,10},{10,... | collective-permute-start | bytes 393224 | tf_op jit(solution)/shard_map/ppermute | solution.py:50
  76.2 9.1 %collective-permute-start.21 = (bf16[64,1024]{1,0:T(8,128)(2,1)S(1)}, bf16[64,1024]{1,0:T(8,128)(2,1)S(1)}, u32[]{:S(2)}, u32[]{:S(2)}) collective-permute-start(bf16[64,1024]{1,0:T(8,128)(2,1)S(1)} %shard_map.53.block), channel_id=1, source_target_pairs={{0,12},{1,13},{2,14},{3,15},{4,8},{5,9},{6,10},{7,11},{8,4},{9,5},... | collective-permute-start | bytes 393224 | tf_op jit(solution)/shard_map/ppermute | solution.py:50
  76.7 8.6 %collective-permute-start.22 = (bf16[64,1024]{1,0:T(8,128)(2,1)S(1)}, bf16[64,1024]{1,0:T(8,128)(2,1)S(1)}, u32[]{:S(2)}, u32[]{:S(2)}) collective-permute-start(bf16[64,1024]{1,0:T(8,128)(2,1)S(1)} %shard_map.53.block), channel_id=1, source_target_pairs={{0,8},{1,9},{2,10},{3,11},{4,12},{5,13},{6,14},{7,15},{8,0},{9,1},... | collective-permute-start | bytes 393224 | tf_op jit(solution)/shard_map/ppermute | solution.py:50
  85.3 7.0 %collective-permute-start.23 = (bf16[3,64,1024]{2,1,0:T(8,128)(2,1)S(1)}, bf16[3,64,1024]{2,1,0:T(8,128)(2,1)S(1)}, u32[]{:S(2)}, u32[]{:S(2)}) collective-permute-start(bf16[3,64,1024]{2,1,0:T(8,128)(2,1)S(1)} %shard_map.54.line), channel_id=1, source_target_pairs={{0,4},{1,5},{2,6},{3,7},{4,0},{5,1},{6,2},{7,3},{8,12},{9,13},{10,... | collective-permute-start | bytes 1179656 | tf_op jit(solution)/shard_map/ppermute | solution.py:50
  85.4 12.4 %collective-permute-start.24 = (bf16[3,64,1024]{2,1,0:T(8,128)(2,1)S(1)}, bf16[3,64,1024]{2,1,0:T(8,128)(2,1)S(1)}, u32[]{:S(2)}, u32[]{:S(2)}) collective-permute-start(bf16[3,64,1024]{2,1,0:T(8,128)(2,1)S(1)} %shard_map.54.line), channel_id=1, source_target_pairs={{0,12},{1,13},{2,14},{3,15},{4,8},{5,9},{6,10},{7,11},{8,4},{9,5},... | collective-permute-start | bytes 1179656 | tf_op jit(solution)/shard_map/ppermute | solution.py:50
  86.5 11.8 %collective-permute-start.25 = (bf16[3,64,1024]{2,1,0:T(8,128)(2,1)S(1)}, bf16[3,64,1024]{2,1,0:T(8,128)(2,1)S(1)}, u32[]{:S(2)}, u32[]{:S(2)}) collective-permute-start(bf16[3,64,1024]{2,1,0:T(8,128)(2,1)S(1)} %shard_map.54.line), channel_id=1, source_target_pairs={{0,8},{1,9},{2,10},{3,11},{4,12},{5,13},{6,14},{7,15},{8,0},{9,1},... | collective-permute-start | bytes 1179656 | tf_op jit(solution)/shard_map/ppermute | solution.py:50
  105.3 12.8 %collective-permute-start.27 = (bf16[128,512]{1,0:T(8,128)(2,1)S(1)}, bf16[128,512]{1,0:T(8,128)(2,1)S(1)}, u32[]{:S(2)}, u32[]{:S(2)}) collective-permute-start(bf16[128,512]{1,0:T(8,128)(2,1)S(1)} %get-tuple-element.66), channel_id=1, source_target_pairs={{0,128},{64,192},{128,0},{192,64},{1,129},{65,193},{129,1},{193,65... | collective-permute-start | bytes 393224 | tf_op jit(solution)/shard_map/ppermute | solution.py:39
  108.9 9.2 %collective-permute-start.28 = (bf16[128,512]{1,0:T(8,128)(2,1)S(1)}, bf16[128,512]{1,0:T(8,128)(2,1)S(1)}, u32[]{:S(2)}, u32[]{:S(2)}) collective-permute-start(bf16[128,512]{1,0:T(8,128)(2,1)S(1)} %get-tuple-element.67), channel_id=1, source_target_pairs={{0,192},{64,128},{128,64},{192,0},{1,193},{65,129},{129,65},{193,1... | collective-permute-start | bytes 393224 | tf_op jit(solution)/shard_map/ppermute | solution.py:39
  109.6 8.5 %collective-permute-start.29 = (bf16[128,512]{1,0:T(8,128)(2,1)S(1)}, bf16[128,512]{1,0:T(8,128)(2,1)S(1)}, u32[]{:S(2)}, u32[]{:S(2)}) collective-permute-start(bf16[128,512]{1,0:T(8,128)(2,1)S(1)} %get-tuple-element.68), channel_id=1, source_target_pairs={{0,64},{64,0},{128,192},{192,128},{1,65},{65,1},{129,193},{193,129... | collective-permute-start | bytes 393224 | tf_op jit(solution)/shard_map/ppermute | solution.py:39
  (14 other events, 87.2 us)

commit v13 on v11

--- a/solution.py
+++ b/solution.py
@@ -259,11 +259,11 @@
     (kv,) = call(sum_kernel, [(per_chunk, HD)], [kv_parts])
 
     moves = [(e, 2 * (e % 4) + e // 4) for e in range(8)]
-    here = lax.ppermute(kv, ROW, moves)
     across = lax.ppermute(
         kv, (*ROW, "zh"), [(2 * e + h, 2 * r + 1 - h) for e, r in moves for h in range(2)]
     )
-    (kv_block,) = call(keys_kernel, [(Y * X, per_chunk, HD)], [here, across, key_cos, key_sin])
+    here = lax.ppermute(kv, ROW, moves)
+    (kv_block,) = call(keys_kernel, [(Y * X, per_chunk, HD)], [across, here, key_cos, key_sin])
     got = [across_plane(parts[s], s, False) for s in STEPS[1:]]
     halves = call(
         halve_kernel,

time: 119 us -> 121 us (1.017)
  waiting for transfers between devices: 41.4 us -> 48.9 us
  starting transfers between devices: 61.7 us -> 55.9 us
    ppermute x13, waiting for transfers between devices: 18.5 us -> 24.6 us  [partner(): return lax.ppermute(block, axis, [(i, i ^ step) for i in range(size)])]
    ppermute x13, starting transfers between devices: 23.8 us -> 19 us  [partner(): return lax.ppermute(block, axis, [(i, i ^ step) for i in range(size)])]
    ppermute x1, waiting for transfers between devices: 0.01 us -> 2.91 us  [shards(): here = lax.ppermute(kv, ROW, moves)]
    ppermute x1, starting transfers between devices: 5.31 us -> 2.92 us  [shards(): here = lax.ppermute(kv, ROW, moves)]
    ppermute x1, starting transfers between devices: 5.95 us -> 8.31 us  [shards(): lax.ppermute(kv, (*ROW, 'zh'), [(2 * e + h, 2 * r + 1 - h) for e, r in mo...]
where the time goes in v13:
time: 121 us; the launch traced here: 120 us
  starting transfers between devices  55.9 us (46%)
  waiting for transfers between devices  48.9 us (40%)
  Pallas kernels  10.8 us (9%)
  local copies, waits for them, and re-layouts  3.13 us (3%)
    ppermute x13, waiting for transfers between devices, partner(): return lax.ppermute(block, axis, [(i, i ^ step) for i in range(size)])  24.6 us
    ppermute x13, starting transfers between devices, partner(): return lax.ppermute(block, axis, [(i, i ^ step) for i in range(size)])  19 us
    ppermute x12, waiting for transfers between devices, across_plane(): return lax.ppermute(block, ('core', *PLANE), pairs)  17.2 us
    ppermute x12, starting transfers between devices, across_plane(): return lax.ppermute(block, ('core', *PLANE), pairs)  14.9 us
    pallas_call x15, Pallas kernels, call(): pl.pallas_call(kernel, out_shape=[s if isinstance(s, jax.ShapeDtypeStruct...  10.8 us
    ppermute x1, starting transfers between devices, shards(): lax.ppermute(kv, (*ROW, 'zh'), [(2 * e + h, 2 * r + 1 - h) for e, r in mo...  8.31 us
    all_to_all x1, starting transfers between devices, shards(): kv_parts = lax.all_to_all(kv_parts, PLANE, 0, 0, tiled=True)  5.65 us
    all_to_all x1, starting transfers between devices, shards(): lax.all_to_all(kv_block, PLANE, 0, 0, tiled=True).reshape(total, HD)  5.13 us
  transfers between devices with their start and end apart: 29, of which 18 were waited for; matrix products, arithmetic and copies ran while one was open for 1% of the time, Pallas kernels for 5%

profile of v13, /device:TPU:1, one launch (start us, length us, event | category | flops | bytes accessed | tf_op | source)
XLA Modules:
  0.0 119.5 jit_solution(7040829662834961323)
XLA Ops:
  0.0 3.2 %collective-permute-start.3 = (bf16[128,512]{1,0:T(8,128)(2,1)}, bf16[128,512]{1,0:T(8,128)(2,1)S(1)}, u32[]{:S(2)}, u32[]{:S(2)}) collective-permute-start(bf16[128,512]{1,0:T(8,128)(2,1)} %refs_0_.1), channel_id=1, source_target_pairs={{0,32},{32,0},{1,33},{33,1},{2,34},{34,2},{3,35},{35,3},{4,36},{36... | collective-permute-start | bytes 393224 | tf_op jit(solution)/shard_map/ppermute | solution.py:39
  9.7 5.5 %collective-permute-done.refs_0_ = bf16[128,512]{1,0:T(8,128)(2,1)S(1)} collective-permute-done((bf16[128,512]{1,0:T(8,128)(2,1)}, bf16[128,512]{1,0:T(8,128)(2,1)S(1)}, u32[]{:S(2)}, u32[]{:S(2)}) %collective-permute-start) | collective-permute-done | bytes 131104 | tf_op jit(solution)/shard_map/ppermute | solution.py:39
  19.8 5.6 %all-to-all-start = ((bf16[16,64,128]{2,1,0:T(8,128)(2,1)}), bf16[16,64,128]{2,1,0:T(8,128)(2,1)S(1)}, u32[]{:S(2)}, u32[]{:S(2)}) async-start(bf16[16,64,128]{2,1,0:T(8,128)(2,1)} %shard_map.50), calls=%async_computation | async-start | bytes 524288 | tf_op jit(solution)/shard_map/all_to_all | solution.py:258
  25.6 2.7 %shard_map.47 = (bf16[4,64,1024]{2,1,0:T(8,128)(2,1)S(1)}, bf16[4,64,1024]{2,1,0:T(8,128)(2,1)}, bf16[4,64,1024]{2,1,0:T(8,128)(2,1)}, bf16[4,64,1024]{2,1,0:T(8,128)(2,1)}) custom-call(s32[4]{0:T(128)S(1)} %pad_add_fusion.place, bf16[128,512]{1,0:T(8,128)(2,1)S(1)} %collective-permute-done.refs_0_, bf16[128,512]{1,0:T(8,128)(2,1)S(1)} %collective-permute-done.1.refs_1_, ...), custom_call_target="tpu_custom_call" | custom-call | tf_op jit(solution)/shard_map/pallas_call | solution.py:195
  29.7 1.8 %collective-permute-start.8 = (bf16[4,64,1024]{2,1,0:T(8,128)(2,1)}, bf16[4,64,1024]{2,1,0:T(8,128)(2,1)S(1)}, u32[]{:S(2)}, u32[]{:S(2)}) collective-permute-start(bf16[4,64,1024]{2,1,0:T(8,128)(2,1)} %get-tuple-element.38), channel_id=1, source_target_pairs={{0,3},{1,2},{2,1},{3,0},{4,7},{5,6},{6,5},{7,4},{8,11},{9,10},{10,... | collective-permute-start | bytes 1572872 | tf_op jit(solution)/shard_map/ppermute | solution.py:50
  33.7 8.3 %collective-permute-start.14 = (bf16[64,128]{1,0:T(8,128)(2,1)S(1)}, bf16[64,128]{1,0:T(8,128)(2,1)S(1)}, u32[]{:S(2)}, u32[]{:S(2)}) collective-permute-start(bf16[64,128]{1,0:T(8,128)(2,1)S(1)} %shard_map.51), channel_id=1, source_target_pairs={{0,16},{16,0},{32,80},{48,64},{64,144},{80,128},{96,208},{112,192}... | collective-permute-start | bytes 49160 | tf_op jit(solution)/shard_map/ppermute | solution.py:262
  42.0 2.9 %collective-permute-start.15 = (bf16[64,128]{1,0:T(8,128)(2,1)S(1)}, bf16[64,128]{1,0:T(8,128)(2,1)S(1)}, u32[]{:S(2)}, u32[]{:S(2)}) collective-permute-start(bf16[64,128]{1,0:T(8,128)(2,1)S(1)} %shard_map.51), channel_id=1, source_target_pairs={{0,0},{32,64},{64,128},{96,192},{128,32},{160,96},{192,160},{224,2... | collective-permute-start | bytes 49160 | tf_op jit(solution)/shard_map/ppermute | solution.py:265
  45.1 2.9 %collective-permute-done.15.b = bf16[64,128]{1,0:T(8,128)(2,1)S(1)} collective-permute-done((bf16[64,128]{1,0:T(8,128)(2,1)S(1)}, bf16[64,128]{1,0:T(8,128)(2,1)S(1)}, u32[]{:S(2)}, u32[]{:S(2)}) %collective-permute-start.15) | collective-permute-done | bytes 16416 | tf_op jit(solution)/shard_map/ppermute | solution.py:265
  48.8 5.1 %all-to-all-start.1 = ((bf16[16,64,128]{2,1,0:T(8,128)(2,1)}), bf16[16,64,128]{2,1,0:T(8,128)(2,1)S(1)}, u32[]{:S(2)}, u32[]{:S(2)}) async-start(bf16[16,64,128]{2,1,0:T(8,128)(2,1)} %shard_map.52), calls=%async_computation.1 | async-start | bytes 524288 | tf_op jit(solution)/shard_map/all_to_all | solution.py:275
  56.2 1.8 %collective-permute-start.11 = (bf16[64,1024]{1,0:T(8,128)(2,1)S(1)}, bf16[64,1024]{1,0:T(8,128)(2,1)S(1)}, u32[]{:S(2)}, u32[]{:S(2)}) collective-permute-start(bf16[64,1024]{1,0:T(8,128)(2,1)S(1)} %get-tuple-element.42), channel_id=1, source_target_pairs={{0,12},{1,13},{2,14},{3,15},{4,8},{5,9},{6,10},{7,11},{8,4},{9,5},... | collective-permute-start | bytes 393224 | tf_op jit(solution)/shard_map/ppermute | solution.py:50
  58.6 2.9 %all-to-all-done.1 = bf16[16,64,128]{2,1,0:T(8,128)(2,1)S(1)} async-done(((bf16[16,64,128]{2,1,0:T(8,128)(2,1)}), bf16[16,64,128]{2,1,0:T(8,128)(2,1)S(1)}, u32[]{:S(2)}, u32[]{:S(2)}) %all-to-all-start.1) | async-done | bytes 262176 | tf_op jit(solution)/shard_map/all_to_all | solution.py:275
  61.5 1.8 %collective-permute-done.12.d = bf16[64,1024]{1,0:T(8,128)(2,1)S(1)} collective-permute-done((bf16[64,1024]{1,0:T(8,128)(2,1)S(1)}, bf16[64,1024]{1,0:T(8,128)(2,1)S(1)}, u32[]{:S(2)}, u32[]{:S(2)}) %collective-permute-start.12) | collective-permute-done | bytes 131104 | tf_op jit(solution)/shard_map/ppermute | solution.py:50
  63.4 2.2 %collective-permute-start.13 = (bf16[64,1024]{1,0:T(8,128)(2,1)S(1)}, bf16[64,1024]{1,0:T(8,128)(2,1)S(1)}, u32[]{:S(2)}, u32[]{:S(2)}) collective-permute-start(bf16[64,1024]{1,0:T(8,128)(2,1)S(1)} %shard_map.49.own), channel_id=1, source_target_pairs={{0,16},{16,0},{1,17},{17,1},{2,18},{18,2},{3,19},{19,3},{4,20},{20... | collective-permute-start | bytes 393224 | tf_op jit(solution)/shard_map/ppermute | solution.py:39
  65.8 8.6 %collective-permute-done.13.got = bf16[64,1024]{1,0:T(8,128)(2,1)S(1)} collective-permute-done((bf16[64,1024]{1,0:T(8,128)(2,1)S(1)}, bf16[64,1024]{1,0:T(8,128)(2,1)S(1)}, u32[]{:S(2)}, u32[]{:S(2)}) %collective-permute-start.13) | collective-permute-done | bytes 131104 | tf_op jit(solution)/shard_map/ppermute | solution.py:39
  74.3 1.6 %shard_map.53.refs_0_ = bf16[64,1024]{1,0:T(8,128)(2,1)S(1)} custom-call(s32[10]{0:T(128)S(1)} %stack.63.base, bf16[64,1024]{1,0:T(8,128)(2,1)S(1)} %shard_map.49.own, bf16[64,1024]{1,0:T(8,128)(2,1)S(1)} %collective-permute-done.13.got, f32[64,128]{1,0:T(8,128)S(1)} %get-tuple-element.68.cosine, f32[64,128]{1,0:T(8,128)S(1)} %get-tuple-element.69.sine_v, ...), custom_call_target="tpu_custom_call" | custom-call | tf_op jit(solution)/shard_map/pallas_call | solution.py:195
  76.4 2.8 %collective-permute-start.19 = (bf16[64,1024]{1,0:T(8,128)(2,1)S(1)}, bf16[64,1024]{1,0:T(8,128)(2,1)S(1)}, u32[]{:S(2)}, u32[]{:S(2)}) collective-permute-start(bf16[64,1024]{1,0:T(8,128)(2,1)S(1)} %shard_map.53.refs_0_), channel_id=1, source_target_pairs={{0,2},{1,3},{2,0},{3,1},{4,6},{5,7},{6,4},{7,5},{8,10},{9,11},{10,... | collective-permute-start | bytes 393224 | tf_op jit(solution)/shard_map/ppermute | solution.py:50
  79.8 3.0 %collective-permute-done.18.refs_2_ = bf16[64,1024]{1,0:T(8,128)(2,1)S(1)} collective-permute-done((bf16[64,1024]{1,0:T(8,128)(2,1)S(1)}, bf16[64,1024]{1,0:T(8,128)(2,1)S(1)}, u32[]{:S(2)}, u32[]{:S(2)}) %collective-permute-start.18) | collective-permute-done | bytes 131104 | tf_op jit(solution)/shard_map/ppermute | solution.py:50
  87.3 4.0 %collective-permute-done.20.line = bf16[4,64,1024]{2,1,0:T(8,128)(2,1)S(1)} collective-permute-done((bf16[4,64,1024]{2,1,0:T(8,128)(2,1)S(1)}, bf16[4,64,1024]{2,1,0:T(8,128)(2,1)S(1)}, u32[]{:S(2)}, u32[]{:S(2)}) %collective-permute-start.20) | collective-permute-done | bytes 524320 | tf_op jit(solution)/shard_map/ppermute | solution.py:50
  91.7 7.8 %collective-permute-done.21.line = bf16[4,64,1024]{2,1,0:T(8,128)(2,1)S(1)} collective-permute-done((bf16[4,64,1024]{2,1,0:T(8,128)(2,1)S(1)}, bf16[4,64,1024]{2,1,0:T(8,128)(2,1)S(1)}, u32[]{:S(2)}, u32[]{:S(2)}) %collective-permute-start.21) | collective-permute-done | bytes 524320 | tf_op jit(solution)/shard_map/ppermute | solution.py:50
  101.0 2.2 %collective-permute-start.23 = (bf16[512,512]{1,0:T(8,128)(2,1)S(1)}, bf16[512,512]{1,0:T(8,128)(2,1)S(1)}, u32[]{:S(2)}, u32[]{:S(2)}) collective-permute-start(bf16[512,512]{1,0:T(8,128)(2,1)S(1)} %bitcast.20), channel_id=1, source_target_pairs={{0,32},{32,0},{1,33},{33,1},{2,34},{34,2},{3,35},{35,3},{4,36},{36... | collective-permute-start | bytes 1572872 | tf_op jit(solution)/shard_map/ppermute | solution.py:39
  103.2 1.5 %collective-permute-done.23.got = bf16[512,512]{1,0:T(8,128)(2,1)S(1)} collective-permute-done((bf16[512,512]{1,0:T(8,128)(2,1)S(1)}, bf16[512,512]{1,0:T(8,128)(2,1)S(1)}, u32[]{:S(2)}, u32[]{:S(2)}) %collective-permute-start.23) | collective-permute-done | bytes 524320 | tf_op jit(solution)/shard_map/ppermute | solution.py:39
  104.8 4.1 %collective-permute-start.24 = (bf16[128,512]{1,0:T(8,128)(2,1)S(1)}, bf16[128,512]{1,0:T(8,128)(2,1)S(1)}, u32[]{:S(2)}, u32[]{:S(2)}) collective-permute-start(bf16[128,512]{1,0:T(8,128)(2,1)S(1)} %get-tuple-element.54), channel_id=1, source_target_pairs={{0,128},{64,192},{128,0},{192,64},{1,129},{65,193},{129,1},{193,65... | collective-permute-start | bytes 393224 | tf_op jit(solution)/shard_map/ppermute | solution.py:39
  108.9 2.7 %collective-permute-start.25 = (bf16[128,512]{1,0:T(8,128)(2,1)S(1)}, bf16[128,512]{1,0:T(8,128)(2,1)S(1)}, u32[]{:S(2)}, u32[]{:S(2)}) collective-permute-start(bf16[128,512]{1,0:T(8,128)(2,1)S(1)} %get-tuple-element.55), channel_id=1, source_target_pairs={{0,192},{64,128},{128,64},{192,0},{1,193},{65,129},{129,65},{193,1... | collective-permute-start | bytes 393224 | tf_op jit(solution)/shard_map/ppermute | solution.py:39
  112.5 5.2 %collective-permute-done.25.c = bf16[128,512]{1,0:T(8,128)(2,1)S(1)} collective-permute-done((bf16[128,512]{1,0:T(8,128)(2,1)S(1)}, bf16[128,512]{1,0:T(8,128)(2,1)S(1)}, u32[]{:S(2)}, u32[]{:S(2)}) %collective-permute-start.25) | collective-permute-done | bytes 131104 | tf_op jit(solution)/shard_map/ppermute | solution.py:39
  (69 shorter events, 29.0 us)
Async XLA Ops:
  0.0 6.1 %collective-permute-start.3 = (bf16[128,512]{1,0:T(8,128)(2,1)}, bf16[128,512]{1,0:T(8,128)(2,1)S(1)}, u32[]{:S(2)}, u32[]{:S(2)}) collective-permute-start(bf16[128,512]{1,0:T(8,128)(2,1)} %refs_0_.1), channel_id=1, source_target_pairs={{0,32},{32,0},{1,33},{33,1},{2,34},{34,2},{3,35},{35,3},{4,36},{36... | collective-permute-start | bytes 393224 | tf_op jit(solution)/shard_map/ppermute | solution.py:39
  3.2 11.9 %collective-permute-start = (bf16[128,512]{1,0:T(8,128)(2,1)}, bf16[128,512]{1,0:T(8,128)(2,1)S(1)}, u32[]{:S(2)}, u32[]{:S(2)}) collective-permute-start(bf16[128,512]{1,0:T(8,128)(2,1)} %refs_0_.1), channel_id=1, source_target_pairs={{0,128},{64,192},{128,0},{192,64},{1,129},{65,193},{129,1},{193,65... | collective-permute-start | bytes 393224 | tf_op jit(solution)/shard_map/ppermute | solution.py:39
  4.5 10.7 %collective-permute-start.1 = (bf16[128,512]{1,0:T(8,128)(2,1)}, bf16[128,512]{1,0:T(8,128)(2,1)S(1)}, u32[]{:S(2)}, u32[]{:S(2)}) collective-permute-start(bf16[128,512]{1,0:T(8,128)(2,1)} %refs_0_.1), channel_id=1, source_target_pairs={{0,192},{64,128},{128,64},{192,0},{1,193},{65,129},{129,65},{193,1... | collective-permute-start | bytes 393224 | tf_op jit(solution)/shard_map/ppermute | solution.py:39
  5.9 10.2 %collective-permute-start.2 = (bf16[128,512]{1,0:T(8,128)(2,1)}, bf16[128,512]{1,0:T(8,128)(2,1)S(1)}, u32[]{:S(2)}, u32[]{:S(2)}) collective-permute-start(bf16[128,512]{1,0:T(8,128)(2,1)} %refs_0_.1), channel_id=1, source_target_pairs={{0,64},{64,0},{128,192},{192,128},{1,65},{65,1},{129,193},{193,129... | collective-permute-start | bytes 393224 | tf_op jit(solution)/shard_map/ppermute | solution.py:39
  19.8 13.8 %all-to-all-start = ((bf16[16,64,128]{2,1,0:T(8,128)(2,1)}), bf16[16,64,128]{2,1,0:T(8,128)(2,1)S(1)}, u32[]{:S(2)}, u32[]{:S(2)}) async-start(bf16[16,64,128]{2,1,0:T(8,128)(2,1)} %shard_map.50), calls=%async_computation | async-start | bytes 524288 | tf_op jit(solution)/shard_map/all_to_all | solution.py:258
  28.3 25.6 %collective-permute-start.7 = (bf16[4,64,1024]{2,1,0:T(8,128)(2,1)}, bf16[4,64,1024]{2,1,0:T(8,128)(2,1)S(1)}, u32[]{:S(2)}, u32[]{:S(2)}) collective-permute-start(bf16[4,64,1024]{2,1,0:T(8,128)(2,1)} %get-tuple-element.37), channel_id=1, source_target_pairs={{0,1},{1,0},{2,3},{3,2},{4,5},{5,4},{6,7},{7,6},{8,9},{9,8},{10,11... | collective-permute-start | bytes 1572872 | tf_op jit(solution)/shard_map/ppermute | solution.py:50
  29.7 24.2 %collective-permute-start.8 = (bf16[4,64,1024]{2,1,0:T(8,128)(2,1)}, bf16[4,64,1024]{2,1,0:T(8,128)(2,1)S(1)}, u32[]{:S(2)}, u32[]{:S(2)}) collective-permute-start(bf16[4,64,1024]{2,1,0:T(8,128)(2,1)} %get-tuple-element.38), channel_id=1, source_target_pairs={{0,3},{1,2},{2,1},{3,0},{4,7},{5,6},{6,5},{7,4},{8,11},{9,10},{10,... | collective-permute-start | bytes 1572872 | tf_op jit(solution)/shard_map/ppermute | solution.py:50
  31.5 22.5 %collective-permute-start.9 = (bf16[4,64,1024]{2,1,0:T(8,128)(2,1)}, bf16[4,64,1024]{2,1,0:T(8,128)(2,1)S(1)}, u32[]{:S(2)}, u32[]{:S(2)}) collective-permute-start(bf16[4,64,1024]{2,1,0:T(8,128)(2,1)} %get-tuple-element.39), channel_id=1, source_target_pairs={{0,2},{1,3},{2,0},{3,1},{4,6},{5,7},{6,4},{7,5},{8,10},{9,11},{10,... | collective-permute-start | bytes 1572872 | tf_op jit(solution)/shard_map/ppermute | solution.py:50
  33.7 11.3 %collective-permute-start.14 = (bf16[64,128]{1,0:T(8,128)(2,1)S(1)}, bf16[64,128]{1,0:T(8,128)(2,1)S(1)}, u32[]{:S(2)}, u32[]{:S(2)}) collective-permute-start(bf16[64,128]{1,0:T(8,128)(2,1)S(1)} %shard_map.51), channel_id=1, source_target_pairs={{0,16},{16,0},{32,80},{48,64},{64,144},{80,128},{96,208},{112,192}... | collective-permute-start | bytes 49160 | tf_op jit(solution)/shard_map/ppermute | solution.py:262
  42.0 5.9 %collective-permute-start.15 = (bf16[64,128]{1,0:T(8,128)(2,1)S(1)}, bf16[64,128]{1,0:T(8,128)(2,1)S(1)}, u32[]{:S(2)}, u32[]{:S(2)}) collective-permute-start(bf16[64,128]{1,0:T(8,128)(2,1)S(1)} %shard_map.51), channel_id=1, source_target_pairs={{0,0},{32,64},{64,128},{96,192},{128,32},{160,96},{192,160},{224,2... | collective-permute-start | bytes 49160 | tf_op jit(solution)/shard_map/ppermute | solution.py:265
  48.8 12.7 %all-to-all-start.1 = ((bf16[16,64,128]{2,1,0:T(8,128)(2,1)}), bf16[16,64,128]{2,1,0:T(8,128)(2,1)S(1)}, u32[]{:S(2)}, u32[]{:S(2)}) async-start(bf16[16,64,128]{2,1,0:T(8,128)(2,1)} %shard_map.52), calls=%async_computation.1 | async-start | bytes 524288 | tf_op jit(solution)/shard_map/all_to_all | solution.py:275
  54.7 6.8 %collective-permute-start.10 = (bf16[64,1024]{1,0:T(8,128)(2,1)S(1)}, bf16[64,1024]{1,0:T(8,128)(2,1)S(1)}, u32[]{:S(2)}, u32[]{:S(2)}) collective-permute-start(bf16[64,1024]{1,0:T(8,128)(2,1)S(1)} %get-tuple-element.41), channel_id=1, source_target_pairs={{0,4},{1,5},{2,6},{3,7},{4,0},{5,1},{6,2},{7,3},{8,12},{9,13},{10,... | collective-permute-start | bytes 393224 | tf_op jit(solution)/shard_map/ppermute | solution.py:50
  56.2 5.3 %collective-permute-start.11 = (bf16[64,1024]{1,0:T(8,128)(2,1)S(1)}, bf16[64,1024]{1,0:T(8,128)(2,1)S(1)}, u32[]{:S(2)}, u32[]{:S(2)}) collective-permute-start(bf16[64,1024]{1,0:T(8,128)(2,1)S(1)} %get-tuple-element.42), channel_id=1, source_target_pairs={{0,12},{1,13},{2,14},{3,15},{4,8},{5,9},{6,10},{7,11},{8,4},{9,5},... | collective-permute-start | bytes 393224 | tf_op jit(solution)/shard_map/ppermute | solution.py:50
  58.0 5.3 %collective-permute-start.12 = (bf16[64,1024]{1,0:T(8,128)(2,1)S(1)}, bf16[64,1024]{1,0:T(8,128)(2,1)S(1)}, u32[]{:S(2)}, u32[]{:S(2)}) collective-permute-start(bf16[64,1024]{1,0:T(8,128)(2,1)S(1)} %get-tuple-element.43), channel_id=1, source_target_pairs={{0,8},{1,9},{2,10},{3,11},{4,12},{5,13},{6,14},{7,15},{8,0},{9,1},... | collective-permute-start | bytes 393224 | tf_op jit(solution)/shard_map/ppermute | solution.py:50
  61.5 4.3 %collective-permute-start.16 = (bf16[1024,128]{1,0:T(8,128)(2,1)S(1)}, bf16[1024,128]{1,0:T(8,128)(2,1)S(1)}, u32[]{:S(2)}, u32[]{:S(2)}) collective-permute-start(bf16[1024,128]{1,0:T(8,128)(2,1)S(1)} %bitcast.17), channel_id=1, source_target_pairs={{0,32},{32,0},{1,33},{33,1},{2,34},{34,2},{3,35},{35,3},{4,36},{36... | collective-permute-start | bytes 786440 | tf_op jit(solution)/shard_map/ppermute | solution.py:39
  63.4 11.0 %collective-permute-start.13 = (bf16[64,1024]{1,0:T(8,128)(2,1)S(1)}, bf16[64,1024]{1,0:T(8,128)(2,1)S(1)}, u32[]{:S(2)}, u32[]{:S(2)}) collective-permute-start(bf16[64,1024]{1,0:T(8,128)(2,1)S(1)} %shard_map.49.own), channel_id=1, source_target_pairs={{0,16},{16,0},{1,17},{17,1},{2,18},{18,2},{3,19},{19,3},{4,20},{20... | collective-permute-start | bytes 393224 | tf_op jit(solution)/shard_map/ppermute | solution.py:39
  76.0 6.8 %collective-permute-start.18 = (bf16[64,1024]{1,0:T(8,128)(2,1)S(1)}, bf16[64,1024]{1,0:T(8,128)(2,1)S(1)}, u32[]{:S(2)}, u32[]{:S(2)}) collective-permute-start(bf16[64,1024]{1,0:T(8,128)(2,1)S(1)} %shard_map.53.refs_0_), channel_id=1, source_target_pairs={{0,3},{1,2},{2,1},{3,0},{4,7},{5,6},{6,5},{7,4},{8,11},{9,10},{10,... | collective-permute-start | bytes 393224 | tf_op jit(solution)/shard_map/ppermute | solution.py:50
  76.4 6.4 %collective-permute-start.19 = (bf16[64,1024]{1,0:T(8,128)(2,1)S(1)}, bf16[64,1024]{1,0:T(8,128)(2,1)S(1)}, u32[]{:S(2)}, u32[]{:S(2)}) collective-permute-start(bf16[64,1024]{1,0:T(8,128)(2,1)S(1)} %shard_map.53.refs_0_), channel_id=1, source_target_pairs={{0,2},{1,3},{2,0},{3,1},{4,6},{5,7},{6,4},{7,5},{8,10},{9,11},{10,... | collective-permute-start | bytes 393224 | tf_op jit(solution)/shard_map/ppermute | solution.py:50
  82.9 8.4 %collective-permute-start.20 = (bf16[4,64,1024]{2,1,0:T(8,128)(2,1)S(1)}, bf16[4,64,1024]{2,1,0:T(8,128)(2,1)S(1)}, u32[]{:S(2)}, u32[]{:S(2)}) collective-permute-start(bf16[4,64,1024]{2,1,0:T(8,128)(2,1)S(1)} %shard_map.54.line), channel_id=1, source_target_pairs={{0,4},{1,5},{2,6},{3,7},{4,0},{5,1},{6,2},{7,3},{8,12},{9,13},{10,... | collective-permute-start | bytes 1572872 | tf_op jit(solution)/shard_map/ppermute | solution.py:50
  84.3 15.2 %collective-permute-start.21 = (bf16[4,64,1024]{2,1,0:T(8,128)(2,1)S(1)}, bf16[4,64,1024]{2,1,0:T(8,128)(2,1)S(1)}, u32[]{:S(2)}, u32[]{:S(2)}) collective-permute-start(bf16[4,64,1024]{2,1,0:T(8,128)(2,1)S(1)} %shard_map.54.line), channel_id=1, source_target_pairs={{0,12},{1,13},{2,14},{3,15},{4,8},{5,9},{6,10},{7,11},{8,4},{9,5},... | collective-permute-start | bytes 1572872 | tf_op jit(solution)/shard_map/ppermute | solution.py:50
  85.7 14.2 %collective-permute-start.22 = (bf16[4,64,1024]{2,1,0:T(8,128)(2,1)S(1)}, bf16[4,64,1024]{2,1,0:T(8,128)(2,1)S(1)}, u32[]{:S(2)}, u32[]{:S(2)}) collective-permute-start(bf16[4,64,1024]{2,1,0:T(8,128)(2,1)S(1)} %shard_map.54.line), channel_id=1, source_target_pairs={{0,8},{1,9},{2,10},{3,11},{4,12},{5,13},{6,14},{7,15},{8,0},{9,1},... | collective-permute-start | bytes 1572872 | tf_op jit(solution)/shard_map/ppermute | solution.py:50
  104.8 7.7 %collective-permute-start.24 = (bf16[128,512]{1,0:T(8,128)(2,1)S(1)}, bf16[128,512]{1,0:T(8,128)(2,1)S(1)}, u32[]{:S(2)}, u32[]{:S(2)}) collective-permute-start(bf16[128,512]{1,0:T(8,128)(2,1)S(1)} %get-tuple-element.54), channel_id=1, source_target_pairs={{0,128},{64,192},{128,0},{192,64},{1,129},{65,193},{129,1},{193,65... | collective-permute-start | bytes 393224 | tf_op jit(solution)/shard_map/ppermute | solution.py:39
  108.9 8.8 %collective-permute-start.25 = (bf16[128,512]{1,0:T(8,128)(2,1)S(1)}, bf16[128,512]{1,0:T(8,128)(2,1)S(1)}, u32[]{:S(2)}, u32[]{:S(2)}) collective-permute-start(bf16[128,512]{1,0:T(8,128)(2,1)S(1)} %get-tuple-element.55), channel_id=1, source_target_pairs={{0,192},{64,128},{128,64},{192,0},{1,193},{65,129},{129,65},{193,1... | collective-permute-start | bytes 393224 | tf_op jit(solution)/shard_map/ppermute | solution.py:39
  111.6 7.2 %collective-permute-start.26 = (bf16[128,512]{1,0:T(8,128)(2,1)S(1)}, bf16[128,512]{1,0:T(8,128)(2,1)S(1)}, u32[]{:S(2)}, u32[]{:S(2)}) collective-permute-start(bf16[128,512]{1,0:T(8,128)(2,1)S(1)} %get-tuple-element.56), channel_id=1, source_target_pairs={{0,64},{64,0},{128,192},{192,128},{1,65},{65,1},{129,193},{193,129... | collective-permute-start | bytes 393224 | tf_op jit(solution)/shard_map/ppermute | solution.py:39
  (11 other events, 62.3 us)

commit v14 on v11

--- a/solution.py
+++ b/solution.py
@@ -15,7 +15,7 @@
 COL = ("zh", "y", "x")
 PLANE = ("y", "x")
 STEPS = (0, 1, 3, 2)
-FAR = (2, 3, 1)
+FAR = (3, 2, 1)
 BF16 = jnp.bfloat16
 F32 = jnp.float32
 VMEM = pl.BlockSpec(memory_space=pltpu.VMEM)

time: 119 us -> 121 us (1.017); the launches traced: 118 us -> 121 us
  waiting for transfers between devices: 41.4 us -> 44.8 us
    ppermute x13, starting transfers between devices: 23.8 us -> 27.8 us  [partner(): return lax.ppermute(block, axis, [(i, i ^ step) for i in range(size)])]
    ppermute x13, waiting for transfers between devices: 18.5 us -> 21.2 us  [partner(): return lax.ppermute(block, axis, [(i, i ^ step) for i in range(size)])]
    ppermute x1, starting transfers between devices: 5.31 us -> 3.38 us  [shards(): here = lax.ppermute(kv, ROW, moves)]
    ppermute x12, starting transfers between devices: 15.9 us -> 14.3 us  [across_plane(): return lax.ppermute(block, ('core', *PLANE), pairs)]
    ppermute x1, starting transfers between devices: 5.95 us -> 4.58 us  [shards(): lax.ppermute(kv, (*ROW, 'zh'), [(2 * e + h, 2 * r + 1 - h) for e, r in mo...]
    ppermute x1, waiting for transfers between devices: 0.77 us -> 2.06 us  [shards(): lax.ppermute(kv, (*ROW, 'zh'), [(2 * e + h, 2 * r + 1 - h) for e, r in mo...]
  transfers between devices with their start and end apart: 29 -> 29, of which waited for: 18 -> 16; matrix products, arithmetic and copies ran while one was open for 1% -> 1% of each run, Pallas kernels for 5% -> 5%
where the time goes in v14:
time: 121 us
  starting transfers between devices  61.5 us (51%)
  waiting for transfers between devices  44.8 us (37%)
  Pallas kernels  10.8 us (9%)
  local copies, waits for them, and re-layouts  3.13 us (3%)
    ppermute x13, starting transfers between devices, partner(): return lax.ppermute(block, axis, [(i, i ^ step) for i in range(size)])  27.8 us
    ppermute x13, waiting for transfers between devices, partner(): return lax.ppermute(block, axis, [(i, i ^ step) for i in range(size)])  21.2 us
    ppermute x12, waiting for transfers between devices, across_plane(): return lax.ppermute(block, ('core', *PLANE), pairs)  17 us
    ppermute x12, starting transfers between devices, across_plane(): return lax.ppermute(block, ('core', *PLANE), pairs)  14.3 us
    pallas_call x15, Pallas kernels, call(): pl.pallas_call(kernel, out_shape=[s if isinstance(s, jax.ShapeDtypeStruct...  10.8 us
    all_to_all x1, starting transfers between devices, shards(): kv_parts = lax.all_to_all(kv_parts, PLANE, 0, 0, tiled=True)  6.75 us
    all_to_all x1, starting transfers between devices, shards(): lax.all_to_all(kv_block, PLANE, 0, 0, tiled=True).reshape(total, HD)  4.68 us
    ppermute x1, starting transfers between devices, shards(): lax.ppermute(kv, (*ROW, 'zh'), [(2 * e + h, 2 * r + 1 - h) for e, r in mo...  4.58 us
  transfers between devices with their start and end apart: 29, of which 16 were waited for; matrix products, arithmetic and copies ran while one was open for 1% of the time, Pallas kernels for 5%

profile of v14, /device:TPU:1, one launch (start us, length us, event | category | flops | bytes accessed | tf_op | source)
XLA Modules:
  0.0 121.0 jit_solution(13081330709275282902)
XLA Ops:
  0.0 3.2 %collective-permute-start.3 = (bf16[128,512]{1,0:T(8,128)(2,1)}, bf16[128,512]{1,0:T(8,128)(2,1)S(1)}, u32[]{:S(2)}, u32[]{:S(2)}) collective-permute-start(bf16[128,512]{1,0:T(8,128)(2,1)} %refs_0_.1), channel_id=1, source_target_pairs={{0,32},{32,0},{1,33},{33,1},{2,34},{34,2},{3,35},{35,3},{4,36},{36... | collective-permute-start | bytes 393224 | tf_op jit(solution)/shard_map/ppermute | solution.py:39
  3.2 2.6 %collective-permute-start = (bf16[128,512]{1,0:T(8,128)(2,1)}, bf16[128,512]{1,0:T(8,128)(2,1)S(1)}, u32[]{:S(2)}, u32[]{:S(2)}) collective-permute-start(bf16[128,512]{1,0:T(8,128)(2,1)} %refs_0_.1), channel_id=1, source_target_pairs={{0,192},{64,128},{128,64},{192,0},{1,193},{65,129},{129,65},{193,1... | collective-permute-start | bytes 393224 | tf_op jit(solution)/shard_map/ppermute | solution.py:39
  10.4 6.5 %collective-permute-done.1.refs_1_ = bf16[128,512]{1,0:T(8,128)(2,1)S(1)} collective-permute-done((bf16[128,512]{1,0:T(8,128)(2,1)}, bf16[128,512]{1,0:T(8,128)(2,1)S(1)}, u32[]{:S(2)}, u32[]{:S(2)}) %collective-permute-start.1) | collective-permute-done | bytes 131104 | tf_op jit(solution)/shard_map/ppermute | solution.py:39
  20.2 6.8 %all-to-all-start = ((bf16[16,64,128]{2,1,0:T(8,128)(2,1)}), bf16[16,64,128]{2,1,0:T(8,128)(2,1)S(1)}, u32[]{:S(2)}, u32[]{:S(2)}) async-start(bf16[16,64,128]{2,1,0:T(8,128)(2,1)} %shard_map.50), calls=%async_computation | async-start | bytes 524288 | tf_op jit(solution)/shard_map/all_to_all | solution.py:258
  27.0 2.7 %shard_map.47 = (bf16[4,64,1024]{2,1,0:T(8,128)(2,1)S(1)}, bf16[4,64,1024]{2,1,0:T(8,128)(2,1)}, bf16[4,64,1024]{2,1,0:T(8,128)(2,1)}, bf16[4,64,1024]{2,1,0:T(8,128)(2,1)}) custom-call(s32[4]{0:T(128)S(1)} %pad_add_fusion.place, bf16[128,512]{1,0:T(8,128)(2,1)S(1)} %collective-permute-done.refs_0_, bf16[128,512]{1,0:T(8,128)(2,1)S(1)} %collective-permute-done.1.refs_1_, ...), custom_call_target="tpu_custom_call" | custom-call | tf_op jit(solution)/shard_map/pallas_call | solution.py:195
  35.1 3.4 %collective-permute-start.14 = (bf16[64,128]{1,0:T(8,128)(2,1)S(1)}, bf16[64,128]{1,0:T(8,128)(2,1)S(1)}, u32[]{:S(2)}, u32[]{:S(2)}) collective-permute-start(bf16[64,128]{1,0:T(8,128)(2,1)S(1)} %shard_map.51), channel_id=1, source_target_pairs={{0,0},{32,64},{64,128},{96,192},{128,32},{160,96},{192,160},{224,2... | collective-permute-start | bytes 49160 | tf_op jit(solution)/shard_map/ppermute | solution.py:262
  38.5 4.6 %collective-permute-start.15 = (bf16[64,128]{1,0:T(8,128)(2,1)S(1)}, bf16[64,128]{1,0:T(8,128)(2,1)S(1)}, u32[]{:S(2)}, u32[]{:S(2)}) collective-permute-start(bf16[64,128]{1,0:T(8,128)(2,1)S(1)} %shard_map.51), channel_id=1, source_target_pairs={{0,16},{16,0},{32,80},{48,64},{64,144},{80,128},{96,208},{112,192}... | collective-permute-start | bytes 49160 | tf_op jit(solution)/shard_map/ppermute | solution.py:263
  43.2 2.1 %collective-permute-done.15.b = bf16[64,128]{1,0:T(8,128)(2,1)S(1)} collective-permute-done((bf16[64,128]{1,0:T(8,128)(2,1)S(1)}, bf16[64,128]{1,0:T(8,128)(2,1)S(1)}, u32[]{:S(2)}, u32[]{:S(2)}) %collective-permute-start.15) | collective-permute-done | bytes 16416 | tf_op jit(solution)/shard_map/ppermute | solution.py:263
  46.1 4.7 %all-to-all-start.1 = ((bf16[16,64,128]{2,1,0:T(8,128)(2,1)}), bf16[16,64,128]{2,1,0:T(8,128)(2,1)S(1)}, u32[]{:S(2)}, u32[]{:S(2)}) async-start(bf16[16,64,128]{2,1,0:T(8,128)(2,1)} %shard_map.52), calls=%async_computation.1 | async-start | bytes 524288 | tf_op jit(solution)/shard_map/all_to_all | solution.py:275
  53.0 1.8 %collective-permute-start.11 = (bf16[64,1024]{1,0:T(8,128)(2,1)S(1)}, bf16[64,1024]{1,0:T(8,128)(2,1)S(1)}, u32[]{:S(2)}, u32[]{:S(2)}) collective-permute-start(bf16[64,1024]{1,0:T(8,128)(2,1)S(1)} %get-tuple-element.42), channel_id=1, source_target_pairs={{0,12},{1,13},{2,14},{3,15},{4,8},{5,9},{6,10},{7,11},{8,4},{9,5},... | collective-permute-start | bytes 393224 | tf_op jit(solution)/shard_map/ppermute | solution.py:50
  55.4 3.3 %all-to-all-done.1 = bf16[16,64,128]{2,1,0:T(8,128)(2,1)S(1)} async-done(((bf16[16,64,128]{2,1,0:T(8,128)(2,1)}), bf16[16,64,128]{2,1,0:T(8,128)(2,1)S(1)}, u32[]{:S(2)}, u32[]{:S(2)}) %all-to-all-start.1) | async-done | bytes 262176 | tf_op jit(solution)/shard_map/all_to_all | solution.py:275
  58.7 2.9 %collective-permute-start.16 = (bf16[1024,128]{1,0:T(8,128)(2,1)S(1)}, bf16[1024,128]{1,0:T(8,128)(2,1)S(1)}, u32[]{:S(2)}, u32[]{:S(2)}) collective-permute-start(bf16[1024,128]{1,0:T(8,128)(2,1)S(1)} %bitcast.17), channel_id=1, source_target_pairs={{0,32},{32,0},{1,33},{33,1},{2,34},{34,2},{3,35},{35,3},{4,36},{36... | collective-permute-start | bytes 786440 | tf_op jit(solution)/shard_map/ppermute | solution.py:39
  61.7 4.9 %collective-permute-start.13 = (bf16[64,1024]{1,0:T(8,128)(2,1)S(1)}, bf16[64,1024]{1,0:T(8,128)(2,1)S(1)}, u32[]{:S(2)}, u32[]{:S(2)}) collective-permute-start(bf16[64,1024]{1,0:T(8,128)(2,1)S(1)} %shard_map.49.own), channel_id=1, source_target_pairs={{0,16},{16,0},{1,17},{17,1},{2,18},{18,2},{3,19},{19,3},{4,20},{20... | collective-permute-start | bytes 393224 | tf_op jit(solution)/shard_map/ppermute | solution.py:39
  66.8 3.0 %collective-permute-done.13.got = bf16[64,1024]{1,0:T(8,128)(2,1)S(1)} collective-permute-done((bf16[64,1024]{1,0:T(8,128)(2,1)S(1)}, bf16[64,1024]{1,0:T(8,128)(2,1)S(1)}, u32[]{:S(2)}, u32[]{:S(2)}) %collective-permute-start.13) | collective-permute-done | bytes 131104 | tf_op jit(solution)/shard_map/ppermute | solution.py:39
  71.6 2.4 %collective-permute-start.18 = (bf16[64,1024]{1,0:T(8,128)(2,1)S(1)}, bf16[64,1024]{1,0:T(8,128)(2,1)S(1)}, u32[]{:S(2)}, u32[]{:S(2)}) collective-permute-start(bf16[64,1024]{1,0:T(8,128)(2,1)S(1)} %shard_map.53.refs_0_), channel_id=1, source_target_pairs={{0,3},{1,2},{2,1},{3,0},{4,7},{5,6},{6,5},{7,4},{8,11},{9,10},{10,... | collective-permute-start | bytes 393224 | tf_op jit(solution)/shard_map/ppermute | solution.py:50
  75.2 2.1 %collective-permute-done.18.refs_2_ = bf16[64,1024]{1,0:T(8,128)(2,1)S(1)} collective-permute-done((bf16[64,1024]{1,0:T(8,128)(2,1)S(1)}, bf16[64,1024]{1,0:T(8,128)(2,1)S(1)}, u32[]{:S(2)}, u32[]{:S(2)}) %collective-permute-start.18) | collective-permute-done | bytes 131104 | tf_op jit(solution)/shard_map/ppermute | solution.py:50
  77.3 2.0 %collective-permute-done.19.refs_3_ = bf16[64,1024]{1,0:T(8,128)(2,1)S(1)} collective-permute-done((bf16[64,1024]{1,0:T(8,128)(2,1)S(1)}, bf16[64,1024]{1,0:T(8,128)(2,1)S(1)}, u32[]{:S(2)}, u32[]{:S(2)}) %collective-permute-start.19) | collective-permute-done | bytes 131104 | tf_op jit(solution)/shard_map/ppermute | solution.py:50
  79.9 2.8 %collective-permute-start.22 = (bf16[4,64,1024]{2,1,0:T(8,128)(2,1)S(1)}, bf16[4,64,1024]{2,1,0:T(8,128)(2,1)S(1)}, u32[]{:S(2)}, u32[]{:S(2)}) collective-permute-start(bf16[4,64,1024]{2,1,0:T(8,128)(2,1)S(1)} %shard_map.54.line), channel_id=1, source_target_pairs={{0,8},{1,9},{2,10},{3,11},{4,12},{5,13},{6,14},{7,15},{8,0},{9,1},... | collective-permute-start | bytes 1572872 | tf_op jit(solution)/shard_map/ppermute | solution.py:50
  83.2 4.6 %collective-permute-done.20.line = bf16[4,64,1024]{2,1,0:T(8,128)(2,1)S(1)} collective-permute-done((bf16[4,64,1024]{2,1,0:T(8,128)(2,1)S(1)}, bf16[4,64,1024]{2,1,0:T(8,128)(2,1)S(1)}, u32[]{:S(2)}, u32[]{:S(2)}) %collective-permute-start.20) | collective-permute-done | bytes 524320 | tf_op jit(solution)/shard_map/ppermute | solution.py:50
  88.1 7.7 %collective-permute-done.21.line = bf16[4,64,1024]{2,1,0:T(8,128)(2,1)S(1)} collective-permute-done((bf16[4,64,1024]{2,1,0:T(8,128)(2,1)S(1)}, bf16[4,64,1024]{2,1,0:T(8,128)(2,1)S(1)}, u32[]{:S(2)}, u32[]{:S(2)}) %collective-permute-start.21) | collective-permute-done | bytes 524320 | tf_op jit(solution)/shard_map/ppermute | solution.py:50
  97.4 7.1 %collective-permute-start.23 = (bf16[512,512]{1,0:T(8,128)(2,1)S(1)}, bf16[512,512]{1,0:T(8,128)(2,1)S(1)}, u32[]{:S(2)}, u32[]{:S(2)}) collective-permute-start(bf16[512,512]{1,0:T(8,128)(2,1)S(1)} %bitcast.20), channel_id=1, source_target_pairs={{0,32},{32,0},{1,33},{33,1},{2,34},{34,2},{3,35},{35,3},{4,36},{36... | collective-permute-start | bytes 1572872 | tf_op jit(solution)/shard_map/ppermute | solution.py:39
  106.1 4.5 %collective-permute-start.24 = (bf16[128,512]{1,0:T(8,128)(2,1)S(1)}, bf16[128,512]{1,0:T(8,128)(2,1)S(1)}, u32[]{:S(2)}, u32[]{:S(2)}) collective-permute-start(bf16[128,512]{1,0:T(8,128)(2,1)S(1)} %get-tuple-element.54), channel_id=1, source_target_pairs={{0,192},{64,128},{128,64},{192,0},{1,193},{65,129},{129,65},{193,1... | collective-permute-start | bytes 393224 | tf_op jit(solution)/shard_map/ppermute | solution.py:39
  111.1 3.2 %collective-permute-done.24.b = bf16[128,512]{1,0:T(8,128)(2,1)S(1)} collective-permute-done((bf16[128,512]{1,0:T(8,128)(2,1)S(1)}, bf16[128,512]{1,0:T(8,128)(2,1)S(1)}, u32[]{:S(2)}, u32[]{:S(2)}) %collective-permute-start.24) | collective-permute-done | bytes 131104 | tf_op jit(solution)/shard_map/ppermute | solution.py:39
  114.2 6.0 %collective-permute-done.25.c = bf16[128,512]{1,0:T(8,128)(2,1)S(1)} collective-permute-done((bf16[128,512]{1,0:T(8,128)(2,1)S(1)}, bf16[128,512]{1,0:T(8,128)(2,1)S(1)}, u32[]{:S(2)}, u32[]{:S(2)}) %collective-permute-start.25) | collective-permute-done | bytes 131104 | tf_op jit(solution)/shard_map/ppermute | solution.py:39
  (69 shorter events, 26.0 us)
Async XLA Ops:
  0.0 6.8 %collective-permute-start.3 = (bf16[128,512]{1,0:T(8,128)(2,1)}, bf16[128,512]{1,0:T(8,128)(2,1)S(1)}, u32[]{:S(2)}, u32[]{:S(2)}) collective-permute-start(bf16[128,512]{1,0:T(8,128)(2,1)} %refs_0_.1), channel_id=1, source_target_pairs={{0,32},{32,0},{1,33},{33,1},{2,34},{34,2},{3,35},{35,3},{4,36},{36... | collective-permute-start | bytes 393224 | tf_op jit(solution)/shard_map/ppermute | solution.py:39
  3.2 7.2 %collective-permute-start = (bf16[128,512]{1,0:T(8,128)(2,1)}, bf16[128,512]{1,0:T(8,128)(2,1)S(1)}, u32[]{:S(2)}, u32[]{:S(2)}) collective-permute-start(bf16[128,512]{1,0:T(8,128)(2,1)} %refs_0_.1), channel_id=1, source_target_pairs={{0,192},{64,128},{128,64},{192,0},{1,193},{65,129},{129,65},{193,1... | collective-permute-start | bytes 393224 | tf_op jit(solution)/shard_map/ppermute | solution.py:39
  5.9 11.0 %collective-permute-start.1 = (bf16[128,512]{1,0:T(8,128)(2,1)}, bf16[128,512]{1,0:T(8,128)(2,1)S(1)}, u32[]{:S(2)}, u32[]{:S(2)}) collective-permute-start(bf16[128,512]{1,0:T(8,128)(2,1)} %refs_0_.1), channel_id=1, source_target_pairs={{0,128},{64,192},{128,0},{192,64},{1,129},{65,193},{129,1},{193,65... | collective-permute-start | bytes 393224 | tf_op jit(solution)/shard_map/ppermute | solution.py:39
  5.9 11.0 %collective-permute-start.2 = (bf16[128,512]{1,0:T(8,128)(2,1)}, bf16[128,512]{1,0:T(8,128)(2,1)S(1)}, u32[]{:S(2)}, u32[]{:S(2)}) collective-permute-start(bf16[128,512]{1,0:T(8,128)(2,1)} %refs_0_.1), channel_id=1, source_target_pairs={{0,64},{64,0},{128,192},{192,128},{1,65},{65,1},{129,193},{193,129... | collective-permute-start | bytes 393224 | tf_op jit(solution)/shard_map/ppermute | solution.py:39
  20.2 14.9 %all-to-all-start = ((bf16[16,64,128]{2,1,0:T(8,128)(2,1)}), bf16[16,64,128]{2,1,0:T(8,128)(2,1)S(1)}, u32[]{:S(2)}, u32[]{:S(2)}) async-start(bf16[16,64,128]{2,1,0:T(8,128)(2,1)} %shard_map.50), calls=%async_computation | async-start | bytes 524288 | tf_op jit(solution)/shard_map/all_to_all | solution.py:258
  29.8 21.0 %collective-permute-start.7 = (bf16[4,64,1024]{2,1,0:T(8,128)(2,1)}, bf16[4,64,1024]{2,1,0:T(8,128)(2,1)S(1)}, u32[]{:S(2)}, u32[]{:S(2)}) collective-permute-start(bf16[4,64,1024]{2,1,0:T(8,128)(2,1)} %get-tuple-element.37), channel_id=1, source_target_pairs={{0,1},{1,0},{2,3},{3,2},{4,5},{5,4},{6,7},{7,6},{8,9},{9,8},{10,11... | collective-permute-start | bytes 1572872 | tf_op jit(solution)/shard_map/ppermute | solution.py:50
  31.1 19.6 %collective-permute-start.8 = (bf16[4,64,1024]{2,1,0:T(8,128)(2,1)}, bf16[4,64,1024]{2,1,0:T(8,128)(2,1)S(1)}, u32[]{:S(2)}, u32[]{:S(2)}) collective-permute-start(bf16[4,64,1024]{2,1,0:T(8,128)(2,1)} %get-tuple-element.38), channel_id=1, source_target_pairs={{0,3},{1,2},{2,1},{3,0},{4,7},{5,6},{6,5},{7,4},{8,11},{9,10},{10,... | collective-permute-start | bytes 1572872 | tf_op jit(solution)/shard_map/ppermute | solution.py:50
  32.9 17.9 %collective-permute-start.9 = (bf16[4,64,1024]{2,1,0:T(8,128)(2,1)}, bf16[4,64,1024]{2,1,0:T(8,128)(2,1)S(1)}, u32[]{:S(2)}, u32[]{:S(2)}) collective-permute-start(bf16[4,64,1024]{2,1,0:T(8,128)(2,1)} %get-tuple-element.39), channel_id=1, source_target_pairs={{0,2},{1,3},{2,0},{3,1},{4,6},{5,7},{6,4},{7,5},{8,10},{9,11},{10,... | collective-permute-start | bytes 1572872 | tf_op jit(solution)/shard_map/ppermute | solution.py:50
  35.1 8.1 %collective-permute-start.14 = (bf16[64,128]{1,0:T(8,128)(2,1)S(1)}, bf16[64,128]{1,0:T(8,128)(2,1)S(1)}, u32[]{:S(2)}, u32[]{:S(2)}) collective-permute-start(bf16[64,128]{1,0:T(8,128)(2,1)S(1)} %shard_map.51), channel_id=1, source_target_pairs={{0,0},{32,64},{64,128},{96,192},{128,32},{160,96},{192,160},{224,2... | collective-permute-start | bytes 49160 | tf_op jit(solution)/shard_map/ppermute | solution.py:262
  38.5 6.7 %collective-permute-start.15 = (bf16[64,128]{1,0:T(8,128)(2,1)S(1)}, bf16[64,128]{1,0:T(8,128)(2,1)S(1)}, u32[]{:S(2)}, u32[]{:S(2)}) collective-permute-start(bf16[64,128]{1,0:T(8,128)(2,1)S(1)} %shard_map.51), channel_id=1, source_target_pairs={{0,16},{16,0},{32,80},{48,64},{64,144},{80,128},{96,208},{112,192}... | collective-permute-start | bytes 49160 | tf_op jit(solution)/shard_map/ppermute | solution.py:263
  46.1 12.7 %all-to-all-start.1 = ((bf16[16,64,128]{2,1,0:T(8,128)(2,1)}), bf16[16,64,128]{2,1,0:T(8,128)(2,1)S(1)}, u32[]{:S(2)}, u32[]{:S(2)}) async-start(bf16[16,64,128]{2,1,0:T(8,128)(2,1)} %shard_map.52), calls=%async_computation.1 | async-start | bytes 524288 | tf_op jit(solution)/shard_map/all_to_all | solution.py:275
  51.6 10.0 %collective-permute-start.10 = (bf16[64,1024]{1,0:T(8,128)(2,1)S(1)}, bf16[64,1024]{1,0:T(8,128)(2,1)S(1)}, u32[]{:S(2)}, u32[]{:S(2)}) collective-permute-start(bf16[64,1024]{1,0:T(8,128)(2,1)S(1)} %get-tuple-element.41), channel_id=1, source_target_pairs={{0,4},{1,5},{2,6},{3,7},{4,0},{5,1},{6,2},{7,3},{8,12},{9,13},{10,... | collective-permute-start | bytes 393224 | tf_op jit(solution)/shard_map/ppermute | solution.py:50
  53.0 8.6 %collective-permute-start.11 = (bf16[64,1024]{1,0:T(8,128)(2,1)S(1)}, bf16[64,1024]{1,0:T(8,128)(2,1)S(1)}, u32[]{:S(2)}, u32[]{:S(2)}) collective-permute-start(bf16[64,1024]{1,0:T(8,128)(2,1)S(1)} %get-tuple-element.42), channel_id=1, source_target_pairs={{0,12},{1,13},{2,14},{3,15},{4,8},{5,9},{6,10},{7,11},{8,4},{9,5},... | collective-permute-start | bytes 393224 | tf_op jit(solution)/shard_map/ppermute | solution.py:50
  54.8 6.8 %collective-permute-start.12 = (bf16[64,1024]{1,0:T(8,128)(2,1)S(1)}, bf16[64,1024]{1,0:T(8,128)(2,1)S(1)}, u32[]{:S(2)}, u32[]{:S(2)}) collective-permute-start(bf16[64,1024]{1,0:T(8,128)(2,1)S(1)} %get-tuple-element.43), channel_id=1, source_target_pairs={{0,8},{1,9},{2,10},{3,11},{4,12},{5,13},{6,14},{7,15},{8,0},{9,1},... | collective-permute-start | bytes 393224 | tf_op jit(solution)/shard_map/ppermute | solution.py:50
  58.7 8.1 %collective-permute-start.16 = (bf16[1024,128]{1,0:T(8,128)(2,1)S(1)}, bf16[1024,128]{1,0:T(8,128)(2,1)S(1)}, u32[]{:S(2)}, u32[]{:S(2)}) collective-permute-start(bf16[1024,128]{1,0:T(8,128)(2,1)S(1)} %bitcast.17), channel_id=1, source_target_pairs={{0,32},{32,0},{1,33},{33,1},{2,34},{34,2},{3,35},{35,3},{4,36},{36... | collective-permute-start | bytes 786440 | tf_op jit(solution)/shard_map/ppermute | solution.py:39
  61.7 8.1 %collective-permute-start.13 = (bf16[64,1024]{1,0:T(8,128)(2,1)S(1)}, bf16[64,1024]{1,0:T(8,128)(2,1)S(1)}, u32[]{:S(2)}, u32[]{:S(2)}) collective-permute-start(bf16[64,1024]{1,0:T(8,128)(2,1)S(1)} %shard_map.49.own), channel_id=1, source_target_pairs={{0,16},{16,0},{1,17},{17,1},{2,18},{18,2},{3,19},{19,3},{4,20},{20... | collective-permute-start | bytes 393224 | tf_op jit(solution)/shard_map/ppermute | solution.py:39
  71.6 5.7 %collective-permute-start.18 = (bf16[64,1024]{1,0:T(8,128)(2,1)S(1)}, bf16[64,1024]{1,0:T(8,128)(2,1)S(1)}, u32[]{:S(2)}, u32[]{:S(2)}) collective-permute-start(bf16[64,1024]{1,0:T(8,128)(2,1)S(1)} %shard_map.53.refs_0_), channel_id=1, source_target_pairs={{0,3},{1,2},{2,1},{3,0},{4,7},{5,6},{6,5},{7,4},{8,11},{9,10},{10,... | collective-permute-start | bytes 393224 | tf_op jit(solution)/shard_map/ppermute | solution.py:50
  79.4 8.3 %collective-permute-start.20 = (bf16[4,64,1024]{2,1,0:T(8,128)(2,1)S(1)}, bf16[4,64,1024]{2,1,0:T(8,128)(2,1)S(1)}, u32[]{:S(2)}, u32[]{:S(2)}) collective-permute-start(bf16[4,64,1024]{2,1,0:T(8,128)(2,1)S(1)} %shard_map.54.line), channel_id=1, source_target_pairs={{0,4},{1,5},{2,6},{3,7},{4,0},{5,1},{6,2},{7,3},{8,12},{9,13},{10,... | collective-permute-start | bytes 1572872 | tf_op jit(solution)/shard_map/ppermute | solution.py:50
  79.5 16.4 %collective-permute-start.21 = (bf16[4,64,1024]{2,1,0:T(8,128)(2,1)S(1)}, bf16[4,64,1024]{2,1,0:T(8,128)(2,1)S(1)}, u32[]{:S(2)}, u32[]{:S(2)}) collective-permute-start(bf16[4,64,1024]{2,1,0:T(8,128)(2,1)S(1)} %shard_map.54.line), channel_id=1, source_target_pairs={{0,12},{1,13},{2,14},{3,15},{4,8},{5,9},{6,10},{7,11},{8,4},{9,5},... | collective-permute-start | bytes 1572872 | tf_op jit(solution)/shard_map/ppermute | solution.py:50
  79.9 16.4 %collective-permute-start.22 = (bf16[4,64,1024]{2,1,0:T(8,128)(2,1)S(1)}, bf16[4,64,1024]{2,1,0:T(8,128)(2,1)S(1)}, u32[]{:S(2)}, u32[]{:S(2)}) collective-permute-start(bf16[4,64,1024]{2,1,0:T(8,128)(2,1)S(1)} %shard_map.54.line), channel_id=1, source_target_pairs={{0,8},{1,9},{2,10},{3,11},{4,12},{5,13},{6,14},{7,15},{8,0},{9,1},... | collective-permute-start | bytes 1572872 | tf_op jit(solution)/shard_map/ppermute | solution.py:50
  97.4 8.6 %collective-permute-start.23 = (bf16[512,512]{1,0:T(8,128)(2,1)S(1)}, bf16[512,512]{1,0:T(8,128)(2,1)S(1)}, u32[]{:S(2)}, u32[]{:S(2)}) collective-permute-start(bf16[512,512]{1,0:T(8,128)(2,1)S(1)} %bitcast.20), channel_id=1, source_target_pairs={{0,32},{32,0},{1,33},{33,1},{2,34},{34,2},{3,35},{35,3},{4,36},{36... | collective-permute-start | bytes 1572872 | tf_op jit(solution)/shard_map/ppermute | solution.py:39
  106.1 8.1 %collective-permute-start.24 = (bf16[128,512]{1,0:T(8,128)(2,1)S(1)}, bf16[128,512]{1,0:T(8,128)(2,1)S(1)}, u32[]{:S(2)}, u32[]{:S(2)}) collective-permute-start(bf16[128,512]{1,0:T(8,128)(2,1)S(1)} %get-tuple-element.54), channel_id=1, source_target_pairs={{0,192},{64,128},{128,64},{192,0},{1,193},{65,129},{129,65},{193,1... | collective-permute-start | bytes 393224 | tf_op jit(solution)/shard_map/ppermute | solution.py:39
  110.7 9.6 %collective-permute-start.25 = (bf16[128,512]{1,0:T(8,128)(2,1)S(1)}, bf16[128,512]{1,0:T(8,128)(2,1)S(1)}, u32[]{:S(2)}, u32[]{:S(2)}) collective-permute-start(bf16[128,512]{1,0:T(8,128)(2,1)S(1)} %get-tuple-element.55), channel_id=1, source_target_pairs={{0,128},{64,192},{128,0},{192,64},{1,129},{65,193},{129,1},{193,65... | collective-permute-start | bytes 393224 | tf_op jit(solution)/shard_map/ppermute | solution.py:39
  110.7 9.6 %collective-permute-start.26 = (bf16[128,512]{1,0:T(8,128)(2,1)S(1)}, bf16[128,512]{1,0:T(8,128)(2,1)S(1)}, u32[]{:S(2)}, u32[]{:S(2)}) collective-permute-start(bf16[128,512]{1,0:T(8,128)(2,1)S(1)} %get-tuple-element.56), channel_id=1, source_target_pairs={{0,64},{64,0},{128,192},{192,128},{1,65},{65,1},{129,193},{193,129... | collective-permute-start | bytes 393224 | tf_op jit(solution)/shard_map/ppermute | solution.py:39
  (11 other events, 58.7 us)

commit v15 on v11

--- a/solution.py
+++ b/solution.py
@@ -14,7 +14,7 @@
 ROW = ("zl", "core")
 COL = ("zh", "y", "x")
 PLANE = ("y", "x")
-STEPS = (0, 1, 3, 2)
+STEPS = (0, 3, 1, 2)
 FAR = (2, 3, 1)
 BF16 = jnp.bfloat16
 F32 = jnp.float32

time: 119 us -> 119 us (level)
  starting transfers between devices: 61.7 us -> 63.2 us
    ppermute x12, waiting for transfers between devices: 17.4 us -> 16.2 us  [across_plane(): return lax.ppermute(block, ('core', *PLANE), pairs)]
  transfers between devices with their start and end apart: 29 -> 29, of which waited for: 18 -> 19; matrix products, arithmetic and copies ran while one was open for 1% -> 1% of each run, Pallas kernels for 5% -> 5%
where the time goes in v15:
time: 119 us; the launch traced here: 118 us
  starting transfers between devices  63.2 us (53%)
  waiting for transfers between devices  40.5 us (34%)
  Pallas kernels  10.8 us (9%)
  local copies, waits for them, and re-layouts  3.13 us (3%)
    ppermute x13, starting transfers between devices, partner(): return lax.ppermute(block, axis, [(i, i ^ step) for i in range(size)])  24.2 us
    ppermute x13, waiting for transfers between devices, partner(): return lax.ppermute(block, axis, [(i, i ^ step) for i in range(size)])  19 us
    ppermute x12, starting transfers between devices, across_plane(): return lax.ppermute(block, ('core', *PLANE), pairs)  16.6 us
    ppermute x12, waiting for transfers between devices, across_plane(): return lax.ppermute(block, ('core', *PLANE), pairs)  16.2 us
    pallas_call x15, Pallas kernels, call(): pl.pallas_call(kernel, out_shape=[s if isinstance(s, jax.ShapeDtypeStruct...  10.8 us
    ppermute x1, starting transfers between devices, shards(): lax.ppermute(kv, (*ROW, 'zh'), [(2 * e + h, 2 * r + 1 - h) for e, r in mo...  5.95 us
    all_to_all x1, starting transfers between devices, shards(): kv_parts = lax.all_to_all(kv_parts, PLANE, 0, 0, tiled=True)  5.65 us
    all_to_all x1, starting transfers between devices, shards(): lax.all_to_all(kv_block, PLANE, 0, 0, tiled=True).reshape(total, HD)  5.45 us
  transfers between devices with their start and end apart: 29, of which 19 were waited for; matrix products, arithmetic and copies ran while one was open for 1% of the time, Pallas kernels for 5%

profile of v15, /device:TPU:1, one launch (start us, length us, event | category | flops | bytes accessed | tf_op | source)
XLA Modules:
  0.0 118.3 jit_solution(14936919024147059470)
XLA Ops:
  0.0 3.2 %collective-permute-start.3 = (bf16[128,512]{1,0:T(8,128)(2,1)}, bf16[128,512]{1,0:T(8,128)(2,1)S(1)}, u32[]{:S(2)}, u32[]{:S(2)}) collective-permute-start(bf16[128,512]{1,0:T(8,128)(2,1)} %refs_0_.1), channel_id=1, source_target_pairs={{0,32},{32,0},{1,33},{33,1},{2,34},{34,2},{3,35},{35,3},{4,36},{36... | collective-permute-start | bytes 393224 | tf_op jit(solution)/shard_map/ppermute | solution.py:39
  9.7 5.5 %collective-permute-done.refs_0_ = bf16[128,512]{1,0:T(8,128)(2,1)S(1)} collective-permute-done((bf16[128,512]{1,0:T(8,128)(2,1)}, bf16[128,512]{1,0:T(8,128)(2,1)S(1)}, u32[]{:S(2)}, u32[]{:S(2)}) %collective-permute-start) | collective-permute-done | bytes 131104 | tf_op jit(solution)/shard_map/ppermute | solution.py:39
  19.8 5.6 %all-to-all-start = ((bf16[16,64,128]{2,1,0:T(8,128)(2,1)}), bf16[16,64,128]{2,1,0:T(8,128)(2,1)S(1)}, u32[]{:S(2)}, u32[]{:S(2)}) async-start(bf16[16,64,128]{2,1,0:T(8,128)(2,1)} %shard_map.50), calls=%async_computation | async-start | bytes 524288 | tf_op jit(solution)/shard_map/all_to_all | solution.py:258
  25.6 2.7 %shard_map.47 = (bf16[4,64,1024]{2,1,0:T(8,128)(2,1)S(1)}, bf16[4,64,1024]{2,1,0:T(8,128)(2,1)}, bf16[4,64,1024]{2,1,0:T(8,128)(2,1)}, bf16[4,64,1024]{2,1,0:T(8,128)(2,1)}) custom-call(s32[4]{0:T(128)S(1)} %pad_add_fusion.place, bf16[128,512]{1,0:T(8,128)(2,1)S(1)} %collective-permute-done.refs_0_, bf16[128,512]{1,0:T(8,128)(2,1)S(1)} %collective-permute-done.1.refs_1_, ...), custom_call_target="tpu_custom_call" | custom-call | tf_op jit(solution)/shard_map/pallas_call | solution.py:195
  28.3 2.6 %collective-permute-start.7 = (bf16[4,64,1024]{2,1,0:T(8,128)(2,1)}, bf16[4,64,1024]{2,1,0:T(8,128)(2,1)S(1)}, u32[]{:S(2)}, u32[]{:S(2)}) collective-permute-start(bf16[4,64,1024]{2,1,0:T(8,128)(2,1)} %get-tuple-element.37), channel_id=1, source_target_pairs={{0,3},{1,2},{2,1},{3,0},{4,7},{5,6},{6,5},{7,4},{8,11},{9,10},{10,... | collective-permute-start | bytes 1572872 | tf_op jit(solution)/shard_map/ppermute | solution.py:50
  33.7 5.3 %collective-permute-start.14 = (bf16[64,128]{1,0:T(8,128)(2,1)S(1)}, bf16[64,128]{1,0:T(8,128)(2,1)S(1)}, u32[]{:S(2)}, u32[]{:S(2)}) collective-permute-start(bf16[64,128]{1,0:T(8,128)(2,1)S(1)} %shard_map.51), channel_id=1, source_target_pairs={{0,0},{32,64},{64,128},{96,192},{128,32},{160,96},{192,160},{224,2... | collective-permute-start | bytes 49160 | tf_op jit(solution)/shard_map/ppermute | solution.py:262
  39.0 5.9 %collective-permute-start.15 = (bf16[64,128]{1,0:T(8,128)(2,1)S(1)}, bf16[64,128]{1,0:T(8,128)(2,1)S(1)}, u32[]{:S(2)}, u32[]{:S(2)}) collective-permute-start(bf16[64,128]{1,0:T(8,128)(2,1)S(1)} %shard_map.51), channel_id=1, source_target_pairs={{0,16},{16,0},{32,80},{48,64},{64,144},{80,128},{96,208},{112,192}... | collective-permute-start | bytes 49160 | tf_op jit(solution)/shard_map/ppermute | solution.py:263
  46.6 5.4 %all-to-all-start.1 = ((bf16[16,64,128]{2,1,0:T(8,128)(2,1)}), bf16[16,64,128]{2,1,0:T(8,128)(2,1)S(1)}, u32[]{:S(2)}, u32[]{:S(2)}) async-start(bf16[16,64,128]{2,1,0:T(8,128)(2,1)} %shard_map.52), calls=%async_computation.1 | async-start | bytes 524288 | tf_op jit(solution)/shard_map/all_to_all | solution.py:275
  52.9 2.7 %collective-permute-start.10 = (bf16[64,1024]{1,0:T(8,128)(2,1)S(1)}, bf16[64,1024]{1,0:T(8,128)(2,1)S(1)}, u32[]{:S(2)}, u32[]{:S(2)}) collective-permute-start(bf16[64,1024]{1,0:T(8,128)(2,1)S(1)} %get-tuple-element.41), channel_id=1, source_target_pairs={{0,12},{1,13},{2,14},{3,15},{4,8},{5,9},{6,10},{7,11},{8,4},{9,5},... | collective-permute-start | bytes 393224 | tf_op jit(solution)/shard_map/ppermute | solution.py:50
  56.9 3.4 %all-to-all-done.1 = bf16[16,64,128]{2,1,0:T(8,128)(2,1)S(1)} async-done(((bf16[16,64,128]{2,1,0:T(8,128)(2,1)}), bf16[16,64,128]{2,1,0:T(8,128)(2,1)S(1)}, u32[]{:S(2)}, u32[]{:S(2)}) %all-to-all-start.1) | async-done | bytes 262176 | tf_op jit(solution)/shard_map/all_to_all | solution.py:275
  61.3 5.9 %collective-permute-start.13 = (bf16[64,1024]{1,0:T(8,128)(2,1)S(1)}, bf16[64,1024]{1,0:T(8,128)(2,1)S(1)}, u32[]{:S(2)}, u32[]{:S(2)}) collective-permute-start(bf16[64,1024]{1,0:T(8,128)(2,1)S(1)} %shard_map.49.own), channel_id=1, source_target_pairs={{0,16},{16,0},{1,17},{17,1},{2,18},{18,2},{3,19},{19,3},{4,20},{20... | collective-permute-start | bytes 393224 | tf_op jit(solution)/shard_map/ppermute | solution.py:39
  67.3 2.2 %collective-permute-done.13.got = bf16[64,1024]{1,0:T(8,128)(2,1)S(1)} collective-permute-done((bf16[64,1024]{1,0:T(8,128)(2,1)S(1)}, bf16[64,1024]{1,0:T(8,128)(2,1)S(1)}, u32[]{:S(2)}, u32[]{:S(2)}) %collective-permute-start.13) | collective-permute-done | bytes 131104 | tf_op jit(solution)/shard_map/ppermute | solution.py:39
  69.5 1.6 %shard_map.53.refs_0_ = bf16[64,1024]{1,0:T(8,128)(2,1)S(1)} custom-call(s32[10]{0:T(128)S(1)} %stack.63.base, bf16[64,1024]{1,0:T(8,128)(2,1)S(1)} %shard_map.49.own, bf16[64,1024]{1,0:T(8,128)(2,1)S(1)} %collective-permute-done.13.got, f32[64,128]{1,0:T(8,128)S(1)} %get-tuple-element.68.cosine, f32[64,128]{1,0:T(8,128)S(1)} %get-tuple-element.69.sine_v, ...), custom_call_target="tpu_custom_call" | custom-call | tf_op jit(solution)/shard_map/pallas_call | solution.py:195
  71.1 3.6 %collective-permute-start.17 = (bf16[64,1024]{1,0:T(8,128)(2,1)S(1)}, bf16[64,1024]{1,0:T(8,128)(2,1)S(1)}, u32[]{:S(2)}, u32[]{:S(2)}) collective-permute-start(bf16[64,1024]{1,0:T(8,128)(2,1)S(1)} %shard_map.53.refs_0_), channel_id=1, source_target_pairs={{0,3},{1,2},{2,1},{3,0},{4,7},{5,6},{6,5},{7,4},{8,11},{9,10},{10,... | collective-permute-start | bytes 393224 | tf_op jit(solution)/shard_map/ppermute | solution.py:50
  78.5 1.5 %collective-permute-done.19.refs_3_ = bf16[64,1024]{1,0:T(8,128)(2,1)S(1)} collective-permute-done((bf16[64,1024]{1,0:T(8,128)(2,1)S(1)}, bf16[64,1024]{1,0:T(8,128)(2,1)S(1)}, u32[]{:S(2)}, u32[]{:S(2)}) %collective-permute-start.19) | collective-permute-done | bytes 131104 | tf_op jit(solution)/shard_map/ppermute | solution.py:50
  80.0 2.3 %collective-permute-start.20 = (bf16[4,64,1024]{2,1,0:T(8,128)(2,1)S(1)}, bf16[4,64,1024]{2,1,0:T(8,128)(2,1)S(1)}, u32[]{:S(2)}, u32[]{:S(2)}) collective-permute-start(bf16[4,64,1024]{2,1,0:T(8,128)(2,1)S(1)} %shard_map.54.line), channel_id=1, source_target_pairs={{0,12},{1,13},{2,14},{3,15},{4,8},{5,9},{6,10},{7,11},{8,4},{9,5},... | collective-permute-start | bytes 1572872 | tf_op jit(solution)/shard_map/ppermute | solution.py:50
  82.4 1.6 %collective-permute-start.22 = (bf16[4,64,1024]{2,1,0:T(8,128)(2,1)S(1)}, bf16[4,64,1024]{2,1,0:T(8,128)(2,1)S(1)}, u32[]{:S(2)}, u32[]{:S(2)}) collective-permute-start(bf16[4,64,1024]{2,1,0:T(8,128)(2,1)S(1)} %shard_map.54.line), channel_id=1, source_target_pairs={{0,8},{1,9},{2,10},{3,11},{4,12},{5,13},{6,14},{7,15},{8,0},{9,1},... | collective-permute-start | bytes 1572872 | tf_op jit(solution)/shard_map/ppermute | solution.py:50
  84.4 5.5 %collective-permute-done.20.line = bf16[4,64,1024]{2,1,0:T(8,128)(2,1)S(1)} collective-permute-done((bf16[4,64,1024]{2,1,0:T(8,128)(2,1)S(1)}, bf16[4,64,1024]{2,1,0:T(8,128)(2,1)S(1)}, u32[]{:S(2)}, u32[]{:S(2)}) %collective-permute-start.20) | collective-permute-done | bytes 524320 | tf_op jit(solution)/shard_map/ppermute | solution.py:50
  91.1 5.3 %collective-permute-done.22.refs_3_ = bf16[4,64,1024]{2,1,0:T(8,128)(2,1)S(1)} collective-permute-done((bf16[4,64,1024]{2,1,0:T(8,128)(2,1)S(1)}, bf16[4,64,1024]{2,1,0:T(8,128)(2,1)S(1)}, u32[]{:S(2)}, u32[]{:S(2)}) %collective-permute-start.22) | collective-permute-done | bytes 524320 | tf_op jit(solution)/shard_map/ppermute | solution.py:50
  97.5 6.0 %collective-permute-start.23 = (bf16[512,512]{1,0:T(8,128)(2,1)S(1)}, bf16[512,512]{1,0:T(8,128)(2,1)S(1)}, u32[]{:S(2)}, u32[]{:S(2)}) collective-permute-start(bf16[512,512]{1,0:T(8,128)(2,1)S(1)} %bitcast.20), channel_id=1, source_target_pairs={{0,32},{32,0},{1,33},{33,1},{2,34},{34,2},{3,35},{35,3},{4,36},{36... | collective-permute-start | bytes 1572872 | tf_op jit(solution)/shard_map/ppermute | solution.py:39
  103.5 1.5 %collective-permute-done.23.got = bf16[512,512]{1,0:T(8,128)(2,1)S(1)} collective-permute-done((bf16[512,512]{1,0:T(8,128)(2,1)S(1)}, bf16[512,512]{1,0:T(8,128)(2,1)S(1)}, u32[]{:S(2)}, u32[]{:S(2)}) %collective-permute-start.23) | collective-permute-done | bytes 524320 | tf_op jit(solution)/shard_map/ppermute | solution.py:39
  105.1 2.8 %collective-permute-start.24 = (bf16[128,512]{1,0:T(8,128)(2,1)S(1)}, bf16[128,512]{1,0:T(8,128)(2,1)S(1)}, u32[]{:S(2)}, u32[]{:S(2)}) collective-permute-start(bf16[128,512]{1,0:T(8,128)(2,1)S(1)} %get-tuple-element.54), channel_id=1, source_target_pairs={{0,128},{64,192},{128,0},{192,64},{1,129},{65,193},{129,1},{193,65... | collective-permute-start | bytes 393224 | tf_op jit(solution)/shard_map/ppermute | solution.py:39
  107.9 1.8 %collective-permute-start.25 = (bf16[128,512]{1,0:T(8,128)(2,1)S(1)}, bf16[128,512]{1,0:T(8,128)(2,1)S(1)}, u32[]{:S(2)}, u32[]{:S(2)}) collective-permute-start(bf16[128,512]{1,0:T(8,128)(2,1)S(1)} %get-tuple-element.55), channel_id=1, source_target_pairs={{0,192},{64,128},{128,64},{192,0},{1,193},{65,129},{129,65},{193,1... | collective-permute-start | bytes 393224 | tf_op jit(solution)/shard_map/ppermute | solution.py:39
  109.7 7.2 %collective-permute-done.24.b = bf16[128,512]{1,0:T(8,128)(2,1)S(1)} collective-permute-done((bf16[128,512]{1,0:T(8,128)(2,1)S(1)}, bf16[128,512]{1,0:T(8,128)(2,1)S(1)}, u32[]{:S(2)}, u32[]{:S(2)}) %collective-permute-start.24) | collective-permute-done | bytes 131104 | tf_op jit(solution)/shard_map/ppermute | solution.py:39
  (69 shorter events, 27.0 us)
Async XLA Ops:
  0.0 6.1 %collective-permute-start.3 = (bf16[128,512]{1,0:T(8,128)(2,1)}, bf16[128,512]{1,0:T(8,128)(2,1)S(1)}, u32[]{:S(2)}, u32[]{:S(2)}) collective-permute-start(bf16[128,512]{1,0:T(8,128)(2,1)} %refs_0_.1), channel_id=1, source_target_pairs={{0,32},{32,0},{1,33},{33,1},{2,34},{34,2},{3,35},{35,3},{4,36},{36... | collective-permute-start | bytes 393224 | tf_op jit(solution)/shard_map/ppermute | solution.py:39
  3.2 11.9 %collective-permute-start = (bf16[128,512]{1,0:T(8,128)(2,1)}, bf16[128,512]{1,0:T(8,128)(2,1)S(1)}, u32[]{:S(2)}, u32[]{:S(2)}) collective-permute-start(bf16[128,512]{1,0:T(8,128)(2,1)} %refs_0_.1), channel_id=1, source_target_pairs={{0,128},{64,192},{128,0},{192,64},{1,129},{65,193},{129,1},{193,65... | collective-permute-start | bytes 393224 | tf_op jit(solution)/shard_map/ppermute | solution.py:39
  4.5 10.7 %collective-permute-start.1 = (bf16[128,512]{1,0:T(8,128)(2,1)}, bf16[128,512]{1,0:T(8,128)(2,1)S(1)}, u32[]{:S(2)}, u32[]{:S(2)}) collective-permute-start(bf16[128,512]{1,0:T(8,128)(2,1)} %refs_0_.1), channel_id=1, source_target_pairs={{0,192},{64,128},{128,64},{192,0},{1,193},{65,129},{129,65},{193,1... | collective-permute-start | bytes 393224 | tf_op jit(solution)/shard_map/ppermute | solution.py:39
  5.9 10.2 %collective-permute-start.2 = (bf16[128,512]{1,0:T(8,128)(2,1)}, bf16[128,512]{1,0:T(8,128)(2,1)S(1)}, u32[]{:S(2)}, u32[]{:S(2)}) collective-permute-start(bf16[128,512]{1,0:T(8,128)(2,1)} %refs_0_.1), channel_id=1, source_target_pairs={{0,64},{64,0},{128,192},{192,128},{1,65},{65,1},{129,193},{193,129... | collective-permute-start | bytes 393224 | tf_op jit(solution)/shard_map/ppermute | solution.py:39
  19.8 13.8 %all-to-all-start = ((bf16[16,64,128]{2,1,0:T(8,128)(2,1)}), bf16[16,64,128]{2,1,0:T(8,128)(2,1)S(1)}, u32[]{:S(2)}, u32[]{:S(2)}) async-start(bf16[16,64,128]{2,1,0:T(8,128)(2,1)} %shard_map.50), calls=%async_computation | async-start | bytes 524288 | tf_op jit(solution)/shard_map/all_to_all | solution.py:258
  28.3 23.8 %collective-permute-start.7 = (bf16[4,64,1024]{2,1,0:T(8,128)(2,1)}, bf16[4,64,1024]{2,1,0:T(8,128)(2,1)S(1)}, u32[]{:S(2)}, u32[]{:S(2)}) collective-permute-start(bf16[4,64,1024]{2,1,0:T(8,128)(2,1)} %get-tuple-element.37), channel_id=1, source_target_pairs={{0,3},{1,2},{2,1},{3,0},{4,7},{5,6},{6,5},{7,4},{8,11},{9,10},{10,... | collective-permute-start | bytes 1572872 | tf_op jit(solution)/shard_map/ppermute | solution.py:50
  30.9 21.2 %collective-permute-start.8 = (bf16[4,64,1024]{2,1,0:T(8,128)(2,1)}, bf16[4,64,1024]{2,1,0:T(8,128)(2,1)S(1)}, u32[]{:S(2)}, u32[]{:S(2)}) collective-permute-start(bf16[4,64,1024]{2,1,0:T(8,128)(2,1)} %get-tuple-element.38), channel_id=1, source_target_pairs={{0,1},{1,0},{2,3},{3,2},{4,5},{5,4},{6,7},{7,6},{8,9},{9,8},{10,11... | collective-permute-start | bytes 1572872 | tf_op jit(solution)/shard_map/ppermute | solution.py:50
  30.9 21.2 %collective-permute-start.9 = (bf16[4,64,1024]{2,1,0:T(8,128)(2,1)}, bf16[4,64,1024]{2,1,0:T(8,128)(2,1)S(1)}, u32[]{:S(2)}, u32[]{:S(2)}) collective-permute-start(bf16[4,64,1024]{2,1,0:T(8,128)(2,1)} %get-tuple-element.39), channel_id=1, source_target_pairs={{0,2},{1,3},{2,0},{3,1},{4,6},{5,7},{6,4},{7,5},{8,10},{9,11},{10,... | collective-permute-start | bytes 1572872 | tf_op jit(solution)/shard_map/ppermute | solution.py:50
  33.7 11.3 %collective-permute-start.14 = (bf16[64,128]{1,0:T(8,128)(2,1)S(1)}, bf16[64,128]{1,0:T(8,128)(2,1)S(1)}, u32[]{:S(2)}, u32[]{:S(2)}) collective-permute-start(bf16[64,128]{1,0:T(8,128)(2,1)S(1)} %shard_map.51), channel_id=1, source_target_pairs={{0,0},{32,64},{64,128},{96,192},{128,32},{160,96},{192,160},{224,2... | collective-permute-start | bytes 49160 | tf_op jit(solution)/shard_map/ppermute | solution.py:262
  39.0 6.8 %collective-permute-start.15 = (bf16[64,128]{1,0:T(8,128)(2,1)S(1)}, bf16[64,128]{1,0:T(8,128)(2,1)S(1)}, u32[]{:S(2)}, u32[]{:S(2)}) collective-permute-start(bf16[64,128]{1,0:T(8,128)(2,1)S(1)} %shard_map.51), channel_id=1, source_target_pairs={{0,16},{16,0},{32,80},{48,64},{64,144},{80,128},{96,208},{112,192}... | collective-permute-start | bytes 49160 | tf_op jit(solution)/shard_map/ppermute | solution.py:263
  46.6 13.6 %all-to-all-start.1 = ((bf16[16,64,128]{2,1,0:T(8,128)(2,1)}), bf16[16,64,128]{2,1,0:T(8,128)(2,1)S(1)}, u32[]{:S(2)}, u32[]{:S(2)}) async-start(bf16[16,64,128]{2,1,0:T(8,128)(2,1)} %shard_map.52), calls=%async_computation.1 | async-start | bytes 524288 | tf_op jit(solution)/shard_map/all_to_all | solution.py:275
  52.9 7.3 %collective-permute-start.10 = (bf16[64,1024]{1,0:T(8,128)(2,1)S(1)}, bf16[64,1024]{1,0:T(8,128)(2,1)S(1)}, u32[]{:S(2)}, u32[]{:S(2)}) collective-permute-start(bf16[64,1024]{1,0:T(8,128)(2,1)S(1)} %get-tuple-element.41), channel_id=1, source_target_pairs={{0,12},{1,13},{2,14},{3,15},{4,8},{5,9},{6,10},{7,11},{8,4},{9,5},... | collective-permute-start | bytes 393224 | tf_op jit(solution)/shard_map/ppermute | solution.py:50
  55.6 5.6 %collective-permute-start.12 = (bf16[64,1024]{1,0:T(8,128)(2,1)S(1)}, bf16[64,1024]{1,0:T(8,128)(2,1)S(1)}, u32[]{:S(2)}, u32[]{:S(2)}) collective-permute-start(bf16[64,1024]{1,0:T(8,128)(2,1)S(1)} %get-tuple-element.43), channel_id=1, source_target_pairs={{0,8},{1,9},{2,10},{3,11},{4,12},{5,13},{6,14},{7,15},{8,0},{9,1},... | collective-permute-start | bytes 393224 | tf_op jit(solution)/shard_map/ppermute | solution.py:50
  60.3 7.1 %collective-permute-start.16 = (bf16[1024,128]{1,0:T(8,128)(2,1)S(1)}, bf16[1024,128]{1,0:T(8,128)(2,1)S(1)}, u32[]{:S(2)}, u32[]{:S(2)}) collective-permute-start(bf16[1024,128]{1,0:T(8,128)(2,1)S(1)} %bitcast.17), channel_id=1, source_target_pairs={{0,32},{32,0},{1,33},{33,1},{2,34},{34,2},{3,35},{35,3},{4,36},{36... | collective-permute-start | bytes 786440 | tf_op jit(solution)/shard_map/ppermute | solution.py:39
  61.3 8.2 %collective-permute-start.13 = (bf16[64,1024]{1,0:T(8,128)(2,1)S(1)}, bf16[64,1024]{1,0:T(8,128)(2,1)S(1)}, u32[]{:S(2)}, u32[]{:S(2)}) collective-permute-start(bf16[64,1024]{1,0:T(8,128)(2,1)S(1)} %shard_map.49.own), channel_id=1, source_target_pairs={{0,16},{16,0},{1,17},{17,1},{2,18},{18,2},{3,19},{19,3},{4,20},{20... | collective-permute-start | bytes 393224 | tf_op jit(solution)/shard_map/ppermute | solution.py:39
  71.1 6.0 %collective-permute-start.17 = (bf16[64,1024]{1,0:T(8,128)(2,1)S(1)}, bf16[64,1024]{1,0:T(8,128)(2,1)S(1)}, u32[]{:S(2)}, u32[]{:S(2)}) collective-permute-start(bf16[64,1024]{1,0:T(8,128)(2,1)S(1)} %shard_map.53.refs_0_), channel_id=1, source_target_pairs={{0,3},{1,2},{2,1},{3,0},{4,7},{5,6},{6,5},{7,4},{8,11},{9,10},{10,... | collective-permute-start | bytes 393224 | tf_op jit(solution)/shard_map/ppermute | solution.py:50
  74.7 5.3 %collective-permute-start.19 = (bf16[64,1024]{1,0:T(8,128)(2,1)S(1)}, bf16[64,1024]{1,0:T(8,128)(2,1)S(1)}, u32[]{:S(2)}, u32[]{:S(2)}) collective-permute-start(bf16[64,1024]{1,0:T(8,128)(2,1)S(1)} %shard_map.53.refs_0_), channel_id=1, source_target_pairs={{0,2},{1,3},{2,0},{3,1},{4,6},{5,7},{6,4},{7,5},{8,10},{9,11},{10,... | collective-permute-start | bytes 393224 | tf_op jit(solution)/shard_map/ppermute | solution.py:50
  80.0 9.9 %collective-permute-start.20 = (bf16[4,64,1024]{2,1,0:T(8,128)(2,1)S(1)}, bf16[4,64,1024]{2,1,0:T(8,128)(2,1)S(1)}, u32[]{:S(2)}, u32[]{:S(2)}) collective-permute-start(bf16[4,64,1024]{2,1,0:T(8,128)(2,1)S(1)} %shard_map.54.line), channel_id=1, source_target_pairs={{0,12},{1,13},{2,14},{3,15},{4,8},{5,9},{6,10},{7,11},{8,4},{9,5},... | collective-permute-start | bytes 1572872 | tf_op jit(solution)/shard_map/ppermute | solution.py:50
  82.4 8.3 %collective-permute-start.21 = (bf16[4,64,1024]{2,1,0:T(8,128)(2,1)S(1)}, bf16[4,64,1024]{2,1,0:T(8,128)(2,1)S(1)}, u32[]{:S(2)}, u32[]{:S(2)}) collective-permute-start(bf16[4,64,1024]{2,1,0:T(8,128)(2,1)S(1)} %shard_map.54.line), channel_id=1, source_target_pairs={{0,4},{1,5},{2,6},{3,7},{4,0},{5,1},{6,2},{7,3},{8,12},{9,13},{10,... | collective-permute-start | bytes 1572872 | tf_op jit(solution)/shard_map/ppermute | solution.py:50
  82.4 14.1 %collective-permute-start.22 = (bf16[4,64,1024]{2,1,0:T(8,128)(2,1)S(1)}, bf16[4,64,1024]{2,1,0:T(8,128)(2,1)S(1)}, u32[]{:S(2)}, u32[]{:S(2)}) collective-permute-start(bf16[4,64,1024]{2,1,0:T(8,128)(2,1)S(1)} %shard_map.54.line), channel_id=1, source_target_pairs={{0,8},{1,9},{2,10},{3,11},{4,12},{5,13},{6,14},{7,15},{8,0},{9,1},... | collective-permute-start | bytes 1572872 | tf_op jit(solution)/shard_map/ppermute | solution.py:50
  97.5 7.5 %collective-permute-start.23 = (bf16[512,512]{1,0:T(8,128)(2,1)S(1)}, bf16[512,512]{1,0:T(8,128)(2,1)S(1)}, u32[]{:S(2)}, u32[]{:S(2)}) collective-permute-start(bf16[512,512]{1,0:T(8,128)(2,1)S(1)} %bitcast.20), channel_id=1, source_target_pairs={{0,32},{32,0},{1,33},{33,1},{2,34},{34,2},{3,35},{35,3},{4,36},{36... | collective-permute-start | bytes 1572872 | tf_op jit(solution)/shard_map/ppermute | solution.py:39
  105.1 11.8 %collective-permute-start.24 = (bf16[128,512]{1,0:T(8,128)(2,1)S(1)}, bf16[128,512]{1,0:T(8,128)(2,1)S(1)}, u32[]{:S(2)}, u32[]{:S(2)}) collective-permute-start(bf16[128,512]{1,0:T(8,128)(2,1)S(1)} %get-tuple-element.54), channel_id=1, source_target_pairs={{0,128},{64,192},{128,0},{192,64},{1,129},{65,193},{129,1},{193,65... | collective-permute-start | bytes 393224 | tf_op jit(solution)/shard_map/ppermute | solution.py:39
  107.9 9.0 %collective-permute-start.25 = (bf16[128,512]{1,0:T(8,128)(2,1)S(1)}, bf16[128,512]{1,0:T(8,128)(2,1)S(1)}, u32[]{:S(2)}, u32[]{:S(2)}) collective-permute-start(bf16[128,512]{1,0:T(8,128)(2,1)S(1)} %get-tuple-element.55), channel_id=1, source_target_pairs={{0,192},{64,128},{128,64},{192,0},{1,193},{65,129},{129,65},{193,1... | collective-permute-start | bytes 393224 | tf_op jit(solution)/shard_map/ppermute | solution.py:39
  109.7 7.9 %collective-permute-start.26 = (bf16[128,512]{1,0:T(8,128)(2,1)S(1)}, bf16[128,512]{1,0:T(8,128)(2,1)S(1)}, u32[]{:S(2)}, u32[]{:S(2)}) collective-permute-start(bf16[128,512]{1,0:T(8,128)(2,1)S(1)} %get-tuple-element.56), channel_id=1, source_target_pairs={{0,64},{64,0},{128,192},{192,128},{1,65},{65,1},{129,193},{193,129... | collective-permute-start | bytes 393224 | tf_op jit(solution)/shard_map/ppermute | solution.py:39
  (11 other events, 58.7 us)
